TPU v7x, 32 devices: a whole 2x2x4 slice. The times are simulated.
32 devices in a mesh: fsdp: 8 (over z, y), tensor: 4 (over x, core).
Axes of the slice: x: 2, y: 2, z: 4, core: 2. Of those that a mesh axis runs over, the one named last changes fastest.
Arguments:
- block_input: float32 [1376, 8, 1024], P('tensor', 'fsdp'), may hold values from -30 to 30
- live_mask: int32 [1376, 8], P(None, 'fsdp'), may hold values from 0 to 1, as said below
- cotangent: float32 [1376, 8, 1024], P('tensor', 'fsdp'), may hold values from -6 to 6
- project_in: float32 [1024, 3, 1024], P('fsdp', None, 'tensor'), may hold values from -4 to 4
- project_out: float32 [1024, 1024], P('tensor', 'fsdp'), may hold values from -3 to 3
- expand: float32 [1024, 4096], P('fsdp', 'tensor'), may hold values from -0.1875 to 0.1875
- contract: float32 [4096, 1024], P('tensor', 'fsdp'), may hold values from -0.09375 to 0.09375
- vectors: float32 [10, 1024], P(None, 'fsdp'), may hold values from -2 to 2
- expand_bias: float32 [4096], P('fsdp'), may hold values from -1.8 to 1.8
- moment_project_in: float32 [1024, 3, 1024], P('fsdp', None, 'tensor'), may hold values from -112 to 112
- second_project_in: float32 [1024, 3, 1024], P('fsdp', None, 'tensor'), may hold values from 4.5 to 22.5
- moment_project_out: float32 [1024, 1024], P('tensor', 'fsdp'), may hold values from -6 to 6
- second_project_out: float32 [1024, 1024], P('tensor', 'fsdp'), may hold values from 0.02 to 0.1
- moment_expand: float32 [1024, 4096], P('fsdp', 'tensor'), may hold values from -40 to 40
- second_expand: float32 [1024, 4096], P('fsdp', 'tensor'), may hold values from 0.72 to 3.6
- moment_contract: float32 [4096, 1024], P('tensor', 'fsdp'), may hold values from -96 to 96
- second_contract: float32 [4096, 1024], P('tensor', 'fsdp'), may hold values from 3 to 15
- moment_vectors: float32 [10, 1024], P(None, 'fsdp'), may hold values from -128 to 128
- second_vectors: float32 [10, 1024], P(None, 'fsdp'), may hold values from 8 to 40
- moment_expand_bias: float32 [4096], P('fsdp'), may hold values from -40 to 40
- second_expand_bias: float32 [4096], P('fsdp'), may hold values from 0.72 to 3.6
Outputs:
- block_output: float32 [1376, 8, 1024], P('tensor', 'fsdp')
- input_grad: float32 [1376, 8, 1024], P('tensor', 'fsdp')
- grad_project_in: float32 [1024, 3, 1024], P('fsdp', None, 'tensor')
- grad_project_out: float32 [1024, 1024], P('tensor', 'fsdp')
- grad_expand: float32 [1024, 4096], P('fsdp', 'tensor')
- grad_contract: float32 [4096, 1024], P('tensor', 'fsdp')
- grad_vectors: float32 [10, 1024], P(None, 'fsdp')
- grad_expand_bias: float32 [4096], P('fsdp')
- new_project_in: float32 [1024, 3, 1024], P('fsdp', None, 'tensor')
- update_project_out: float32 [1024, 1024], P('tensor', 'fsdp')
- new_expand: float32 [1024, 4096], P('fsdp', 'tensor')
- new_contract: float32 [4096, 1024], P('tensor', 'fsdp')
- update_vectors: float32 [10, 1024], P(None, 'fsdp')
- update_expand_bias: float32 [4096], P('fsdp')
- new_moment_project_in: float32 [1024, 3, 1024], P('fsdp', None, 'tensor')
- new_second_project_in: float32 [1024, 3, 1024], P('fsdp', None, 'tensor')
- new_moment_project_out: float32 [1024, 1024], P('tensor', 'fsdp')
- new_second_project_out: float32 [1024, 1024], P('tensor', 'fsdp')
- new_moment_expand: float32 [1024, 4096], P('fsdp', 'tensor')
- new_second_expand: float32 [1024, 4096], P('fsdp', 'tensor')
- new_moment_contract: float32 [4096, 1024], P('tensor', 'fsdp')
- new_second_contract: float32 [4096, 1024], P('tensor', 'fsdp')
- new_moment_vectors: float32 [10, 1024], P(None, 'fsdp')
- new_second_vectors: float32 [10, 1024], P(None, 'fsdp')
- new_moment_expand_bias: float32 [4096], P('fsdp')
- new_second_expand_bias: float32 [4096], P('fsdp')
- shift_gradient: float32 [1024], P('fsdp')
Inputs may be any that keep to these rules, and one draw needn't show every extreme that they name: `live_mask`: 1 marks a real token, 0 a pad token; in every image the pad tokens are its last 1 to 8 positions, and the first image has exactly 8.
All inputs are finite; a program needn't handle non-finite values.
Results may differ from a plain program's by a relative error of at most 0.023.
Values may be sent and summed in bfloat16 or wider, within the bound.
No kernel may reach another device: no remote copies, remote signals or barrier semaphores. Data moves between devices by JAX's collectives and lax.ppermute only.
A program may use at most 128 MiB of HBM per device.

v0:
```python
import jax
import jax.numpy as jnp
from jax import lax
from jax.sharding import PartitionSpec as P

HEAD_DIM = 64
STEP = 3


NORM_EPS = 1e-06
BETA_FIRST = 0.9
BETA_SECOND = 0.999
LEARN_RATE = 0.004
WEIGHT_DECAY = 0.04
ADAM_EPS = 1e-08
MASKED_SCORE = -1e30
ROOT_HALF = 0.7071067811865476
DENSITY_NORM = 0.3989422804014327


def norm_forward(values, norm_gain, norm_shift):
    center = jnp.mean(values, axis=-1, keepdims=True)
    offset = values - center
    spread = jnp.mean(offset * offset, axis=-1, keepdims=True)
    inverse = lax.rsqrt(spread + NORM_EPS)
    scaled = offset * inverse
    return (scaled, inverse, scaled * norm_gain + norm_shift)


def norm_backward(scaled, inverse, grad_normed, norm_gain):
    grad_scaled = grad_normed * norm_gain
    first_mean = jnp.mean(grad_scaled, axis=-1, keepdims=True)
    second_mean = jnp.mean(grad_scaled * scaled, axis=-1, keepdims=True)
    return inverse * (grad_scaled - first_mean - scaled * second_mean)


def gelu_parts(hidden):
    normal_cdf = 0.5 * (1.0 + lax.erf(hidden * ROOT_HALF))
    density = DENSITY_NORM * jnp.exp(-0.5 * hidden * hidden)
    return (hidden * normal_cdf, normal_cdf + hidden * density)


def head_scores(queries, key_rows, usable):
    scores = jnp.dot(queries, key_rows.T, preferred_element_type=jnp.float32) * HEAD_DIM ** (-0.5)
    return jnp.where(usable[None, :], scores, MASKED_SCORE)


def head_forward(inputs):
    queries, key_rows, value_rows, usable = inputs
    scores = head_scores(queries, key_rows, usable)
    highest = jnp.max(scores, axis=-1, keepdims=True)
    summed = jnp.sum(jnp.exp(scores - highest), axis=-1, keepdims=True)
    log_total = highest + jnp.log(summed)
    weights = jnp.exp(scores - log_total).astype(jnp.bfloat16)
    output = jnp.dot(weights, value_rows, preferred_element_type=jnp.float32)
    return (output.astype(jnp.bfloat16), log_total[:, 0])


def head_backward(inputs):
    queries, key_rows, value_rows, usable, log_total, grad_output = inputs
    scores = head_scores(queries, key_rows, usable)
    weights = jnp.exp(scores - log_total[:, None])
    grad_values = jnp.dot(
        weights.astype(jnp.bfloat16).T, grad_output, preferred_element_type=jnp.float32
    )
    grad_weights = jnp.dot(grad_output, value_rows.T, preferred_element_type=jnp.float32)
    row_inner = jnp.sum(weights * grad_weights, axis=-1, keepdims=True)
    grad_scores = (weights * (grad_weights - row_inner)).astype(jnp.bfloat16)
    score_scale = HEAD_DIM ** (-0.5)
    grad_queries = jnp.dot(grad_scores, key_rows, preferred_element_type=jnp.float32) * score_scale
    grad_keys = jnp.dot(grad_scores.T, queries, preferred_element_type=jnp.float32) * score_scale
    return (
        grad_queries.astype(jnp.bfloat16),
        grad_keys.astype(jnp.bfloat16),
        grad_values.astype(jnp.bfloat16),
    )


def split_heads(stacked, heads_here):
    seq_len, images, features = stacked.shape
    head_dim = features // heads_here
    moved = stacked.reshape(seq_len, images, heads_here, head_dim).transpose(1, 2, 0, 3)
    return moved.reshape(images * heads_here, seq_len, head_dim)


def merge_heads(stacked, images):
    groups, seq_len, head_dim = stacked.shape
    heads_here = groups // images
    moved = stacked.reshape(images, heads_here, seq_len, head_dim).transpose(2, 0, 1, 3)
    return moved.reshape(seq_len, images, heads_here * head_dim)


def gather_weights(masters):
    copies = tuple((master.astype(jnp.bfloat16) for master in masters))
    return (
        lax.all_gather(copies[0], "fsdp", axis=0, tiled=True),
        lax.all_gather(copies[1], "fsdp", axis=1, tiled=True),
        lax.all_gather(copies[2], "fsdp", axis=0, tiled=True),
        lax.all_gather(copies[3], "fsdp", axis=1, tiled=True),
        lax.all_gather(copies[4], "fsdp", axis=1, tiled=True),
        lax.all_gather(copies[5], "fsdp", axis=0, tiled=True),
    )


def adam_step(master, gradient, first, second, decay):
    first_new = BETA_FIRST * first + (1.0 - BETA_FIRST) * gradient
    second_new = BETA_SECOND * second + (1.0 - BETA_SECOND) * gradient * gradient
    first_hat = first_new / (1.0 - BETA_FIRST**STEP)
    second_hat = second_new / (1.0 - BETA_SECOND**STEP)
    change = -LEARN_RATE * (first_hat / (jnp.sqrt(second_hat) + ADAM_EPS) + decay * master)
    return (change, first_new, second_new)


def body(
    block_input,
    live_mask,
    cotangent,
    project_in,
    project_out,
    expand,
    contract,
    vectors,
    expand_bias,
    moment_project_in,
    second_project_in,
    moment_project_out,
    second_project_out,
    moment_expand,
    second_expand,
    moment_contract,
    second_contract,
    moment_vectors,
    second_vectors,
    moment_expand_bias,
    second_expand_bias,
):
    local_len, images, features = block_input.shape
    tensor_rank = lax.axis_index("tensor")
    head_width = project_in.shape[2]
    heads_here = head_width // HEAD_DIM
    hidden_width = expand.shape[1]
    masters = (project_in, project_out, expand, contract, vectors, expand_bias)
    forward_copies = gather_weights(masters)
    full_in, full_out, full_expand, full_contract, full_vectors, full_bias = forward_copies
    rows_now = full_vectors.astype(jnp.float32)
    bias_now = full_bias.astype(jnp.float32)
    usable_all = live_mask > 0
    usable_here = lax.dynamic_slice_in_dim(live_mask, tensor_rank * local_len, local_len, 0) > 0
    key_usable = jnp.repeat(usable_all.T, heads_here, axis=0)
    scaled_one, inverse_one, normed = norm_forward(block_input, rows_now[0], rows_now[1])
    normed_one = normed.astype(jnp.bfloat16)
    gathered_one = lax.all_gather(normed_one, "tensor", axis=0, tiled=True)
    query_bias = lax.dynamic_slice_in_dim(rows_now[2], tensor_rank * head_width, head_width)
    value_bias = lax.dynamic_slice_in_dim(rows_now[3], tensor_rank * head_width, head_width)
    bias_rows = jnp.stack([query_bias, jnp.zeros_like(query_bias), value_bias])
    mixed = jnp.einsum("sbd,dce->sbce", gathered_one, full_in, preferred_element_type=jnp.float32)
    mixed = (mixed + bias_rows).astype(jnp.bfloat16)
    queries = split_heads(mixed[:, :, 0], heads_here)
    key_rows = split_heads(mixed[:, :, 1], heads_here)
    value_rows = split_heads(mixed[:, :, 2], heads_here)
    outputs, log_totals = lax.map(head_forward, (queries, key_rows, value_rows, key_usable))
    attended = merge_heads(outputs, images)
    picked = attended
    attn_sum = (
        lax.psum_scatter(
            jnp.einsum("sbe,ed->sbd", picked, full_out, preferred_element_type=jnp.float32).astype(
                jnp.bfloat16
            ),
            "tensor",
            scatter_dimension=0,
            tiled=True,
        ).astype(jnp.float32)
        + rows_now[4]
    )
    residual = block_input + rows_now[5] * attn_sum
    scaled_two, inverse_two, normed = norm_forward(residual, rows_now[6], rows_now[7])
    normed_two = normed.astype(jnp.bfloat16)
    gathered_two = lax.all_gather(normed_two, "tensor", axis=0, tiled=True)
    bias_here = lax.dynamic_slice_in_dim(bias_now, tensor_rank * hidden_width, hidden_width)
    hidden = (
        jnp.einsum("sbd,df->sbf", gathered_two, full_expand, preferred_element_type=jnp.float32)
        + bias_here
    )
    activated, slope = gelu_parts(hidden)
    activated = activated.astype(jnp.bfloat16)
    picked = activated
    branch_sum = lax.psum_scatter(
        jnp.einsum("sbf,fd->sbd", picked, full_contract, preferred_element_type=jnp.float32).astype(
            jnp.bfloat16
        ),
        "tensor",
        scatter_dimension=0,
        tiled=True,
    ).astype(jnp.float32)
    branch = branch_sum + rows_now[8]
    block_output = residual + rows_now[9] * branch
    backward_copies = gather_weights(masters)
    back_in = backward_copies[0]
    back_out = backward_copies[1]
    back_expand = backward_copies[2]
    back_contract = backward_copies[3]
    grad_top = cotangent * usable_here.astype(jnp.float32)[:, :, None]
    grad_scale_two = jnp.sum(grad_top * branch, axis=(0, 1))
    grad_down_bias = jnp.sum(grad_top * rows_now[9], axis=(0, 1))
    grad_branch = (grad_top * rows_now[9]).astype(jnp.bfloat16)
    arrived = lax.all_gather(grad_branch, "tensor", axis=0, tiled=True)
    weight_sum = jnp.einsum("sbf,sbd->fd", activated, arrived, preferred_element_type=jnp.float32)
    grad_act = jnp.einsum("sbd,fd->sbf", arrived, back_contract, preferred_element_type=jnp.float32)
    new_rows = (grad_act * slope).astype(jnp.bfloat16)
    buffer = new_rows
    grad_contract = weight_sum
    grad_hidden = buffer
    grad_expand = jnp.einsum(
        "sbd,sbf->df", gathered_two, grad_hidden, preferred_element_type=jnp.float32
    )
    grad_expand_bias = lax.dynamic_update_slice_in_dim(
        jnp.zeros((bias_now.shape[0],), jnp.float32),
        jnp.sum(grad_hidden.astype(jnp.float32), axis=(0, 1)),
        tensor_rank * hidden_width,
        0,
    )
    picked = grad_hidden
    grad_normed_two = lax.psum_scatter(
        jnp.einsum("sbf,df->sbd", picked, back_expand, preferred_element_type=jnp.float32).astype(
            jnp.bfloat16
        ),
        "tensor",
        scatter_dimension=0,
        tiled=True,
    ).astype(jnp.float32)
    grad_gain_two = jnp.sum(grad_normed_two * scaled_two, axis=(0, 1))
    grad_shift_two = jnp.sum(grad_normed_two, axis=(0, 1))
    grad_residual = grad_top + norm_backward(scaled_two, inverse_two, grad_normed_two, rows_now[6])
    grad_scale_one = jnp.sum(grad_residual * attn_sum, axis=(0, 1))
    grad_out_bias = jnp.sum(grad_residual * rows_now[5], axis=(0, 1))
    grad_attn = (grad_residual * rows_now[5]).astype(jnp.bfloat16)
    arrived = lax.all_gather(grad_attn, "tensor", axis=0, tiled=True)
    weight_sum = jnp.einsum("sbe,sbd->ed", attended, arrived, preferred_element_type=jnp.float32)
    new_rows = jnp.einsum(
        "sbd,ed->sbe", arrived, back_out, preferred_element_type=jnp.float32
    ).astype(jnp.bfloat16)
    buffer = new_rows
    grad_heads = lax.map(
        head_backward,
        (queries, key_rows, value_rows, key_usable, log_totals, split_heads(buffer, heads_here)),
    )
    grad_mixed = jnp.stack([merge_heads(grad_part, images) for grad_part in grad_heads], axis=2)
    grad_project_in = jnp.einsum(
        "sbd,sbce->dce", gathered_one, grad_mixed, preferred_element_type=jnp.float32
    )
    bias_sums = jnp.sum(grad_mixed.astype(jnp.float32), axis=(0, 1))
    empty_row = jnp.zeros((features,), jnp.float32)
    grad_query_bias = lax.dynamic_update_slice_in_dim(
        empty_row, bias_sums[0], tensor_rank * head_width, 0
    )
    grad_value_bias = lax.dynamic_update_slice_in_dim(
        empty_row, bias_sums[2], tensor_rank * head_width, 0
    )
    picked = grad_mixed
    grad_normed_one = lax.psum_scatter(
        jnp.einsum("sbce,dce->sbd", picked, back_in, preferred_element_type=jnp.float32).astype(
            jnp.bfloat16
        ),
        "tensor",
        scatter_dimension=0,
        tiled=True,
    ).astype(jnp.float32)
    grad_gain_one = jnp.sum(grad_normed_one * scaled_one, axis=(0, 1))
    grad_shift_one = jnp.sum(grad_normed_one, axis=(0, 1))
    input_grad = grad_residual + norm_backward(
        scaled_one, inverse_one, grad_normed_one, rows_now[0]
    )
    grad_rows = jnp.stack(
        [
            grad_gain_one,
            grad_shift_one,
            grad_query_bias,
            grad_value_bias,
            grad_out_bias,
            grad_scale_one,
            grad_gain_two,
            grad_shift_two,
            grad_down_bias,
            grad_scale_two,
        ]
    )
    reduced = (
        lax.psum_scatter(
            grad_project_in.astype(jnp.bfloat16), "fsdp", scatter_dimension=0, tiled=True
        ).astype(jnp.float32),
        lax.psum_scatter(
            weight_sum.astype(jnp.bfloat16), "fsdp", scatter_dimension=1, tiled=True
        ).astype(jnp.float32),
        lax.psum_scatter(
            grad_expand.astype(jnp.bfloat16), "fsdp", scatter_dimension=0, tiled=True
        ).astype(jnp.float32),
        lax.psum_scatter(
            grad_contract.astype(jnp.bfloat16), "fsdp", scatter_dimension=1, tiled=True
        ).astype(jnp.float32),
        lax.psum_scatter(
            grad_rows.astype(jnp.bfloat16), "fsdp", scatter_dimension=1, tiled=True
        ).astype(jnp.float32),
        lax.psum_scatter(
            grad_expand_bias.astype(jnp.bfloat16), "fsdp", scatter_dimension=0, tiled=True
        ).astype(jnp.float32),
    )
    shard_rows, shard_bias = lax.psum((reduced[4], reduced[5]), "tensor")
    totals = (reduced[0], reduced[1], reduced[2], reduced[3], shard_rows, shard_bias)
    firsts = (
        moment_project_in,
        moment_project_out,
        moment_expand,
        moment_contract,
        moment_vectors,
        moment_expand_bias,
    )
    seconds = (
        second_project_in,
        second_project_out,
        second_expand,
        second_contract,
        second_vectors,
        second_expand_bias,
    )
    decays = (WEIGHT_DECAY, WEIGHT_DECAY, WEIGHT_DECAY, WEIGHT_DECAY, 0.0, 0.0)
    results = [
        adam_step(
            masters[position],
            totals[position],
            firsts[position],
            seconds[position],
            decays[position],
        )
        for position in range(6)
    ]
    changes = tuple((result[0] for result in results))
    moments = []
    for result in results:
        moments.append(result[1])
        moments.append(result[2])
    return (
        block_output,
        input_grad,
        totals[0],
        totals[1],
        totals[2],
        totals[3],
        totals[4],
        totals[5],
        masters[0] + changes[0],
        changes[1],
        masters[2] + changes[2],
        masters[3] + changes[3],
        changes[4],
        changes[5],
        moments[0],
        moments[1],
        moments[2],
        moments[3],
        moments[4],
        moments[5],
        moments[6],
        moments[7],
        moments[8],
        moments[9],
        moments[10],
        moments[11],
        shard_rows[7],
    )


def solution(mesh):
    placed = (
        P("tensor", "fsdp", None),
        P(None, "fsdp"),
        P("tensor", "fsdp", None),
        P("fsdp", None, "tensor"),
        P("tensor", "fsdp"),
        P("fsdp", "tensor"),
        P("tensor", "fsdp"),
        P(None, "fsdp"),
        P("fsdp"),
        P("fsdp", None, "tensor"),
        P("fsdp", None, "tensor"),
        P("tensor", "fsdp"),
        P("tensor", "fsdp"),
        P("fsdp", "tensor"),
        P("fsdp", "tensor"),
        P("tensor", "fsdp"),
        P("tensor", "fsdp"),
        P(None, "fsdp"),
        P(None, "fsdp"),
        P("fsdp"),
        P("fsdp"),
    )
    return jax.shard_map(
        body,
        mesh=mesh,
        in_specs=placed,
        out_specs=(
            P("tensor", "fsdp", None),
            P("tensor", "fsdp", None),
            P("fsdp", None, "tensor"),
            P("tensor", "fsdp"),
            P("fsdp", "tensor"),
            P("tensor", "fsdp"),
            P(None, "fsdp"),
            P("fsdp"),
            P("fsdp", None, "tensor"),
            P("tensor", "fsdp"),
            P("fsdp", "tensor"),
            P("tensor", "fsdp"),
            P(None, "fsdp"),
            P("fsdp"),
            P("fsdp", None, "tensor"),
            P("fsdp", None, "tensor"),
            P("tensor", "fsdp"),
            P("tensor", "fsdp"),
            P("fsdp", "tensor"),
            P("fsdp", "tensor"),
            P("tensor", "fsdp"),
            P("tensor", "fsdp"),
            P(None, "fsdp"),
            P(None, "fsdp"),
            P("fsdp"),
            P("fsdp"),
            P("fsdp"),
        ),
        check_vma=False,
    )
```

profile of v0, /device:TPU:0, one launch (start us, length us, event | category | flops | bytes accessed | tf_op | source)
XLA Modules:
  0.0 868.6 jit_solution(13363182723339998792)
XLA Ops:
  9.8 2.7 reduce_sum.180
  12.5 27.9 %all_gather.34 = bf16[10,1024]{1,0:T(8,128)(2,1)S(1)} all-gather(bf16[10,128]{1,0:T(8,128)(2,1)S(1)} %convert_element_type.165), channel_id=1, replica_groups=mesh['fsdp'=8,'tensor'=4] {'fsdp'}, dimensions={1}, use_global_device_ids=true | all-gather | bytes 23040 | tf_op jit(solution)/shard_map/all_gather | solution.py:100
  43.1 30.5 %all_gather.37 = bf16[256,1024]{1,0:T(8,128)(2,1)} all-gather(bf16[256,128]{1,0:T(8,128)(2,1)S(1)} %convert_element_type.171), channel_id=1, replica_groups=mesh['fsdp'=8,'tensor'=4] {'fsdp'}, dimensions={1}, use_global_device_ids=true | all-gather | bytes 589824 | tf_op jit(solution)/shard_map/all_gather | solution.py:97
  73.6 18.7 %all-gather.9.cloned.1.call-done = bf16[1376,1,1024]{2,0,1:T(8,128)(2,1)} async-done(((bf16[344,1,1024]{2,0,1:T(8,128)(2,1)}), bf16[1376,1,1024]{2,0,1:T(8,128)(2,1)}) %all-gather.9.cloned.1.call-update) | async-done | bytes 2818064 | tf_op jit(solution)/shard_map/all_gather | solution.py:152
  92.3 4.6 fusion.64
  103.9 32.4 %while.26 = (s32[]{:T(128)}, bf16[4,1376,64]{1,2,0:T(8,128)(2,1)S(1)}, f32[4,1376]{1,0:T(4,128)}, pred[4,1376]{1,0:T(4,128)(4,1)S(1)}, bf16[4,1376,64]{2,1,0:T(8...) while((s32[]{:T(128)}, ...), condition=%wide.region_5.6_spmd, body=%wide.region_2.5_spmd.sunk | while | flops 498044576 | bytes 24203820 | solution.py:161
  137.1 3.5 fusion.60
  143.0 33.8 %reduce-scatter.16.cloned.1.call-done = bf16[344,1,1024]{2,0,1:T(8,128)(2,1)} async-done(((bf16[1376,1,1024]{2,0,1:T(8,128)(2,1)}), bf16[344,1,1024]{2,0,1:T(8,128)(2,1)}) %reduce-scatter.16.cloned.1.call-update) | async-done | bytes 704528 | tf_op jit(solution)/shard_map/reduce_scatter | solution.py:165
  180.8 26.1 %all-gather = bf16[8,1,512]{2,1,0:T(2,128)(2,1)S(1)} all-gather(bf16[1,1,512]{2,1,0:T(2,128)(2,1)S(1)} %reshape.376), channel_id=1, replica_groups=mesh['fsdp'=8,'tensor'=4] {'fsdp'}, dimensions={0}, use_global_device_ids=true | all-gather | bytes 9216 | tf_op jit(solution)/shard_map/all_gather | solution.py:101
  206.9 22.1 %all-gather.15.cloned.1.call-done = bf16[1024,1024]{1,0:T(8,128)(2,1)} async-done(((bf16[128,1024]{1,0:T(8,128)(2,1)}), bf16[1024,1024]{1,0:T(8,128)(2,1)}) %all-gather.15.cloned.1.call-update) | async-done | bytes 2097168 | tf_op jit(solution)/shard_map/all_gather | solution.py:98
  229.0 26.7 %all-gather.13.cloned.1.call-done = bf16[1376,1,1024]{2,0,1:T(8,128)(2,1)} async-done(((bf16[344,1,1024]{2,0,1:T(8,128)(2,1)}), bf16[1376,1,1024]{2,0,1:T(8,128)(2,1)}) %all-gather.13.cloned.1.call-update) | async-done | bytes 2818064 | tf_op jit(solution)/shard_map/all_gather | solution.py:178
  255.7 8.2 multiply_convert_fusion.1
  263.9 45.5 %all-gather.17.cloned.1.call-done = bf16[1024,1024]{1,0:T(8,128)(2,1)} async-done(((bf16[1024,128]{1,0:T(8,128)(2,1)}), bf16[1024,1024]{1,0:T(8,128)(2,1)}) %all-gather.17.cloned.1.call-update) | async-done | bytes 2097168 | tf_op jit(solution)/shard_map/all_gather | solution.py:99
  309.5 7.1 fusion.62
  317.5 33.3 %reduce-scatter.18.cloned.1.call-done = bf16[344,1,1024]{2,0,1:T(8,128)(2,1)} async-done(((bf16[1376,1,1024]{2,0,1:T(8,128)(2,1)}), bf16[344,1,1024]{2,0,1:T(8,128)(2,1)}) %reduce-scatter.18.cloned.1.call-update) | async-done | bytes 704528 | tf_op jit(solution)/shard_map/reduce_scatter | solution.py:187
  350.8 3.1 multiply_reduce_fusion.1
  354.0 26.8 %all-gather.19.cloned.1.call-done = bf16[1376,1,1024]{2,0,1:T(8,128)(2,1)} async-done(((bf16[344,1,1024]{2,0,1:T(8,128)(2,1)}), bf16[1376,1,1024]{2,0,1:T(8,128)(2,1)}) %all-gather.19.cloned.1.call-update) | async-done | bytes 2818064 | tf_op jit(solution)/shard_map/all_gather | solution.py:206
  380.7 9.1 %convert_reduce_fusion = (bf16[1024]{0:T(1024)(128)(2,1)}, bf16[1376,1024]{1,0:T(8,128)(2,1)S(1)}) fusion(f32[1376,1024]{1,0:T(8,128)} %get-tuple-element.330, f32[1024]{0:T(1024)S(1)} %dynamic_slice.47, bf16[1024,1024]{1,0:T(8,128)(2,1)} %all-gather.17.cloned.1.call-done, bf16[1376,1,1024]{2,0,1:T(8,128)(2,1)} %all-gather.19.cloned.1.call-done), kind=kOutput, calls=%fused_computation.68 | convolution fusion | flops 2903997440 | bytes 13375488 | tf_op jit(solution)/shard_map/sbd,fd->sbf/dot_general | solution.py:208
  391.4 4.5 fusion.63
  396.2 35.9 %reduce-scatter.20.cloned.1.call-done = bf16[344,1,1024]{2,0,1:T(8,128)(2,1)} async-done(((bf16[1376,1,1024]{2,0,1:T(8,128)(2,1)}), bf16[344,1,1024]{2,0,1:T(8,128)(2,1)}) %reduce-scatter.20.cloned.1.call-update) | async-done | bytes 704528 | tf_op jit(solution)/shard_map/reduce_scatter | solution.py:223
  434.5 3.5 multiply_reduce_fusion.2
  440.3 6.1 fusion.87
  449.0 7.4 fusion.84
  456.6 10.5 %all-gather.21.cloned.1.call-done = bf16[1376,1,1024]{2,0,1:T(8,128)(2,1)} async-done(((bf16[344,1,1024]{2,0,1:T(8,128)(2,1)}), bf16[1376,1,1024]{2,0,1:T(8,128)(2,1)}) %all-gather.21.cloned.1.call-update) | async-done | bytes 2818064 | tf_op jit(solution)/shard_map/all_gather | solution.py:237
  467.1 2.8 fusion.111
  470.8 2.7 fusion.79
  477.0 101.4 %while.27 = (s32[]{:T(128)}, bf16[4,1376,64]{1,2,0:T(8,128)(2,1)}, bf16[4,1376,64]{1,2,0:T(8,128)(2,1)}, bf16[4,1376,64]{1,2,0:T(8,128)(2,1)}, pred[4,1376]{1,0:...) while((s32[]{:T(128)}, bf16[4,1376,64]{1,2,0:T(8,128)(2,1)}, ...), condition=%wide.region_15.16_spmd, body=%wide.region_13.15_spmd.sunk | while | flops 1229239936 | bytes 75091288 | solution.py:243
  479.9 6.4 multiply_reduce_fusion.8
  486.3 6.4 multiply_convert_fusion.5
  492.7 5.3 fusion.178
  505.3 6.4 multiply_reduce_fusion.8
  511.7 6.4 multiply_convert_fusion.5
  518.0 5.3 fusion.178
  530.6 6.4 multiply_reduce_fusion.8
  537.0 6.4 multiply_convert_fusion.5
  543.3 5.3 fusion.178
  555.9 6.4 multiply_reduce_fusion.8
  562.3 6.4 multiply_convert_fusion.5
  568.7 5.3 fusion.178
  581.5 5.9 fusion.96
  587.5 5.4 fusion.61
  596.2 21.4 %all-reduce = bf16[4096]{0:T(1024)(128)(2,1)S(1)} all-reduce(bf16[4096]{0:T(1024)(128)(2,1)S(1)} %dynamic_update_slice.30), channel_id=11, replica_groups=mesh['fsdp'=8,'tensor'=4] {'fsdp'}, use_global_device_ids=true, to_apply=%region_35.36.clone | all-reduce | flops 4096 | bytes 16384
  620.9 3.0 multiply_add_fusion.4
  631.7 42.5 %reduce-scatter.28.cloned.1.call-done = bf16[128,256]{1,0:T(8,128)(2,1)} async-done(((bf16[1024,256]{1,0:T(8,128)(2,1)}), bf16[128,256]{1,0:T(8,128)(2,1)}) %reduce-scatter.28.cloned.1.call-update) | async-done | bytes 65552
  677.1 64.9 %reduce-scatter.24.cloned.1.call-done = bf16[128,3,256]{2,0,1:T(8,128)(2,1)} async-done(((bf16[1024,3,256]{2,0,1:T(8,128)(2,1)}), bf16[128,3,256]{2,0,1:T(8,128)(2,1)}) %reduce-scatter.24.cloned.1.call-update) | async-done | bytes 196624 | tf_op jit(solution)/shard_map/reduce_scatter | solution.py:288
  744.4 35.1 %reduce-scatter.22.cloned.1.call-done = bf16[344,1,1024]{2,0,1:T(8,128)(2,1)} async-done(((bf16[1376,1,1024]{2,0,1:T(8,128)(2,1)}), bf16[344,1,1024]{2,0,1:T(8,128)(2,1)}) %reduce-scatter.22.cloned.1.call-update) | async-done | bytes 704528 | tf_op jit(solution)/shard_map/reduce_scatter | solution.py:260
  791.5 57.4 %reduce-scatter.32.cloned.1.call-done = bf16[128,10]{1,0:T(8,128)(2,1)} async-done(((bf16[1024,10]{1,0:T(8,128)(2,1)}), bf16[128,10]{1,0:T(8,128)(2,1)}) %reduce-scatter.32.cloned.1.call-update) | async-done | bytes 2576
  849.7 10.1 %all-reduce.1 = (f32[10,128]{1,0:T(8,128)S(1)}, f32[512]{0:T(512)S(1)}) all-reduce(bf16[10,128]{1,0:T(8,128)(2,1)S(1)} %copy.103, f32[512]{0:T(512)S(1)} %copy-done.54), channel_id=1, replica_groups=mesh['fsdp'=8,'tensor'=4] {'tensor'}, use_global_device_ids=true, to_apply=%region_33.34 | all-reduce | flops 1792 | bytes 11776 | tf_op jit(solution)/shard_map/psum | solution.py:307
  (300 shorter events, 131.6 us)
Async XLA Ops:
  7.2 33.2 %copy-start.1 = (f32[344,1,1024]{2,1,0:T(1,128)S(1)}, f32[344,1,1024]{2,1,0:T(1,128)}, u32[]{:S(2)}) copy-start(f32[344,1,1024]{2,1,0:T(1,128)} %param.25) | copy-start | bytes 4227076
  7.2 66.4 %all-gather.11.cloned.1.call-start = ((), (), s32[]{:S(2)}) async-start(), calls=%async_computation.10 | async-start | bytes 1769472 | tf_op jit(solution)/shard_map/all_gather | solution.py:96
  9.1 83.2 %all-gather.9.cloned.1.call-start = ((), (), s32[]{:S(2)}) async-start(), calls=%async_computation.9 | async-start | bytes 3522560 | tf_op jit(solution)/shard_map/all_gather | solution.py:152
  42.8 134.0 %reduce-scatter.16.cloned.1.call-start = ((), (), s32[]{:S(2)}) async-start(), calls=%async_computation.11 | async-start | bytes 3522560 | tf_op jit(solution)/shard_map/reduce_scatter | solution.py:165
  140.7 36.1 %copy-start.37 = (f32[1,1024]{1,0:T(1,128)S(1)}, f32[1,1024]{1,0:T(1,128)}, u32[]{:S(2)}) copy-start(f32[1,1024]{1,0:T(1,128)} %get-tuple-element.324) | copy-start | bytes 12292
  140.7 88.3 %all-gather.15.cloned.1.call-start = ((), (), s32[]{:S(2)}) async-start(), calls=%async_computation.13 | async-start | bytes 2359296 | tf_op jit(solution)/shard_map/all_gather | solution.py:98
  142.5 113.2 %all-gather.13.cloned.1.call-start = ((), (), s32[]{:S(2)}) async-start(), calls=%async_computation.12 | async-start | bytes 3522560 | tf_op jit(solution)/shard_map/all_gather | solution.py:178
  179.9 129.6 %all-gather.17.cloned.1.call-start = ((), (), s32[]{:S(2)}) async-start(), calls=%async_computation.14 | async-start | bytes 2359296 | tf_op jit(solution)/shard_map/all_gather | solution.py:99
  180.7 170.1 %reduce-scatter.18.cloned.1.call-start = ((), (), s32[]{:S(2)}) async-start(), calls=%async_computation.15 | async-start | bytes 3522560 | tf_op jit(solution)/shard_map/reduce_scatter | solution.py:187
  316.5 34.3 %copy-start.10 = (f32[344,1,1024]{2,1,0:T(1,128)S(1)}, f32[344,1,1024]{2,1,0:T(1,128)}, u32[]{:S(2)}) copy-start(f32[344,1,1024]{2,1,0:T(1,128)} %param.27) | copy-start | bytes 4227076
  316.5 34.3 %copy-start.35 = (f32[1,1024]{1,0:T(1,128)S(1)}, f32[1,1024]{1,0:T(1,128)}, u32[]{:S(2)}) copy-start(f32[1,1024]{1,0:T(1,128)} %get-tuple-element.319) | copy-start | bytes 12292
  316.5 34.3 %copy-start.36 = (f32[1,1024]{1,0:T(1,128)S(1)}, f32[1,1024]{1,0:T(1,128)}, u32[]{:S(2)}) copy-start(f32[1,1024]{1,0:T(1,128)} %get-tuple-element.320) | copy-start | bytes 12292
  316.5 64.2 %all-gather.19.cloned.1.call-start = ((), (), s32[]{:S(2)}) async-start(), calls=%async_computation.16 | async-start | bytes 3522560 | tf_op jit(solution)/shard_map/all_gather | solution.py:206
  317.5 72.4 %copy-start.43 = (f32[344]{0:T(512)}, f32[344]{0:T(512)S(1)}, u32[]{:S(2)}) copy-start(f32[344]{0:T(512)S(1)} %fusion.121) | copy-start | bytes 4132
  353.9 78.1 %reduce-scatter.20.cloned.1.call-start = ((), (), s32[]{:S(2)}) async-start(), calls=%async_computation.17 | async-start | bytes 3522560 | tf_op jit(solution)/shard_map/reduce_scatter | solution.py:223
  380.7 10.6 %copy-start.61 = (bf16[1024,1024]{1,0:T(8,128)(2,1)S(1)}, bf16[1024,1024]{1,0:T(8,128)(2,1)}, u32[]{:S(2)}) copy-start(bf16[1024,1024]{1,0:T(8,128)(2,1)} %all-gather.15.cloned.1.call-done) | copy-start | bytes 6291460
  395.9 36.1 %copy-start.34 = (f32[344]{0:T(512)S(1)}, f32[344]{0:T(512)}, u32[]{:S(2)}) copy-start(f32[344]{0:T(512)} %copy-done.33) | copy-start | bytes 4132
  395.9 38.6 %copy-start.15 = (bf16[344,1,1024]{2,0,1:T(8,128)(2,1)S(1)}, bf16[344,1,1024]{2,0,1:T(8,128)(2,1)}, u32[]{:S(2)}) copy-start(bf16[344,1,1024]{2,0,1:T(8,128)(2,1)} %reduce-scatter.16.cloned.1.call-done) | copy-start | bytes 2113540
  395.9 38.6 %copy-start.38 = (f32[1,1024]{1,0:T(1,128)S(1)}, f32[1,1024]{1,0:T(1,128)}, u32[]{:S(2)}) copy-start(f32[1,1024]{1,0:T(1,128)} %get-tuple-element.324) | copy-start | bytes 12292
  395.9 71.1 %all-gather.21.cloned.1.call-start = ((), (), s32[]{:S(2)}) async-start(), calls=%async_computation.18 | async-start | bytes 3522560 | tf_op jit(solution)/shard_map/all_gather | solution.py:237
  440.2 178.1 %reduce-scatter.30.cloned.1.call-start = ((), (), s32[]{:S(2)}) async-start(), calls=%async_computation.23 | async-start | bytes 2359296
  449.0 171.9 %reduce-scatter.26.cloned.1.call-start = ((), (), s32[]{:S(2)}) async-start(), calls=%async_computation.21 | async-start | bytes 2359296 | tf_op jit(solution)/shard_map/reduce_scatter | solution.py:294
  456.5 10.6 %copy-start.22 = (bf16[4,1376,64]{1,2,0:T(8,128)(2,1)S(1)}, bf16[4,1376,64]{1,2,0:T(8,128)(2,1)}, u32[]{:S(2)}) copy-start(bf16[4,1376,64]{1,2,0:T(8,128)(2,1)} %copy-done.21) | copy-start | bytes 2113540
  456.5 14.3 %copy-start.27 = (bf16[256,1024]{1,0:T(8,128)(2,1)S(1)}, bf16[256,1024]{1,0:T(8,128)(2,1)}, u32[]{:S(2)}) copy-start(bf16[256,1024]{1,0:T(8,128)(2,1)} %all_gather.37) | copy-start | bytes 1572868
  456.5 217.7 %reduce-scatter.28.cloned.1.call-start = ((), (), s32[]{:S(2)}) async-start(), calls=%async_computation.22 | async-start | bytes 589824
  474.0 268.0 %reduce-scatter.24.cloned.1.call-start = ((), (), s32[]{:S(2)}) async-start(), calls=%async_computation.20 | async-start | bytes 1769472 | tf_op jit(solution)/shard_map/reduce_scatter | solution.py:288
  581.5 6.0 copy-start.13
  587.5 192.0 %reduce-scatter.22.cloned.1.call-start = ((), (), s32[]{:S(2)}) async-start(), calls=%async_computation.19 | async-start | bytes 3522560 | tf_op jit(solution)/shard_map/reduce_scatter | solution.py:260
  592.9 26.5 %copy-start.18 = (f32[1024,128]{1,0:T(8,128)S(1)}, f32[1024,128]{1,0:T(8,128)}, u32[]{:S(2)}) copy-start(f32[1024,128]{1,0:T(8,128)} %param.31) | copy-start | bytes 1572868
  592.9 26.5 %copy-start.23 = (f32[1024,128]{1,0:T(8,128)S(1)}, f32[1024,128]{1,0:T(8,128)}, u32[]{:S(2)}) copy-start(f32[1024,128]{1,0:T(8,128)} %param.40) | copy-start | bytes 1572868
  592.9 26.5 %copy-start.24 = (f32[1024,128]{1,0:T(8,128)S(1)}, f32[1024,128]{1,0:T(8,128)}, u32[]{:S(2)}) copy-start(f32[1024,128]{1,0:T(8,128)} %param.41) | copy-start | bytes 1572868
  593.0 255.9 %reduce-scatter.32.cloned.1.call-start = ((), (), s32[]{:S(2)}) async-start(), calls=%async_computation.24 | async-start | bytes 294912
  620.9 5.6 copy-start.11
  629.0 46.1 %copy-start.26 = (f32[256,128]{1,0:T(8,128)S(1)}, f32[256,128]{1,0:T(8,128)}, u32[]{:S(2)}) copy-start(f32[256,128]{1,0:T(8,128)} %param.29) | copy-start | bytes 393220
  629.0 113.0 %copy-start.20 = (f32[128,3,256]{2,0,1:T(8,128)S(1)}, f32[128,3,256]{2,0,1:T(8,128)}, u32[]{:S(2)}) copy-start(f32[128,3,256]{2,0,1:T(8,128)} %param.28) | copy-start | bytes 1179652
  675.1 106.3 %copy-start.2 = (f32[344,1,1024]{2,1,0:T(1,128)S(1)}, f32[344,1,1024]{2,1,0:T(1,128)}, u32[]{:S(2)}) copy-start(f32[344,1,1024]{2,1,0:T(1,128)} %param.25) | copy-start | bytes 4227076
  675.2 106.3 %copy-start.30 = (f32[1,1024]{1,0:T(1,128)S(1)}, f32[1,1024]{1,0:T(1,128)}, u32[]{:S(2)}) copy-start(f32[1,1024]{1,0:T(1,128)} %copy-done.29) | copy-start | bytes 12292
  675.2 106.3 %copy-start.32 = (f32[344]{0:T(512)S(1)}, f32[344]{0:T(512)}, u32[]{:S(2)}) copy-start(f32[344]{0:T(512)} %copy-done.31) | copy-start | bytes 4132
  675.2 106.3 %copy-start.41 = (f32[344]{0:T(512)S(1)}, f32[344]{0:T(512)}, u32[]{:S(2)}) copy-start(f32[344]{0:T(512)} %copy-done.40) | copy-start | bytes 4132
  744.4 43.2 %copy-start.6 = (f32[344,1,1024]{2,0,1:T(8,128)S(1)}, f32[344,1,1024]{2,0,1:T(8,128)}, u32[]{:S(2)}) copy-start(f32[344,1,1024]{2,0,1:T(8,128)} %copy-done.5) | copy-start | bytes 4227076
  779.5 8.1 copy-start.9
  788.9 60.8 %copy-start.54 = (f32[512]{0:T(512)S(1)}, f32[512]{0:T(512)}, u32[]{:S(2)}) copy-start(f32[512]{0:T(512)} %dynamic-slice_convert_fusion) | copy-start | bytes 6148
  788.9 71.5 %copy-start.39 = (f32[10,128]{1,0:T(8,128)S(1)}, f32[10,128]{1,0:T(8,128)}, u32[]{:S(2)}) copy-start(f32[10,128]{1,0:T(8,128)} %param.32) | copy-start | bytes 15364
  788.9 71.5 %copy-start.51 = (f32[10,128]{1,0:T(8,128)S(1)}, f32[10,128]{1,0:T(8,128)}, u32[]{:S(2)}) copy-start(f32[10,128]{1,0:T(8,128)} %param.42) | copy-start | bytes 15364
  788.9 71.5 %copy-start.52 = (f32[10,128]{1,0:T(8,128)S(1)}, f32[10,128]{1,0:T(8,128)}, u32[]{:S(2)}) copy-start(f32[10,128]{1,0:T(8,128)} %param.43) | copy-start | bytes 15364
  788.9 72.1 %copy-start.56 = (f32[512]{0:T(512)S(1)}, f32[512]{0:T(512)}, u32[]{:S(2)}) copy-start(f32[512]{0:T(512)} %param.33) | copy-start | bytes 6148
  788.9 72.1 %copy-start.57 = (f32[512]{0:T(512)S(1)}, f32[512]{0:T(512)}, u32[]{:S(2)}) copy-start(f32[512]{0:T(512)} %param.44) | copy-start | bytes 6148
  788.9 72.1 %copy-start.58 = (f32[512]{0:T(512)S(1)}, f32[512]{0:T(512)}, u32[]{:S(2)}) copy-start(f32[512]{0:T(512)} %param.45) | copy-start | bytes 6148
  (35 other events, 96.5 us)
Sparse Core Ops, SparseCore 0:
  10.8 49.6 all-gather.10
  62.6 29.6 all-gather.8
  140.8 35.9 reduce-scatter.15
  179.5 49.4 all-gather.14
  230.5 25.1 all-gather.12
  258.3 51.0 all-gather.16
  316.7 34.0 reduce-scatter.17
  354.0 26.6 all-gather.18
  396.1 35.9 reduce-scatter.19
  440.3 26.6 all-gather.20
  471.0 67.8 reduce-scatter.29
  542.7 66.8 reduce-scatter.25
  613.3 60.8 reduce-scatter.27
  677.5 64.4 reduce-scatter.23
  744.6 34.8 reduce-scatter.21
  787.7 61.1 reduce-scatter.31
where the time goes:
time: 879 us; the launch traced here: 869 us
  waiting for transfers between devices  454 us (52%)
  matrix products  160 us (18%)
  blocking collectives  116 us (13%)
  other arithmetic  69.4 us (8%)
  local copies, waits for them, and re-layouts  52.4 us (6%)
  between operations  15.7 us (2%)
    unnamed x19, waiting for transfers between devices  100 us
    reduce_scatter x1, waiting for transfers between devices, body(): lax.psum_scatter(grad_project_in.astype(jnp.bfloat16), 'fsdp', scatter_di...  64.9 us
    all_gather x1, waiting for transfers between devices, gather_weights(): lax.all_gather(copies[3], 'fsdp', axis=1, tiled=True)  45.5 us
    dot_general x8, matrix products, head_scores(): jnp.dot(queries, key_rows.T, preferred_element_type=jnp.float32)  35.9 us
    reduce_scatter x1, waiting for transfers between devices, body(): lax.psum_scatter(jnp.einsum('sbf,df->sbd', picked, back_expand, preferred...  35.9 us
    reduce_scatter x1, waiting for transfers between devices, body(): lax.psum_scatter(jnp.einsum('sbce,dce->sbd', picked, back_in, preferred_e...  35.1 us
    reduce_scatter x1, waiting for transfers between devices, body(): lax.psum_scatter(jnp.einsum('sbe,ed->sbd', picked, full_out, preferred_el...  33.8 us
    reduce_scatter x1, waiting for transfers between devices, body(): lax.psum_scatter(jnp.einsum('sbf,fd->sbd', picked, full_contract, preferr...  33.3 us
  transfers between devices with their start and end apart: 16, of which 13 were waited for; matrix products, arithmetic and copies ran while one was open for 21% of the time, Pallas kernels for 0%

commit v1 on v0

v1 whole, which is shorter than its diff:
```python
import functools

import jax
import jax.numpy as jnp
from jax import lax
from jax.experimental import pallas as pl
from jax.experimental.pallas import tpu as pltpu
from jax.sharding import PartitionSpec as P

HEAD_DIM = 64
STEP = 3
NORM_EPS = 1e-06
BETA_FIRST = 0.9
BETA_SECOND = 0.999
LEARN_RATE = 0.004
WEIGHT_DECAY = 0.04
ADAM_EPS = 1e-08
MASKED_SCORE = -1e30
ROOT_HALF = 0.7071067811865476
DENSITY_NORM = 0.3989422804014327
SCORE_SCALE = HEAD_DIM ** (-0.5)
LANES = 128
TILE = 352
VMEM_LIMIT = 56 * 2**20
F32 = jnp.float32
BF16 = jnp.bfloat16


def dot_nn(left, right):
    return lax.dot_general(left, right, (((1,), (0,)), ((), ())), preferred_element_type=F32)


def dot_nt(left, right):
    return lax.dot_general(left, right, (((1,), (1,)), ((), ())), preferred_element_type=F32)


def dot_tn(left, right):
    return lax.dot_general(left, right, (((0,), (0,)), ((), ())), preferred_element_type=F32)


def tiles_of(total, tile):
    return [(low, min(tile, total - low)) for low in range(0, total, tile)]


def norm_forward(values):
    center = jnp.mean(values, axis=-1, keepdims=True)
    offset = values - center
    spread = jnp.mean(offset * offset, axis=-1, keepdims=True)
    inverse = lax.rsqrt(spread + NORM_EPS)
    return offset * inverse, inverse


def norm_backward(scaled, inverse, grad_normed, norm_gain):
    grad_scaled = grad_normed * norm_gain
    first_mean = jnp.mean(grad_scaled, axis=-1, keepdims=True)
    second_mean = jnp.mean(grad_scaled * scaled, axis=-1, keepdims=True)
    return inverse * (grad_scaled - first_mean - scaled * second_mean)


def gelu_parts(hidden):
    normal_cdf = 0.5 * (1.0 + lax.erf(hidden * ROOT_HALF))
    density = DENSITY_NORM * jnp.exp(-0.5 * hidden * hidden)
    return (hidden * normal_cdf, normal_cdf + hidden * density)


def project_kernel(x_ref, rows_ref, weight_ref, bias_ref, normed_ref, qkv_ref):
    for low, count in tiles_of(x_ref.shape[0], TILE):
        at = slice(low, low + count)
        scaled, _ = norm_forward(x_ref[at, :].astype(F32))
        normed = (scaled * rows_ref[0:1, :] + rows_ref[1:2, :]).astype(BF16)
        normed_ref[at, :] = normed
        qkv_ref[at, :] = (dot_nn(normed, weight_ref[...]) + bias_ref[...]).astype(BF16)


def project(x_full, rows, weight, bias):
    seq, features = x_full.shape
    width = weight.shape[1]
    block = seq // 2
    return pl.pallas_call(
        project_kernel,
        grid=(2,),
        in_specs=[
            pl.BlockSpec((block, features), lambda i: (i, 0)),
            pl.BlockSpec(rows.shape, lambda i: (0, 0)),
            pl.BlockSpec(weight.shape, lambda i: (0, 0)),
            pl.BlockSpec(bias.shape, lambda i: (0, 0)),
        ],
        out_specs=[
            pl.BlockSpec((block, features), lambda i: (i, 0)),
            pl.BlockSpec((block, width), lambda i: (i, 0)),
        ],
        out_shape=[
            jax.ShapeDtypeStruct((seq, features), BF16),
            jax.ShapeDtypeStruct((seq, width), BF16),
        ],
        compiler_params=pltpu.CompilerParams(vmem_limit_bytes=VMEM_LIMIT),
        cost_estimate=pl.CostEstimate(
            flops=2 * seq * features * width,
            bytes_accessed=2 * (2 * seq * features + features * width + seq * width),
            transcendentals=0,
        ),
        name="project",
    )(x_full, rows, weight, bias)


def attend_kernel(live_ref, qkv_ref, attended_ref, query_ref, key_ref, value_ref):
    seq = qkv_ref.shape[0]
    lane = lax.broadcasted_iota(jnp.int32, (seq, LANES), 1)
    bias = jnp.where(live_ref[...] > 0, 0.0, MASKED_SCORE).astype(F32)
    key_rows = qkv_ref[:, LANES : 2 * LANES].astype(F32)
    value_rows = qkv_ref[:, 2 * LANES : 3 * LANES].astype(F32)
    for head in range(2):
        own = (lane // HEAD_DIM) == head
        spare = HEAD_DIM * (1 - head)
        extra = jnp.where(lane == spare, bias, 0.0)
        key_ref[head] = jnp.where(own, key_rows, extra).astype(BF16)
        extra = jnp.where(lane == spare, 1.0, 0.0)
        value_ref[head] = jnp.where(own, value_rows, extra).astype(BF16)
    for low, count in tiles_of(seq, TILE):
        at = slice(low, low + count)
        lane = lax.broadcasted_iota(jnp.int32, (count, LANES), 1)
        queries = qkv_ref[at, 0:LANES].astype(F32) * SCORE_SCALE
        both = None
        for head in range(2):
            own = (lane // HEAD_DIM) == head
            spare = HEAD_DIM * (1 - head)
            extra = jnp.where(lane == spare, 1.0, 0.0)
            mine = jnp.where(own, queries, extra).astype(BF16)
            scores = dot_nt(mine, key_ref[head])
            highest = jnp.max(scores, axis=-1, keepdims=True)
            weights = jnp.exp(scores - highest).astype(BF16)
            output = dot_nn(weights, value_ref[head])
            summed = output[:, spare : spare + 1]
            output = output / summed
            both = output if head == 0 else jnp.where(own, output, both)
            rest = -(highest + jnp.log(summed))
            extra = jnp.where(lane == spare + 3, 1.0, 0.0)
            for place in range(3):
                part = rest.astype(BF16).astype(F32)
                extra = jnp.where(lane == spare + place, part, extra)
                rest = rest - part
            query_ref[at, LANES * head : LANES * (head + 1)] = jnp.where(
                own, queries, extra
            ).astype(BF16)
        attended_ref[at, :] = both.astype(BF16)


def attend(live, qkv):
    seq = qkv.shape[0]
    pairs = qkv.shape[1] // (3 * LANES)
    return pl.pallas_call(
        attend_kernel,
        grid=(pairs,),
        in_specs=[
            pl.BlockSpec((seq, 1), lambda p: (0, 0)),
            pl.BlockSpec((seq, 3 * LANES), lambda p: (0, p)),
        ],
        out_specs=[
            pl.BlockSpec((seq, LANES), lambda p: (0, p)),
            pl.BlockSpec((seq, 2 * LANES), lambda p: (0, p)),
        ],
        out_shape=[
            jax.ShapeDtypeStruct((seq, pairs * LANES), BF16),
            jax.ShapeDtypeStruct((seq, pairs * 2 * LANES), BF16),
        ],
        scratch_shapes=[pltpu.VMEM((2, seq, LANES), BF16), pltpu.VMEM((2, seq, LANES), BF16)],
        compiler_params=pltpu.CompilerParams(vmem_limit_bytes=VMEM_LIMIT),
        cost_estimate=pl.CostEstimate(
            flops=pairs * 32 * seq * seq * HEAD_DIM,
            bytes_accessed=seq * pairs * 768 * 2,
            transcendentals=pairs * 2 * seq * seq,
        ),
        name="attend",
    )(live, qkv)


def attend_back_kernel(
    live_ref, qkv_ref, query_ref, attended_ref, grad_ref, out_ref, sums_ref, held_ref, query_sum_ref
):
    seq = qkv_ref.shape[0]
    lane = lax.broadcasted_iota(jnp.int32, (seq, LANES), 1)
    grad = grad_ref[...].astype(F32)
    product = grad * attended_ref[...].astype(F32)
    for head in range(2):
        own = (lane // HEAD_DIM) == head
        spare = HEAD_DIM * (1 - head)
        inner = -jnp.sum(jnp.where(own, product, 0.0), axis=-1, keepdims=True)
        first = inner.astype(BF16).astype(F32)
        extra = jnp.where(lane == spare, first, jnp.where(lane == spare + 1, inner - first, 0.0))
        held_ref[head] = jnp.where(own, grad, extra).astype(BF16)
    value_sum = jnp.zeros((1, LANES), F32)
    for index, (low, count) in enumerate(tiles_of(seq, TILE)):
        at = slice(low, low + count)
        lane = lax.broadcasted_iota(jnp.int32, (count, LANES), 1)
        bias = jnp.where(live_ref[at, :] > 0, 0.0, MASKED_SCORE).astype(F32)
        key_rows = qkv_ref[at, LANES : 2 * LANES].astype(F32)
        value_rows = qkv_ref[at, 2 * LANES : 3 * LANES].astype(F32)
        grad_keys = grad_values = None
        for head in range(2):
            own = (lane // HEAD_DIM) == head
            spare = HEAD_DIM * (1 - head)
            ones = jnp.where((lane >= spare) & (lane < spare + 3), 1.0, 0.0)
            extra = jnp.where(lane == spare + 3, bias, ones)
            keys = jnp.where(own, key_rows, extra).astype(BF16)
            values = jnp.where(own, value_rows, ones).astype(BF16)
            queries = query_ref[:, LANES * head : LANES * (head + 1)]
            above = held_ref[head]
            weights = jnp.exp(dot_nt(keys, queries))
            grad_scores = (weights * dot_nt(values, above)).astype(BF16)
            value_part = dot_nn(weights.astype(BF16), above)
            key_part = dot_nn(grad_scores, queries)
            query_part = dot_tn(keys, grad_scores)[HEAD_DIM * head : HEAD_DIM * (head + 1)]
            rows = slice(HEAD_DIM * head, HEAD_DIM * (head + 1))
            if index == 0:
                query_sum_ref[rows] = query_part
            else:
                query_sum_ref[rows] += query_part
            grad_keys = key_part if head == 0 else jnp.where(own, key_part, grad_keys)
            grad_values = value_part if head == 0 else jnp.where(own, value_part, grad_values)
        grad_values = grad_values.astype(BF16)
        out_ref[at, LANES : 2 * LANES] = grad_keys.astype(BF16)
        out_ref[at, 2 * LANES : 3 * LANES] = grad_values
        value_sum += jnp.sum(grad_values.astype(F32), axis=0, keepdims=True)
    grad_queries = (query_sum_ref[...].T * SCORE_SCALE).astype(BF16)
    out_ref[:, 0:LANES] = grad_queries
    sums_ref[0:1, :] = jnp.sum(grad_queries.astype(F32), axis=0, keepdims=True)
    sums_ref[1:2, :] = value_sum


def attend_back(live, qkv, queries, attended, grad):
    seq = qkv.shape[0]
    pairs = qkv.shape[1] // (3 * LANES)
    return pl.pallas_call(
        attend_back_kernel,
        grid=(pairs,),
        in_specs=[
            pl.BlockSpec((seq, 1), lambda p: (0, 0)),
            pl.BlockSpec((seq, 3 * LANES), lambda p: (0, p)),
            pl.BlockSpec((seq, 2 * LANES), lambda p: (0, p)),
            pl.BlockSpec((seq, LANES), lambda p: (0, p)),
            pl.BlockSpec((seq, LANES), lambda p: (0, p)),
        ],
        out_specs=[
            pl.BlockSpec((seq, 3 * LANES), lambda p: (0, p)),
            pl.BlockSpec((8, LANES), lambda p: (0, p)),
        ],
        out_shape=[
            jax.ShapeDtypeStruct((seq, pairs * 3 * LANES), BF16),
            jax.ShapeDtypeStruct((8, pairs * LANES), F32),
        ],
        scratch_shapes=[pltpu.VMEM((2, seq, LANES), BF16), pltpu.VMEM((LANES, seq), F32)],
        compiler_params=pltpu.CompilerParams(vmem_limit_bytes=VMEM_LIMIT),
        cost_estimate=pl.CostEstimate(
            flops=pairs * 80 * seq * seq * HEAD_DIM,
            bytes_accessed=seq * pairs * 1280 * 2,
            transcendentals=pairs * 2 * seq * seq,
        ),
        name="attend_back",
    )(live, qkv, queries, attended, grad)


def middle_kernel(
    x_ref,
    att_a,
    att_b,
    att_c,
    att_d,
    out_a,
    out_b,
    out_c,
    out_d,
    rows_ref,
    expand_ref,
    contract_ref,
    bias_ref,
    top_ref,
    attn_ref,
    normed_ref,
    act_ref,
    hidden_ref,
    grad_ref,
    branch_ref,
    back_ref,
    sums_ref,
):
    @pl.when(pl.program_id(0) == 0)
    def _():
        sums_ref[...] = jnp.zeros_like(sums_ref)

    pieces = ((att_a, out_a), (att_b, out_b), (att_c, out_c), (att_d, out_d))
    for low, count in tiles_of(x_ref.shape[0], TILE):
        at = slice(low, low + count)
        attn_sum = rows_ref[4:5, :]
        for att_ref, out_ref in pieces:
            attn_sum = attn_sum + dot_nt(att_ref[at, :], out_ref[...])
        attn_ref[at, :] = attn_sum
        residual = x_ref[at, :].astype(F32) + rows_ref[5:6, :] * attn_sum
        scaled, _ = norm_forward(residual)
        normed = (scaled * rows_ref[6:7, :] + rows_ref[7:8, :]).astype(BF16)
        normed_ref[at, :] = normed
        activated, slope = gelu_parts(dot_nn(normed, expand_ref[...]) + bias_ref[...])
        activated = activated.astype(BF16)
        act_ref[at, :] = activated
        grad_branch = (top_ref[at, :].astype(F32) * rows_ref[9:10, :]).astype(BF16)
        grad_ref[at, :] = grad_branch
        grad_hidden = (dot_nn(grad_branch, contract_ref[...]) * slope).astype(BF16)
        hidden_ref[at, :] = grad_hidden
        branch_ref[at, :] = dot_nt(activated, contract_ref[...]).astype(BF16)
        back = dot_nt(grad_hidden, expand_ref[...])
        back_ref[at, :] = back.astype(BF16)
        sums_ref[0:1, :] += jnp.sum(grad_hidden.astype(F32), axis=0, keepdims=True)
        sums_ref[1:2, :] += jnp.sum(back * scaled, axis=0, keepdims=True)
        sums_ref[2:3, :] += jnp.sum(back, axis=0, keepdims=True)


def middle(x_full, att, out, rows, expand, contract, bias, top):
    seq, features = x_full.shape
    hidden = expand.shape[1]
    width = att[0].shape[1]
    block = seq // 2
    part = lambda n: pl.BlockSpec((block, n), lambda i: (i, 0))
    whole = lambda a: pl.BlockSpec(a.shape, lambda i: (0, 0))
    return pl.pallas_call(
        middle_kernel,
        grid=(2,),
        in_specs=[part(features)]
        + [part(width)] * 4
        + [whole(o) for o in out]
        + [whole(rows), whole(expand), whole(contract), whole(bias), part(features)],
        out_specs=[
            part(features),
            part(features),
            part(hidden),
            part(hidden),
            part(features),
            part(features),
            part(features),
            pl.BlockSpec((8, features), lambda i: (0, 0)),
        ],
        out_shape=[
            jax.ShapeDtypeStruct((seq, features), F32),
            jax.ShapeDtypeStruct((seq, features), BF16),
            jax.ShapeDtypeStruct((seq, hidden), BF16),
            jax.ShapeDtypeStruct((seq, hidden), BF16),
            jax.ShapeDtypeStruct((seq, features), BF16),
            jax.ShapeDtypeStruct((seq, features), BF16),
            jax.ShapeDtypeStruct((seq, features), BF16),
            jax.ShapeDtypeStruct((8, features), F32),
        ],
        compiler_params=pltpu.CompilerParams(vmem_limit_bytes=VMEM_LIMIT),
        cost_estimate=pl.CostEstimate(
            flops=2 * seq * features * (features + 4 * hidden),
            bytes_accessed=seq * (9 * features + 4 * hidden + 4 * width) + 4 * features * hidden,
            transcendentals=2 * seq * hidden,
        ),
        name="middle",
    )(x_full, *att, *out, rows, expand, contract, bias, top)


def adam_step(master, gradient, first, second, decay):
    first_new = BETA_FIRST * first + (1.0 - BETA_FIRST) * gradient
    second_new = BETA_SECOND * second + (1.0 - BETA_SECOND) * gradient * gradient
    first_hat = first_new / (1.0 - BETA_FIRST**STEP)
    second_hat = second_new / (1.0 - BETA_SECOND**STEP)
    change = -LEARN_RATE * (first_hat / (jnp.sqrt(second_hat) + ADAM_EPS) + decay * master)
    return (change, first_new, second_new)


def tensor_swap(array, bit):
    return lax.ppermute(array, "tensor", [(rank, rank ^ bit) for rank in range(4)])


def gather_positions(block, rank):
    beside = tensor_swap(block, 1)
    across = tensor_swap(block, 2)
    corner = tensor_swap(across, 1)
    rows = block.shape[0]
    whole = jnp.zeros((4 * rows, block.shape[1]), block.dtype)
    for bit, piece in enumerate((block, beside, across, corner)):
        whole = lax.dynamic_update_slice_in_dim(whole, piece, (rank ^ bit) * rows, 0)
    return whole


def add_beside(partial, core, rows):
    blocks = partial.reshape(2, 2, rows, partial.shape[1])
    give = lax.dynamic_index_in_dim(blocks, 1 - core, 1, keepdims=False)
    keep = lax.dynamic_index_in_dim(blocks, core, 1, keepdims=False)
    return (keep.astype(F32) + tensor_swap(give, 1).astype(F32)).astype(BF16)


def scatter_positions(partial, core, half, rows):
    chip = add_beside(partial, core, rows)
    give = lax.dynamic_index_in_dim(chip, 1 - half, 0, keepdims=False)
    keep = lax.dynamic_index_in_dim(chip, half, 0, keepdims=False)
    return keep.astype(F32) + tensor_swap(give, 2).astype(F32)


def body(
    block_input,
    live_mask,
    cotangent,
    project_in,
    project_out,
    expand,
    contract,
    vectors,
    expand_bias,
    moment_project_in,
    second_project_in,
    moment_project_out,
    second_project_out,
    moment_expand,
    second_expand,
    moment_contract,
    second_contract,
    moment_vectors,
    second_vectors,
    moment_expand_bias,
    second_expand_bias,
):
    rows, _, features = block_input.shape
    shard, _, head_width = project_in.shape
    hidden_width = expand.shape[1]
    pairs = head_width // LANES
    groups = features // shard
    rank = lax.axis_index("tensor")
    core, half = rank % 2, rank // 2
    masters = (project_in, project_out, expand, contract, vectors, expand_bias)

    in_shard = (
        project_in.astype(BF16).reshape(shard, 3, pairs, LANES).transpose(0, 2, 1, 3)
    ).reshape(shard, 3 * head_width)
    out_shard = project_out.astype(BF16).T
    bias_shard = expand_bias.astype(BF16).reshape(-1, shard)
    small_rows = vectors.shape[0] + bias_shard.shape[0]
    small_shard = jnp.concatenate(
        [vectors.astype(BF16), bias_shard, jnp.zeros((LANES - small_rows, shard), BF16)]
    ).T
    first_copy = lax.all_gather(
        jnp.concatenate([in_shard, out_shard, small_shard], axis=1), "fsdp", axis=0, tiled=True
    )
    full_in = first_copy[:, : 3 * head_width]
    full_out = first_copy[:, 3 * head_width : 4 * head_width]
    small = first_copy[:, 4 * head_width :].T
    rows_now = jnp.concatenate([small[: vectors.shape[0]].astype(F32), jnp.zeros((6, features), F32)])
    bias_now = small[vectors.shape[0] : small_rows].astype(F32)
    bias_now = bias_now.reshape(-1, groups, shard).transpose(1, 0, 2).reshape(-1)
    second_copy = lax.all_gather(
        jnp.concatenate([expand.astype(BF16), contract.astype(BF16).T], axis=1),
        "fsdp",
        axis=0,
        tiled=True,
    )
    full_expand = second_copy[:, :hidden_width]
    full_contract = second_copy[:, hidden_width:]

    x_own = block_input[:, 0]
    live_own = lax.dynamic_slice_in_dim(live_mask, rank * rows, rows, 0) > 0
    top_own = cotangent[:, 0] * live_own.astype(F32)
    x_full = gather_positions(x_own.astype(BF16), rank)
    top_full = gather_positions(top_own.astype(BF16), rank)

    query_bias = lax.dynamic_slice_in_dim(rows_now[2], rank * head_width, head_width)
    value_bias = lax.dynamic_slice_in_dim(rows_now[3], rank * head_width, head_width)
    mixed_bias = jnp.stack([query_bias, jnp.zeros_like(query_bias), value_bias])
    mixed_bias = mixed_bias.reshape(3, pairs, LANES).transpose(1, 0, 2).reshape(1, -1)
    normed_one, qkv = project(x_full, rows_now, full_in, mixed_bias)
    attended, queries = attend(live_mask, qkv)

    out_across = tensor_swap(full_out, 2)
    out_all = (full_out, tensor_swap(full_out, 1), out_across, tensor_swap(out_across, 1))
    across = tensor_swap(attended, 2)
    att_all = (attended, tensor_swap(attended, 1), across, tensor_swap(across, 1))
    bias_here = lax.dynamic_slice_in_dim(bias_now, rank * hidden_width, hidden_width)
    attn_full, normed_two, activated, grad_hidden, grad_branch, branch_part, back_part, sums = middle(
        x_full, att_all, out_all, rows_now, full_expand, full_contract, bias_here[None], top_full
    )

    chip_sum = add_beside(back_part, core, rows)
    other_sum = tensor_swap(chip_sum, 2)
    back_sum = chip_sum.astype(F32) + other_sum.astype(F32)

    def block_of(full, index):
        return lax.dynamic_slice_in_dim(full, index * rows, rows, 0)

    def residual_back(x_block, attn_block, top_block, grad_block):
        scaled, inverse = norm_forward(x_block + rows_now[5] * attn_block)
        return top_block + norm_backward(scaled, inverse, grad_block, rows_now[6])

    attn_own = block_of(attn_full, rank)
    pick = lambda array, index: lax.dynamic_index_in_dim(array, index, 0, keepdims=False)
    grad_residual = residual_back(x_own, attn_own, top_own, pick(back_sum, half))
    partner = rank ^ 2
    grad_partner = residual_back(
        block_of(x_full, partner).astype(F32),
        block_of(attn_full, partner),
        block_of(top_full, partner).astype(F32),
        pick(back_sum, 1 - half),
    )
    attn_mine = (grad_residual * rows_now[5]).astype(BF16)
    attn_partner = (grad_partner * rows_now[5]).astype(BF16)
    low = jnp.where(half == 0, attn_mine, attn_partner)
    high = jnp.where(half == 0, attn_partner, attn_mine)
    mine = jnp.stack([low, high])
    other = tensor_swap(mine, 1)
    grad_attn = jnp.where(
        core == 0, jnp.stack([mine, other], axis=1), jnp.stack([other, mine], axis=1)
    ).reshape(4 * rows, features)

    grad_attended = dot_nn(grad_attn, full_out).astype(BF16)
    grad_mixed, head_sums = attend_back(live_mask, qkv, queries, attended, grad_attended)

    branch = scatter_positions(branch_part, core, half, rows) + rows_now[8]
    residual = x_own + rows_now[5] * attn_own
    block_output = residual + rows_now[9] * branch

    grad_expand = dot_tn(normed_two, grad_hidden).astype(BF16)
    grad_contract = dot_tn(grad_branch, activated).astype(BF16)
    grad_out = dot_tn(grad_attn, attended).astype(BF16)
    grad_in = dot_tn(normed_one, grad_mixed).astype(BF16)
    second_sum = lax.psum_scatter(
        jnp.concatenate([grad_expand, grad_contract], axis=1),
        "fsdp",
        scatter_dimension=0,
        tiled=True,
    ).astype(F32)

    normed_part = dot_nt(grad_mixed, full_in).astype(BF16)
    grad_normed_one = scatter_positions(normed_part, core, half, rows)
    scaled_one, inverse_one = norm_forward(x_own)
    input_grad = grad_residual + norm_backward(
        scaled_one, inverse_one, grad_normed_one, rows_now[0]
    )

    place = lambda values, start, total: lax.dynamic_update_slice_in_dim(
        jnp.zeros((total,), F32), values, start, 0
    )
    grad_rows = jnp.stack(
        [
            jnp.sum(grad_normed_one * scaled_one, axis=0),
            jnp.sum(grad_normed_one, axis=0),
            place(head_sums[0], rank * head_width, features),
            place(head_sums[1], rank * head_width, features),
            jnp.sum(grad_residual * rows_now[5], axis=0),
            jnp.sum(grad_residual * attn_own, axis=0),
            sums[1],
            sums[2],
            jnp.sum(top_own * rows_now[9], axis=0),
            jnp.sum(top_own * branch, axis=0),
        ]
    )
    grad_bias = place(sums[0], rank * hidden_width, expand_bias.shape[0] * groups)
    grad_bias = grad_bias.reshape(groups, -1, shard).transpose(1, 0, 2).reshape(-1, features)
    grad_small = jnp.concatenate([grad_rows, grad_bias])
    grad_small = grad_small + tensor_swap(grad_small, 2)
    grad_small = grad_small + tensor_swap(grad_small, 1)
    small_lanes = jnp.concatenate(
        [grad_small, jnp.zeros((LANES - small_rows, features), F32)]
    ).T.astype(BF16)
    first_sum = lax.psum_scatter(
        jnp.concatenate([grad_in, grad_out, small_lanes], axis=1),
        "fsdp",
        scatter_dimension=0,
        tiled=True,
    ).astype(F32)

    sum_in = first_sum[:, : 3 * head_width].reshape(shard, pairs, 3, LANES).transpose(0, 2, 1, 3)
    sum_out = first_sum[:, 3 * head_width : 4 * head_width].T
    sum_small = first_sum[:, 4 * head_width :].T
    shard_rows = sum_small[: vectors.shape[0]]
    totals = (
        sum_in.reshape(project_in.shape),
        sum_out,
        second_sum[:, :hidden_width],
        second_sum[:, hidden_width:].T,
        shard_rows,
        sum_small[vectors.shape[0] : small_rows].reshape(-1),
    )
    firsts = (
        moment_project_in,
        moment_project_out,
        moment_expand,
        moment_contract,
        moment_vectors,
        moment_expand_bias,
    )
    seconds = (
        second_project_in,
        second_project_out,
        second_expand,
        second_contract,
        second_vectors,
        second_expand_bias,
    )
    decays = (WEIGHT_DECAY, WEIGHT_DECAY, WEIGHT_DECAY, WEIGHT_DECAY, 0.0, 0.0)
    results = [adam_step(*each) for each in zip(masters, totals, firsts, seconds, decays)]
    changes = tuple((result[0] for result in results))
    moments = []
    for result in results:
        moments.append(result[1])
        moments.append(result[2])
    return (
        block_output[:, None],
        input_grad[:, None],
        *totals,
        masters[0] + changes[0],
        changes[1],
        masters[2] + changes[2],
        masters[3] + changes[3],
        changes[4],
        changes[5],
        *moments,
        shard_rows[7],
    )


def solution(mesh):
    tokens = P("tensor", "fsdp", None)
    into = P("fsdp", None, "tensor")
    wide = P("fsdp", "tensor")
    tall = P("tensor", "fsdp")
    row = P(None, "fsdp")
    line = P("fsdp")
    params = (into, tall, wide, tall, row, line)
    moments = (into, into, tall, tall, wide, wide, tall, tall, row, row, line, line)
    return jax.shard_map(
        body,
        mesh=mesh,
        in_specs=(tokens, row, tokens) + params + moments,
        out_specs=(tokens, tokens) + params + params + moments + (line,),
        check_vma=False,
    )
```

time: 879 us -> 431 us (0.49)
  waiting for transfers between devices: 454 us -> 177 us
  matrix products: 160 us -> 21.1 us
  blocking collectives: 116 us -> 0 us
  Pallas kernels: 0 us -> 71 us
  local copies, waits for them, and re-layouts: 52.4 us -> 89.9 us
  other arithmetic: 69.4 us -> 38.5 us
  starting transfers between devices: 1.77 us -> 14.3 us
    reduce_scatter x6 -> x0, waiting for transfers between devices: 203 us -> none  [the longest x1 64.9 us: body(): lax.psum_scatter(grad_project_in.astype(jnp.bfloat16), 'fsdp', scatter_di...]
    dot_general x40 -> x6, matrix products: 160 us -> 21.1 us  [the longest x4 15.4 us: dot_tn(): lax.dot_general(left, right, (((0,), (0,)), ((), ())), preferred_element_...]
    all_gather x7 -> x2, waiting for transfers between devices: 150 us -> 34.7 us  [the longest x1 21.8 us: body(): lax.all_gather(jnp.concatenate([in_shard, out_shard, small_shard], axis=1...]
    all_gather x3 -> x0, blocking collectives: 84.5 us -> none  [the longest x1 30.5 us: gather_weights(): lax.all_gather(copies[1], 'fsdp', axis=1, tiled=True)]
    ppermute x0 -> x21, waiting for transfers between devices: none -> 83 us  [tensor_swap(): lax.ppermute(array, 'tensor', [(rank, rank ^ bit) for rank in range(4)])]
    pallas_call x0 -> x4, Pallas kernels: none -> 71 us  [the longest x1 24.6 us: middle(): pl.pallas_call(middle_kernel, grid=(2,), in_specs=[part(features)] + [par...]
    unnamed x19 -> x6, waiting for transfers between devices: 100 us -> 59.2 us
    convert_element_type x15 -> x9, other arithmetic: 33.7 us -> 4.57 us  [the longest x3 3.31 us: add_beside(): return (keep.astype(F32) + tensor_swap(give, 1).astype(F32)).astype(BF16)]
  transfers between devices with their start and end apart: 16 -> 25, of which waited for: 13 -> 9; matrix products, arithmetic and copies ran while one was open for 21% -> 28% of each run, Pallas kernels for 0% -> 11%
where the time goes in v1:
time: 431 us; the launch traced here: 427 us
  waiting for transfers between devices  177 us (41%)
  local copies, waits for them, and re-layouts  89.9 us (21%)
  Pallas kernels  71 us (16%)
  other arithmetic  38.5 us (9%)
  matrix products  21.1 us (5%)
  between operations  15 us (3%)
  starting transfers between devices  14.3 us (3%)
    ppermute x21, waiting for transfers between devices, tensor_swap(): lax.ppermute(array, 'tensor', [(rank, rank ^ bit) for rank in range(4)])  83 us
    unnamed x6, waiting for transfers between devices  59.2 us
    unnamed x119, local copies, waits for them, and re-layouts  40.7 us
    pallas_call x1, Pallas kernels, middle(): pl.pallas_call(middle_kernel, grid=(2,), in_specs=[part(features)] + [par...  24.6 us
    pallas_call x1, Pallas kernels, attend_back(): pl.pallas_call(attend_back_kernel, grid=(pairs,), in_specs=[pl.BlockSpec(...  24.3 us
    all_gather x1, waiting for transfers between devices, body(): lax.all_gather(jnp.concatenate([in_shard, out_shard, small_shard], axis=1...  21.8 us
    pallas_call x1, Pallas kernels, attend(): pl.pallas_call(attend_kernel, grid=(pairs,), in_specs=[pl.BlockSpec((seq,...  15.7 us
    dot_general x4, matrix products, dot_tn(): lax.dot_general(left, right, (((0,), (0,)), ((), ())), preferred_element_...  15.4 us
  transfers between devices with their start and end apart: 25, of which 9 were waited for; matrix products, arithmetic and copies ran while one was open for 28% of the time, Pallas kernels for 11%

profile of v1, /device:TPU:0, one launch (start us, length us, event | category | flops | bytes accessed | tf_op | source)
XLA Modules:
  0.0 426.7 jit_solution(10597462977609026861)
XLA Ops:
  13.3 2.9 collective-permute-start.1
  16.2 16.0 %collective-permute-done.1 = bf16[344,1024]{1,0:T(8,128)(2,1)S(1)} collective-permute-done((bf16[344,1024]{1,0:T(8,128)(2,1)}, bf16[344,1024]{1,0:T(8,128)(2,1)S(1)}, u32[]{:S(2)}, u32[]{:S(2)}) %collective-permute-start.1) | collective-permute-done | bytes 704544 | tf_op jit(solution)/shard_map/ppermute | solution.py:370
  37.0 1.7 collective-permute-start.10
  40.5 2.0 constant_dynamic-update-slice_fusion.8
  43.4 2.0 constant_dynamic-update-slice_fusion.6.x_ref
  45.4 21.8 %all-gather.3.cloned.1.call-done = bf16[1024,1152]{0,1:T(8,128)(2,1)} async-done(((bf16[128,1152]{0,1:T(8,128)(2,1)}), bf16[1024,1152]{0,1:T(8,128)(2,1)}) %all-gather.3.cloned.1.call-update) | async-done | bytes 2359312 | tf_op jit(solution)/shard_map/all_gather | solution.py:439
  70.9 2.7 slice.117
  73.5 2.7 copy.95.weight_ref
  78.9 6.4 %project.1 = (bf16[1376,1024]{1,0:T(8,128)(2,1)}, bf16[1376,768]{1,0:T(8,128)(2,1)}) custom-call(bf16[1376,1024]{1,0:T(8,128)(2,1)} %constant_dynamic-update-slice_fusion.6.x_ref, f32[16,1024]{1,0:T(8,128)} %concatenate.28.rows_ref, bf16[1024,768]{1,0:T(8,128)(2,1)} %copy.95.weight_ref, f32[1,768]{1,0:T(1,128)} %reshape.192.bias_ref), custom_call_target="tpu_custom_call" | custom-call | flops 2164260864 | bytes 9322496 | tf_op jit(solution)/shard_map/project/pallas_call | solution.py:79
  85.4 15.7 %attend.1 = (bf16[1376,256]{1,0:T(8,128)(2,1)}, bf16[1376,512]{1,0:T(8,128)(2,1)}) custom-call(s32[1376,1]{1,0:T(8,128)} %copy.96.live_ref, bf16[1376,768]{1,0:T(8,128)(2,1)} %get-tuple-element.41.qkv_ref), custom_call_target="tpu_custom_call" | custom-call | flops 7755268096 | bytes 4227072 | tf_op jit(solution)/shard_map/attend/pallas_call | solution.py:151
  102.1 2.1 constant_dynamic-update-slice_fusion.4
  104.2 2.0 constant_dynamic-update-slice_fusion.3
  106.7 11.5 %collective-permute-done.4.att_c = bf16[1376,256]{1,0:T(8,128)(2,1)} collective-permute-done((bf16[1376,256]{1,0:T(8,128)(2,1)}, bf16[1376,256]{1,0:T(8,128)(2,1)}, u32[]{:S(2)}, u32[]{:S(2)}) %collective-permute-start.4) | collective-permute-done | bytes 704544 | tf_op jit(solution)/shard_map/ppermute | solution.py:370
  118.2 2.0 constant_dynamic-update-slice_fusion.2.top_ref
  122.5 2.0 copy.101.out_c
  124.6 2.0 copy.100.out_b
  126.6 2.0 copy.102.out_d
  128.7 12.9 %all-gather.5.cloned.1.call-done = bf16[1024,2048]{1,0:T(8,128)(2,1)} async-done(((bf16[128,2048]{1,0:T(8,128)(2,1)}), bf16[1024,2048]{1,0:T(8,128)(2,1)}) %all-gather.5.cloned.1.call-update) | async-done | bytes 4194320 | tf_op jit(solution)/shard_map/all_gather | solution.py:448
  141.5 4.7 %fusion.33 = (bf16[1024,1024]{1,0:T(8,128)(2,1)}, bf16[1024,1024]{1,0:T(8,128)(2,1)}) fusion(bf16[1024,2048]{1,0:T(8,128)(2,1)} %all-gather.5.cloned.1.call-done), kind=kLoop, calls=%fused_computation.133 | loop fusion | bytes 8388608 | tf_op jit(solution)/shard_map/slice | solution.py:455
  146.2 24.6 %middle.1 = (f32[1376,1024]{1,0:T(8,128)}, bf16[1376,1024]{1,0:T(8,128)(2,1)}, bf16[1376,1024]{1,0:T(8,128)(2,1)}, bf16[1376,1024]{1,0:T(8,128)(2,1)}, bf16[1376...) custom-call(bf16[1376,1024]{1,0:T(8,128)(2,1)} %constant_dynamic-update-slice_fu, ...), custom_call_target="tpu_custom_call" | custom-call | flops 14428405760 | bytes 23920640 | tf_op jit(solution)/shard_map/middle/pallas_call | solution.py:323
  170.9 2.6 dynamic-slice_bitcast_fusion.1
  177.0 3.3 fusion.31
  180.6 2.1 fusion.1
  184.2 4.1 convolution_convert_fusion.3
  189.8 26.6 %collective-permute-done.15 = bf16[2,344,1024]{2,1,0:T(8,128)(2,1)S(1)} collective-permute-done((bf16[2,344,1024]{2,1,0:T(8,128)(2,1)S(1)}, bf16[2,344,1024]{2,1,0:T(8,128)(2,1)S(1)}, u32[]{:S(2)}, u32[]{:S(2)}) %collective-permute-start.15) | collective-permute-done | bytes 1409056 | tf_op jit(solution)/shard_map/ppermute | solution.py:370
  217.0 14.2 %collective-permute-done.13 = bf16[344,1024]{1,0:T(8,128)(2,1)S(1)} collective-permute-done((bf16[344,1024]{1,0:T(8,128)(2,1)S(1)}, bf16[344,1024]{1,0:T(8,128)(2,1)S(1)}, u32[]{:S(2)}, u32[]{:S(2)}) %collective-permute-start.13) | collective-permute-done | bytes 704544 | tf_op jit(solution)/shard_map/ppermute | solution.py:370
  231.1 2.8 multiply_reduce_fusion
  236.3 2.0 select_bitcast_fusion.1
  242.1 3.8 convolution_convert_fusion.2
  245.9 2.6 pad_maximum_fusion
  248.4 6.5 %copy.121 = bf16[1024,2048]{1,0:T(8,128)(2,1)} copy(bf16[1024,2048]{0,1:T(8,128)(2,1)} %pad_maximum_fusion) | data formatting | bytes 8388608
  255.1 3.4 maximum_select_fusion
  258.8 2.2 copy-done.12
  261.1 1.8 convolution_convert_fusion.1.grad_ref
  262.9 24.3 %attend_back.1 = (bf16[1376,768]{1,0:T(8,128)(2,1)}, f32[8,256]{1,0:T(8,128)}) custom-call(s32[1376,1]{1,0:T(8,128)} %copy.96.live_ref, bf16[1376,768]{1,0:T(8,128)(2,1)} %get-tuple-element.41.qkv_ref, bf16[1376,512]{1,0:T(8,128)(2,1)} %get-tuple-element.46.query_ref, bf16[1376,256]{1,0:T(8,128)(2,1)} %get-tuple-element.42.att_a.attended_ref, ...), custom_call_target="tpu_custom_call" | custom-call | flops 19388170240 | bytes 7045120 | tf_op jit(solution)/shard_map/attend_back/pallas_call | solution.py:233
  287.1 4.0 convolution_convert_fusion
  291.3 3.2 collective-permute-done.17
  301.6 11.5 %collective-permute-done.18 = bf16[344,1024]{1,0:T(8,128)(2,1)S(1)} collective-permute-done((bf16[344,1024]{1,0:T(8,128)(2,1)S(1)}, bf16[344,1024]{1,0:T(8,128)(2,1)S(1)}, u32[]{:S(2)}, u32[]{:S(2)}) %collective-permute-start.18) | collective-permute-done | bytes 704544 | tf_op jit(solution)/shard_map/ppermute | solution.py:370
  314.6 2.8 concatenate.30
  318.8 5.3 %convolution_convert_fusion.4 = bf16[1024,768]{0,1:T(8,128)(2,1)S(1)} fusion(bf16[1376,1024]{1,0:T(8,128)(2,1)} %get-tuple-element.48, bf16[1376,768]{1,0:T(8,128)(2,1)} %get-tuple-element.47), kind=kOutput, calls=%fused_computation.14 | convolution fusion | flops 2165047296 | bytes 6504448 | tf_op jit(solution)/shard_map/dot_general | solution.py:38
  324.3 2.1 convolution_convert_fusion.5
  328.2 4.6 %copy.119 = bf16[1024,1152]{1,0:T(8,128)(2,1)} copy(bf16[1024,1152]{0,1:T(8,128)(2,1)} %pad_maximum_fusion.1) | data formatting | bytes 4718592
  332.8 2.0 copy.112
  334.8 2.0 copy.109
  336.9 2.0 copy.110
  338.9 4.0 copy.113
  343.6 2.5 copy.114
  355.0 59.1 %reduce-scatter.7.cloned.1.call-done = bf16[128,1152]{1,0:T(8,128)(2,1)} async-done(((bf16[1024,1152]{1,0:T(8,128)(2,1)}), bf16[128,1152]{1,0:T(8,128)(2,1)}) %reduce-scatter.7.cloned.1.call-update) | async-done | bytes 294928
  (239 shorter events, 64.3 us)
Async XLA Ops:
  7.2 59.9 %all-gather.3.cloned.1.call-start = ((), (), s32[]{:S(2)}) async-start(), calls=%async_computation.2 | async-start | bytes 2654208 | tf_op jit(solution)/shard_map/all_gather | solution.py:439
  9.7 131.9 %all-gather.5.cloned.1.call-start = ((), (), s32[]{:S(2)}) async-start(), calls=%async_computation.3 | async-start | bytes 4718592 | tf_op jit(solution)/shard_map/all_gather | solution.py:448
  10.8 335.4 %reduce-scatter.9.cloned.1.call-start = ((), (), s32[]{:S(2)}) async-start(), calls=%async_computation.5 | async-start | bytes 4718592
  12.2 20.0 %copy-start.36 = (s32[1376,1]{0,1:T(1,128)S(1)}, s32[1376,1]{0,1:T(1,128)}, u32[]{:S(2)}) copy-start(s32[1376,1]{0,1:T(1,128)} %param.22) | copy-start | bytes 16516
  13.3 19.4 %copy-start.3 = (bf16[1376,1024]{1,0:T(8,128)(2,1)}, bf16[1376,1024]{1,0:T(8,128)(2,1)S(1)}, u32[]{:S(2)}) copy-start(bf16[1376,1024]{1,0:T(8,128)(2,1)S(1)} %get-tuple-element.178) | copy-start | bytes 8454148
  13.3 18.9 %collective-permute-start.1 = (bf16[344,1024]{1,0:T(8,128)(2,1)}, bf16[344,1024]{1,0:T(8,128)(2,1)S(1)}, u32[]{:S(2)}, u32[]{:S(2)}) collective-permute-start(bf16[344,1024]{1,0:T(8,128)(2,1)} %get-tuple-element.179), channel_id=1, source_target_pairs={{0,2},{1,3},{2,0},{3,1},{4,6},{5,7},{6,4},{7,5},{8,10},{9,11},{10,... | collective-permute-start | bytes 2113544 | tf_op jit(solution)/shard_map/ppermute | solution.py:370
  16.2 24.2 %collective-permute-start = (bf16[344,1024]{1,0:T(8,128)(2,1)}, bf16[344,1024]{1,0:T(8,128)(2,1)}, u32[]{:S(2)}, u32[]{:S(2)}) collective-permute-start(bf16[344,1024]{1,0:T(8,128)(2,1)} %get-tuple-element.179), channel_id=1, source_target_pairs={{0,1},{1,0},{2,3},{3,2},{4,5},{5,4},{6,7},{7,6},{8,9},{9,8},{10,11... | collective-permute-start | bytes 2113544 | tf_op jit(solution)/shard_map/ppermute | solution.py:370
  32.2 11.2 %collective-permute-start.2 = (bf16[344,1024]{1,0:T(8,128)(2,1)S(1)}, bf16[344,1024]{1,0:T(8,128)(2,1)}, u32[]{:S(2)}, u32[]{:S(2)}) collective-permute-start(bf16[344,1024]{1,0:T(8,128)(2,1)S(1)} %collective-permute-done.1), channel_id=1, source_target_pairs={{0,1},{1,0},{2,3},{3,2},{4,5},{5,4},{6,7},{7,6},{8,9},{9,8},{10,11... | collective-permute-start | bytes 2113544 | tf_op jit(solution)/shard_map/ppermute | solution.py:370
  36.5 65.6 %collective-permute-start.9 = (bf16[344,1024]{1,0:T(8,128)(2,1)}, bf16[344,1024]{1,0:T(8,128)(2,1)}, u32[]{:S(2)}, u32[]{:S(2)}) collective-permute-start(bf16[344,1024]{1,0:T(8,128)(2,1)} %get-tuple-element.177), channel_id=1, source_target_pairs={{0,1},{1,0},{2,3},{3,2},{4,5},{5,4},{6,7},{7,6},{8,9},{9,8},{10,11... | collective-permute-start | bytes 2113544 | tf_op jit(solution)/shard_map/ppermute | solution.py:370
  37.0 64.6 %collective-permute-start.10 = (bf16[344,1024]{1,0:T(8,128)(2,1)}, bf16[344,1024]{1,0:T(8,128)(2,1)}, u32[]{:S(2)}, u32[]{:S(2)}) collective-permute-start(bf16[344,1024]{1,0:T(8,128)(2,1)} %get-tuple-element.177), channel_id=1, source_target_pairs={{0,2},{1,3},{2,0},{3,1},{4,6},{5,7},{6,4},{7,5},{8,10},{9,11},{10,... | collective-permute-start | bytes 2113544 | tf_op jit(solution)/shard_map/ppermute | solution.py:370
  77.4 24.7 %collective-permute-start.7 = (bf16[1024,256]{0,1:T(8,128)(2,1)S(1)}, bf16[1024,256]{0,1:T(8,128)(2,1)}, u32[]{:S(2)}, u32[]{:S(2)}) collective-permute-start(bf16[1024,256]{0,1:T(8,128)(2,1)S(1)} %slice.120), channel_id=1, source_target_pairs={{0,2},{1,3},{2,0},{3,1},{4,6},{5,7},{6,4},{7,5},{8,10},{9,11},{10,... | collective-permute-start | bytes 1572872 | tf_op jit(solution)/shard_map/ppermute | solution.py:370
  101.0 17.2 %collective-permute-start.4 = (bf16[1376,256]{1,0:T(8,128)(2,1)}, bf16[1376,256]{1,0:T(8,128)(2,1)}, u32[]{:S(2)}, u32[]{:S(2)}) collective-permute-start(bf16[1376,256]{1,0:T(8,128)(2,1)} %get-tuple-element.42.att_a.attended_ref), channel_id=1, source_target_pairs={{0,2},{1,3},{2,0},{3,1},{4,6},{5,7},{6,4},{7,5},{8,10},{9,11},{10,... | collective-permute-start | bytes 2113544 | tf_op jit(solution)/shard_map/ppermute | solution.py:370
  101.6 16.6 %collective-permute-start.11 = (bf16[344,1024]{1,0:T(8,128)(2,1)}, bf16[344,1024]{1,0:T(8,128)(2,1)}, u32[]{:S(2)}, u32[]{:S(2)}) collective-permute-start(bf16[344,1024]{1,0:T(8,128)(2,1)} %collective-permute-done.10), channel_id=1, source_target_pairs={{0,1},{1,0},{2,3},{3,2},{4,5},{5,4},{6,7},{7,6},{8,9},{9,8},{10,11... | collective-permute-start | bytes 2113544 | tf_op jit(solution)/shard_map/ppermute | solution.py:370
  101.6 23.0 %collective-permute-start.6 = (bf16[1024,256]{0,1:T(8,128)(2,1)S(1)}, bf16[1024,256]{0,1:T(8,128)(2,1)}, u32[]{:S(2)}, u32[]{:S(2)}) collective-permute-start(bf16[1024,256]{0,1:T(8,128)(2,1)S(1)} %slice.120), channel_id=1, source_target_pairs={{0,1},{1,0},{2,3},{3,2},{4,5},{5,4},{6,7},{7,6},{8,9},{9,8},{10,11... | collective-permute-start | bytes 1572872 | tf_op jit(solution)/shard_map/ppermute | solution.py:370
  102.1 24.5 %collective-permute-start.8 = (bf16[1024,256]{0,1:T(8,128)(2,1)}, bf16[1024,256]{0,1:T(8,128)(2,1)}, u32[]{:S(2)}, u32[]{:S(2)}) collective-permute-start(bf16[1024,256]{0,1:T(8,128)(2,1)} %collective-permute-done.7), channel_id=1, source_target_pairs={{0,1},{1,0},{2,3},{3,2},{4,5},{5,4},{6,7},{7,6},{8,9},{9,8},{10,11... | collective-permute-start | bytes 1572872 | tf_op jit(solution)/shard_map/ppermute | solution.py:370
  106.2 40.0 %collective-permute-start.3 = (bf16[1376,256]{1,0:T(8,128)(2,1)}, bf16[1376,256]{1,0:T(8,128)(2,1)}, u32[]{:S(2)}, u32[]{:S(2)}) collective-permute-start(bf16[1376,256]{1,0:T(8,128)(2,1)} %get-tuple-element.42.att_a.attended_ref), channel_id=1, source_target_pairs={{0,1},{1,0},{2,3},{3,2},{4,5},{5,4},{6,7},{7,6},{8,9},{9,8},{10,11... | collective-permute-start | bytes 2113544 | tf_op jit(solution)/shard_map/ppermute | solution.py:370
  118.2 28.0 %collective-permute-start.5 = (bf16[1376,256]{1,0:T(8,128)(2,1)}, bf16[1376,256]{1,0:T(8,128)(2,1)}, u32[]{:S(2)}, u32[]{:S(2)}) collective-permute-start(bf16[1376,256]{1,0:T(8,128)(2,1)} %collective-permute-done.4.att_c), channel_id=1, source_target_pairs={{0,1},{1,0},{2,3},{3,2},{4,5},{5,4},{6,7},{7,6},{8,9},{9,8},{10,11... | collective-permute-start | bytes 2113544 | tf_op jit(solution)/shard_map/ppermute | solution.py:370
  173.4 7.1 %collective-permute-start.14 = (bf16[2,344,1024]{2,1,0:T(8,128)(2,1)}, bf16[2,344,1024]{2,1,0:T(8,128)(2,1)}, u32[]{:S(2)}, u32[]{:S(2)}) collective-permute-start(bf16[2,344,1024]{2,1,0:T(8,128)(2,1)} %dynamic-slice_bitcast_fusion.1), channel_id=1, source_target_pairs={{0,1},{1,0},{2,3},{3,2},{4,5},{5,4},{6,7},{7,6},{8,9},{9,8},{10,11... | collective-permute-start | bytes 4227080 | tf_op jit(solution)/shard_map/ppermute | solution.py:370
  176.4 12.0 %collective-permute-start.12 = (bf16[2,344,1024]{2,1,0:T(8,128)(2,1)S(1)}, bf16[2,344,1024]{2,1,0:T(8,128)(2,1)S(1)}, u32[]{:S(2)}, u32[]{:S(2)}) collective-permute-start(bf16[2,344,1024]{2,1,0:T(8,128)(2,1)S(1)} %dynamic-slice_bitcast_fusion.2), channel_id=1, source_target_pairs={{0,1},{1,0},{2,3},{3,2},{4,5},{5,4},{6,7},{7,6},{8,9},{9,8},{10,11... | collective-permute-start | bytes 4227080 | tf_op jit(solution)/shard_map/ppermute | solution.py:370
  177.0 3.6 copy-start.11
  180.2 4.0 copy-start.49
  180.5 3.7 copy-start.48
  182.7 33.7 %collective-permute-start.15 = (bf16[2,344,1024]{2,1,0:T(8,128)(2,1)S(1)}, bf16[2,344,1024]{2,1,0:T(8,128)(2,1)S(1)}, u32[]{:S(2)}, u32[]{:S(2)}) collective-permute-start(bf16[2,344,1024]{2,1,0:T(8,128)(2,1)S(1)} %fusion.1), channel_id=1, source_target_pairs={{0,2},{1,3},{2,0},{3,1},{4,6},{5,7},{6,4},{7,5},{8,10},{9,11},{10,... | collective-permute-start | bytes 4227080 | tf_op jit(solution)/shard_map/ppermute | solution.py:370
  184.2 4.2 copy-start.8
  188.4 45.6 %slice-start = ((s8[5636096]{0:T(1024)(128)(4,1)}), s8[4194304]{0:T(1024)(128)(4,1)S(1)}, s32[]{:S(2)}) async-start(s8[5636096]{0:T(1024)(128)(4,1)} %bitcast.178), calls=%async_computation.6 | async-start | bytes 8388608
  189.1 42.0 %collective-permute-start.13 = (bf16[344,1024]{1,0:T(8,128)(2,1)S(1)}, bf16[344,1024]{1,0:T(8,128)(2,1)S(1)}, u32[]{:S(2)}, u32[]{:S(2)}) collective-permute-start(bf16[344,1024]{1,0:T(8,128)(2,1)S(1)} %dynamic-slice_bitcast_fusion.4), channel_id=1, source_target_pairs={{0,2},{1,3},{2,0},{3,1},{4,6},{5,7},{6,4},{7,5},{8,10},{9,11},{10,... | collective-permute-start | bytes 2113544 | tf_op jit(solution)/shard_map/ppermute | solution.py:370
  189.8 44.1 %slice-start.1 = ((s8[5636096]{0:T(1024)(128)(4,1)}), s8[1441792]{0:T(1024)(128)(4,1)S(1)}, s32[]{:S(2)}) async-start(s8[5636096]{0:T(1024)(128)(4,1)} %bitcast.178), calls=%async_computation.7 | async-start | bytes 2883584
  238.6 3.5 copy-start.46
  240.4 14.7 %collective-permute-start.16 = (bf16[2,344,1024]{2,1,0:T(8,128)(2,1)}, bf16[2,344,1024]{2,1,0:T(8,128)(2,1)}, u32[]{:S(2)}, u32[]{:S(2)}) collective-permute-start(bf16[2,344,1024]{2,1,0:T(8,128)(2,1)} %get-tuple-element.188), channel_id=1, source_target_pairs={{0,1},{1,0},{2,3},{3,2},{4,5},{5,4},{6,7},{7,6},{8,9},{9,8},{10,11... | collective-permute-start | bytes 4227080 | tf_op jit(solution)/shard_map/ppermute | solution.py:370
  255.0 159.0 %reduce-scatter.7.cloned.1.call-start = ((), (), s32[]{:S(2)}) async-start(), calls=%async_computation.4 | async-start | bytes 2654208
  258.8 4.0 copy-start.9
  291.2 3.2 collective-permute-start.17
  295.1 19.5 %copy-start.5 = (bf16[2,344,1024]{2,1,0:T(8,128)(2,1)}, bf16[2,344,1024]{2,1,0:T(8,128)(2,1)S(1)}, u32[]{:S(2)}) copy-start(bf16[2,344,1024]{2,1,0:T(8,128)(2,1)S(1)} %fusion) | copy-start | bytes 4227076
  295.1 3.9 copy-start.37
  295.2 17.9 %collective-permute-start.18 = (bf16[344,1024]{1,0:T(8,128)(2,1)S(1)}, bf16[344,1024]{1,0:T(8,128)(2,1)S(1)}, u32[]{:S(2)}, u32[]{:S(2)}) collective-permute-start(bf16[344,1024]{1,0:T(8,128)(2,1)S(1)} %dynamic-slice_bitcast_fusion.3), channel_id=1, source_target_pairs={{0,2},{1,3},{2,0},{3,1},{4,6},{5,7},{6,4},{7,5},{8,10},{9,11},{10,... | collective-permute-start | bytes 2113544 | tf_op jit(solution)/shard_map/ppermute | solution.py:370
  299.0 15.6 %copy-start.33 = (f32[344]{0:T(512)}, f32[344]{0:T(512)S(1)}, u32[]{:S(2)}) copy-start(f32[344]{0:T(512)S(1)} %add_rsqrt_fusion.1) | copy-start | bytes 4132
  301.6 11.5 %copy-start.35 = (f32[1,1024]{1,0:T(1,128)}, f32[1,1024]{1,0:T(1,128)S(1)}, u32[]{:S(2)}) copy-start(f32[1,1024]{1,0:T(1,128)S(1)} %constant_dynamic-update-slice_fusion.1) | copy-start | bytes 12292
  317.4 6.7 %collective-permute-start.19 = (f32[14,1024]{1,0:T(8,128)}, f32[14,1024]{1,0:T(8,128)S(1)}, u32[]{:S(2)}, u32[]{:S(2)}) collective-permute-start(f32[14,1024]{1,0:T(8,128)} %concatenate.30), channel_id=1, source_target_pairs={{0,2},{1,3},{2,0},{3,1},{4,6},{5,7},{6,4},{7,5},{8,10},{9,11},{10,... | collective-permute-start | bytes 172040 | tf_op jit(solution)/shard_map/ppermute | solution.py:370
  318.8 5.3 %copy-start.29 = (f32[14,1024]{1,0:T(8,128)S(1)}, f32[14,1024]{1,0:T(8,128)}, u32[]{:S(2)}) copy-start(f32[14,1024]{1,0:T(8,128)} %concatenate.30) | copy-start | bytes 172036
  318.8 5.4 %copy-start.10 = (bf16[2,2,344,1024]{3,2,1,0:T(8,128)(2,1)S(1)}, bf16[2,2,344,1024]{3,2,1,0:T(8,128)(2,1)}, u32[]{:S(2)}) copy-start(bf16[2,2,344,1024]{3,2,1,0:T(8,128)(2,1)} %copy-done.9) | copy-start | bytes 8454148
  324.2 2.2 collective-permute-start.20
  338.9 4.0 copy-start.39
  338.9 4.0 copy-start.38
  338.9 4.0 copy-start.6
  338.9 4.0 copy-start.34
  415.4 3.3 copy-start.20
  415.4 3.2 copy-start.26
  416.0 3.9 copy-start.21
  (29 other events, 56.0 us)
Sparse Core Ops, SparseCore 0:
  10.7 56.4 all-gather.2
  69.9 71.6 all-gather.4
  255.1 86.3 reduce-scatter.8
  345.3 68.7 reduce-scatter.6

commit v2 on v1

v2 whole, which is shorter than its diff:
```python
import functools

import jax
import jax.numpy as jnp
from jax import lax
from jax.experimental import pallas as pl
from jax.experimental.pallas import tpu as pltpu
from jax.sharding import PartitionSpec as P

HEAD_DIM = 64
STEP = 3
NORM_EPS = 1e-06
BETA_FIRST = 0.9
BETA_SECOND = 0.999
LEARN_RATE = 0.004
WEIGHT_DECAY = 0.04
ADAM_EPS = 1e-08
MASKED_SCORE = -1e30
ROOT_HALF = 0.7071067811865476
DENSITY_NORM = 0.3989422804014327
SCORE_SCALE = HEAD_DIM ** (-0.5)
LANES = 128
TILE = 352
CHUNK = 256
LONG = 4
VMEM_LIMIT = 56 * 2**20
F32 = jnp.float32
BF16 = jnp.bfloat16


def dot_nn(left, right):
    return lax.dot_general(left, right, (((1,), (0,)), ((), ())), preferred_element_type=F32)


def dot_nt(left, right):
    return lax.dot_general(left, right, (((1,), (1,)), ((), ())), preferred_element_type=F32)


def dot_tn(left, right):
    return lax.dot_general(left, right, (((0,), (0,)), ((), ())), preferred_element_type=F32)


def tiles_of(total, tile):
    return [(low, min(tile, total - low)) for low in range(0, total, tile)]


def norm_forward(values):
    center = jnp.mean(values, axis=-1, keepdims=True)
    offset = values - center
    spread = jnp.mean(offset * offset, axis=-1, keepdims=True)
    inverse = lax.rsqrt(spread + NORM_EPS)
    return offset * inverse, inverse


def norm_backward(scaled, inverse, grad_normed, norm_gain):
    grad_scaled = grad_normed * norm_gain
    first_mean = jnp.mean(grad_scaled, axis=-1, keepdims=True)
    second_mean = jnp.mean(grad_scaled * scaled, axis=-1, keepdims=True)
    return inverse * (grad_scaled - first_mean - scaled * second_mean)


def gelu_parts(hidden):
    normal_cdf = 0.5 * (1.0 + lax.erf(hidden * ROOT_HALF))
    density = DENSITY_NORM * jnp.exp(-0.5 * hidden * hidden)
    return (hidden * normal_cdf, normal_cdf + hidden * density)


def call(kernel, ids, args, in_specs, outs, out_specs, name, cost=(0, 0, 0), grid=(1,), scratch=(), aliases=None, after=()):
    count = 1 + len(args)
    waits = len(after)

    def run(*refs):
        kernel(*refs[:count], *refs[count + waits :])

    several = isinstance(outs, (list, tuple))
    return pl.pallas_call(
        run,
        grid_spec=pltpu.PrefetchScalarGridSpec(
            num_scalar_prefetch=1,
            grid=grid,
            in_specs=list(in_specs) + [pl.BlockSpec(memory_space=pl.ANY)] * waits,
            out_specs=out_specs,
            scratch_shapes=scratch,
        ),
        out_shape=outs,
        input_output_aliases=aliases or {},
        compiler_params=pltpu.CompilerParams(vmem_limit_bytes=VMEM_LIMIT),
        cost_estimate=pl.CostEstimate(flops=cost[0], bytes_accessed=cost[1], transcendentals=cost[2]),
        name=name,
    )(ids, *args, *after)


def whole(array):
    zeros = (0,) * len(array.shape)
    return pl.BlockSpec(array.shape, lambda *i: zeros)


def plain(kernel, ids, args, outs, name, **more):
    return call(kernel, ids, args, [whole(a) for a in args], outs, [whole(o) for o in outs], name, **more)


def shape_of(shape, dtype):
    return jax.ShapeDtypeStruct(shape, dtype)


ANYWHERE = pl.BlockSpec(memory_space=pl.ANY)


def low_bit(ids_ref):
    return lax.rem(ids_ref[0], 2)


def pack_kernel(ids_ref, in_ref, out_ref, expand_ref, contract_ref, small_ref, first, second, third):
    for pair, packed in enumerate((first, second)):
        for part in range(3):
            packed[:, part * LANES : (part + 1) * LANES] = in_ref[
                part, :, pair * LANES : (pair + 1) * LANES
            ].astype(BF16)
    first[:, 3 * LANES :] = small_ref[...].T.astype(BF16)
    second[:, 3 * LANES :] = out_ref[...].T.astype(BF16)
    hidden = expand_ref.shape[1]
    third[:, :hidden] = expand_ref[...].astype(BF16)
    third[:, hidden:] = contract_ref[...].T.astype(BF16)


def pack(ids, project_in, project_out, expand, contract, small):
    _, shard, head_width = project_in.shape
    widths = (4 * LANES, 3 * LANES + head_width, 2 * expand.shape[1])
    args = (project_in, project_out, expand, contract, small)
    outs = [shape_of((shard, width), BF16) for width in widths]
    return plain(pack_kernel, ids, args, outs, "pack")


def place_rows(ids_ref, near_ref, far_ref, write):
    count, shard = near_ref.shape[0], near_ref.shape[1]
    mine = ids_ref[0]
    for step in range(count):
        for low, ref in enumerate((near_ref, far_ref)):
            owner = lax.bitwise_xor(mine, 2 * step + low)
            write(pl.ds(pl.multiple_of(owner * shard, shard), shard), ref[step])


def flatten_kernel(ids_ref, normed_ref, flat_ref):
    flat_ref[...] = normed_ref[...].T


def flatten(ids, normed, after=()):
    seq, features = normed.shape
    return plain(flatten_kernel, ids, (normed,), [shape_of((features, seq), BF16)], "flatten", after=after)[0]


def unpack_kernel(ids_ref, near_ref, far_ref, out_ref):
    def write(at, values):
        out_ref[at, :] = values[:, 3 * LANES :]

    place_rows(ids_ref, near_ref, far_ref, write)


def unpack(ids, near, far, after=()):
    count, shard, width = near.shape
    outs = [shape_of((2 * count * shard, width - 3 * LANES), BF16)]
    return plain(unpack_kernel, ids, (near, far), outs, "unpack", after=after)[0]


def attend_kernel(pair, ids_ref, live_ref, near_ref, far_ref, normed_ref, *refs):
    if pair == 0:
        x_ref = normed_ref
        rows_ref, normed_ref, scaled_ref, held_ref = refs[0], refs[1], refs[2], refs[-1]
        weight_ref, qkv_ref, attended_ref, query_ref, key_ref, value_ref = refs[3:-1]
    else:
        rows_ref, weight_ref, qkv_ref, attended_ref, query_ref, key_ref, value_ref = refs
    seq = normed_ref.shape[0]
    width = 3 * LANES

    def write(at, values):
        weight_ref[at, :] = values[:, :width]
        if pair == 0:
            held_ref[at, :] = values[:, width:].astype(F32)

    place_rows(ids_ref, near_ref, far_ref, write)
    if pair == 0:
        rows_ref[...] = held_ref[...].T[0 : rows_ref.shape[0]]
    start = pl.multiple_of(ids_ref[1] * (2 * LANES) + pair * LANES, LANES)
    bias_row = jnp.concatenate(
        [rows_ref[2:3, pl.ds(start, LANES)], jnp.zeros((1, LANES), F32), rows_ref[3:4, pl.ds(start, LANES)]],
        axis=1,
    )
    for low, count in tiles_of(seq, TILE):
        at = slice(low, low + count)
        if pair == 0:
            scaled, _ = norm_forward(x_ref[at, :].astype(F32))
            scaled_ref[at, :] = scaled.astype(BF16)
            normed_ref[at, :] = (scaled * rows_ref[0:1, :] + rows_ref[1:2, :]).astype(BF16)
        mixed = dot_nn(normed_ref[at, :], weight_ref[...]) + bias_row
        qkv_ref[at, :] = mixed.astype(BF16)
    lane = lax.broadcasted_iota(jnp.int32, (seq, LANES), 1)
    bias = jnp.where(live_ref[...] > 0, 0.0, MASKED_SCORE).astype(F32)
    key_rows = qkv_ref[:, LANES : 2 * LANES].astype(F32)
    value_rows = qkv_ref[:, 2 * LANES : 3 * LANES].astype(F32)
    for head in range(2):
        own = (lane // HEAD_DIM) == head
        spare = HEAD_DIM * (1 - head)
        extra = jnp.where(lane == spare, bias, 0.0)
        key_ref[head] = jnp.where(own, key_rows, extra).astype(BF16)
        extra = jnp.where(lane == spare, 1.0, 0.0)
        value_ref[head] = jnp.where(own, value_rows, extra).astype(BF16)
    for low, count in tiles_of(seq, TILE):
        at = slice(low, low + count)
        lane = lax.broadcasted_iota(jnp.int32, (count, LANES), 1)
        queries = qkv_ref[at, 0:LANES].astype(F32) * SCORE_SCALE
        both = None
        for head in range(2):
            own = (lane // HEAD_DIM) == head
            spare = HEAD_DIM * (1 - head)
            extra = jnp.where(lane == spare, 1.0, 0.0)
            mine = jnp.where(own, queries, extra).astype(BF16)
            scores = dot_nt(mine, key_ref[head])
            highest = jnp.max(scores, axis=-1, keepdims=True)
            weights = jnp.exp(scores - highest).astype(BF16)
            output = dot_nn(weights, value_ref[head])
            summed = output[:, spare : spare + 1]
            output = output / summed
            both = output if head == 0 else jnp.where(own, output, both)
            rest = -(highest + jnp.log(summed))
            extra = jnp.where(lane == spare + 3, 1.0, 0.0)
            for place in range(3):
                part = rest.astype(BF16).astype(F32)
                extra = jnp.where(lane == spare + place, part, extra)
                rest = rest - part
            query_ref[at, LANES * head : LANES * (head + 1)] = jnp.where(
                own, queries, extra
            ).astype(BF16)
        attended_ref[at, :] = both.astype(BF16)


def attend(pair, ids, live, near, far, normed, rows=None, after=()):
    seq, features = normed.shape
    outs = [
        shape_of((features, 3 * LANES), BF16),
        shape_of((seq, 3 * LANES), BF16),
        shape_of((seq, LANES), BF16),
        shape_of((seq, 2 * LANES), BF16),
    ]
    scratch = [pltpu.VMEM((2, seq, LANES), BF16), pltpu.VMEM((2, seq, LANES), BF16)]
    args = (live, near, far, normed)
    if pair == 0:
        outs = [shape_of((16, features), F32)] + [shape_of((seq, features), BF16)] * 2 + outs
        scratch.append(pltpu.VMEM((features, LANES), F32))
    else:
        args += (rows,)
    return plain(
        functools.partial(attend_kernel, pair),
        ids,
        args,
        outs,
        f"attend_{pair}",
        cost=(LONG * 160 * seq * seq * HEAD_DIM, 0, 0),
        scratch=scratch,
        after=after,
    )


def attend_back_kernel(
    ids_ref,
    live_ref,
    qkv_ref,
    query_ref,
    attended_ref,
    mine_a,
    other_a,
    mine_b,
    other_b,
    out_ref,
    mixed_ref,
    sums_ref,
    grad_ref,
    held_ref,
    query_sum_ref,
):
    seq = qkv_ref.shape[0]
    rows = mine_a.shape[0]
    core = ids_ref[2]
    for index, ref in enumerate((mine_a, other_a, mine_b, other_b)):
        block = 2 * (index // 2) + lax.bitwise_xor(core, index % 2)
        grad_ref[pl.ds(pl.multiple_of(block * rows, 8), rows), :] = dot_nn(ref[...], out_ref[...])
    lane = lax.broadcasted_iota(jnp.int32, (seq, LANES), 1)
    grad = grad_ref[...].astype(BF16).astype(F32)
    product = grad * attended_ref[...].astype(F32)
    for head in range(2):
        own = (lane // HEAD_DIM) == head
        spare = HEAD_DIM * (1 - head)
        inner = -jnp.sum(jnp.where(own, product, 0.0), axis=-1, keepdims=True)
        first = inner.astype(BF16).astype(F32)
        extra = jnp.where(lane == spare, first, jnp.where(lane == spare + 1, inner - first, 0.0))
        held_ref[head] = jnp.where(own, grad, extra).astype(BF16)
    value_sum = jnp.zeros((1, LANES), F32)
    for index, (low, count) in enumerate(tiles_of(seq, TILE)):
        at = slice(low, low + count)
        lane = lax.broadcasted_iota(jnp.int32, (count, LANES), 1)
        bias = jnp.where(live_ref[at, :] > 0, 0.0, MASKED_SCORE).astype(F32)
        key_rows = qkv_ref[at, LANES : 2 * LANES].astype(F32)
        value_rows = qkv_ref[at, 2 * LANES : 3 * LANES].astype(F32)
        grad_keys = grad_values = None
        for head in range(2):
            own = (lane // HEAD_DIM) == head
            spare = HEAD_DIM * (1 - head)
            ones = jnp.where((lane >= spare) & (lane < spare + 3), 1.0, 0.0)
            extra = jnp.where(lane == spare + 3, bias, ones)
            keys = jnp.where(own, key_rows, extra).astype(BF16)
            values = jnp.where(own, value_rows, ones).astype(BF16)
            queries = query_ref[:, LANES * head : LANES * (head + 1)]
            above = held_ref[head]
            weights = jnp.exp(dot_nt(keys, queries))
            grad_scores = (weights * dot_nt(values, above)).astype(BF16)
            value_part = dot_nn(weights.astype(BF16), above)
            key_part = dot_nn(grad_scores, queries)
            part = slice(HEAD_DIM * head, HEAD_DIM * (head + 1))
            query_part = dot_tn(keys, grad_scores)[part]
            if index == 0:
                query_sum_ref[part] = query_part
            else:
                query_sum_ref[part] += query_part
            grad_keys = key_part if head == 0 else jnp.where(own, key_part, grad_keys)
            grad_values = value_part if head == 0 else jnp.where(own, value_part, grad_values)
        grad_values = grad_values.astype(BF16)
        mixed_ref[at, LANES : 2 * LANES] = grad_keys.astype(BF16)
        mixed_ref[at, 2 * LANES : 3 * LANES] = grad_values
        value_sum += jnp.sum(grad_values.astype(F32), axis=0, keepdims=True)
    grad_queries = (query_sum_ref[...].T * SCORE_SCALE).astype(BF16)
    mixed_ref[:, 0:LANES] = grad_queries
    sums_ref[0:1, :] = jnp.sum(grad_queries.astype(F32), axis=0, keepdims=True)
    sums_ref[1:2, :] = value_sum


def attend_back(pair, ids, live, qkv, queries, attended, grads, out_own, after=()):
    seq = qkv.shape[0]
    features = out_own.shape[0]
    outs = [shape_of((seq, 3 * LANES), BF16), shape_of((8, LANES), F32)]
    args = (live, qkv, queries, attended, *grads)
    return call(
        attend_back_kernel,
        ids,
        (*args, out_own),
        [whole(a) for a in args] + [pl.BlockSpec((features, LANES), lambda i, _: (0, pair))],
        outs,
        [whole(o) for o in outs],
        f"attend_back_{pair}",
        cost=(LONG * 80 * seq * seq * HEAD_DIM, 0, 0),
        scratch=[
            pltpu.VMEM((seq, LANES), F32),
            pltpu.VMEM((2, seq, LANES), BF16),
            pltpu.VMEM((LANES, seq), F32),
        ],
        after=after,
    )


def middle_kernel(ids_ref, x_ref, *refs):
    att_refs, out_refs = refs[:8], refs[8:12]
    rows_ref, expand_ref, contract_ref, bias_ref, top_ref = refs[12:17]
    outs = refs[-14:-4]
    normed_ref, act_ref, hidden_ref, grad_ref = outs[:4]
    branch_refs, attn_ref, back_refs, sums_ref = outs[4:6], outs[6], outs[7:9], outs[9]
    held_ref, normed_held, act_held, hidden_held = refs[-4:]
    step = pl.program_id(0)

    @pl.when(step == 0)
    def _():
        sums_ref[...] = jnp.zeros_like(sums_ref)

    attn_sum = rows_ref[4:5, :]
    for device, out_ref in enumerate(out_refs):
        held_ref[:, :LANES] = att_refs[2 * device][0]
        held_ref[:, LANES:] = att_refs[2 * device + 1][0]
        attn_sum = attn_sum + dot_nt(held_ref[...], out_ref[...])

    @pl.when(step == 1)
    def _():
        attn_ref[...] = attn_sum

    residual = x_ref[0].astype(F32) + rows_ref[5:6, :] * attn_sum
    scaled, _ = norm_forward(residual)
    normed_held[...] = (scaled * rows_ref[6:7, :] + rows_ref[7:8, :]).astype(BF16)
    normed_ref[0] = normed_held[...]
    grad_ref[0] = (top_ref[0].astype(F32) * rows_ref[9:10, :]).astype(BF16)
    for low in range(0, act_held.shape[1], CHUNK):
        at = slice(low, low + CHUNK)
        activated, slope = gelu_parts(dot_nn(normed_held[...], expand_ref[:, at]) + bias_ref[:, at])
        act_held[:, at] = activated.astype(BF16)
        grad_hidden = (dot_nn(grad_ref[0], contract_ref[:, at]) * slope).astype(BF16)
        hidden_held[:, at] = grad_hidden
        sums_ref[0:1, at] += jnp.sum(grad_hidden.astype(F32), axis=0, keepdims=True)
    act_ref[0] = act_held[...]
    hidden_ref[0] = hidden_held[...]
    back = dot_nt(hidden_held[...], expand_ref[...])
    sums_ref[1:2, :] += jnp.sum(back * scaled, axis=0, keepdims=True)
    sums_ref[2:3, :] += jnp.sum(back, axis=0, keepdims=True)
    branch = dot_nt(act_held[...], contract_ref[...]).astype(BF16)
    for index in range(2):

        @pl.when(step == index)
        def _():
            back_refs[index][...] = back.astype(BF16)
            branch_refs[index][0] = branch


def middle(half, ids, x_full, att, out_all, rows, weights, bias, top_full, before=(), after=()):
    _, count, features = x_full.shape
    hidden = weights.shape[1] // 2
    block = lambda i, ids_ref: 2 * half + lax.bitwise_xor(ids_ref[2], 1 - i)
    part = lambda n: pl.BlockSpec((1, count, n), lambda i, ids_ref: (block(i, ids_ref), 0, 0))
    held = lambda n: pl.BlockSpec((1, count, n), lambda i, _: (half, 0, 0))
    column = lambda c: pl.BlockSpec((features, hidden), lambda i, _: (0, c))
    full = lambda n: shape_of((4, count, n), BF16)
    outs = [full(features), full(hidden), full(hidden), full(features)]
    specs = [part(features), part(hidden), part(hidden), part(features)]
    outs += [shape_of((2, count, features), BF16)] * 2
    specs += [held(features)] * 2
    rest = [
        shape_of((count, features), F32),
        shape_of((count, features), BF16),
        shape_of((count, features), BF16),
        shape_of((8, features), F32),
    ]
    args = (x_full, *att, *out_all, rows, weights, weights, bias, top_full)
    seq = 2 * count
    results = call(
        middle_kernel,
        ids,
        (*args, *before),
        [part(features)]
        + [part(LANES)] * len(att)
        + [whole(o) for o in out_all]
        + [whole(rows), column(0), column(1), whole(bias), part(features)]
        + [ANYWHERE] * len(before),
        outs + rest,
        specs + [whole(o) for o in rest],
        f"middle_{half}",
        (2 * seq * features * (features + 4 * hidden), seq * 24 * features + 6 * features * hidden, 2 * seq * hidden),
        grid=(2,),
        scratch=[pltpu.VMEM((count, 2 * LANES), BF16)] + [pltpu.VMEM((count, features), BF16)] * 3,
        aliases={1 + len(args) + index: index for index in range(len(before))},
        after=after,
    )
    return results[:6], results[6:]


def pair_sum_kernel(ids_ref, keep_ref, arrived_ref, sum_ref):
    sum_ref[...] = (keep_ref[...].astype(F32) + arrived_ref[...].astype(F32)).astype(BF16)


def pair_sum(ids, keep, arrived, name, after=()):
    outs = [shape_of(keep.shape, BF16)]
    return plain(pair_sum_kernel, ids, (keep, arrived), outs, name, after=after)[0]


def split_sum_kernel(ids_ref, keep_ref, arrived_ref, give_ref, stay_ref):
    half = ids_ref[3]
    total = keep_ref[...].astype(F32) + arrived_ref[...].astype(F32)
    give_ref[...] = jnp.where(half == 0, total[1], total[0]).astype(BF16)
    stay_ref[...] = jnp.where(half == 0, total[0], total[1]).astype(BF16)


def split_sum(ids, keep, arrived, name, after=()):
    outs = [shape_of(keep.shape[1:], BF16)] * 2
    return plain(split_sum_kernel, ids, (keep, arrived), outs, name, after=after)


def residual_kernel(ids_ref, chip_ref, arrived_ref, x_ref, attn_ref, top_ref, rows_ref, grad_ref):
    total = chip_ref[...].astype(F32) + arrived_ref[...].astype(F32)
    scaled, inverse = norm_forward(x_ref[0].astype(F32) + rows_ref[5:6, :] * attn_ref[...])
    grad = top_ref[0].astype(F32) + norm_backward(scaled, inverse, total, rows_ref[6:7, :])
    grad_ref[...] = (grad * rows_ref[5:6, :]).astype(BF16)


def residual_back(half, ids, chip, arrived, x_full, attn, top_full, rows, after=()):
    count, features = chip.shape
    part = pl.BlockSpec((1, count, features), lambda i, ids_ref: (2 * half + ids_ref[2], 0, 0))
    out = shape_of((count, features), BF16)
    return call(
        residual_kernel,
        ids,
        (chip, arrived, x_full, attn, top_full, rows),
        [whole(chip), whole(arrived), part, whole(attn), part, whole(rows)],
        [out],
        [whole(out)],
        f"residual_back_{half}",
        after=after,
    )[0]


def own_kernel(
    ids_ref,
    x_ref,
    top_ref,
    attn_a,
    attn_b,
    chip_a,
    chip_b,
    arrived_a,
    arrived_b,
    stay_ref,
    branch_ref,
    rows_ref,
    output_ref,
    grad_ref,
    sums_ref,
):
    first = ids_ref[3] == 0
    choose = lambda a, b: jnp.where(first, a[...].astype(F32), b[...].astype(F32))
    attn_sum = choose(attn_a, attn_b)
    total = choose(chip_a, chip_b) + choose(arrived_a, arrived_b)
    residual = x_ref[...] + rows_ref[5:6, :] * attn_sum
    branch = stay_ref[...].astype(F32) + branch_ref[...].astype(F32) + rows_ref[8:9, :]
    output_ref[:, 0, :] = residual + rows_ref[9:10, :] * branch
    scaled, inverse = norm_forward(residual)
    top = top_ref[...]
    grad = top + norm_backward(scaled, inverse, total, rows_ref[6:7, :])
    grad_ref[...] = grad
    for row, values in enumerate((grad * rows_ref[5:6, :], grad * attn_sum, top * rows_ref[9:10, :], top * branch)):
        sums_ref[row : row + 1, :] = jnp.sum(values, axis=0, keepdims=True)


def own_block(ids, x_own, top_own, attn, chips, arrived, stay, branch, rows, after=()):
    rows_count, features = x_own.shape
    outs = [
        shape_of((rows_count, 1, features), F32),
        shape_of(x_own.shape, F32),
        shape_of((8, features), F32),
    ]
    args = (x_own, top_own, *attn, *chips, *arrived, stay, branch, rows)
    return plain(own_kernel, ids, args, outs, "own_block", after=after)


def matrices_kernel(ids_ref, left_a, left_b, right_a, right_b, out_ref, flat_ref):
    step = pl.program_id(0)
    per = pl.num_programs(0) // 2

    @pl.when(step == 0)
    def _():
        flat_ref[...] = left_a[...].T

    @pl.when(step == per)
    def _():
        flat_ref[...] = left_b[...].T

    right = jnp.where(step < per, right_a[...], right_b[...])
    out_ref[...] = dot_nn(flat_ref[...], right).astype(BF16)


def matrices(ids, normed, hidden, grad, activated, after=()):
    seq, features = normed.shape
    width = hidden.shape[1]
    block = 512
    per = width // block
    out = shape_of((features, 2 * width), BF16)
    return call(
        matrices_kernel,
        ids,
        (normed, grad, hidden, activated),
        [
            whole(normed),
            whole(grad),
            pl.BlockSpec((seq, block), lambda i, _: (0, jnp.minimum(i, per - 1))),
            pl.BlockSpec((seq, block), lambda i, _: (0, jnp.maximum(i - per, 0))),
        ],
        [out],
        [pl.BlockSpec((features, block), lambda i, _: (0, i))],
        "matrices",
        grid=(2 * per,),
        scratch=[pltpu.VMEM((features, seq), BF16)],
        after=after,
    )[0]


def store_shards(ids_ref, index, values, give_ref, keep_ref):
    @pl.when(low_bit(ids_ref) == index % 2)
    def _():
        keep_ref[index // 2] = values

    @pl.when(low_bit(ids_ref) != index % 2)
    def _():
        give_ref[index // 2] = values


def out_grad_kernel(ids_ref, att_a, att_b, mine_a, other_a, mine_b, other_b, give_ref, keep_ref):
    core = ids_ref[2]
    total = [None, None]
    for index, ref in enumerate((mine_a, other_a, mine_b, other_b)):
        block = 2 * (index // 2) + lax.bitwise_xor(core, index % 2)
        for pair, att_ref in enumerate((att_a, att_b)):
            part = dot_tn(att_ref[block], ref[...])
            total[pair] = part if index == 0 else total[pair] + part
    count, _, shard = give_ref.shape
    for place in range(2 * count):
        values = jnp.concatenate([t[:, place * shard : (place + 1) * shard] for t in total]).astype(BF16)
        store_shards(ids_ref, place, values, give_ref, keep_ref)


def out_grad(ids, attended, grads, places, after=()):
    count, features = grads[0].shape
    outs = [shape_of((places // 2, 2 * LANES, features // places), BF16)] * 2
    args = [a.reshape(4, count, LANES) for a in attended] + list(grads)
    return plain(out_grad_kernel, ids, args, outs, "out_grad", after=after)


def in_grad_kernel(ids_ref, flat_ref, mixed_ref, give_ref, keep_ref):
    shard = give_ref.shape[1]
    values = dot_nn(flat_ref[...], mixed_ref[...]).astype(BF16)
    for place in range(values.shape[0] // shard):
        store_shards(ids_ref, place, values[place * shard : (place + 1) * shard], give_ref, keep_ref)


def in_grad(pair, ids, flat, mixed, places, after=()):
    features, seq = flat.shape
    width = mixed.shape[1]
    outs = [shape_of((places // 2, features // places, width), BF16)] * 2
    return plain(in_grad_kernel, ids, (flat, mixed), outs, f"in_grad_{pair}", after=after)


def low_sum_kernel(ids_ref, keep_ref, arrived_ref, *out_refs):
    high = lax.div(ids_ref[0], 2)
    for step, out_ref in enumerate(out_refs):
        at = lax.bitwise_xor(high, step)
        out_ref[...] = (keep_ref[at].astype(F32) + arrived_ref[at].astype(F32)).astype(BF16)


def low_sum(ids, keep, arrived, name, after=()):
    outs = [shape_of(keep.shape[1:], BF16)] * keep.shape[0]
    return plain(low_sum_kernel, ids, (keep, arrived), outs, name, after=after)


def input_back_kernel(ids_ref, scaled_ref, mixed_a, mixed_b, weight_a, weight_b, give_ref, keep_ref, sums_ref):
    step = pl.program_id(0)

    @pl.when(step == 0)
    def _():
        sums_ref[...] = jnp.zeros_like(sums_ref)

    total = dot_nt(mixed_a[0], weight_a[...]) + dot_nt(mixed_b[0], weight_b[...])
    sums_ref[0:1, :] += jnp.sum(total * scaled_ref[0].astype(F32), axis=0, keepdims=True)
    sums_ref[1:2, :] += jnp.sum(total, axis=0, keepdims=True)

    @pl.when(step < 2)
    def _():
        give_ref[0] = total.astype(BF16)

    @pl.when(step >= 2)
    def _():
        keep_ref[0] = total.astype(BF16)


def input_back(ids, scaled, mixed, weights, after=()):
    _, count, features = scaled.shape
    width = mixed[0].shape[2]
    def part(n):
        return pl.BlockSpec(
            (1, count, n),
            lambda i, ids_ref: (2 * lax.rem(i, 2) + lax.bitwise_xor(ids_ref[2], 1 - lax.div(i, 2)), 0, 0),
        )
    outs = [shape_of((2, count, features), BF16)] * 2 + [shape_of((8, features), F32)]
    return call(
        input_back_kernel,
        ids,
        (scaled, *mixed, *weights),
        [part(features), part(width), part(width)] + [whole(w) for w in weights],
        outs,
        [
            pl.BlockSpec((1, count, features), lambda i, _: (jnp.minimum(i, 1), 0, 0)),
            pl.BlockSpec((1, count, features), lambda i, _: (jnp.maximum(i - 2, 0), 0, 0)),
            whole(outs[2]),
        ],
        "input_back",
        grid=(4,),
        after=after,
    )


def input_kernel(ids_ref, stay_ref, arrived_ref, x_ref, grad_ref, rows_ref, out_ref):
    total = stay_ref[...].astype(F32) + arrived_ref[...].astype(F32)
    scaled, inverse = norm_forward(x_ref[...])
    out_ref[:, 0, :] = grad_ref[...] + norm_backward(scaled, inverse, total, rows_ref[0:1, :])


def input_grad_of(ids, stay, arrived, x_own, grad_residual, rows, after=()):
    outs = [shape_of((x_own.shape[0], 1, x_own.shape[1]), F32)]
    args = (stay, arrived, x_own, grad_residual, rows)
    return plain(input_kernel, ids, args, outs, "input_grad", after=after)[0]


def adam_step(master, gradient, first, second, decay):
    first_new = BETA_FIRST * first + (1.0 - BETA_FIRST) * gradient
    second_new = BETA_SECOND * second + (1.0 - BETA_SECOND) * gradient * gradient
    first_hat = first_new / (1.0 - BETA_FIRST**STEP)
    second_hat = second_new / (1.0 - BETA_SECOND**STEP)
    change = -LEARN_RATE * (first_hat / (jnp.sqrt(second_hat) + ADAM_EPS) + decay * master)
    return (change, first_new, second_new)


def adam_kernel(gradients, decay, keep_change, ids_ref, *refs):
    count = len(refs) - 7
    parts, (master, first, second), outs = refs[:count], refs[count:-4], refs[-4:]
    for at, gradient in gradients(parts):
        change, first_new, second_new = adam_step(master[at], gradient, first[at], second[at], decay)
        outs[0][at] = gradient
        outs[1][at] = change if keep_change else master[at] + change
        outs[2][at] = first_new
        outs[3][at] = second_new


def adam(gradients, decay, keep_change, ids, parts, master, first, second, name, after=()):
    outs = [shape_of(master.shape, F32)] * 4
    return plain(
        functools.partial(adam_kernel, gradients, decay, keep_change),
        ids,
        (*parts, master, first, second),
        outs,
        name,
        after=after,
    )


def sum_refs(refs):
    total = refs[0][...].astype(F32)
    for ref in refs[1:]:
        total = total + ref[...].astype(F32)
    return total


def high_sum_kernel(ids_ref, *refs):
    refs[-1][...] = sum_refs(refs[:-1])


def high_sum(ids, parts, name, after=()):
    out = shape_of(parts[0].shape, F32)
    return plain(high_sum_kernel, ids, parts, [out], name, after=after)[0]


def in_gradients(parts):
    totals = (parts[0][...], sum_refs(parts[1:]))
    for pair, total in enumerate(totals):
        columns = slice(pair * LANES, (pair + 1) * LANES)
        for part in range(3):
            yield (part, slice(None), columns), total[:, part * LANES : (part + 1) * LANES]


def out_gradients(parts):
    yield (slice(None), slice(None)), sum_refs(parts)


def expand_gradients(parts):
    yield (slice(None), slice(None)), parts[0][:, : parts[0].shape[1] // 2].astype(F32)


def contract_gradients(parts):
    yield (slice(None), slice(None)), parts[0][:, parts[0].shape[1] // 2 :].astype(F32).T


def tensor_swap(array, bit):
    return lax.ppermute(array, "tensor", [(rank, rank ^ bit) for rank in range(4)])


def fsdp_swap(array, bit):
    size = lax.axis_size("fsdp")
    return lax.ppermute(array, "fsdp", [(rank, rank ^ bit) for rank in range(size)])


def behind(array, *others):
    return lax.optimization_barrier((array,) + others)[0]


def around(array):
    across = tensor_swap(array, 2)
    return (array, tensor_swap(array, 1), across, tensor_swap(across, 1))


def gather_positions(block, rank):
    full = jnp.zeros((4,) + block.shape, block.dtype)
    for bit, piece in enumerate(around(block)):
        full = lax.dynamic_update_slice_in_dim(full, piece[None], rank ^ bit, 0)
    return full


def gather_shards(piece):
    count = lax.axis_size("fsdp") // 2
    near = jnp.stack([piece] + [fsdp_swap(piece, 2 * step) for step in range(1, count)])
    return near, fsdp_swap(near, 1)


def body(
    block_input,
    live_mask,
    cotangent,
    project_in,
    project_out,
    expand,
    contract,
    vectors,
    expand_bias,
    moment_project_in,
    second_project_in,
    moment_project_out,
    second_project_out,
    moment_expand,
    second_expand,
    moment_contract,
    second_contract,
    moment_vectors,
    second_vectors,
    moment_expand_bias,
    second_expand_bias,
):
    rows, _, features = block_input.shape
    shard, _, head_width = project_in.shape
    hidden_width = expand.shape[1]
    seq = 4 * rows
    places = lax.axis_size("fsdp")
    rank = lax.axis_index("tensor")
    place = lax.axis_index("fsdp")
    ids = jnp.stack([place, rank, rank % 2, rank // 2]).astype(jnp.int32)
    parts_first = lambda array: array.transpose(1, 0, 2)

    bias_shard = expand_bias.reshape(-1, shard)
    vector_rows = vectors.shape[0]
    small_rows = vector_rows + bias_shard.shape[0]
    small_shard = jnp.concatenate(
        [vectors, bias_shard, jnp.zeros((LANES - small_rows, shard), F32)]
    )
    packed = pack(ids, parts_first(project_in), project_out, expand, contract, small_shard)
    first_shards = gather_shards(packed[0])
    second_shards = gather_shards(behind(packed[1], first_shards[0]))
    weights = lax.all_gather(
        behind(packed[2], second_shards[0]), "fsdp", axis=0, tiled=True
    )

    x_own = block_input[:, 0]
    live_own = lax.dynamic_slice_in_dim(live_mask, rank * rows, rows, 0) > 0
    top_own = cotangent[:, 0] * live_own.astype(F32)
    x_full = gather_positions(x_own.astype(BF16), rank)
    top_full = gather_positions(behind(top_own.astype(BF16), x_full), rank)

    rows_now, normed_one, scaled_one, *heads = attend(
        0, ids, live_mask, *first_shards, x_full.reshape(seq, features)
    )
    heads = [heads]
    out_own = unpack(ids, *second_shards, after=(heads[0][2],))
    heads.append(attend(1, ids, live_mask, *second_shards, normed_one, rows_now, (out_own,)))
    normed_flat = flatten(ids, normed_one, (heads[1][2],))
    held = (normed_flat,)
    out_all = around(out_own)
    att_sets = [around(each[2]) for each in heads]
    att_all = [
        att_sets[pair][device].reshape(4, rows, LANES) for device in range(4) for pair in range(2)
    ]
    bias_now = rows_now[vector_rows:small_rows]
    bias_now = bias_now.reshape(-1, places, shard).transpose(1, 0, 2).reshape(1, -1)
    bias_here = lax.dynamic_slice_in_dim(bias_now, rank * hidden_width, hidden_width, 1)

    kept = ()
    sums, attn, chips, arrived = [], [], [], []
    grads = []
    for half in range(2):
        kept, (attn_part, back_give, back_keep, sums_part) = middle(
            half, ids, x_full, att_all, out_all, rows_now, weights, bias_here, top_full, kept, held
        )
        arrived_part = tensor_swap(back_give, 1)
        if half == 1:
            grads.append(
                residual_back(
                    0, ids, chips[0], arrived[0], x_full, attn[0], top_full, rows_now, (back_give,)
                )
            )
            grads.append(tensor_swap(grads[0], 1))
        chip = pair_sum(ids, back_keep, arrived_part, f"back_sum_{half}", grads[:1])
        held = (chip,)
        chips.append(chip)
        arrived.append(tensor_swap(chip, 2))
        attn.append(attn_part)
        sums.append(sums_part)
    normed_two, activated, grad_hidden, grad_branch = [
        array.reshape(seq, array.shape[2]) for array in kept[:4]
    ]
    branch_give, branch_keep = kept[4:]
    sums = sums[0] + sums[1]
    grad_second = matrices(ids, normed_two, grad_hidden, grad_branch, activated, held)
    grads.append(
        residual_back(
            1, ids, chips[1], arrived[1], x_full, attn[1], top_full, rows_now, (grad_second,)
        )
    )
    grads.append(tensor_swap(grads[2], 1))
    second_sum = lax.psum_scatter(
        behind(grad_second, grads[2]), "fsdp", scatter_dimension=0, tiled=True
    )

    branch_arrived = tensor_swap(behind(branch_give, chips[1]), 1)
    give, branch_stay = split_sum(ids, branch_keep, branch_arrived, "branch_sum", (grads[2],))
    branch_arrived = tensor_swap(give, 2)

    out_give, out_keep = out_grad(ids, [each[2] for each in heads], grads, places)
    out_arrived = fsdp_swap(out_give, 1)
    mixed, head_sums = [], []
    sends = lambda low: [low[0]] + [fsdp_swap(low[step], 2 * step) for step in range(1, places // 2)]
    wait = (out_give, give)
    for pair in range(2):
        weight, qkv, attended, queries = heads[pair]
        mixed_pair, pair_sums = attend_back(
            pair, ids, live_mask, qkv, queries, attended, grads, out_own, wait
        )
        mixed.append(mixed_pair)
        head_sums.append(pair_sums)
        if pair == 1:
            in_low = low_sum(ids, *in_parts, "in_low_0", (mixed_pair,))
            in_sums = sends(in_low)
            wait = (in_low[0],)
        else:
            wait = ()
        in_give, in_keep = in_grad(pair, ids, normed_flat, mixed_pair, places, wait)
        in_parts = (in_keep, fsdp_swap(in_give, 1))
        if pair == 0:
            out_low = low_sum(ids, out_keep, out_arrived, "out_low", (in_give,))
            wait = (in_give, out_low[0], branch_arrived)
    input_give, input_keep, input_sums = input_back(
        ids,
        scaled_one.reshape(4, rows, features),
        [each.reshape(4, rows, each.shape[1]) for each in mixed],
        [each[0] for each in heads],
        (in_give,),
    )
    out_sums = sends(out_low)
    give, stay = split_sum(ids, input_keep, tensor_swap(input_give, 1), "input_sum")
    input_arrived = tensor_swap(give, 2)
    block_output, grad_residual, own_sums = own_block(
        ids, x_own, top_own, attn, chips, arrived, branch_stay, branch_arrived, rows_now, (input_give,)
    )
    sum_first = high_sum(ids, in_sums, "in_sum_0", (own_sums,))
    in_sums = [sum_first] + sends(low_sum(ids, *in_parts, "in_low_1", (sum_first,)))
    input_grad = input_grad_of(ids, stay, input_arrived, x_own, grad_residual, rows_now)

    lay = lambda values, start, total: lax.dynamic_update_slice_in_dim(
        jnp.zeros((total,), F32), values, start, 0
    )
    head_sums = jnp.concatenate(head_sums, axis=1)
    grad_rows = jnp.stack(
        [
            input_sums[0],
            input_sums[1],
            lay(head_sums[0], rank * head_width, features),
            lay(head_sums[1], rank * head_width, features),
            own_sums[0],
            own_sums[1],
            sums[1],
            sums[2],
            own_sums[2],
            own_sums[3],
        ]
    )
    grad_bias = lay(sums[0], rank * hidden_width, expand_bias.shape[0] * places)
    grad_bias = grad_bias.reshape(places, -1, shard).transpose(1, 0, 2).reshape(-1, features)
    small = jnp.concatenate([grad_rows, grad_bias])
    small = sum([tensor_swap(small, bit) for bit in (1, 2, 3)], small)
    small = small + fsdp_swap(small, 1)
    small = sum([fsdp_swap(small, 2 * step) for step in range(1, places // 2)], small)
    small = lax.dynamic_slice_in_dim(small, place * shard, shard, 1)
    grad_vectors = small[:vector_rows]
    grad_bias = small[vector_rows:small_rows].reshape(-1)

    new_in = adam(
        in_gradients,
        WEIGHT_DECAY,
        False,
        ids,
        in_sums,
        parts_first(project_in),
        parts_first(moment_project_in),
        parts_first(second_project_in),
        "adam_in",
    )
    new_in = [parts_first(array) for array in new_in]
    new_out = adam(
        out_gradients,
        WEIGHT_DECAY,
        True,
        ids,
        out_sums,
        project_out,
        moment_project_out,
        second_project_out,
        "adam_out",
    )
    second = (second_sum,)
    new_expand = adam(
        expand_gradients, WEIGHT_DECAY, False, ids, second, expand, moment_expand, second_expand, "adam_expand"
    )
    new_contract = adam(
        contract_gradients,
        WEIGHT_DECAY,
        False,
        ids,
        second,
        contract,
        moment_contract,
        second_contract,
        "adam_contract",
    )
    change, first, second = adam_step(vectors, grad_vectors, moment_vectors, second_vectors, 0.0)
    new_vectors = (grad_vectors, change, first, second)
    change, first, second = adam_step(
        expand_bias, grad_bias, moment_expand_bias, second_expand_bias, 0.0
    )
    new_bias = (grad_bias, change, first, second)
    updated = (new_in, new_out, new_expand, new_contract, new_vectors, new_bias)
    return (
        block_output,
        input_grad,
        *[each[0] for each in updated],
        *[each[1] for each in updated],
        *[array for each in updated for array in each[2:]],
        grad_vectors[7],
    )


def solution(mesh):
    tokens = P("tensor", "fsdp", None)
    into = P("fsdp", None, "tensor")
    wide = P("fsdp", "tensor")
    tall = P("tensor", "fsdp")
    row = P(None, "fsdp")
    line = P("fsdp")
    params = (into, tall, wide, tall, row, line)
    moments = (into, into, tall, tall, wide, wide, tall, tall, row, row, line, line)
    return jax.shard_map(
        body,
        mesh=mesh,
        in_specs=(tokens, row, tokens) + params + moments,
        out_specs=(tokens, tokens) + params + params + moments + (line,),
        check_vma=False,
    )
```

time: 431 us -> 372 us (0.86)
  Pallas kernels: 71 us -> 204 us
  waiting for transfers between devices: 177 us -> 55.2 us
  local copies, waits for them, and re-layouts: 89.9 us -> 35.2 us
  starting transfers between devices: 14.3 us -> 51.2 us
  other arithmetic: 38.5 us -> 7.23 us
  matrix products: 21.1 us -> 0 us
    pallas_call x4 -> x30, Pallas kernels: 71 us -> 204 us  [call(): pl.pallas_call(run, grid_spec=pltpu.PrefetchScalarGridSpec(num_scalar_pre...]
    ppermute x21 -> x28, waiting for transfers between devices: 83 us -> 16.7 us  [tensor_swap(): lax.ppermute(array, 'tensor', [(rank, rank ^ bit) for rank in range(4)])]
    unnamed x6 -> x2, waiting for transfers between devices: 59.2 us -> 0.03 us
    ppermute x0 -> x24, starting transfers between devices: none -> 35.3 us  [fsdp_swap(): lax.ppermute(array, 'fsdp', [(rank, rank ^ bit) for rank in range(size)])]
    ppermute x0 -> x24, waiting for transfers between devices: none -> 26.4 us  [fsdp_swap(): lax.ppermute(array, 'fsdp', [(rank, rank ^ bit) for rank in range(size)])]
    all_gather x2 -> x1, waiting for transfers between devices: 34.7 us -> 12.1 us  [body(): lax.all_gather(behind(packed[2], second_shards[0]), 'fsdp', axis=0, tiled...]
    dot_general x6 -> x0, matrix products: 21.1 us -> none  [the longest x4 15.4 us: dot_tn(): lax.dot_general(left, right, (((0,), (0,)), ((), ())), preferred_element_...]
    unnamed x119 -> x124, local copies, waits for them, and re-layouts: 40.7 us -> 20.7 us
  transfers between devices with their start and end apart: 25 -> 54, of which waited for: 9 -> 17; matrix products, arithmetic and copies ran while one was open for 28% -> 7% of each run, Pallas kernels for 11% -> 47%
where the time goes in v2:
time: 372 us; the launch traced here: 368 us
  Pallas kernels  204 us (55%)
  waiting for transfers between devices  55.2 us (15%)
  starting transfers between devices  51.2 us (14%)
  local copies, waits for them, and re-layouts  35.2 us (9%)
  between operations  14.9 us (4%)
  other arithmetic  7.23 us (2%)
    pallas_call x30, Pallas kernels, call(): pl.pallas_call(run, grid_spec=pltpu.PrefetchScalarGridSpec(num_scalar_pre...  204 us
    ppermute x24, starting transfers between devices, fsdp_swap(): lax.ppermute(array, 'fsdp', [(rank, rank ^ bit) for rank in range(size)])  35.3 us
    ppermute x24, waiting for transfers between devices, fsdp_swap(): lax.ppermute(array, 'fsdp', [(rank, rank ^ bit) for rank in range(size)])  26.4 us
    unnamed x124, local copies, waits for them, and re-layouts  20.7 us
    ppermute x28, waiting for transfers between devices, tensor_swap(): lax.ppermute(array, 'tensor', [(rank, rank ^ bit) for rank in range(4)])  16.7 us
    ppermute x28, starting transfers between devices, tensor_swap(): lax.ppermute(array, 'tensor', [(rank, rank ^ bit) for rank in range(4)])  15.6 us
    all_gather x1, waiting for transfers between devices, body(): lax.all_gather(behind(packed[2], second_shards[0]), 'fsdp', axis=0, tiled...  12.1 us
    dynamic_update_slice x8, local copies, waits for them, and re-layouts, gather_positions(): full = lax.dynamic_update_slice_in_dim(full, piece[None], rank ^ bit, 0)  9.81 us
  transfers between devices with their start and end apart: 54, of which 17 were waited for; matrix products, arithmetic and copies ran while one was open for 7% of the time, Pallas kernels for 47%

profile of v2, /device:TPU:0, one launch (start us, length us, event | category | flops | bytes accessed | tf_op | source)
XLA Modules:
  0.0 367.8 jit_solution(356533725363839868)
XLA Ops:
  7.3 2.5 copy.79
  9.8 2.9 collective-permute-start.1
  14.9 3.1 pack.1
  19.5 2.6 collective-permute-start.4
  24.6 7.8 %collective-permute-done.4 = bf16[128,512]{1,0:T(8,128)(2,1)S(1)} collective-permute-done((bf16[128,512]{1,0:T(8,128)(2,1)}, bf16[128,512]{1,0:T(8,128)(2,1)S(1)}, u32[]{:S(2)}, u32[]{:S(2)}) %collective-permute-start.4) | collective-permute-done | bytes 131104 | tf_op jit(solution)/shard_map/ppermute | solution.py:765
  33.2 2.0 collective-permute-start.7
  42.5 6.6 %collective-permute-done.8 = bf16[128,640]{1,0:T(8,128)(2,1)S(1)} collective-permute-done((bf16[128,640]{1,0:T(8,128)(2,1)S(1)}, bf16[128,640]{1,0:T(8,128)(2,1)S(1)}, u32[]{:S(2)}, u32[]{:S(2)}) %collective-permute-start.8) | collective-permute-done | bytes 163872 | tf_op jit(solution)/shard_map/ppermute | solution.py:765
  58.1 14.0 %attend_0.1 = (f32[16,1024]{1,0:T(8,128)}, bf16[1376,1024]{1,0:T(8,128)(2,1)}, bf16[1376,1024]{1,0:T(8,128)(2,1)}, bf16[1024,384]{1,0:T(8,128)(2,1)}, bf16[1376,...) custom-call(s32[4]{0:T(128)} %pad_add_fusion.refs_0_, s32[1376,1]{1,0:T(8,128)} %copy.61.refs_1_, ...), custom_call_target="tpu_custom_call" | custom-call | flops 77552680960 | tf_op jit(solution)/shard_map/attend_0/pallas_call | solution.py:76
  72.0 3.2 collective-permute-done.10.refs_2_.refs_3_
  75.3 2.8 unpack.1.refs_6_.refs_10_.refs_9_
  78.6 12.7 %attend_1.1 = (bf16[1024,384]{1,0:T(8,128)(2,1)}, bf16[1376,384]{1,0:T(8,128)(2,1)}, bf16[1376,128]{1,0:T(8,128)(2,1)}, bf16[1376,256]{1,0:T(8,128)(2,1)}) custom-call(s32[4]{0:T(128)} %pad_add_fusion.refs_0_, s32[1376,1]{1,0:T(8,128)} %copy.61.refs_1_, bf16[4,128,640]{2,1,0:T(8,128)(2,1)} %copy-done.8, ...), custom_call_target="tpu_custom_call" | custom-call | flops 77552680960 | tf_op jit(solution)/shard_map/attend_1/pallas_call | solution.py:76
  92.8 5.0 %flatten.1.refs_19_.refs_1_ = bf16[1024,1376]{1,0:T(8,128)(2,1)} custom-call(s32[4]{0:T(128)} %pad_add_fusion.refs_0_, bf16[1376,1024]{1,0:T(8,128)(2,1)} %get-tuple-element.118.refs_4_.refs_1_, bf16[1376,128]{1,0:T(8,128)(2,1)} %get-tuple-element.120.refs_2_.refs_4_), custom_call_target="tpu_custom_call" | custom-call | tf_op jit(solution)/shard_map/flatten/pallas_call | solution.py:76
  105.1 5.8 %collective-permute-done.13 = bf16[1376,128]{1,0:T(8,128)(2,1)S(1)} collective-permute-done((bf16[1376,128]{1,0:T(8,128)(2,1)S(1)}, bf16[1376,128]{1,0:T(8,128)(2,1)S(1)}, u32[]{:S(2)}, u32[]{:S(2)}) %collective-permute-start.13) | collective-permute-done | bytes 352288 | tf_op jit(solution)/shard_map/ppermute | solution.py:760
  116.4 12.1 %all-gather.2.cloned.1.call-done.refs_15_.refs_16_ = bf16[1024,2048]{1,0:T(8,128)(2,1)} async-done(((bf16[128,2048]{1,0:T(8,128)(2,1)}), bf16[1024,2048]{1,0:T(8,128)(2,1)}) %all-gather.2.cloned.1.call-update) | async-done | bytes 4194320 | tf_op jit(solution)/shard_map/all_gather | solution.py:832
  128.6 17.7 %middle_0.1 = (bf16[4,344,1024]{2,1,0:T(8,128)(2,1)}, bf16[4,344,1024]{2,1,0:T(8,128)(2,1)}, bf16[4,344,1024]{2,1,0:T(8,128)(2,1)}, bf16[4,344,1024]{2,1,0:T(8,1...) custom-call(s32[4]{0:T(128)} %pad_add_fusion.refs_0_, ...), custom_call_target="tpu_custom_call" | custom-call | flops 7214202880 | bytes 23199744 | tf_op jit(solution)/shard_map/middle_0/pallas_call | solution.py:76
  146.3 2.4 collective-permute-done.23.refs_2_
  149.6 3.0 back_sum_0.1.refs_25_.refs_1_.refs_5_
  154.0 17.5 %middle_1.1 = (bf16[4,344,1024]{2,1,0:T(8,128)(2,1)}, bf16[4,344,1024]{2,1,0:T(8,128)(2,1)}, bf16[4,344,1024]{2,1,0:T(8,128)(2,1)}, bf16[4,344,1024]{2,1,0:T(8,1...) custom-call(s32[4]{0:T(128)} %pad_add_fusion.refs_0_, ...), custom_call_target="tpu_custom_call", output_to_operand_aliasing={{0}: (19, {}), {1}: (20, {}), {2}: (21, {}), {3}: (22, {}),... | custom-call | flops 7214202880 | bytes 23199744 | tf_op jit(solution)/shard_map/middle_1/pallas_call | solution.py:76
  172.5 4.9 %residual_back_0.1.refs_3_.refs_5_ = bf16[344,1024]{1,0:T(8,128)(2,1)} custom-call(s32[4]{0:T(128)} %pad_add_fusion.refs_0_, bf16[344,1024]{1,0:T(8,128)(2,1)} %back_sum_0.1.refs_25_.refs_1_.refs_5_, bf16[344,1024]{1,0:T(8,128)(2,1)} %copy-done.6, bf16[4,344,1024]{2,1,0:T(8,128)(2,1)} %copy-done.1, f32[344,1024]{1,0:T(8,128)} %get-tuple-element.124.refs_4_.refs_3_, ...), custom_call_target="tpu_custom_call" | custom-call | tf_op jit(solution)/shard_map/residual_back_0/pallas_call | solution.py:76
  178.2 3.0 back_sum_1.1.refs_5_.refs_1_.refs_6_
  182.3 14.1 %matrices.1.refs_7_ = bf16[1024,2048]{1,0:T(8,128)(2,1)} custom-call(s32[4]{0:T(128)} %pad_add_fusion.refs_0_, bf16[1376,1024]{1,0:T(8,128)(2,1)} %bitcast.82, bf16[1376,1024]{1,0:T(8,128)(2,1)} %bitcast.85, bf16[1376,1024]{1,0:T(8,128)(2,1)} %bitcast.84, bf16[1376,1024]{1,0:T(8,128)(2,1)} %bitcast.83, bf16[344,1024]{1,0:T(8,128)(2,1)} %back_sum_1.1.refs_5_.refs_1_.refs_6_), custom_call_target="tpu_custom_call" | custom-call | tf_op jit(solution)/shard_map/matrices/pallas_call | solution.py:76
  196.4 3.2 collective-permute-done.26.refs_2_.refs_8_
  200.5 4.9 %residual_back_1.1.refs_3_.refs_5_.refs_7_ = bf16[344,1024]{1,0:T(8,128)(2,1)} custom-call(s32[4]{0:T(128)} %pad_add_fusion.refs_0_, bf16[344,1024]{1,0:T(8,128)(2,1)} %back_sum_1.1.refs_5_.refs_1_.refs_6_, bf16[344,1024]{1,0:T(8,128)(2,1)} %copy-done.7, bf16[4,344,1024]{2,1,0:T(8,128)(2,1)} %copy-done.1, f32[344,1024]{1,0:T(8,128)} %get-tuple-element.133.refs_4_, ...), custom_call_target="tpu_custom_call" | custom-call | tf_op jit(solution)/shard_map/residual_back_1/pallas_call | solution.py:76
  205.4 2.3 collective-permute-done.30.refs_6_.refs_8_
  208.6 5.6 %out_grad.1 = (bf16[4,256,128]{2,1,0:T(8,128)(2,1)}, bf16[4,256,128]{2,1,0:T(8,128)(2,1)}) custom-call(s32[4]{0:T(128)} %pad_add_fusion.refs_0_, bf16[4,344,128]{2,1,0:T(8,128)(2,1)} %bitcast.90, bf16[4,344,128]{2,1,0:T(8,128)(2,1)} %bitcast.93, bf16[344,1024]{1,0:T(8,128)(2,1)} %residual_back_0.1.refs_3_.refs_5_, bf16[344,1024]{1,0:T(8,128)(2,1)} %copy-done.15, ...), custom_call_target="tpu_custom_call" | custom-call | tf_op jit(solution)/shard_map/out_grad/pallas_call | solution.py:76
  215.6 3.9 %branch_sum.1 = (bf16[344,1024]{1,0:T(8,128)(2,1)}, bf16[344,1024]{1,0:T(8,128)(2,1)}) custom-call(s32[4]{0:T(128)} %pad_add_fusion.refs_0_, bf16[2,344,1024]{2,1,0:T(8,128)(2,1)} %get-tuple-element.136.refs_1_, bf16[2,344,1024]{2,1,0:T(8,128)(2,1)} %copy-done.12, bf16[344,1024]{1,0:T(8,128)(2,1)} %residual_back_1.1.refs_3_.refs_5_.refs_7_), custom_call_target="tpu_custom_call" | custom-call | tf_op jit(solution)/shard_map/branch_sum/pallas_call | solution.py:76
  220.0 15.5 %attend_back_0.1 = (bf16[1376,384]{1,0:T(8,128)(2,1)}, f32[8,128]{1,0:T(8,128)}) custom-call(s32[4]{0:T(128)} %pad_add_fusion.refs_0_, s32[1376,1]{1,0:T(8,128)} %copy.61.refs_1_, bf16[1376,384]{1,0:T(8,128)(2,1)} %get-tuple-element.146.refs_2_, bf16[1376,256]{1,0:T(8,128)(2,1)} %get-tuple-element.147.refs_3_, ...), custom_call_target="tpu_custom_call" | custom-call | flops 38776340480 | tf_op jit(solution)/shard_map/attend_back_0/pallas_call | solution.py:76
  235.5 5.7 %in_grad_0.1 = (bf16[4,128,384]{2,1,0:T(8,128)(2,1)}, bf16[4,128,384]{2,1,0:T(8,128)(2,1)}) custom-call(s32[4]{0:T(128)} %pad_add_fusion.refs_0_, bf16[1024,1376]{1,0:T(8,128)(2,1)} %flatten.1.refs_19_.refs_1_, bf16[1376,384]{1,0:T(8,128)(2,1)} %get-tuple-element.149.refs_2_), custom_call_target="tpu_custom_call" | custom-call | tf_op jit(solution)/shard_map/in_grad_0/pallas_call | solution.py:76
  243.4 2.4 out_low.1
  246.7 15.5 %attend_back_1.1 = (bf16[1376,384]{1,0:T(8,128)(2,1)}, f32[8,128]{1,0:T(8,128)}) custom-call(s32[4]{0:T(128)} %pad_add_fusion.refs_0_, s32[1376,1]{1,0:T(8,128)} %copy.61.refs_1_, bf16[1376,384]{1,0:T(8,128)(2,1)} %get-tuple-element.150.refs_2_, bf16[1376,256]{1,0:T(8,128)(2,1)} %get-tuple-element.151.refs_3_, ...), custom_call_target="tpu_custom_call" | custom-call | flops 38776340480 | tf_op jit(solution)/shard_map/attend_back_1/pallas_call | solution.py:76
  262.9 2.5 in_low_0.1
  265.4 5.8 %in_grad_1.1 = (bf16[4,128,384]{2,1,0:T(8,128)(2,1)}, bf16[4,128,384]{2,1,0:T(8,128)(2,1)}) custom-call(s32[4]{0:T(128)} %pad_add_fusion.refs_0_, bf16[1024,1376]{1,0:T(8,128)(2,1)} %flatten.1.refs_19_.refs_1_, bf16[1376,384]{1,0:T(8,128)(2,1)} %get-tuple-element.155.refs_3_.refs_2_, bf16[128,384]{1,0:T(8,128)(2,1)} %get-tuple-element.159.refs_3_.refs_1_), custom_call_target="tpu_custom_call" | custom-call | tf_op jit(solution)/shard_map/in_grad_1/pallas_call | solution.py:76
  271.3 8.5 %input_back.1 = (bf16[2,344,1024]{2,1,0:T(8,128)(2,1)}, bf16[2,344,1024]{2,1,0:T(8,128)(2,1)}, f32[8,1024]{1,0:T(8,128)}) custom-call(s32[4]{0:T(128)} %pad_add_fusion.refs_0_, bf16[4,344,1024]{2,1,0:T(8,128)(2,1)} %bitcast.94, bf16[4,344,384]{2,1,0:T(8,128)(2,1)} %bitcast.87, bf16[4,344,384]{2,1,0:T(8,128)(2,1)} %bitcast.86, ...), custom_call_target="tpu_custom_call" | custom-call | tf_op jit(solution)/shard_map/input_back/pallas_call | solution.py:76
  282.5 8.0 %own_block.1 = (f32[344,1,1024]{2,1,0:T(1,128)}, f32[344,1024]{1,0:T(8,128)}, f32[8,1024]{1,0:T(8,128)}) custom-call(s32[4]{0:T(128)} %pad_add_fusion.refs_0_, f32[344,1024]{1,0:T(8,128)} %bitcast.80, f32[344,1024]{1,0:T(8,128)} %get-tuple-element.210.refs_2_, f32[344,1024]{1,0:T(8,128)} %get-tuple-element.124.refs_4_.refs_3_, ...), custom_call_target="tpu_custom_call" | custom-call | tf_op jit(solution)/shard_map/own_block/pallas_call | solution.py:76
  296.4 1.9 collective-permute-done.47
  301.4 2.4 collective-permute-start.44
  305.2 3.0 collective-permute-done.44.refs_4_
  308.2 5.1 %collective-permute-start.49 = (f32[14,1024]{1,0:T(8,128)S(1)}, f32[14,1024]{1,0:T(8,128)S(1)}, u32[]{:S(2)}, u32[]{:S(2)}) collective-permute-start(f32[14,1024]{1,0:T(8,128)S(1)} %add.103), channel_id=1, source_target_pairs={{0,8},{4,12},{8,0},{12,4},{16,24},{20,28},{24,16},{28,20},{1,9},{5... | collective-permute-start | bytes 172040 | tf_op jit(solution)/shard_map/ppermute | solution.py:765
  313.8 2.0 collective-permute-start.51
  315.8 2.7 adam_out.1
  320.2 2.4 in_sum_0.1.refs_3_.refs_1_
  323.8 3.9 %input_sum.1 = (bf16[344,1024]{1,0:T(8,128)(2,1)}, bf16[344,1024]{1,0:T(8,128)(2,1)}) custom-call(s32[4]{0:T(128)} %pad_add_fusion.refs_0_, bf16[2,344,1024]{2,1,0:T(8,128)(2,1)} %get-tuple-element.163.refs_1_, bf16[2,344,1024]{2,1,0:T(8,128)(2,1)} %copy-done.11), custom_call_target="tpu_custom_call" | custom-call | tf_op jit(solution)/shard_map/input_sum/pallas_call | solution.py:76
  330.7 2.5 in_low_1.1
  339.0 2.4 collective-permute-done.40.refs_4_
  343.3 3.6 adam_in.1
  347.8 5.1 %input_grad.1 = f32[344,1,1024]{2,1,0:T(1,128)} custom-call(s32[4]{0:T(128)} %pad_add_fusion.refs_0_, bf16[344,1024]{1,0:T(8,128)(2,1)} %get-tuple-element.164.refs_1_, bf16[344,1024]{1,0:T(8,128)(2,1)} %copy-done.16, f32[344,1024]{1,0:T(8,128)} %bitcast.81, f32[344,1024]{1,0:T(8,128)} %get-tuple-element.166.refs_4_, ...), custom_call_target="tpu_custom_call" | custom-call | tf_op jit(solution)/shard_map/input_grad/pallas_call | solution.py:76
  352.9 4.0 %adam_contract.1 = (f32[1024,128]{1,0:T(8,128)}, f32[1024,128]{1,0:T(8,128)}, f32[1024,128]{1,0:T(8,128)}, f32[1024,128]{1,0:T(8,128)}) custom-call(s32[4]{0:T(128)} %pad_add_fusion.refs_0_, bf16[128,2048]{1,0:T(8,128)(2,1)} %reduce-scatter.2.cloned.1.call-done.refs_1_, f32[1024,128]{1,0:T(8,128)} %refs_2_.5, f32[1024,128]{1,0:T(8,128)} %refs_3_.5, ...), custom_call_target="tpu_custom_call" | custom-call | tf_op jit(solution)/shard_map/adam_contract/pallas_call | solution.py:76
  356.8 3.9 %adam_expand.1 = (f32[128,1024]{1,0:T(8,128)}, f32[128,1024]{1,0:T(8,128)}, f32[128,1024]{1,0:T(8,128)}, f32[128,1024]{1,0:T(8,128)}) custom-call(s32[4]{0:T(128)} %pad_add_fusion.refs_0_, bf16[128,2048]{1,0:T(8,128)(2,1)} %reduce-scatter.2.cloned.1.call-done.refs_1_, f32[128,1024]{1,0:T(8,128)} %refs_2_.4, f32[128,1024]{1,0:T(8,128)} %refs_3_.4, ...), custom_call_target="tpu_custom_call" | custom-call | tf_op jit(solution)/shard_map/adam_expand/pallas_call | solution.py:76
  (255 shorter events, 78.5 us)
Async XLA Ops:
  7.2 121.3 %all-gather.2.cloned.1.call-start = ((), (), s32[]{:S(2)}) async-start(), calls=%async_computation.1 | async-start | bytes 4718592 | tf_op jit(solution)/shard_map/all_gather | solution.py:832
  9.8 27.9 %collective-permute-start.1 = (bf16[344,1024]{1,0:T(8,128)(2,1)}, bf16[344,1024]{1,0:T(8,128)(2,1)}, u32[]{:S(2)}, u32[]{:S(2)}) collective-permute-start(bf16[344,1024]{1,0:T(8,128)(2,1)} %bitcast.78), channel_id=1, source_target_pairs={{0,2},{1,3},{2,0},{3,1},{4,6},{5,7},{6,4},{7,5},{8,10},{9,11},{10,... | collective-permute-start | bytes 2113544 | tf_op jit(solution)/shard_map/ppermute | solution.py:760
  17.9 6.6 %collective-permute-start.3 = (bf16[128,512]{1,0:T(8,128)(2,1)}, bf16[128,512]{1,0:T(8,128)(2,1)S(1)}, u32[]{:S(2)}, u32[]{:S(2)}) collective-permute-start(bf16[128,512]{1,0:T(8,128)(2,1)} %get-tuple-element.114), channel_id=1, source_target_pairs={{0,8},{4,12},{8,0},{12,4},{16,24},{20,28},{24,16},{28,20},{1,9},{5... | collective-permute-start | bytes 393224 | tf_op jit(solution)/shard_map/ppermute | solution.py:765
  19.5 12.9 %collective-permute-start.4 = (bf16[128,512]{1,0:T(8,128)(2,1)}, bf16[128,512]{1,0:T(8,128)(2,1)S(1)}, u32[]{:S(2)}, u32[]{:S(2)}) collective-permute-start(bf16[128,512]{1,0:T(8,128)(2,1)} %get-tuple-element.114), channel_id=1, source_target_pairs={{0,16},{4,20},{8,24},{12,28},{16,0},{20,4},{24,8},{28,12},{1,17},{... | collective-permute-start | bytes 393224 | tf_op jit(solution)/shard_map/ppermute | solution.py:765
  22.1 10.3 %collective-permute-start.5 = (bf16[128,512]{1,0:T(8,128)(2,1)}, bf16[128,512]{1,0:T(8,128)(2,1)S(1)}, u32[]{:S(2)}, u32[]{:S(2)}) collective-permute-start(bf16[128,512]{1,0:T(8,128)(2,1)} %get-tuple-element.114), channel_id=1, source_target_pairs={{0,24},{4,28},{8,16},{12,20},{16,8},{20,12},{24,0},{28,4},{1,25},{... | collective-permute-start | bytes 393224 | tf_op jit(solution)/shard_map/ppermute | solution.py:765
  22.3 30.6 %collective-permute-start = (bf16[344,1024]{1,0:T(8,128)(2,1)}, bf16[344,1024]{1,0:T(8,128)(2,1)}, u32[]{:S(2)}, u32[]{:S(2)}) collective-permute-start(bf16[344,1024]{1,0:T(8,128)(2,1)} %bitcast.78), channel_id=1, source_target_pairs={{0,1},{1,0},{2,3},{3,2},{4,5},{5,4},{6,7},{7,6},{8,9},{9,8},{10,11... | collective-permute-start | bytes 2113544 | tf_op jit(solution)/shard_map/ppermute | solution.py:760
  33.2 7.7 %collective-permute-start.7 = (bf16[128,640]{1,0:T(8,128)(2,1)S(1)}, bf16[128,640]{1,0:T(8,128)(2,1)S(1)}, u32[]{:S(2)}, u32[]{:S(2)}) collective-permute-start(bf16[128,640]{1,0:T(8,128)(2,1)S(1)} %copy-done.29), channel_id=1, source_target_pairs={{0,8},{4,12},{8,0},{12,4},{16,24},{20,28},{24,16},{28,20},{1,9},{5... | collective-permute-start | bytes 491528 | tf_op jit(solution)/shard_map/ppermute | solution.py:765
  35.2 13.9 %collective-permute-start.8 = (bf16[128,640]{1,0:T(8,128)(2,1)S(1)}, bf16[128,640]{1,0:T(8,128)(2,1)S(1)}, u32[]{:S(2)}, u32[]{:S(2)}) collective-permute-start(bf16[128,640]{1,0:T(8,128)(2,1)S(1)} %copy-done.29), channel_id=1, source_target_pairs={{0,16},{4,20},{8,24},{12,28},{16,0},{20,4},{24,8},{28,12},{1,17},{... | collective-permute-start | bytes 491528 | tf_op jit(solution)/shard_map/ppermute | solution.py:765
  36.2 12.9 %collective-permute-start.9 = (bf16[128,640]{1,0:T(8,128)(2,1)S(1)}, bf16[128,640]{1,0:T(8,128)(2,1)S(1)}, u32[]{:S(2)}, u32[]{:S(2)}) collective-permute-start(bf16[128,640]{1,0:T(8,128)(2,1)S(1)} %copy-done.29), channel_id=1, source_target_pairs={{0,24},{4,28},{8,16},{12,20},{16,8},{20,12},{24,0},{28,4},{1,25},{... | collective-permute-start | bytes 491528 | tf_op jit(solution)/shard_map/ppermute | solution.py:765
  37.7 17.6 %collective-permute-start.2 = (bf16[344,1024]{1,0:T(8,128)(2,1)}, bf16[344,1024]{1,0:T(8,128)(2,1)}, u32[]{:S(2)}, u32[]{:S(2)}) collective-permute-start(bf16[344,1024]{1,0:T(8,128)(2,1)} %collective-permute-done.1), channel_id=1, source_target_pairs={{0,1},{1,0},{2,3},{3,2},{4,5},{5,4},{6,7},{7,6},{8,9},{9,8},{10,11... | collective-permute-start | bytes 2113544 | tf_op jit(solution)/shard_map/ppermute | solution.py:760
  41.0 16.2 %collective-permute-start.6 = (bf16[4,128,512]{2,1,0:T(8,128)(2,1)}, bf16[4,128,512]{2,1,0:T(8,128)(2,1)}, u32[]{:S(2)}, u32[]{:S(2)}) collective-permute-start(bf16[4,128,512]{2,1,0:T(8,128)(2,1)} %pad_maximum_fusion.1.refs_2_), channel_id=1, source_target_pairs={{0,4},{4,0},{8,12},{12,8},{16,20},{20,16},{24,28},{28,24},{1,5},{5... | collective-permute-start | bytes 1572872 | tf_op jit(solution)/shard_map/ppermute | solution.py:765
  51.1 24.2 %collective-permute-start.10 = (bf16[4,128,640]{2,1,0:T(8,128)(2,1)S(1)}, bf16[4,128,640]{2,1,0:T(8,128)(2,1)}, u32[]{:S(2)}, u32[]{:S(2)}) collective-permute-start(bf16[4,128,640]{2,1,0:T(8,128)(2,1)S(1)} %pad_maximum_fusion.refs_1_.refs_2_), channel_id=1, source_target_pairs={{0,4},{4,0},{8,12},{12,8},{16,20},{20,16},{24,28},{28,24},{1,5},{5... | collective-permute-start | bytes 1966088 | tf_op jit(solution)/shard_map/ppermute | solution.py:765
  52.7 300.2 %reduce-scatter.2.cloned.1.call-start = ((), (), s32[]{:S(2)}) async-start(), calls=%async_computation.2 | async-start | bytes 4718592 | tf_op jit(solution)/shard_map/reduce_scatter | solution.py:892
  56.5 46.8 %collective-permute-start.20 = (bf16[344,1024]{1,0:T(8,128)(2,1)}, bf16[344,1024]{1,0:T(8,128)(2,1)}, u32[]{:S(2)}, u32[]{:S(2)}) collective-permute-start(bf16[344,1024]{1,0:T(8,128)(2,1)} %get-tuple-element.123), channel_id=1, source_target_pairs={{0,1},{1,0},{2,3},{3,2},{4,5},{5,4},{6,7},{7,6},{8,9},{9,8},{10,11... | collective-permute-start | bytes 2113544 | tf_op jit(solution)/shard_map/ppermute | solution.py:760
  56.5 36.2 %collective-permute-start.21 = (bf16[344,1024]{1,0:T(8,128)(2,1)}, bf16[344,1024]{1,0:T(8,128)(2,1)}, u32[]{:S(2)}, u32[]{:S(2)}) collective-permute-start(bf16[344,1024]{1,0:T(8,128)(2,1)} %get-tuple-element.123), channel_id=1, source_target_pairs={{0,2},{1,3},{2,0},{3,1},{4,6},{5,7},{6,4},{7,5},{8,10},{9,11},{10,... | collective-permute-start | bytes 2113544 | tf_op jit(solution)/shard_map/ppermute | solution.py:760
  78.1 25.2 %collective-permute-start.18 = (bf16[1024,256]{1,0:T(8,128)(2,1)}, bf16[1024,256]{1,0:T(8,128)(2,1)}, u32[]{:S(2)}, u32[]{:S(2)}) collective-permute-start(bf16[1024,256]{1,0:T(8,128)(2,1)} %unpack.1.refs_6_.refs_10_.refs_9_), channel_id=1, source_target_pairs={{0,2},{1,3},{2,0},{3,1},{4,6},{5,7},{6,4},{7,5},{8,10},{9,11},{10,... | collective-permute-start | bytes 1572872 | tf_op jit(solution)/shard_map/ppermute | solution.py:760
  91.3 9.6 %collective-permute-start.14 = (bf16[1376,128]{1,0:T(8,128)(2,1)}, bf16[1376,128]{1,0:T(8,128)(2,1)}, u32[]{:S(2)}, u32[]{:S(2)}) collective-permute-start(bf16[1376,128]{1,0:T(8,128)(2,1)} %get-tuple-element.120.refs_2_.refs_4_), channel_id=1, source_target_pairs={{0,2},{1,3},{2,0},{3,1},{4,6},{5,7},{6,4},{7,5},{8,10},{9,11},{10,... | collective-permute-start | bytes 1056776 | tf_op jit(solution)/shard_map/ppermute | solution.py:760
  92.8 18.1 %collective-permute-start.22 = (bf16[344,1024]{1,0:T(8,128)(2,1)}, bf16[344,1024]{1,0:T(8,128)(2,1)}, u32[]{:S(2)}, u32[]{:S(2)}) collective-permute-start(bf16[344,1024]{1,0:T(8,128)(2,1)} %collective-permute-done.21), channel_id=1, source_target_pairs={{0,1},{1,0},{2,3},{3,2},{4,5},{5,4},{6,7},{7,6},{8,9},{9,8},{10,11... | collective-permute-start | bytes 2113544 | tf_op jit(solution)/shard_map/ppermute | solution.py:760
  97.8 7.1 %collective-permute-start.12 = (bf16[1376,128]{1,0:T(8,128)(2,1)S(1)}, bf16[1376,128]{1,0:T(8,128)(2,1)S(1)}, u32[]{:S(2)}, u32[]{:S(2)}) collective-permute-start(bf16[1376,128]{1,0:T(8,128)(2,1)S(1)} %copy-done.5), channel_id=1, source_target_pairs={{0,1},{1,0},{2,3},{3,2},{4,5},{5,4},{6,7},{7,6},{8,9},{9,8},{10,11... | collective-permute-start | bytes 1056776 | tf_op jit(solution)/shard_map/ppermute | solution.py:760
  101.0 10.0 %collective-permute-start.13 = (bf16[1376,128]{1,0:T(8,128)(2,1)S(1)}, bf16[1376,128]{1,0:T(8,128)(2,1)S(1)}, u32[]{:S(2)}, u32[]{:S(2)}) collective-permute-start(bf16[1376,128]{1,0:T(8,128)(2,1)S(1)} %copy-done.4), channel_id=1, source_target_pairs={{0,2},{1,3},{2,0},{3,1},{4,6},{5,7},{6,4},{7,5},{8,10},{9,11},{10,... | collective-permute-start | bytes 1056776 | tf_op jit(solution)/shard_map/ppermute | solution.py:760
  103.3 10.5 %collective-permute-start.17 = (bf16[1024,256]{1,0:T(8,128)(2,1)S(1)}, bf16[1024,256]{1,0:T(8,128)(2,1)S(1)}, u32[]{:S(2)}, u32[]{:S(2)}) collective-permute-start(bf16[1024,256]{1,0:T(8,128)(2,1)S(1)} %copy-done.9), channel_id=1, source_target_pairs={{0,1},{1,0},{2,3},{3,2},{4,5},{5,4},{6,7},{7,6},{8,9},{9,8},{10,11... | collective-permute-start | bytes 1572872 | tf_op jit(solution)/shard_map/ppermute | solution.py:760
  103.3 13.1 %collective-permute-start.19 = (bf16[1024,256]{1,0:T(8,128)(2,1)}, bf16[1024,256]{1,0:T(8,128)(2,1)}, u32[]{:S(2)}, u32[]{:S(2)}) collective-permute-start(bf16[1024,256]{1,0:T(8,128)(2,1)} %collective-permute-done.18.refs_12_), channel_id=1, source_target_pairs={{0,1},{1,0},{2,3},{3,2},{4,5},{5,4},{6,7},{7,6},{8,9},{9,8},{10,11... | collective-permute-start | bytes 1572872 | tf_op jit(solution)/shard_map/ppermute | solution.py:760
  105.0 8.8 %collective-permute-start.11 = (bf16[1376,128]{1,0:T(8,128)(2,1)S(1)}, bf16[1376,128]{1,0:T(8,128)(2,1)S(1)}, u32[]{:S(2)}, u32[]{:S(2)}) collective-permute-start(bf16[1376,128]{1,0:T(8,128)(2,1)S(1)} %copy-done.4), channel_id=1, source_target_pairs={{0,1},{1,0},{2,3},{3,2},{4,5},{5,4},{6,7},{7,6},{8,9},{9,8},{10,11... | collective-permute-start | bytes 1056776 | tf_op jit(solution)/shard_map/ppermute | solution.py:760
  152.6 19.0 %collective-permute-start.25 = (bf16[344,1024]{1,0:T(8,128)(2,1)}, bf16[344,1024]{1,0:T(8,128)(2,1)S(1)}, u32[]{:S(2)}, u32[]{:S(2)}) collective-permute-start(bf16[344,1024]{1,0:T(8,128)(2,1)} %back_sum_0.1.refs_25_.refs_1_.refs_5_), channel_id=1, source_target_pairs={{0,2},{1,3},{2,0},{3,1},{4,6},{5,7},{6,4},{7,5},{8,10},{9,11},{10,... | collective-permute-start | bytes 2113544 | tf_op jit(solution)/shard_map/ppermute | solution.py:760
  171.5 5.8 %collective-permute-start.24 = (bf16[344,1024]{1,0:T(8,128)(2,1)}, bf16[344,1024]{1,0:T(8,128)(2,1)S(1)}, u32[]{:S(2)}, u32[]{:S(2)}) collective-permute-start(bf16[344,1024]{1,0:T(8,128)(2,1)} %get-tuple-element.135.refs_7_), channel_id=1, source_target_pairs={{0,1},{1,0},{2,3},{3,2},{4,5},{5,4},{6,7},{7,6},{8,9},{9,8},{10,11... | collective-permute-start | bytes 2113544 | tf_op jit(solution)/shard_map/ppermute | solution.py:760
  181.2 18.4 %collective-permute-start.26 = (bf16[344,1024]{1,0:T(8,128)(2,1)}, bf16[344,1024]{1,0:T(8,128)(2,1)S(1)}, u32[]{:S(2)}, u32[]{:S(2)}) collective-permute-start(bf16[344,1024]{1,0:T(8,128)(2,1)} %back_sum_1.1.refs_5_.refs_1_.refs_6_), channel_id=1, source_target_pairs={{0,2},{1,3},{2,0},{3,1},{4,6},{5,7},{6,4},{7,5},{8,10},{9,11},{10,... | collective-permute-start | bytes 2113544 | tf_op jit(solution)/shard_map/ppermute | solution.py:760
  181.8 32.7 %collective-permute-start.27 = (bf16[2,344,1024]{2,1,0:T(8,128)(2,1)}, bf16[2,344,1024]{2,1,0:T(8,128)(2,1)S(1)}, u32[]{:S(2)}, u32[]{:S(2)}) collective-permute-start(bf16[2,344,1024]{2,1,0:T(8,128)(2,1)} %get-tuple-element.138), channel_id=1, source_target_pairs={{0,1},{1,0},{2,3},{3,2},{4,5},{5,4},{6,7},{7,6},{8,9},{9,8},{10,11... | collective-permute-start | bytes 4227080 | tf_op jit(solution)/shard_map/ppermute | solution.py:760
  182.0 23.4 %collective-permute-start.29 = (bf16[344,1024]{1,0:T(8,128)(2,1)S(1)}, bf16[344,1024]{1,0:T(8,128)(2,1)S(1)}, u32[]{:S(2)}, u32[]{:S(2)}) collective-permute-start(bf16[344,1024]{1,0:T(8,128)(2,1)S(1)} %copy-done.3), channel_id=1, source_target_pairs={{0,1},{1,0},{2,3},{3,2},{4,5},{5,4},{6,7},{7,6},{8,9},{9,8},{10,11... | collective-permute-start | bytes 2113544 | tf_op jit(solution)/shard_map/ppermute | solution.py:760
  214.2 28.4 %collective-permute-start.31 = (bf16[4,256,128]{2,1,0:T(8,128)(2,1)}, bf16[4,256,128]{2,1,0:T(8,128)(2,1)S(1)}, u32[]{:S(2)}, u32[]{:S(2)}) collective-permute-start(bf16[4,256,128]{2,1,0:T(8,128)(2,1)} %get-tuple-element.148.refs_10_), channel_id=1, source_target_pairs={{0,4},{4,0},{8,12},{12,8},{16,20},{20,16},{24,28},{28,24},{1,5},{5... | collective-permute-start | bytes 786440 | tf_op jit(solution)/shard_map/ppermute | solution.py:765
  219.5 26.3 %collective-permute-start.28 = (bf16[344,1024]{1,0:T(8,128)(2,1)}, bf16[344,1024]{1,0:T(8,128)(2,1)S(1)}, u32[]{:S(2)}, u32[]{:S(2)}) collective-permute-start(bf16[344,1024]{1,0:T(8,128)(2,1)} %get-tuple-element.144.refs_11_), channel_id=1, source_target_pairs={{0,2},{1,3},{2,0},{3,1},{4,6},{5,7},{6,4},{7,5},{8,10},{9,11},{10,... | collective-permute-start | bytes 2113544 | tf_op jit(solution)/shard_map/ppermute | solution.py:760
  241.2 20.9 %collective-permute-start.32 = (bf16[4,128,384]{2,1,0:T(8,128)(2,1)}, bf16[4,128,384]{2,1,0:T(8,128)(2,1)S(1)}, u32[]{:S(2)}, u32[]{:S(2)}) collective-permute-start(bf16[4,128,384]{2,1,0:T(8,128)(2,1)} %get-tuple-element.152.refs_3_.refs_10_), channel_id=1, source_target_pairs={{0,4},{4,0},{8,12},{12,8},{16,20},{20,16},{24,28},{28,24},{1,5},{5... | collective-permute-start | bytes 1179656 | tf_op jit(solution)/shard_map/ppermute | solution.py:765
  279.7 42.9 %collective-permute-start.33 = (bf16[2,344,1024]{2,1,0:T(8,128)(2,1)}, bf16[2,344,1024]{2,1,0:T(8,128)(2,1)S(1)}, u32[]{:S(2)}, u32[]{:S(2)}) collective-permute-start(bf16[2,344,1024]{2,1,0:T(8,128)(2,1)} %get-tuple-element.161.refs_12_), channel_id=1, source_target_pairs={{0,1},{1,0},{2,3},{3,2},{4,5},{5,4},{6,7},{7,6},{8,9},{9,8},{10,11... | collective-permute-start | bytes 4227080 | tf_op jit(solution)/shard_map/ppermute | solution.py:760
  293.9 4.4 %collective-permute-start.47 = (f32[14,1024]{1,0:T(8,128)S(1)}, f32[14,1024]{1,0:T(8,128)S(1)}, u32[]{:S(2)}, u32[]{:S(2)}) collective-permute-start(f32[14,1024]{1,0:T(8,128)S(1)} %concatenate.12), channel_id=1, source_target_pairs={{0,3},{1,2},{2,1},{3,0},{4,7},{5,6},{6,5},{7,4},{8,11},{9,10},{10,... | collective-permute-start | bytes 172040 | tf_op jit(solution)/shard_map/ppermute | solution.py:760
  293.9 5.6 %collective-permute-start.42 = (bf16[256,128]{1,0:T(8,128)(2,1)S(1)}, bf16[256,128]{1,0:T(8,128)(2,1)S(1)}, u32[]{:S(2)}, u32[]{:S(2)}) collective-permute-start(bf16[256,128]{1,0:T(8,128)(2,1)S(1)} %copy-done.59), channel_id=1, source_target_pairs={{0,8},{4,12},{8,0},{12,4},{16,24},{20,28},{24,16},{28,20},{1,9},{5... | collective-permute-start | bytes 196616 | tf_op jit(solution)/shard_map/ppermute | solution.py:765
  294.7 6.7 %collective-permute-start.43 = (bf16[256,128]{1,0:T(8,128)(2,1)S(1)}, bf16[256,128]{1,0:T(8,128)(2,1)S(1)}, u32[]{:S(2)}, u32[]{:S(2)}) collective-permute-start(bf16[256,128]{1,0:T(8,128)(2,1)S(1)} %copy-done.58), channel_id=1, source_target_pairs={{0,16},{4,20},{8,24},{12,28},{16,0},{20,4},{24,8},{28,12},{1,17},{... | collective-permute-start | bytes 196616 | tf_op jit(solution)/shard_map/ppermute | solution.py:765
  298.3 5.5 %collective-permute-start.48 = (f32[14,1024]{1,0:T(8,128)S(1)}, f32[14,1024]{1,0:T(8,128)S(1)}, u32[]{:S(2)}, u32[]{:S(2)}) collective-permute-start(f32[14,1024]{1,0:T(8,128)S(1)} %add_add_fusion), channel_id=1, source_target_pairs={{0,4},{4,0},{8,12},{12,8},{16,20},{20,16},{24,28},{28,24},{1,5},{5... | collective-permute-start | bytes 172040 | tf_op jit(solution)/shard_map/ppermute | solution.py:765
  298.9 14.4 %collective-permute-start.35 = (bf16[128,384]{1,0:T(8,128)(2,1)S(1)}, bf16[128,384]{1,0:T(8,128)(2,1)S(1)}, u32[]{:S(2)}, u32[]{:S(2)}) collective-permute-start(bf16[128,384]{1,0:T(8,128)(2,1)S(1)} %copy-done.56), channel_id=1, source_target_pairs={{0,8},{4,12},{8,0},{12,4},{16,24},{20,28},{24,16},{28,20},{1,9},{5... | collective-permute-start | bytes 294920 | tf_op jit(solution)/shard_map/ppermute | solution.py:765
  299.5 14.3 %collective-permute-start.36 = (bf16[128,384]{1,0:T(8,128)(2,1)S(1)}, bf16[128,384]{1,0:T(8,128)(2,1)S(1)}, u32[]{:S(2)}, u32[]{:S(2)}) collective-permute-start(bf16[128,384]{1,0:T(8,128)(2,1)S(1)} %copy-done.55), channel_id=1, source_target_pairs={{0,16},{4,20},{8,24},{12,28},{16,0},{20,4},{24,8},{28,12},{1,17},{... | collective-permute-start | bytes 294920 | tf_op jit(solution)/shard_map/ppermute | solution.py:765
  301.4 6.9 %collective-permute-start.44 = (bf16[256,128]{1,0:T(8,128)(2,1)S(1)}, bf16[256,128]{1,0:T(8,128)(2,1)S(1)}, u32[]{:S(2)}, u32[]{:S(2)}) collective-permute-start(bf16[256,128]{1,0:T(8,128)(2,1)S(1)} %copy-done.57), channel_id=1, source_target_pairs={{0,24},{4,28},{8,16},{12,20},{16,8},{20,12},{24,0},{28,4},{1,25},{... | collective-permute-start | bytes 196616 | tf_op jit(solution)/shard_map/ppermute | solution.py:765
  303.8 14.8 %collective-permute-start.37 = (bf16[128,384]{1,0:T(8,128)(2,1)S(1)}, bf16[128,384]{1,0:T(8,128)(2,1)S(1)}, u32[]{:S(2)}, u32[]{:S(2)}) collective-permute-start(bf16[128,384]{1,0:T(8,128)(2,1)S(1)} %copy-done.54), channel_id=1, source_target_pairs={{0,24},{4,28},{8,16},{12,20},{16,8},{20,12},{24,0},{28,4},{1,25},{... | collective-permute-start | bytes 294920 | tf_op jit(solution)/shard_map/ppermute | solution.py:765
  308.2 20.4 %collective-permute-start.49 = (f32[14,1024]{1,0:T(8,128)S(1)}, f32[14,1024]{1,0:T(8,128)S(1)}, u32[]{:S(2)}, u32[]{:S(2)}) collective-permute-start(f32[14,1024]{1,0:T(8,128)S(1)} %add.103), channel_id=1, source_target_pairs={{0,8},{4,12},{8,0},{12,4},{16,24},{20,28},{24,16},{28,20},{1,9},{5... | collective-permute-start | bytes 172040 | tf_op jit(solution)/shard_map/ppermute | solution.py:765
  313.3 15.3 %collective-permute-start.50 = (f32[14,1024]{1,0:T(8,128)S(1)}, f32[14,1024]{1,0:T(8,128)S(1)}, u32[]{:S(2)}, u32[]{:S(2)}) collective-permute-start(f32[14,1024]{1,0:T(8,128)S(1)} %add.103), channel_id=1, source_target_pairs={{0,16},{4,20},{8,24},{12,28},{16,0},{20,4},{24,8},{28,12},{1,17},{... | collective-permute-start | bytes 172040 | tf_op jit(solution)/shard_map/ppermute | solution.py:765
  313.8 14.8 %collective-permute-start.51 = (f32[14,1024]{1,0:T(8,128)S(1)}, f32[14,1024]{1,0:T(8,128)S(1)}, u32[]{:S(2)}, u32[]{:S(2)}) collective-permute-start(f32[14,1024]{1,0:T(8,128)S(1)} %add.103), channel_id=1, source_target_pairs={{0,24},{4,28},{8,16},{12,20},{16,8},{20,12},{24,0},{28,4},{1,25},{... | collective-permute-start | bytes 172040 | tf_op jit(solution)/shard_map/ppermute | solution.py:765
  318.6 11.4 %collective-permute-start.38 = (bf16[4,128,384]{2,1,0:T(8,128)(2,1)S(1)}, bf16[4,128,384]{2,1,0:T(8,128)(2,1)S(1)}, u32[]{:S(2)}, u32[]{:S(2)}) collective-permute-start(bf16[4,128,384]{2,1,0:T(8,128)(2,1)S(1)} %copy-done.22), channel_id=1, source_target_pairs={{0,4},{4,0},{8,12},{12,8},{16,20},{20,16},{24,28},{28,24},{1,5},{5... | collective-permute-start | bytes 1179656 | tf_op jit(solution)/shard_map/ppermute | solution.py:765
  327.6 19.3 %collective-permute-start.34 = (bf16[344,1024]{1,0:T(8,128)(2,1)}, bf16[344,1024]{1,0:T(8,128)(2,1)S(1)}, u32[]{:S(2)}, u32[]{:S(2)}) collective-permute-start(bf16[344,1024]{1,0:T(8,128)(2,1)} %get-tuple-element.165), channel_id=1, source_target_pairs={{0,2},{1,3},{2,0},{3,1},{4,6},{5,7},{6,4},{7,5},{8,10},{9,11},{10,... | collective-permute-start | bytes 2113544 | tf_op jit(solution)/shard_map/ppermute | solution.py:760
  333.2 5.8 %collective-permute-start.39 = (bf16[128,384]{1,0:T(8,128)(2,1)}, bf16[128,384]{1,0:T(8,128)(2,1)S(1)}, u32[]{:S(2)}, u32[]{:S(2)}) collective-permute-start(bf16[128,384]{1,0:T(8,128)(2,1)} %get-tuple-element.173), channel_id=1, source_target_pairs={{0,8},{4,12},{8,0},{12,4},{16,24},{20,28},{24,16},{28,20},{1,9},{5... | collective-permute-start | bytes 294920 | tf_op jit(solution)/shard_map/ppermute | solution.py:765
  334.3 7.1 %collective-permute-start.40 = (bf16[128,384]{1,0:T(8,128)(2,1)}, bf16[128,384]{1,0:T(8,128)(2,1)S(1)}, u32[]{:S(2)}, u32[]{:S(2)}) collective-permute-start(bf16[128,384]{1,0:T(8,128)(2,1)} %get-tuple-element.174), channel_id=1, source_target_pairs={{0,16},{4,20},{8,24},{12,28},{16,0},{20,4},{24,8},{28,12},{1,17},{... | collective-permute-start | bytes 294920 | tf_op jit(solution)/shard_map/ppermute | solution.py:765
  336.0 6.7 %collective-permute-start.41 = (bf16[128,384]{1,0:T(8,128)(2,1)}, bf16[128,384]{1,0:T(8,128)(2,1)S(1)}, u32[]{:S(2)}, u32[]{:S(2)}) collective-permute-start(bf16[128,384]{1,0:T(8,128)(2,1)} %get-tuple-element.175), channel_id=1, source_target_pairs={{0,24},{4,28},{8,16},{12,20},{16,8},{20,12},{24,0},{28,4},{1,25},{... | collective-permute-start | bytes 294920 | tf_op jit(solution)/shard_map/ppermute | solution.py:765
  (66 other events, 633.9 us)
Sparse Core Ops, SparseCore 0:
  52.8 75.6 all-gather.1
  205.5 89.5 reduce-scatter.1

commit v3 on v2

--- a/solution.py
+++ b/solution.py
@@ -23,7 +23,10 @@
 TILE = 352
 CHUNK = 256
 LONG = 4
-VMEM_LIMIT = 56 * 2**20
+SMALL = 16
+LARGE = 32
+ALL = 56
+TOKENS = {}
 F32 = jnp.float32
 BF16 = jnp.bfloat16
 
@@ -65,29 +68,37 @@
     return (hidden * normal_cdf, normal_cdf + hidden * density)
 
 
-def call(kernel, ids, args, in_specs, outs, out_specs, name, cost=(0, 0, 0), grid=(1,), scratch=(), aliases=None, after=()):
+def call(kernel, ids, args, in_specs, outs, out_specs, name, cost=(0, 0, 0), grid=(1,), scratch=(), aliases=None, after=(), vmem=SMALL):
     count = 1 + len(args)
     waits = len(after)
+    token = shape_of((8, LANES), F32)
 
     def run(*refs):
-        kernel(*refs[:count], *refs[count + waits :])
-
-    several = isinstance(outs, (list, tuple))
-    return pl.pallas_call(
+        place = count + waits + len(outs)
+        refs[place][...] = jnp.zeros_like(refs[place])
+        kernel(*refs[:count], *refs[count + waits : place], *refs[place + 1 :])
+
+    *results, done = pl.pallas_call(
         run,
         grid_spec=pltpu.PrefetchScalarGridSpec(
             num_scalar_prefetch=1,
             grid=grid,
             in_specs=list(in_specs) + [pl.BlockSpec(memory_space=pl.ANY)] * waits,
-            out_specs=out_specs,
+            out_specs=list(out_specs) + [whole(token)],
             scratch_shapes=scratch,
         ),
-        out_shape=outs,
+        out_shape=list(outs) + [token],
         input_output_aliases=aliases or {},
-        compiler_params=pltpu.CompilerParams(vmem_limit_bytes=VMEM_LIMIT),
+        compiler_params=pltpu.CompilerParams(vmem_limit_bytes=vmem * 2**20),
         cost_estimate=pl.CostEstimate(flops=cost[0], bytes_accessed=cost[1], transcendentals=cost[2]),
         name=name,
     )(ids, *args, *after)
+    TOKENS[name] = done
+    return results
+
+
+def done(*names):
+    return tuple(TOKENS[name] for name in names)
 
 
 def whole(array):
@@ -128,7 +139,7 @@
     widths = (4 * LANES, 3 * LANES + head_width, 2 * expand.shape[1])
     args = (project_in, project_out, expand, contract, small)
     outs = [shape_of((shard, width), BF16) for width in widths]
-    return plain(pack_kernel, ids, args, outs, "pack")
+    return plain(pack_kernel, ids, args, outs, "pack", vmem=ALL)
 
 
 def place_rows(ids_ref, near_ref, far_ref, write):
@@ -255,6 +266,7 @@
         outs,
         f"attend_{pair}",
         cost=(LONG * 160 * seq * seq * HEAD_DIM, 0, 0),
+        vmem=LARGE,
         scratch=scratch,
         after=after,
     )
@@ -346,6 +358,7 @@
         [whole(o) for o in outs],
         f"attend_back_{pair}",
         cost=(LONG * 80 * seq * seq * HEAD_DIM, 0, 0),
+        vmem=LARGE,
         scratch=[
             pltpu.VMEM((seq, LANES), F32),
             pltpu.VMEM((2, seq, LANES), BF16),
@@ -376,7 +389,7 @@
 
     @pl.when(step == 1)
     def _():
-        attn_ref[...] = attn_sum
+        attn_ref[...] = attn_sum.astype(BF16)
 
     residual = x_ref[0].astype(F32) + rows_ref[5:6, :] * attn_sum
     scaled, _ = norm_forward(residual)
@@ -417,7 +430,7 @@
     outs += [shape_of((2, count, features), BF16)] * 2
     specs += [held(features)] * 2
     rest = [
-        shape_of((count, features), F32),
+        shape_of((count, features), BF16),
         shape_of((count, features), BF16),
         shape_of((count, features), BF16),
         shape_of((8, features), F32),
@@ -441,6 +454,7 @@
         scratch=[pltpu.VMEM((count, 2 * LANES), BF16)] + [pltpu.VMEM((count, features), BF16)] * 3,
         aliases={1 + len(args) + index: index for index in range(len(before))},
         after=after,
+        vmem=ALL,
     )
     return results[:6], results[6:]
 
@@ -466,70 +480,62 @@
     return plain(split_sum_kernel, ids, (keep, arrived), outs, name, after=after)
 
 
-def residual_kernel(ids_ref, chip_ref, arrived_ref, x_ref, attn_ref, top_ref, rows_ref, grad_ref):
+def residual_kernel(ids_ref, chip_ref, arrived_ref, x_ref, attn_ref, top_ref, rows_ref, grad_ref, residual_ref):
     total = chip_ref[...].astype(F32) + arrived_ref[...].astype(F32)
-    scaled, inverse = norm_forward(x_ref[0].astype(F32) + rows_ref[5:6, :] * attn_ref[...])
+    attn_sum = attn_ref[...].astype(F32)
+    scaled, inverse = norm_forward(x_ref[0].astype(F32) + rows_ref[5:6, :] * attn_sum)
     grad = top_ref[0].astype(F32) + norm_backward(scaled, inverse, total, rows_ref[6:7, :])
+    residual_ref[...] = grad.astype(BF16)
     grad_ref[...] = (grad * rows_ref[5:6, :]).astype(BF16)
 
 
 def residual_back(half, ids, chip, arrived, x_full, attn, top_full, rows, after=()):
     count, features = chip.shape
     part = pl.BlockSpec((1, count, features), lambda i, ids_ref: (2 * half + ids_ref[2], 0, 0))
-    out = shape_of((count, features), BF16)
+    outs = [shape_of((count, features), BF16)] * 2
     return call(
         residual_kernel,
         ids,
         (chip, arrived, x_full, attn, top_full, rows),
         [whole(chip), whole(arrived), part, whole(attn), part, whole(rows)],
-        [out],
-        [whole(out)],
+        outs,
+        [whole(out) for out in outs],
         f"residual_back_{half}",
         after=after,
-    )[0]
+        vmem=ALL,
+    )
 
 
 def own_kernel(
-    ids_ref,
-    x_ref,
-    top_ref,
-    attn_a,
-    attn_b,
-    chip_a,
-    chip_b,
-    arrived_a,
-    arrived_b,
-    stay_ref,
-    branch_ref,
-    rows_ref,
-    output_ref,
-    grad_ref,
-    sums_ref,
+    ids_ref, x_ref, top_ref, attn_a, attn_b, grad_a, grad_b, stay_ref, branch_ref, rows_ref, output_ref, sums_ref
 ):
     first = ids_ref[3] == 0
     choose = lambda a, b: jnp.where(first, a[...].astype(F32), b[...].astype(F32))
     attn_sum = choose(attn_a, attn_b)
-    total = choose(chip_a, chip_b) + choose(arrived_a, arrived_b)
-    residual = x_ref[...] + rows_ref[5:6, :] * attn_sum
+    grad = choose(grad_a, grad_b)
     branch = stay_ref[...].astype(F32) + branch_ref[...].astype(F32) + rows_ref[8:9, :]
-    output_ref[:, 0, :] = residual + rows_ref[9:10, :] * branch
-    scaled, inverse = norm_forward(residual)
-    top = top_ref[...]
-    grad = top + norm_backward(scaled, inverse, total, rows_ref[6:7, :])
-    grad_ref[...] = grad
+    output_ref[:, 0, :] = x_ref[0].astype(F32) + rows_ref[5:6, :] * attn_sum + rows_ref[9:10, :] * branch
+    top = top_ref[0].astype(F32)
     for row, values in enumerate((grad * rows_ref[5:6, :], grad * attn_sum, top * rows_ref[9:10, :], top * branch)):
         sums_ref[row : row + 1, :] = jnp.sum(values, axis=0, keepdims=True)
 
 
-def own_block(ids, x_own, top_own, attn, chips, arrived, stay, branch, rows, after=()):
-    rows_count, features = x_own.shape
-    outs = [
-        shape_of((rows_count, 1, features), F32),
-        shape_of(x_own.shape, F32),
-        shape_of((8, features), F32),
-    ]
-    args = (x_own, top_own, *attn, *chips, *arrived, stay, branch, rows)
-    return plain(own_kernel, ids, args, outs, "own_block", after=after)
+def own_block(ids, x_full, top_full, attn, grads, stay, branch, rows, after=()):
+    _, count, features = x_full.shape
+    part = pl.BlockSpec((1, count, features), lambda i, ids_ref: (ids_ref[1], 0, 0))
+    outs = [shape_of((count, 1, features), F32), shape_of((8, features), F32)]
+    rest = (*attn, *grads, stay, branch, rows)
+    return call(
+        own_kernel,
+        ids,
+        (x_full, top_full, *rest),
+        [part, part] + [whole(a) for a in rest],
+        outs,
+        [whole(o) for o in outs],
+        "own_block",
+        after=after,
+        vmem=24,
+    )
 
 
 def matrices_kernel(ids_ref, left_a, left_b, right_a, right_b, out_ref, flat_ref):
@@ -570,6 +576,7 @@
         grid=(2 * per,),
         scratch=[pltpu.VMEM((features, seq), BF16)],
         after=after,
+        vmem=ALL,
     )[0]
 
 
@@ -604,18 +611,27 @@
     return plain(out_grad_kernel, ids, args, outs, "out_grad", after=after)
 
 
-def in_grad_kernel(ids_ref, flat_ref, mixed_ref, give_ref, keep_ref):
-    shard = give_ref.shape[1]
+def in_grad_kernel(ids_ref, flat_ref, mixed_ref, *refs):
+    give_ref, keep_ref = refs[-2:]
+    count, held, width = give_ref.shape
     values = dot_nn(flat_ref[...], mixed_ref[...]).astype(BF16)
-    for place in range(values.shape[0] // shard):
-        store_shards(ids_ref, place, values[place * shard : (place + 1) * shard], give_ref, keep_ref)
-
-
-def in_grad(pair, ids, flat, mixed, places, after=()):
-    features, seq = flat.shape
-    width = mixed.shape[1]
-    outs = [shape_of((places // 2, features // places, width), BF16)] * 2
-    return plain(in_grad_kernel, ids, (flat, mixed), outs, f"in_grad_{pair}", after=after)
+    shard = values.shape[0] // (2 * count)
+    for place in range(2 * count):
+        at = slice(place * shard, (place + 1) * shard)
+        part = values[at]
+        if held > shard:
+            below = refs[0][:, at].astype(BF16)
+            below = jnp.concatenate([below, jnp.zeros((held - shard, width - shard), BF16)], axis=1)
+            part = jnp.concatenate([part, below])
+        store_shards(ids_ref, place, part, give_ref, keep_ref)
+
+
+def in_grad(pair, ids, flat, mixed, places, after=(), small=None):
+    features = flat.shape[0]
+    held = features // places + (0 if small is None else small.shape[0])
+    outs = [shape_of((places // 2, held, mixed.shape[1]), BF16)] * 2
+    args = (flat, mixed) if small is None else (flat, mixed, small)
+    return plain(in_grad_kernel, ids, args, outs, f"in_grad_{pair}", after=after)
 
 
 def low_sum_kernel(ids_ref, keep_ref, arrived_ref, *out_refs):
@@ -676,16 +692,28 @@
     )
 
 
-def input_kernel(ids_ref, stay_ref, arrived_ref, x_ref, grad_ref, rows_ref, out_ref):
+def input_kernel(ids_ref, stay_ref, arrived_ref, x_ref, grad_a, grad_b, rows_ref, out_ref):
     total = stay_ref[...].astype(F32) + arrived_ref[...].astype(F32)
-    scaled, inverse = norm_forward(x_ref[...])
-    out_ref[:, 0, :] = grad_ref[...] + norm_backward(scaled, inverse, total, rows_ref[0:1, :])
-
-
-def input_grad_of(ids, stay, arrived, x_own, grad_residual, rows, after=()):
-    outs = [shape_of((x_own.shape[0], 1, x_own.shape[1]), F32)]
-    args = (stay, arrived, x_own, grad_residual, rows)
-    return plain(input_kernel, ids, args, outs, "input_grad", after=after)[0]
+    scaled, inverse = norm_forward(x_ref[0].astype(F32))
+    grad = jnp.where(ids_ref[3] == 0, grad_a[...].astype(F32), grad_b[...].astype(F32))
+    out_ref[:, 0, :] = grad + norm_backward(scaled, inverse, total, rows_ref[0:1, :])
+
+
+def input_grad_of(ids, stay, arrived, x_full, grads, rows, after=()):
+    _, count, features = x_full.shape
+    part = pl.BlockSpec((1, count, features), lambda i, ids_ref: (ids_ref[1], 0, 0))
+    outs = [shape_of((count, 1, features), F32)]
+    return call(
+        input_kernel,
+        ids,
+        (stay, arrived, x_full, *grads, rows),
+        [whole(stay), whole(arrived), part, whole(grads[0]), whole(grads[1]), whole(rows)],
+        outs,
+        [whole(o) for o in outs],
+        "input_grad",
+        after=after,
+        vmem=ALL,
+    )[0]
 
 
 def adam_step(master, gradient, first, second, decay):
@@ -717,6 +745,7 @@
         outs,
         name,
         after=after,
+        vmem=ALL,
     )
 
 
@@ -741,7 +770,8 @@
     for pair, total in enumerate(totals):
         columns = slice(pair * LANES, (pair + 1) * LANES)
         for part in range(3):
-            yield (part, slice(None), columns), total[:, part * LANES : (part + 1) * LANES]
+            values = total[: parts[0].shape[0], part * LANES : (part + 1) * LANES]
+            yield (part, slice(None), columns), values
 
 
 def out_gradients(parts):
@@ -830,7 +860,7 @@
     first_shards = gather_shards(packed[0])
     second_shards = gather_shards(behind(packed[1], first_shards[0]))
     weights = lax.all_gather(
-        behind(packed[2], second_shards[0]), "fsdp", axis=0, tiled=True
+        behind(packed[2], first_shards[0]), "fsdp", axis=0, tiled=True
     )
 
     x_own = block_input[:, 0]
@@ -843,10 +873,10 @@
         0, ids, live_mask, *first_shards, x_full.reshape(seq, features)
     )
     heads = [heads]
-    out_own = unpack(ids, *second_shards, after=(heads[0][2],))
-    heads.append(attend(1, ids, live_mask, *second_shards, normed_one, rows_now, (out_own,)))
-    normed_flat = flatten(ids, normed_one, (heads[1][2],))
-    held = (normed_flat,)
+    out_own = unpack(ids, *second_shards, after=done("attend_0"))
+    heads.append(attend(1, ids, live_mask, *second_shards, normed_one, rows_now, done("unpack")))
+    normed_flat = flatten(ids, normed_one, done("attend_1"))
+    held = done("flatten")
     out_all = around(out_own)
     att_sets = [around(each[2]) for each in heads]
     att_all = [
@@ -858,21 +888,23 @@
 
     kept = ()
     sums, attn, chips, arrived = [], [], [], []
-    grads = []
+    grads, grads_peer = [], []
     for half in range(2):
         kept, (attn_part, back_give, back_keep, sums_part) = middle(
             half, ids, x_full, att_all, out_all, rows_now, weights, bias_here, top_full, kept, held
         )
         arrived_part = tensor_swap(back_give, 1)
+        held = ()
         if half == 1:
             grads.append(
                 residual_back(
-                    0, ids, chips[0], arrived[0], x_full, attn[0], top_full, rows_now, (back_give,)
+                    0, ids, chips[0], arrived[0], x_full, attn[0], top_full, rows_now, done("middle_1")
                 )
             )
-            grads.append(tensor_swap(grads[0], 1))
-        chip = pair_sum(ids, back_keep, arrived_part, f"back_sum_{half}", grads[:1])
-        held = (chip,)
+            grads_peer.append(tensor_swap(grads[0][0], 1))
+            held = done("residual_back_0")
+        chip = pair_sum(ids, back_keep, arrived_part, f"back_sum_{half}", held)
+        held = done(f"back_sum_{half}")
         chips.append(chip)
         arrived.append(tensor_swap(chip, 2))
         attn.append(attn_part)
@@ -885,57 +917,57 @@
     grad_second = matrices(ids, normed_two, grad_hidden, grad_branch, activated, held)
     grads.append(
         residual_back(
-            1, ids, chips[1], arrived[1], x_full, attn[1], top_full, rows_now, (grad_second,)
+            1, ids, chips[1], arrived[1], x_full, attn[1], top_full, rows_now, done("matrices")
         )
     )
-    grads.append(tensor_swap(grads[2], 1))
+    grads_peer.append(tensor_swap(grads[1][0], 1))
+    attn_grads = (grads[0][0], grads_peer[0], grads[1][0], grads_peer[1])
+    residual_grads = (grads[0][1], grads[1][1])
     second_sum = lax.psum_scatter(
-        behind(grad_second, grads[2]), "fsdp", scatter_dimension=0, tiled=True
-    )
-
+        behind(grad_second, arrived[1]), "fsdp", scatter_dimension=0, tiled=True
+    )
+
+    sends = lambda low: [low[0]] + [fsdp_swap(low[step], 2 * step) for step in range(1, places // 2)]
+    out_give, out_keep = out_grad(ids, [each[2] for each in heads], attn_grads, places)
+    out_arrived = fsdp_swap(out_give, 1)
     branch_arrived = tensor_swap(behind(branch_give, chips[1]), 1)
-    give, branch_stay = split_sum(ids, branch_keep, branch_arrived, "branch_sum", (grads[2],))
+    give, branch_stay = split_sum(ids, branch_keep, branch_arrived, "branch_sum", done("out_grad"))
     branch_arrived = tensor_swap(give, 2)
-
-    out_give, out_keep = out_grad(ids, [each[2] for each in heads], grads, places)
-    out_arrived = fsdp_swap(out_give, 1)
     mixed, head_sums = [], []
-    sends = lambda low: [low[0]] + [fsdp_swap(low[step], 2 * step) for step in range(1, places // 2)]
-    wait = (out_give, give)
+    wait = done("branch_sum")
     for pair in range(2):
         weight, qkv, attended, queries = heads[pair]
         mixed_pair, pair_sums = attend_back(
-            pair, ids, live_mask, qkv, queries, attended, grads, out_own, wait
+            pair, ids, live_mask, qkv, queries, attended, attn_grads, out_own, wait
         )
         mixed.append(mixed_pair)
         head_sums.append(pair_sums)
-        if pair == 1:
-            in_low = low_sum(ids, *in_parts, "in_low_0", (mixed_pair,))
-            in_sums = sends(in_low)
-            wait = (in_low[0],)
-        else:
-            wait = ()
-        in_give, in_keep = in_grad(pair, ids, normed_flat, mixed_pair, places, wait)
-        in_parts = (in_keep, fsdp_swap(in_give, 1))
         if pair == 0:
-            out_low = low_sum(ids, out_keep, out_arrived, "out_low", (in_give,))
-            wait = (in_give, out_low[0], branch_arrived)
+            in_give, in_keep = in_grad(0, ids, normed_flat, mixed_pair, places)
+            in_arrived = fsdp_swap(in_give, 1)
+            block_output, own_sums = own_block(
+                ids,
+                x_full,
+                top_full,
+                attn,
+                residual_grads,
+                branch_stay,
+                branch_arrived,
+                rows_now,
+                done("in_grad_0"),
+            )
+            out_low = low_sum(ids, out_keep, out_arrived, "out_low", done("own_block"))
+            wait = done("out_low")
+    in_low = low_sum(ids, in_keep, in_arrived, "in_low_0", done("attend_back_1"))
+    in_sums = sends(in_low)
+    out_sums = sends(out_low)
     input_give, input_keep, input_sums = input_back(
         ids,
         scaled_one.reshape(4, rows, features),
         [each.reshape(4, rows, each.shape[1]) for each in mixed],
         [each[0] for each in heads],
-        (in_give,),
-    )
-    out_sums = sends(out_low)
-    give, stay = split_sum(ids, input_keep, tensor_swap(input_give, 1), "input_sum")
-    input_arrived = tensor_swap(give, 2)
-    block_output, grad_residual, own_sums = own_block(
-        ids, x_own, top_own, attn, chips, arrived, branch_stay, branch_arrived, rows_now, (input_give,)
-    )
-    sum_first = high_sum(ids, in_sums, "in_sum_0", (own_sums,))
-    in_sums = [sum_first] + sends(low_sum(ids, *in_parts, "in_low_1", (sum_first,)))
-    input_grad = input_grad_of(ids, stay, input_arrived, x_own, grad_residual, rows_now)
+        done("in_low_0"),
+    )
 
     lay = lambda values, start, total: lax.dynamic_update_slice_in_dim(
         jnp.zeros((total,), F32), values, start, 0
@@ -957,14 +989,56 @@
     )
     grad_bias = lay(sums[0], rank * hidden_width, expand_bias.shape[0] * places)
     grad_bias = grad_bias.reshape(places, -1, shard).transpose(1, 0, 2).reshape(-1, features)
-    small = jnp.concatenate([grad_rows, grad_bias])
-    small = sum([tensor_swap(small, bit) for bit in (1, 2, 3)], small)
-    small = small + fsdp_swap(small, 1)
-    small = sum([fsdp_swap(small, 2 * step) for step in range(1, places // 2)], small)
-    small = lax.dynamic_slice_in_dim(small, place * shard, shard, 1)
-    grad_vectors = small[:vector_rows]
-    grad_bias = small[vector_rows:small_rows].reshape(-1)
-
+    small = jnp.concatenate([grad_rows, grad_bias, jnp.zeros((16 - small_rows, features), F32)])
+    in_give, in_keep = in_grad(1, ids, normed_flat, mixed[1], places, (), small)
+    in_arrived = fsdp_swap(in_give, 1)
+    give, stay = split_sum(ids, input_keep, tensor_swap(input_give, 1), "input_sum", done("in_grad_1"))
+    input_arrived = tensor_swap(give, 2)
+    sum_first = high_sum(ids, in_sums, "in_sum_0", done("input_sum"))
+    in_low = low_sum(
+        ids, in_keep, behind(in_arrived, input_arrived), "in_low_1", done("in_sum_0")
+    )
+    in_sums = [sum_first] + sends(in_low)
+    input_grad = input_grad_of(
+        ids, stay, input_arrived, x_full, residual_grads, rows_now, done("in_low_1")
+    )
+    new_out = adam(
+        out_gradients,
+        WEIGHT_DECAY,
+        True,
+        ids,
+        out_sums,
+        project_out,
+        moment_project_out,
+        second_project_out,
+        "adam_out",
+        done("input_grad"),
+    )
+    second = (second_sum,)
+    new_expand = adam(
+        expand_gradients,
+        WEIGHT_DECAY,
+        False,
+        ids,
+        second,
+        expand,
+        moment_expand,
+        second_expand,
+        "adam_expand",
+        done("adam_out"),
+    )
+    new_contract = adam(
+        contract_gradients,
+        WEIGHT_DECAY,
+        False,
+        ids,
+        second,
+        contract,
+        moment_contract,
+        second_contract,
+        "adam_contract",
+        done("adam_expand"),
+    )
     new_in = adam(
         in_gradients,
         WEIGHT_DECAY,
@@ -975,34 +1049,14 @@
         parts_first(moment_project_in),
         parts_first(second_project_in),
         "adam_in",
+        done("adam_contract"),
     )
     new_in = [parts_first(array) for array in new_in]
-    new_out = adam(
-        out_gradients,
-        WEIGHT_DECAY,
-        True,
-        ids,
-        out_sums,
-        project_out,
-        moment_project_out,
-        second_project_out,
-        "adam_out",
-    )
-    second = (second_sum,)
-    new_expand = adam(
-        expand_gradients, WEIGHT_DECAY, False, ids, second, expand, moment_expand, second_expand, "adam_expand"
-    )
-    new_contract = adam(
-        contract_gradients,
-        WEIGHT_DECAY,
-        False,
-        ids,
-        second,
-        contract,
-        moment_contract,
-        second_contract,
-        "adam_contract",
-    )
+    small = sum(each[shard:, :shard].astype(F32) for each in in_sums[1:])
+    small = behind(small, *done("adam_contract"))
+    small = sum([tensor_swap(small, bit) for bit in (1, 2, 3)], small)
+    grad_vectors = small[:vector_rows]
+    grad_bias = small[vector_rows:small_rows].reshape(-1)
     change, first, second = adam_step(vectors, grad_vectors, moment_vectors, second_vectors, 0.0)
     new_vectors = (grad_vectors, change, first, second)
     change, first, second = adam_step(

time: 372 us -> 328 us (0.88)
  Pallas kernels: 204 us -> 157 us
  starting transfers between devices: 51.2 us -> 46.8 us
  local copies, waits for them, and re-layouts: 35.2 us -> 39.3 us
  waiting for transfers between devices: 55.2 us -> 59 us
    pallas_call x30, Pallas kernels: 204 us -> 157 us  [call(): pl.pallas_call(run, grid_spec=pltpu.PrefetchScalarGridSpec(num_scalar_pre...]
    ppermute x24 -> x20, waiting for transfers between devices: 26.4 us -> 41 us  [fsdp_swap(): lax.ppermute(array, 'fsdp', [(rank, rank ^ bit) for rank in range(size)])]
    all_gather x1, waiting for transfers between devices: 12.1 us -> 3.82 us  [body(): lax.all_gather(behind(packed[2], first_shards[0]), 'fsdp', axis=0, tiled=...]
    unnamed x124 -> x185, local copies, waits for them, and re-layouts: 20.7 us -> 27.2 us
    ppermute x24 -> x20, starting transfers between devices: 35.3 us -> 30.8 us  [fsdp_swap(): lax.ppermute(array, 'fsdp', [(rank, rank ^ bit) for rank in range(size)])]
  transfers between devices with their start and end apart: 54 -> 50, of which waited for: 17 -> 16; matrix products, arithmetic and copies ran while one was open for 7% -> 6% of each run, Pallas kernels for 47% -> 40%
where the time goes in v3:
time: 328 us; the launch traced here: 325 us
  Pallas kernels  157 us (48%)
  waiting for transfers between devices  59 us (18%)
  starting transfers between devices  46.8 us (14%)
  local copies, waits for them, and re-layouts  39.3 us (12%)
  between operations  15.5 us (5%)
  other arithmetic  6.72 us (2%)
    pallas_call x30, Pallas kernels, call(): pl.pallas_call(run, grid_spec=pltpu.PrefetchScalarGridSpec(num_scalar_pre...  157 us
    ppermute x20, waiting for transfers between devices, fsdp_swap(): lax.ppermute(array, 'fsdp', [(rank, rank ^ bit) for rank in range(size)])  41 us
    ppermute x20, starting transfers between devices, fsdp_swap(): lax.ppermute(array, 'fsdp', [(rank, rank ^ bit) for rank in range(size)])  30.8 us
    unnamed x185, local copies, waits for them, and re-layouts  27.2 us
    ppermute x28, starting transfers between devices, tensor_swap(): lax.ppermute(array, 'tensor', [(rank, rank ^ bit) for rank in range(4)])  15.8 us
    ppermute x28, waiting for transfers between devices, tensor_swap(): lax.ppermute(array, 'tensor', [(rank, rank ^ bit) for rank in range(4)])  14.1 us
    dynamic_update_slice x8, local copies, waits for them, and re-layouts, gather_positions(): full = lax.dynamic_update_slice_in_dim(full, piece[None], rank ^ bit, 0)  9.83 us
  transfers between devices with their start and end apart: 50, of which 16 were waited for; matrix products, arithmetic and copies ran while one was open for 6% of the time, Pallas kernels for 40%

profile of v3, /device:TPU:0, one launch (start us, length us, event | category | flops | bytes accessed | tf_op | source)
XLA Modules:
  0.0 324.8 jit_solution(8403122789206820476)
XLA Ops:
  7.3 2.5 copy.73
  9.8 2.9 collective-permute-start.1
  14.8 3.1 pack.1
  19.5 2.6 collective-permute-start.7
  24.5 7.8 %collective-permute-done.7 = bf16[128,512]{1,0:T(8,128)(2,1)S(1)} collective-permute-done((bf16[128,512]{1,0:T(8,128)(2,1)}, bf16[128,512]{1,0:T(8,128)(2,1)S(1)}, u32[]{:S(2)}, u32[]{:S(2)}) %collective-permute-start.7) | collective-permute-done | bytes 131104 | tf_op jit(solution)/shard_map/ppermute | solution.py:795
  33.3 2.0 collective-permute-start.10
  38.2 1.7 bitcast_dynamic-update-slice_fusion.7
  42.9 6.4 %collective-permute-done.11 = bf16[128,640]{1,0:T(8,128)(2,1)} collective-permute-done((bf16[128,640]{1,0:T(8,128)(2,1)S(1)}, bf16[128,640]{1,0:T(8,128)(2,1)}, u32[]{:S(2)}, u32[]{:S(2)}) %collective-permute-start.11) | collective-permute-done | bytes 163872 | tf_op jit(solution)/shard_map/ppermute | solution.py:795
  50.6 1.7 collective-permute-start.13
  56.4 4.4 %collective-permute-done.9.refs_3_ = bf16[4,128,512]{2,1,0:T(8,128)(2,1)S(1)} collective-permute-done((bf16[4,128,512]{2,1,0:T(8,128)(2,1)S(1)}, bf16[4,128,512]{2,1,0:T(8,128)(2,1)S(1)}, u32[]{:S(2)}, u32[]{:S(2)}) %collective-permute-start.9) | collective-permute-done | bytes 524320 | tf_op jit(solution)/shard_map/ppermute | solution.py:795
  60.8 10.1 %attend_0.1 = (f32[16,1024]{1,0:T(8,128)S(1)}, bf16[1376,1024]{1,0:T(8,128)(2,1)S(1)}, bf16[1376,1024]{1,0:T(8,128)(2,1)S(1)}, bf16[1024,384]{1,0:T(8,128)(2,1)S...) custom-call(s32[4]{0:T(128)S(1)} %copy-done.42, ...), custom_call_target="tpu_custom_call" | custom-call | flops 77552680960 | tf_op jit(solution)/shard_map/attend_0/pallas_call | solution.py:81
  73.3 2.1 collective-permute-done.13.refs_2_.refs_3_
  77.3 9.2 %attend_1.1 = (bf16[1024,384]{1,0:T(8,128)(2,1)S(1)}, bf16[1376,384]{1,0:T(8,128)(2,1)S(1)}, bf16[1376,128]{1,0:T(8,128)(2,1)S(1)}, bf16[1376,256]{1,0:T(8,128)(2,1)S(1)}, f32[8,128]{1,0:T(8,128)S(1)}) custom-call(s32[4]{0:T(128)S(1)} %copy-done.42, s32[1376,1]{1,0:T(8,128)S(1)} %copy-done.34, bf16[4,128,640]{2,1,0:T(8,128)(2,1)S(1)} %pad_maximum_fusion.refs_1_.refs_2_, ...), custom_call_target="tpu_custom_call" | custom-call | flops 77552680960 | tf_op jit(solution)/shard_map/attend_1/pallas_call | solution.py:81
  91.4 1.8 copy-done.15
  94.6 1.7 copy-done.4
  103.0 5.6 %collective-permute-done.16 = bf16[1376,128]{1,0:T(8,128)(2,1)S(1)} collective-permute-done((bf16[1376,128]{1,0:T(8,128)(2,1)S(1)}, bf16[1376,128]{1,0:T(8,128)(2,1)S(1)}, u32[]{:S(2)}, u32[]{:S(2)}) %collective-permute-start.16) | collective-permute-done | bytes 352288 | tf_op jit(solution)/shard_map/ppermute | solution.py:790
  113.3 3.8 %all-gather.2.cloned.1.call-done.refs_15_.refs_16_ = bf16[1024,2048]{1,0:T(8,128)(2,1)} async-done(((bf16[128,2048]{1,0:T(8,128)(2,1)}), bf16[1024,2048]{1,0:T(8,128)(2,1)}) %all-gather.2.cloned.1.call-update) | async-done | bytes 4194320 | tf_op jit(solution)/shard_map/all_gather | solution.py:862
  117.1 17.5 %middle_0.1 = (bf16[4,344,1024]{2,1,0:T(8,128)(2,1)}, bf16[4,344,1024]{2,1,0:T(8,128)(2,1)}, bf16[4,344,1024]{2,1,0:T(8,128)(2,1)}, bf16[4,344,1024]{2,1,0:T(8,1...) custom-call(s32[4]{0:T(128)} %pad_add_fusion.refs_0_, ...), custom_call_target="tpu_custom_call" | custom-call | flops 7214202880 | bytes 23199744 | tf_op jit(solution)/shard_map/middle_0/pallas_call | solution.py:81
  134.7 2.4 collective-permute-done.23.refs_2_
  141.0 17.2 %middle_1.1 = (bf16[4,344,1024]{2,1,0:T(8,128)(2,1)}, bf16[4,344,1024]{2,1,0:T(8,128)(2,1)}, bf16[4,344,1024]{2,1,0:T(8,128)(2,1)}, bf16[4,344,1024]{2,1,0:T(8,1...) custom-call(s32[4]{0:T(128)} %pad_add_fusion.refs_0_, ...), custom_call_target="tpu_custom_call", output_to_operand_aliasing={{0}: (19, {}), {1}: (20, {}), {2}: (21, {}), {3}: (22, {}),... | custom-call | flops 7214202880 | bytes 23199744 | tf_op jit(solution)/shard_map/middle_1/pallas_call | solution.py:81
  159.2 5.1 %residual_back_0.1 = (bf16[344,1024]{1,0:T(8,128)(2,1)}, bf16[344,1024]{1,0:T(8,128)(2,1)}, f32[8,128]{1,0:T(8,128)}) custom-call(s32[4]{0:T(128)} %pad_add_fusion.refs_0_, bf16[344,1024]{1,0:T(8,128)(2,1)} %copy-done.40, bf16[344,1024]{1,0:T(8,128)(2,1)} %copy-done.68, bf16[4,344,1024]{2,1,0:T(8,128)(2,1)} %copy-done, ...), custom_call_target="tpu_custom_call" | custom-call | tf_op jit(solution)/shard_map/residual_back_0/pallas_call | solution.py:81
  167.4 14.1 %matrices.1 = (bf16[1024,2048]{1,0:T(8,128)(2,1)}, f32[8,128]{1,0:T(8,128)}) custom-call(s32[4]{0:T(128)} %pad_add_fusion.refs_0_, bf16[1376,1024]{1,0:T(8,128)(2,1)} %bitcast.85, bf16[1376,1024]{1,0:T(8,128)(2,1)} %bitcast.88, bf16[1376,1024]{1,0:T(8,128)(2,1)} %bitcast.87, bf16[1376,1024]{1,0:T(8,128)(2,1)} %bitcast.86, f32[8,128]{1,0:T(8,128)} %copy-done.51), custom_call_target="tpu_custom_call" | custom-call | tf_op jit(solution)/shard_map/matrices/pallas_call | solution.py:81
  181.5 3.0 collective-permute-done.26.refs_2_
  185.4 4.9 %residual_back_1.1 = (bf16[344,1024]{1,0:T(8,128)(2,1)}, bf16[344,1024]{1,0:T(8,128)(2,1)}, f32[8,128]{1,0:T(8,128)}) custom-call(s32[4]{0:T(128)} %pad_add_fusion.refs_0_, bf16[344,1024]{1,0:T(8,128)(2,1)} %copy-done.41, bf16[344,1024]{1,0:T(8,128)(2,1)} %copy-done.69, bf16[4,344,1024]{2,1,0:T(8,128)(2,1)} %copy-done, ...), custom_call_target="tpu_custom_call" | custom-call | tf_op jit(solution)/shard_map/residual_back_1/pallas_call | solution.py:81
  190.4 2.4 collective-permute-done.29.refs_6_.refs_8_
  194.0 4.3 %out_grad.1 = (bf16[4,256,128]{2,1,0:T(8,128)(2,1)S(1)}, bf16[4,256,128]{2,1,0:T(8,128)(2,1)S(1)}, f32[8,128]{1,0:T(8,128)S(1)}) custom-call(s32[4]{0:T(128)S(1)} %copy-done.45, bf16[4,344,128]{2,1,0:T(8,128)(2,1)S(1)} %bitcast.84, bf16[4,344,128]{2,1,0:T(8,128)(2,1)S(1)} %bitcast.81, bf16[344,1024]{1,0:T(8,128)(2,1)S(1)} %copy-done.36, ...), custom_call_target="tpu_custom_call" | custom-call | tf_op jit(solution)/shard_map/out_grad/pallas_call | solution.py:81
  198.6 2.3 branch_sum.1
  201.6 13.5 %attend_back_0.1 = (bf16[1376,384]{1,0:T(8,128)(2,1)S(1)}, f32[8,128]{1,0:T(8,128)S(1)}, f32[8,128]{1,0:T(8,128)}) custom-call(s32[4]{0:T(128)S(1)} %copy-done.45, s32[1376,1]{1,0:T(8,128)S(1)} %copy-done.35, bf16[1376,384]{1,0:T(8,128)(2,1)S(1)} %copy-done.61, bf16[1376,256]{1,0:T(8,128)(2,1)S(1)} %copy-done.65, bf16[1376,128]{1,0:T(8,128)(2,1)S(1)} %copy-done.24, ...), custom_call_target="tpu_custom_call" | custom-call | flops 38776340480 | tf_op jit(solution)/shard_map/attend_back_0/pallas_call | solution.py:81
  215.2 2.6 in_grad_0.1
  219.5 3.1 own_block.1
  224.4 13.8 %attend_back_1.1 = (bf16[1376,384]{1,0:T(8,128)(2,1)S(1)}, f32[8,128]{1,0:T(8,128)S(1)}, f32[8,128]{1,0:T(8,128)S(1)}) custom-call(s32[4]{0:T(128)S(1)} %copy-done.45, s32[1376,1]{1,0:T(8,128)S(1)} %copy-done.35, bf16[1376,384]{1,0:T(8,128)(2,1)S(1)} %copy-done.59, bf16[1376,256]{1,0:T(8,128)(2,1)S(1)} %copy-done.63, bf16[1376,128]{1,0:T(8,128)(2,1)S(1)} %copy-done.21, ...), custom_call_target="tpu_custom_call" | custom-call | flops 38776340480 | tf_op jit(solution)/shard_map/attend_back_1/pallas_call | solution.py:81
  239.0 5.6 %input_back.1 = (bf16[2,344,1024]{2,1,0:T(8,128)(2,1)}, bf16[2,344,1024]{2,1,0:T(8,128)(2,1)S(1)}, f32[8,1024]{1,0:T(8,128)S(1)}, f32[8,128]{1,0:T(8,128)}) custom-call(s32[4]{0:T(128)S(1)} %copy-done.45, bf16[4,344,1024]{2,1,0:T(8,128)(2,1)S(1)} %bitcast.78, bf16[4,344,384]{2,1,0:T(8,128)(2,1)S(1)} %bitcast.77, bf16[4,344,384]{2,1,0:T(8,128)(2,1)S(1)} %bitcast.76, ...), custom_call_target="tpu_custom_call" | custom-call | tf_op jit(solution)/shard_map/input_back/pallas_call | solution.py:81
  247.6 2.5 in_grad_1.1
  250.1 2.3 input_sum.1
  253.3 1.8 collective-permute-start.34
  257.4 2.3 collective-permute-start.38
  259.6 6.0 %collective-permute-done.36.refs_2_ = bf16[128,384]{1,0:T(8,128)(2,1)S(1)} collective-permute-done((bf16[128,384]{1,0:T(8,128)(2,1)S(1)}, bf16[128,384]{1,0:T(8,128)(2,1)S(1)}, u32[]{:S(2)}, u32[]{:S(2)}) %collective-permute-start.36) | collective-permute-done | bytes 98336 | tf_op jit(solution)/shard_map/ppermute | solution.py:795
  265.6 5.2 %collective-permute-done.37.refs_3_ = bf16[128,384]{1,0:T(8,128)(2,1)S(1)} collective-permute-done((bf16[128,384]{1,0:T(8,128)(2,1)S(1)}, bf16[128,384]{1,0:T(8,128)(2,1)S(1)}, u32[]{:S(2)}, u32[]{:S(2)}) %collective-permute-start.37) | collective-permute-done | bytes 98336 | tf_op jit(solution)/shard_map/ppermute | solution.py:795
  274.3 6.5 %collective-permute-start.39 = (bf16[144,384]{1,0:T(8,128)(2,1)S(1)}, bf16[144,384]{1,0:T(8,128)(2,1)S(1)}, u32[]{:S(2)}, u32[]{:S(2)}) collective-permute-start(bf16[144,384]{1,0:T(8,128)(2,1)S(1)} %get-tuple-element.243), channel_id=1, source_target_pairs={{0,8},{4,12},{8,0},{12,4},{16,24},{20,28},{24,16},{28,20},{1,9},{5... | collective-permute-start | bytes 331784 | tf_op jit(solution)/shard_map/ppermute | solution.py:795
  281.5 1.7 collective-permute-start.41
  283.1 1.8 collective-permute-start.43
  285.0 1.7 collective-permute-start.44
  286.6 5.0 %input_grad.1 = (f32[344,1,1024]{2,1,0:T(1,128)}, f32[8,128]{1,0:T(8,128)}) custom-call(s32[4]{0:T(128)} %pad_add_fusion.refs_0_, bf16[344,1024]{1,0:T(8,128)(2,1)} %copy-done.31, bf16[344,1024]{1,0:T(8,128)(2,1)} %copy-done.67, bf16[4,344,1024]{2,1,0:T(8,128)(2,1)} %copy-done, bf16[344,1024]{1,0:T(8,128)(2,1)} %get-tuple-element.178.refs_5_.refs_4_, ...), custom_call_target="tpu_custom_call" | custom-call | tf_op jit(solution)/shard_map/input_grad/pallas_call | solution.py:81
  291.7 7.2 %collective-permute-done.43.refs_3_ = bf16[256,128]{1,0:T(8,128)(2,1)S(1)} collective-permute-done((bf16[256,128]{1,0:T(8,128)(2,1)S(1)}, bf16[256,128]{1,0:T(8,128)(2,1)S(1)}, u32[]{:S(2)}, u32[]{:S(2)}) %collective-permute-start.43) | collective-permute-done | bytes 65568 | tf_op jit(solution)/shard_map/ppermute | solution.py:795
  299.5 2.7 adam_out.1
  302.5 4.0 %adam_expand.1 = (f32[128,1024]{1,0:T(8,128)}, f32[128,1024]{1,0:T(8,128)}, f32[128,1024]{1,0:T(8,128)}, f32[128,1024]{1,0:T(8,128)}, f32[8,128]{1,0:T(8,128)}) custom-call(s32[4]{0:T(128)} %pad_add_fusion.refs_0_, bf16[128,2048]{1,0:T(8,128)(2,1)} %reduce-scatter.2.cloned.1.call-done.refs_1_, f32[128,1024]{1,0:T(8,128)} %refs_2_.4, f32[128,1024]{1,0:T(8,128)} %refs_3_.4, ...), custom_call_target="tpu_custom_call" | custom-call | tf_op jit(solution)/shard_map/adam_expand/pallas_call | solution.py:81
  306.5 4.0 %adam_contract.1 = (f32[1024,128]{1,0:T(8,128)}, f32[1024,128]{1,0:T(8,128)}, f32[1024,128]{1,0:T(8,128)}, f32[1024,128]{1,0:T(8,128)}, f32[8,128]{1,0:T(8,128)}) custom-call(s32[4]{0:T(128)} %pad_add_fusion.refs_0_, bf16[128,2048]{1,0:T(8,128)(2,1)} %reduce-scatter.2.cloned.1.call-done.refs_1_, f32[1024,128]{1,0:T(8,128)} %refs_2_.5, f32[1024,128]{1,0:T(8,128)} %refs_3_.5, ...), custom_call_target="tpu_custom_call" | custom-call | tf_op jit(solution)/shard_map/adam_contract/pallas_call | solution.py:81
  312.3 3.6 %adam_in.1 = (f32[3,128,256]{2,1,0:T(8,128)}, f32[3,128,256]{2,1,0:T(8,128)}, f32[3,128,256]{2,1,0:T(8,128)}, f32[3,128,256]{2,1,0:T(8,128)}, f32[8,128]{1,0:T(8,128)}) custom-call(s32[4]{0:T(128)} %pad_add_fusion.refs_0_, f32[128,384]{1,0:T(8,128)} %copy-done.46, bf16[144,384]{1,0:T(8,128)(2,1)} %copy-done.47, bf16[144,384]{1,0:T(8,128)(2,1)} %copy-done.76, ...), custom_call_target="tpu_custom_call" | custom-call | tf_op jit(solution)/shard_map/adam_in/pallas_call | solution.py:81
  (308 shorter events, 69.5 us)
Async XLA Ops:
  7.2 109.9 %all-gather.2.cloned.1.call-start = ((), (), s32[]{:S(2)}) async-start(), calls=%async_computation.1 | async-start | bytes 4718592 | tf_op jit(solution)/shard_map/all_gather | solution.py:862
  9.8 28.0 %collective-permute-start.1 = (bf16[344,1024]{1,0:T(8,128)(2,1)}, bf16[344,1024]{1,0:T(8,128)(2,1)}, u32[]{:S(2)}, u32[]{:S(2)}) collective-permute-start(bf16[344,1024]{1,0:T(8,128)(2,1)} %bitcast.74), channel_id=1, source_target_pairs={{0,2},{1,3},{2,0},{3,1},{4,6},{5,7},{6,4},{7,5},{8,10},{9,11},{10,... | collective-permute-start | bytes 2113544 | tf_op jit(solution)/shard_map/ppermute | solution.py:790
  17.9 6.6 %collective-permute-start.6 = (bf16[128,512]{1,0:T(8,128)(2,1)}, bf16[128,512]{1,0:T(8,128)(2,1)S(1)}, u32[]{:S(2)}, u32[]{:S(2)}) collective-permute-start(bf16[128,512]{1,0:T(8,128)(2,1)} %get-tuple-element.151), channel_id=1, source_target_pairs={{0,8},{4,12},{8,0},{12,4},{16,24},{20,28},{24,16},{28,20},{1,9},{5... | collective-permute-start | bytes 393224 | tf_op jit(solution)/shard_map/ppermute | solution.py:795
  19.5 12.9 %collective-permute-start.7 = (bf16[128,512]{1,0:T(8,128)(2,1)}, bf16[128,512]{1,0:T(8,128)(2,1)S(1)}, u32[]{:S(2)}, u32[]{:S(2)}) collective-permute-start(bf16[128,512]{1,0:T(8,128)(2,1)} %get-tuple-element.151), channel_id=1, source_target_pairs={{0,16},{4,20},{8,24},{12,28},{16,0},{20,4},{24,8},{28,12},{1,17},{... | collective-permute-start | bytes 393224 | tf_op jit(solution)/shard_map/ppermute | solution.py:795
  22.1 10.3 %collective-permute-start.8 = (bf16[128,512]{1,0:T(8,128)(2,1)}, bf16[128,512]{1,0:T(8,128)(2,1)S(1)}, u32[]{:S(2)}, u32[]{:S(2)}) collective-permute-start(bf16[128,512]{1,0:T(8,128)(2,1)} %get-tuple-element.151), channel_id=1, source_target_pairs={{0,24},{4,28},{8,16},{12,20},{16,8},{20,12},{24,0},{28,4},{1,25},{... | collective-permute-start | bytes 393224 | tf_op jit(solution)/shard_map/ppermute | solution.py:795
  22.3 30.0 %collective-permute-start = (bf16[344,1024]{1,0:T(8,128)(2,1)}, bf16[344,1024]{1,0:T(8,128)(2,1)}, u32[]{:S(2)}, u32[]{:S(2)}) collective-permute-start(bf16[344,1024]{1,0:T(8,128)(2,1)} %bitcast.74), channel_id=1, source_target_pairs={{0,1},{1,0},{2,3},{3,2},{4,5},{5,4},{6,7},{7,6},{8,9},{9,8},{10,11... | collective-permute-start | bytes 2113544 | tf_op jit(solution)/shard_map/ppermute | solution.py:790
  33.3 8.0 %collective-permute-start.10 = (bf16[128,640]{1,0:T(8,128)(2,1)S(1)}, bf16[128,640]{1,0:T(8,128)(2,1)}, u32[]{:S(2)}, u32[]{:S(2)}) collective-permute-start(bf16[128,640]{1,0:T(8,128)(2,1)S(1)} %copy-done.75), channel_id=1, source_target_pairs={{0,8},{4,12},{8,0},{12,4},{16,24},{20,28},{24,16},{28,20},{1,9},{5... | collective-permute-start | bytes 491528 | tf_op jit(solution)/shard_map/ppermute | solution.py:795
  35.4 14.0 %collective-permute-start.11 = (bf16[128,640]{1,0:T(8,128)(2,1)S(1)}, bf16[128,640]{1,0:T(8,128)(2,1)}, u32[]{:S(2)}, u32[]{:S(2)}) collective-permute-start(bf16[128,640]{1,0:T(8,128)(2,1)S(1)} %copy-done.75), channel_id=1, source_target_pairs={{0,16},{4,20},{8,24},{12,28},{16,0},{20,4},{24,8},{28,12},{1,17},{... | collective-permute-start | bytes 491528 | tf_op jit(solution)/shard_map/ppermute | solution.py:795
  36.4 12.9 %collective-permute-start.12 = (bf16[128,640]{1,0:T(8,128)(2,1)S(1)}, bf16[128,640]{1,0:T(8,128)(2,1)}, u32[]{:S(2)}, u32[]{:S(2)}) collective-permute-start(bf16[128,640]{1,0:T(8,128)(2,1)S(1)} %copy-done.75), channel_id=1, source_target_pairs={{0,24},{4,28},{8,16},{12,20},{16,8},{20,12},{24,0},{28,4},{1,25},{... | collective-permute-start | bytes 491528 | tf_op jit(solution)/shard_map/ppermute | solution.py:795
  37.8 16.7 %collective-permute-start.2 = (bf16[344,1024]{1,0:T(8,128)(2,1)}, bf16[344,1024]{1,0:T(8,128)(2,1)}, u32[]{:S(2)}, u32[]{:S(2)}) collective-permute-start(bf16[344,1024]{1,0:T(8,128)(2,1)} %collective-permute-done.1), channel_id=1, source_target_pairs={{0,1},{1,0},{2,3},{3,2},{4,5},{5,4},{6,7},{7,6},{8,9},{9,8},{10,11... | collective-permute-start | bytes 2113544 | tf_op jit(solution)/shard_map/ppermute | solution.py:790
  41.1 261.3 %reduce-scatter.2.cloned.1.call-start = ((), (), s32[]{:S(2)}) async-start(), calls=%async_computation.2 | async-start | bytes 4718592 | tf_op jit(solution)/shard_map/reduce_scatter | solution.py:926
  41.3 19.4 %collective-permute-start.9 = (bf16[4,128,512]{2,1,0:T(8,128)(2,1)S(1)}, bf16[4,128,512]{2,1,0:T(8,128)(2,1)S(1)}, u32[]{:S(2)}, u32[]{:S(2)}) collective-permute-start(bf16[4,128,512]{2,1,0:T(8,128)(2,1)S(1)} %pad_maximum_fusion.1.refs_2_), channel_id=1, source_target_pairs={{0,4},{4,0},{8,12},{12,8},{16,20},{20,16},{24,28},{28,24},{1,5},{5... | collective-permute-start | bytes 1572872 | tf_op jit(solution)/shard_map/ppermute | solution.py:795
  50.6 24.8 %collective-permute-start.13 = (bf16[4,128,640]{2,1,0:T(8,128)(2,1)S(1)}, bf16[4,128,640]{2,1,0:T(8,128)(2,1)S(1)}, u32[]{:S(2)}, u32[]{:S(2)}) collective-permute-start(bf16[4,128,640]{2,1,0:T(8,128)(2,1)S(1)} %pad_maximum_fusion.refs_1_.refs_2_), channel_id=1, source_target_pairs={{0,4},{4,0},{8,12},{12,8},{16,20},{20,16},{24,28},{28,24},{1,5},{5... | collective-permute-start | bytes 1966088 | tf_op jit(solution)/shard_map/ppermute | solution.py:795
  55.8 45.4 %collective-permute-start.3 = (bf16[344,1024]{1,0:T(8,128)(2,1)}, bf16[344,1024]{1,0:T(8,128)(2,1)}, u32[]{:S(2)}, u32[]{:S(2)}) collective-permute-start(bf16[344,1024]{1,0:T(8,128)(2,1)} %fusion), channel_id=1, source_target_pairs={{0,1},{1,0},{2,3},{3,2},{4,5},{5,4},{6,7},{7,6},{8,9},{9,8},{10,11... | collective-permute-start | bytes 2113544 | tf_op jit(solution)/shard_map/ppermute | solution.py:790
  55.8 35.0 %collective-permute-start.4 = (bf16[344,1024]{1,0:T(8,128)(2,1)}, bf16[344,1024]{1,0:T(8,128)(2,1)}, u32[]{:S(2)}, u32[]{:S(2)}) collective-permute-start(bf16[344,1024]{1,0:T(8,128)(2,1)} %fusion), channel_id=1, source_target_pairs={{0,2},{1,3},{2,0},{3,1},{4,6},{5,7},{6,4},{7,5},{8,10},{9,11},{10,... | collective-permute-start | bytes 2113544 | tf_op jit(solution)/shard_map/ppermute | solution.py:790
  76.8 24.3 %collective-permute-start.21 = (bf16[1024,256]{1,0:T(8,128)(2,1)}, bf16[1024,256]{1,0:T(8,128)(2,1)}, u32[]{:S(2)}, u32[]{:S(2)}) collective-permute-start(bf16[1024,256]{1,0:T(8,128)(2,1)} %get-tuple-element.160.refs_10_.refs_9_), channel_id=1, source_target_pairs={{0,2},{1,3},{2,0},{3,1},{4,6},{5,7},{6,4},{7,5},{8,10},{9,11},{10,... | collective-permute-start | bytes 1572872 | tf_op jit(solution)/shard_map/ppermute | solution.py:790
  89.4 9.7 %collective-permute-start.17 = (bf16[1376,128]{1,0:T(8,128)(2,1)S(1)}, bf16[1376,128]{1,0:T(8,128)(2,1)}, u32[]{:S(2)}, u32[]{:S(2)}) collective-permute-start(bf16[1376,128]{1,0:T(8,128)(2,1)S(1)} %get-tuple-element.159.refs_4_), channel_id=1, source_target_pairs={{0,2},{1,3},{2,0},{3,1},{4,6},{5,7},{6,4},{7,5},{8,10},{9,11},{10,... | collective-permute-start | bytes 1056776 | tf_op jit(solution)/shard_map/ppermute | solution.py:790
  90.9 17.7 %collective-permute-start.5 = (bf16[344,1024]{1,0:T(8,128)(2,1)}, bf16[344,1024]{1,0:T(8,128)(2,1)}, u32[]{:S(2)}, u32[]{:S(2)}) collective-permute-start(bf16[344,1024]{1,0:T(8,128)(2,1)} %collective-permute-done.4), channel_id=1, source_target_pairs={{0,1},{1,0},{2,3},{3,2},{4,5},{5,4},{6,7},{7,6},{8,9},{9,8},{10,11... | collective-permute-start | bytes 2113544 | tf_op jit(solution)/shard_map/ppermute | solution.py:790
  90.9 11.9 %collective-permute-start.15 = (bf16[1376,128]{1,0:T(8,128)(2,1)S(1)}, bf16[1376,128]{1,0:T(8,128)(2,1)S(1)}, u32[]{:S(2)}, u32[]{:S(2)}) collective-permute-start(bf16[1376,128]{1,0:T(8,128)(2,1)S(1)} %get-tuple-element.159.refs_4_), channel_id=1, source_target_pairs={{0,1},{1,0},{2,3},{3,2},{4,5},{5,4},{6,7},{7,6},{8,9},{9,8},{10,11... | collective-permute-start | bytes 1056776 | tf_op jit(solution)/shard_map/ppermute | solution.py:790
  99.0 9.5 %collective-permute-start.16 = (bf16[1376,128]{1,0:T(8,128)(2,1)S(1)}, bf16[1376,128]{1,0:T(8,128)(2,1)S(1)}, u32[]{:S(2)}, u32[]{:S(2)}) collective-permute-start(bf16[1376,128]{1,0:T(8,128)(2,1)S(1)} %copy-done.23), channel_id=1, source_target_pairs={{0,2},{1,3},{2,0},{3,1},{4,6},{5,7},{6,4},{7,5},{8,10},{9,11},{10,... | collective-permute-start | bytes 1056776 | tf_op jit(solution)/shard_map/ppermute | solution.py:790
  101.1 10.3 %collective-permute-start.20 = (bf16[1024,256]{1,0:T(8,128)(2,1)}, bf16[1024,256]{1,0:T(8,128)(2,1)}, u32[]{:S(2)}, u32[]{:S(2)}) collective-permute-start(bf16[1024,256]{1,0:T(8,128)(2,1)} %get-tuple-element.160.refs_10_.refs_9_), channel_id=1, source_target_pairs={{0,1},{1,0},{2,3},{3,2},{4,5},{5,4},{6,7},{7,6},{8,9},{9,8},{10,11... | collective-permute-start | bytes 1572872 | tf_op jit(solution)/shard_map/ppermute | solution.py:790
  101.1 12.1 %collective-permute-start.22 = (bf16[1024,256]{1,0:T(8,128)(2,1)}, bf16[1024,256]{1,0:T(8,128)(2,1)}, u32[]{:S(2)}, u32[]{:S(2)}) collective-permute-start(bf16[1024,256]{1,0:T(8,128)(2,1)} %collective-permute-done.21.refs_12_), channel_id=1, source_target_pairs={{0,1},{1,0},{2,3},{3,2},{4,5},{5,4},{6,7},{7,6},{8,9},{9,8},{10,11... | collective-permute-start | bytes 1572872 | tf_op jit(solution)/shard_map/ppermute | solution.py:790
  102.8 8.6 %collective-permute-start.14 = (bf16[1376,128]{1,0:T(8,128)(2,1)S(1)}, bf16[1376,128]{1,0:T(8,128)(2,1)S(1)}, u32[]{:S(2)}, u32[]{:S(2)}) collective-permute-start(bf16[1376,128]{1,0:T(8,128)(2,1)S(1)} %copy-done.23), channel_id=1, source_target_pairs={{0,1},{1,0},{2,3},{3,2},{4,5},{5,4},{6,7},{7,6},{8,9},{9,8},{10,11... | collective-permute-start | bytes 1056776 | tf_op jit(solution)/shard_map/ppermute | solution.py:790
  108.6 2.9 collective-permute-start.19
  108.6 2.9 collective-permute-start.18
  139.5 18.8 %collective-permute-start.24 = (bf16[344,1024]{1,0:T(8,128)(2,1)S(1)}, bf16[344,1024]{1,0:T(8,128)(2,1)S(1)}, u32[]{:S(2)}, u32[]{:S(2)}) collective-permute-start(bf16[344,1024]{1,0:T(8,128)(2,1)S(1)} %get-tuple-element.176.refs_1_), channel_id=1, source_target_pairs={{0,2},{1,3},{2,0},{3,1},{4,6},{5,7},{6,4},{7,5},{8,10},{9,11},{10,... | collective-permute-start | bytes 2113544 | tf_op jit(solution)/shard_map/ppermute | solution.py:790
  158.3 6.1 %collective-permute-start.25 = (bf16[344,1024]{1,0:T(8,128)(2,1)}, bf16[344,1024]{1,0:T(8,128)(2,1)S(1)}, u32[]{:S(2)}, u32[]{:S(2)}) collective-permute-start(bf16[344,1024]{1,0:T(8,128)(2,1)} %get-tuple-element.180), channel_id=1, source_target_pairs={{0,1},{1,0},{2,3},{3,2},{4,5},{5,4},{6,7},{7,6},{8,9},{9,8},{10,11... | collective-permute-start | bytes 2113544 | tf_op jit(solution)/shard_map/ppermute | solution.py:790
  166.3 18.2 %collective-permute-start.26 = (bf16[344,1024]{1,0:T(8,128)(2,1)S(1)}, bf16[344,1024]{1,0:T(8,128)(2,1)S(1)}, u32[]{:S(2)}, u32[]{:S(2)}) collective-permute-start(bf16[344,1024]{1,0:T(8,128)(2,1)S(1)} %get-tuple-element.182.refs_1_), channel_id=1, source_target_pairs={{0,2},{1,3},{2,0},{3,1},{4,6},{5,7},{6,4},{7,5},{8,10},{9,11},{10,... | collective-permute-start | bytes 2113544 | tf_op jit(solution)/shard_map/ppermute | solution.py:790
  166.9 31.7 %collective-permute-start.27 = (bf16[2,344,1024]{2,1,0:T(8,128)(2,1)}, bf16[2,344,1024]{2,1,0:T(8,128)(2,1)}, u32[]{:S(2)}, u32[]{:S(2)}) collective-permute-start(bf16[2,344,1024]{2,1,0:T(8,128)(2,1)} %get-tuple-element.192), channel_id=1, source_target_pairs={{0,1},{1,0},{2,3},{3,2},{4,5},{5,4},{6,7},{7,6},{8,9},{9,8},{10,11... | collective-permute-start | bytes 4227080 | tf_op jit(solution)/shard_map/ppermute | solution.py:790
  167.1 23.3 %collective-permute-start.28 = (bf16[344,1024]{1,0:T(8,128)(2,1)}, bf16[344,1024]{1,0:T(8,128)(2,1)}, u32[]{:S(2)}, u32[]{:S(2)}) collective-permute-start(bf16[344,1024]{1,0:T(8,128)(2,1)} %get-tuple-element.193.refs_3_.refs_5_), channel_id=1, source_target_pairs={{0,1},{1,0},{2,3},{3,2},{4,5},{5,4},{6,7},{7,6},{8,9},{9,8},{10,11... | collective-permute-start | bytes 2113544 | tf_op jit(solution)/shard_map/ppermute | solution.py:790
  198.3 24.2 %collective-permute-start.31 = (bf16[4,256,128]{2,1,0:T(8,128)(2,1)S(1)}, bf16[4,256,128]{2,1,0:T(8,128)(2,1)S(1)}, u32[]{:S(2)}, u32[]{:S(2)}) collective-permute-start(bf16[4,256,128]{2,1,0:T(8,128)(2,1)S(1)} %get-tuple-element.209), channel_id=1, source_target_pairs={{0,4},{4,0},{8,12},{12,8},{16,20},{20,16},{24,28},{28,24},{1,5},{5... | collective-permute-start | bytes 786440 | tf_op jit(solution)/shard_map/ppermute | solution.py:795
  200.9 18.5 %collective-permute-start.30 = (bf16[344,1024]{1,0:T(8,128)(2,1)S(1)}, bf16[344,1024]{1,0:T(8,128)(2,1)S(1)}, u32[]{:S(2)}, u32[]{:S(2)}) collective-permute-start(bf16[344,1024]{1,0:T(8,128)(2,1)S(1)} %get-tuple-element.197), channel_id=1, source_target_pairs={{0,2},{1,3},{2,0},{3,1},{4,6},{5,7},{6,4},{7,5},{8,10},{9,11},{10,... | collective-permute-start | bytes 2113544 | tf_op jit(solution)/shard_map/ppermute | solution.py:790
  217.8 20.5 %collective-permute-start.32 = (bf16[4,128,384]{2,1,0:T(8,128)(2,1)S(1)}, bf16[4,128,384]{2,1,0:T(8,128)(2,1)S(1)}, u32[]{:S(2)}, u32[]{:S(2)}) collective-permute-start(bf16[4,128,384]{2,1,0:T(8,128)(2,1)S(1)} %get-tuple-element.216), channel_id=1, source_target_pairs={{0,4},{4,0},{8,12},{12,8},{16,20},{20,16},{24,28},{28,24},{1,5},{5... | collective-permute-start | bytes 1179656 | tf_op jit(solution)/shard_map/ppermute | solution.py:795
  245.8 4.3 %collective-permute-start.33 = (bf16[2,344,1024]{2,1,0:T(8,128)(2,1)}, bf16[2,344,1024]{2,1,0:T(8,128)(2,1)}, u32[]{:S(2)}, u32[]{:S(2)}) collective-permute-start(bf16[2,344,1024]{2,1,0:T(8,128)(2,1)} %get-tuple-element.220), channel_id=1, source_target_pairs={{0,1},{1,0},{2,3},{3,2},{4,5},{5,4},{6,7},{7,6},{8,9},{9,8},{10,11... | collective-permute-start | bytes 4227080 | tf_op jit(solution)/shard_map/ppermute | solution.py:790
  253.3 19.7 %collective-permute-start.34 = (bf16[344,1024]{1,0:T(8,128)(2,1)S(1)}, bf16[344,1024]{1,0:T(8,128)(2,1)S(1)}, u32[]{:S(2)}, u32[]{:S(2)}) collective-permute-start(bf16[344,1024]{1,0:T(8,128)(2,1)S(1)} %get-tuple-element.229), channel_id=1, source_target_pairs={{0,2},{1,3},{2,0},{3,1},{4,6},{5,7},{6,4},{7,5},{8,10},{9,11},{10,... | collective-permute-start | bytes 2113544 | tf_op jit(solution)/shard_map/ppermute | solution.py:790
  255.1 17.9 %collective-permute-start.35 = (bf16[4,144,384]{2,1,0:T(8,128)(2,1)S(1)}, bf16[4,144,384]{2,1,0:T(8,128)(2,1)S(1)}, u32[]{:S(2)}, u32[]{:S(2)}) collective-permute-start(bf16[4,144,384]{2,1,0:T(8,128)(2,1)S(1)} %get-tuple-element.231), channel_id=1, source_target_pairs={{0,4},{4,0},{8,12},{12,8},{16,20},{20,16},{24,28},{28,24},{1,5},{5... | collective-permute-start | bytes 1327112 | tf_op jit(solution)/shard_map/ppermute | solution.py:795
  255.2 10.4 %collective-permute-start.36 = (bf16[128,384]{1,0:T(8,128)(2,1)S(1)}, bf16[128,384]{1,0:T(8,128)(2,1)S(1)}, u32[]{:S(2)}, u32[]{:S(2)}) collective-permute-start(bf16[128,384]{1,0:T(8,128)(2,1)S(1)} %get-tuple-element.234), channel_id=1, source_target_pairs={{0,8},{4,12},{8,0},{12,4},{16,24},{20,28},{24,16},{28,20},{1,9},{5... | collective-permute-start | bytes 294920 | tf_op jit(solution)/shard_map/ppermute | solution.py:795
  256.1 14.8 %collective-permute-start.37 = (bf16[128,384]{1,0:T(8,128)(2,1)S(1)}, bf16[128,384]{1,0:T(8,128)(2,1)S(1)}, u32[]{:S(2)}, u32[]{:S(2)}) collective-permute-start(bf16[128,384]{1,0:T(8,128)(2,1)S(1)} %get-tuple-element.235), channel_id=1, source_target_pairs={{0,16},{4,20},{8,24},{12,28},{16,0},{20,4},{24,8},{28,12},{1,17},{... | collective-permute-start | bytes 294920 | tf_op jit(solution)/shard_map/ppermute | solution.py:795
  257.4 14.1 %collective-permute-start.38 = (bf16[128,384]{1,0:T(8,128)(2,1)S(1)}, bf16[128,384]{1,0:T(8,128)(2,1)S(1)}, u32[]{:S(2)}, u32[]{:S(2)}) collective-permute-start(bf16[128,384]{1,0:T(8,128)(2,1)S(1)} %get-tuple-element.236), channel_id=1, source_target_pairs={{0,24},{4,28},{8,16},{12,20},{16,8},{20,12},{24,0},{28,4},{1,25},{... | collective-permute-start | bytes 294920 | tf_op jit(solution)/shard_map/ppermute | solution.py:795
  265.6 19.4 %collective-permute-start.42 = (bf16[256,128]{1,0:T(8,128)(2,1)S(1)}, bf16[256,128]{1,0:T(8,128)(2,1)S(1)}, u32[]{:S(2)}, u32[]{:S(2)}) collective-permute-start(bf16[256,128]{1,0:T(8,128)(2,1)S(1)} %copy-done.56), channel_id=1, source_target_pairs={{0,8},{4,12},{8,0},{12,4},{16,24},{20,28},{24,16},{28,20},{1,9},{5... | collective-permute-start | bytes 196616 | tf_op jit(solution)/shard_map/ppermute | solution.py:795
  274.3 28.0 %collective-permute-start.39 = (bf16[144,384]{1,0:T(8,128)(2,1)S(1)}, bf16[144,384]{1,0:T(8,128)(2,1)S(1)}, u32[]{:S(2)}, u32[]{:S(2)}) collective-permute-start(bf16[144,384]{1,0:T(8,128)(2,1)S(1)} %get-tuple-element.243), channel_id=1, source_target_pairs={{0,8},{4,12},{8,0},{12,4},{16,24},{20,28},{24,16},{28,20},{1,9},{5... | collective-permute-start | bytes 331784 | tf_op jit(solution)/shard_map/ppermute | solution.py:795
  280.8 21.5 %collective-permute-start.40 = (bf16[144,384]{1,0:T(8,128)(2,1)S(1)}, bf16[144,384]{1,0:T(8,128)(2,1)S(1)}, u32[]{:S(2)}, u32[]{:S(2)}) collective-permute-start(bf16[144,384]{1,0:T(8,128)(2,1)S(1)} %get-tuple-element.244), channel_id=1, source_target_pairs={{0,16},{4,20},{8,24},{12,28},{16,0},{20,4},{24,8},{28,12},{1,17},{... | collective-permute-start | bytes 331784 | tf_op jit(solution)/shard_map/ppermute | solution.py:795
  281.5 20.8 %collective-permute-start.41 = (bf16[144,384]{1,0:T(8,128)(2,1)S(1)}, bf16[144,384]{1,0:T(8,128)(2,1)S(1)}, u32[]{:S(2)}, u32[]{:S(2)}) collective-permute-start(bf16[144,384]{1,0:T(8,128)(2,1)S(1)} %get-tuple-element.245), channel_id=1, source_target_pairs={{0,24},{4,28},{8,16},{12,20},{16,8},{20,12},{24,0},{28,4},{1,25},{... | collective-permute-start | bytes 331784 | tf_op jit(solution)/shard_map/ppermute | solution.py:795
  283.1 15.7 %collective-permute-start.43 = (bf16[256,128]{1,0:T(8,128)(2,1)S(1)}, bf16[256,128]{1,0:T(8,128)(2,1)S(1)}, u32[]{:S(2)}, u32[]{:S(2)}) collective-permute-start(bf16[256,128]{1,0:T(8,128)(2,1)S(1)} %copy-done.54), channel_id=1, source_target_pairs={{0,16},{4,20},{8,24},{12,28},{16,0},{20,4},{24,8},{28,12},{1,17},{... | collective-permute-start | bytes 196616 | tf_op jit(solution)/shard_map/ppermute | solution.py:795
  285.0 13.9 %collective-permute-start.44 = (bf16[256,128]{1,0:T(8,128)(2,1)S(1)}, bf16[256,128]{1,0:T(8,128)(2,1)S(1)}, u32[]{:S(2)}, u32[]{:S(2)}) collective-permute-start(bf16[256,128]{1,0:T(8,128)(2,1)S(1)} %get-tuple-element.251), channel_id=1, source_target_pairs={{0,24},{4,28},{8,16},{12,20},{16,8},{20,12},{24,0},{28,4},{1,25},{... | collective-permute-start | bytes 196616 | tf_op jit(solution)/shard_map/ppermute | solution.py:795
  310.4 5.5 %collective-permute-start.45 = (f32[16,128]{1,0:T(8,128)S(1)}, f32[16,128]{1,0:T(8,128)S(1)}, u32[]{:S(2)}, u32[]{:S(2)}) collective-permute-start(f32[16,128]{1,0:T(8,128)S(1)} %convert_add_fusion), channel_id=1, source_target_pairs={{0,1},{1,0},{2,3},{3,2},{4,5},{5,4},{6,7},{7,6},{8,9},{9,8},{10,11... | collective-permute-start | bytes 24584 | tf_op jit(solution)/shard_map/ppermute | solution.py:790
  310.4 5.5 %collective-permute-start.46 = (f32[16,128]{1,0:T(8,128)S(1)}, f32[16,128]{1,0:T(8,128)S(1)}, u32[]{:S(2)}, u32[]{:S(2)}) collective-permute-start(f32[16,128]{1,0:T(8,128)S(1)} %convert_add_fusion), channel_id=1, source_target_pairs={{0,2},{1,3},{2,0},{3,1},{4,6},{5,7},{6,4},{7,5},{8,10},{9,11},{10,... | collective-permute-start | bytes 24584 | tf_op jit(solution)/shard_map/ppermute | solution.py:790
  311.2 4.7 %collective-permute-start.47 = (f32[16,128]{1,0:T(8,128)S(1)}, f32[16,128]{1,0:T(8,128)S(1)}, u32[]{:S(2)}, u32[]{:S(2)}) collective-permute-start(f32[16,128]{1,0:T(8,128)S(1)} %convert_add_fusion), channel_id=1, source_target_pairs={{0,3},{1,2},{2,1},{3,0},{4,7},{5,6},{6,5},{7,4},{8,11},{9,10},{10,... | collective-permute-start | bytes 24584 | tf_op jit(solution)/shard_map/ppermute | solution.py:790
  (93 other events, 770.7 us)
Sparse Core Ops, SparseCore 0:
  41.2 75.8 all-gather.1
  190.5 96.2 reduce-scatter.1

commit v4 on v3

--- a/solution.py
+++ b/solution.py
@@ -20,7 +20,7 @@
 DENSITY_NORM = 0.3989422804014327
 SCORE_SCALE = HEAD_DIM ** (-0.5)
 LANES = 128
-TILE = 352
+TILE = 512
 CHUNK = 256
 LONG = 4
 SMALL = 16
@@ -357,7 +357,7 @@
         outs,
         [whole(o) for o in outs],
         f"attend_back_{pair}",
-        cost=(LONG * 80 * seq * seq * HEAD_DIM, 0, 0),
+        cost=(80 * seq * seq * HEAD_DIM, 0, 0),
         vmem=LARGE,
         scratch=[
             pltpu.VMEM((seq, LANES), F32),
@@ -371,10 +371,10 @@
 def middle_kernel(ids_ref, x_ref, *refs):
     att_refs, out_refs = refs[:8], refs[8:12]
     rows_ref, expand_ref, contract_ref, bias_ref, top_ref = refs[12:17]
-    outs = refs[-14:-4]
-    normed_ref, act_ref, hidden_ref, grad_ref = outs[:4]
-    branch_refs, attn_ref, back_refs, sums_ref = outs[4:6], outs[6], outs[7:9], outs[9]
-    held_ref, normed_held, act_held, hidden_held = refs[-4:]
+    outs = refs[-14:-5]
+    normed_ref, act_ref, hidden_ref = outs[:3]
+    branch_refs, attn_ref, back_refs, sums_ref = outs[3:5], outs[5], outs[6:8], outs[8]
+    held_ref, normed_held, act_held, hidden_held, grad_held = refs[-5:]
     step = pl.program_id(0)
 
     @pl.when(step == 0)
@@ -387,20 +387,20 @@
         held_ref[:, LANES:] = att_refs[2 * device + 1][0]
         attn_sum = attn_sum + dot_nt(held_ref[...], out_ref[...])
 
-    @pl.when(step == 1)
+    @pl.when(lax.rem(step, 2) == 1)
     def _():
-        attn_ref[...] = attn_sum.astype(BF16)
+        attn_ref[0] = attn_sum.astype(BF16)
 
     residual = x_ref[0].astype(F32) + rows_ref[5:6, :] * attn_sum
     scaled, _ = norm_forward(residual)
     normed_held[...] = (scaled * rows_ref[6:7, :] + rows_ref[7:8, :]).astype(BF16)
     normed_ref[0] = normed_held[...]
-    grad_ref[0] = (top_ref[0].astype(F32) * rows_ref[9:10, :]).astype(BF16)
+    grad_held[...] = (top_ref[0].astype(F32) * rows_ref[9:10, :]).astype(BF16)
     for low in range(0, act_held.shape[1], CHUNK):
         at = slice(low, low + CHUNK)
         activated, slope = gelu_parts(dot_nn(normed_held[...], expand_ref[:, at]) + bias_ref[:, at])
         act_held[:, at] = activated.astype(BF16)
-        grad_hidden = (dot_nn(grad_ref[0], contract_ref[:, at]) * slope).astype(BF16)
+        grad_hidden = (dot_nn(grad_held[...], contract_ref[:, at]) * slope).astype(BF16)
         hidden_held[:, at] = grad_hidden
         sums_ref[0:1, at] += jnp.sum(grad_hidden.astype(F32), axis=0, keepdims=True)
     act_ref[0] = act_held[...]
@@ -411,61 +411,57 @@
     branch = dot_nt(act_held[...], contract_ref[...]).astype(BF16)
     for index in range(2):
 
-        @pl.when(step == index)
+        @pl.when(lax.rem(step, 2) == index)
         def _():
-            back_refs[index][...] = back.astype(BF16)
+            back_refs[index][0] = back.astype(BF16)
             branch_refs[index][0] = branch
 
 
-def middle(half, ids, x_full, att, out_all, rows, weights, bias, top_full, before=(), after=()):
+def middle(ids, x_full, att, out_all, rows, weights, bias, top_full, after=()):
     _, count, features = x_full.shape
     hidden = weights.shape[1] // 2
-    block = lambda i, ids_ref: 2 * half + lax.bitwise_xor(ids_ref[2], 1 - i)
+
+    def block(i, ids_ref):
+        return 2 * lax.div(i, 2) + lax.bitwise_xor(ids_ref[2], 1 - lax.rem(i, 2))
+
     part = lambda n: pl.BlockSpec((1, count, n), lambda i, ids_ref: (block(i, ids_ref), 0, 0))
-    held = lambda n: pl.BlockSpec((1, count, n), lambda i, _: (half, 0, 0))
+    held = pl.BlockSpec((1, count, features), lambda i, _: (lax.div(i, 2), 0, 0))
     column = lambda c: pl.BlockSpec((features, hidden), lambda i, _: (0, c))
-    full = lambda n: shape_of((4, count, n), BF16)
-    outs = [full(features), full(hidden), full(hidden), full(features)]
-    specs = [part(features), part(hidden), part(hidden), part(features)]
-    outs += [shape_of((2, count, features), BF16)] * 2
-    specs += [held(features)] * 2
-    rest = [
-        shape_of((count, features), BF16),
-        shape_of((count, features), BF16),
-        shape_of((count, features), BF16),
-        shape_of((8, features), F32),
-    ]
-    args = (x_full, *att, *out_all, rows, weights, weights, bias, top_full)
-    seq = 2 * count
-    results = call(
+    sums = shape_of((8, features), F32)
+    outs = [shape_of((4, count, n), BF16) for n in (features, hidden, hidden)]
+    outs += [shape_of((2, count, features), BF16)] * 5 + [sums]
+    specs = [part(features), part(hidden), part(hidden)] + [held] * 5 + [whole(sums)]
+    seq = 4 * count
+    return call(
         middle_kernel,
         ids,
-        (*args, *before),
+        (x_full, *att, *out_all, rows, weights, weights, bias, top_full),
         [part(features)]
         + [part(LANES)] * len(att)
         + [whole(o) for o in out_all]
-        + [whole(rows), column(0), column(1), whole(bias), part(features)]
-        + [ANYWHERE] * len(before),
-        outs + rest,
-        specs + [whole(o) for o in rest],
-        f"middle_{half}",
-        (2 * seq * features * (features + 4 * hidden), seq * 24 * features + 6 * features * hidden, 2 * seq * hidden),
-        grid=(2,),
-        scratch=[pltpu.VMEM((count, 2 * LANES), BF16)] + [pltpu.VMEM((count, features), BF16)] * 3,
-        aliases={1 + len(args) + index: index for index in range(len(before))},
+        + [whole(rows), column(0), column(1), whole(bias), part(features)],
+        outs,
+        specs,
+        "middle",
+        cost=(2 * seq * features * (features + 4 * hidden), 0, 0),
+        grid=(4,),
+        scratch=[pltpu.VMEM((count, 2 * LANES), BF16)] + [pltpu.VMEM((count, features), BF16)] * 4,
         after=after,
         vmem=ALL,
     )
-    return results[:6], results[6:]
 
 
 def pair_sum_kernel(ids_ref, keep_ref, arrived_ref, sum_ref):
     sum_ref[...] = (keep_ref[...].astype(F32) + arrived_ref[...].astype(F32)).astype(BF16)
 
 
-def pair_sum(ids, keep, arrived, name, after=()):
-    outs = [shape_of(keep.shape, BF16)]
-    return plain(pair_sum_kernel, ids, (keep, arrived), outs, name, after=after)[0]
+def pair_sum(half, ids, keep, arrived):
+    _, count, features = keep.shape
+    part = pl.BlockSpec((None, count, features), lambda i, _: (half, 0, 0))
+    out = shape_of((count, features), BF16)
+    return call(
+        pair_sum_kernel, ids, (keep, arrived), [part, part], [out], [whole(out)], f"back_sum_{half}"
+    )[0]
 
 
 def split_sum_kernel(ids_ref, keep_ref, arrived_ref, give_ref, stay_ref):
@@ -492,12 +488,13 @@
 def residual_back(half, ids, chip, arrived, x_full, attn, top_full, rows, after=()):
     count, features = chip.shape
     part = pl.BlockSpec((1, count, features), lambda i, ids_ref: (2 * half + ids_ref[2], 0, 0))
+    held = pl.BlockSpec((None, count, features), lambda i, _: (half, 0, 0))
     outs = [shape_of((count, features), BF16)] * 2
     return call(
         residual_kernel,
         ids,
         (chip, arrived, x_full, attn, top_full, rows),
-        [whole(chip), whole(arrived), part, whole(attn), part, whole(rows)],
+        [whole(chip), whole(arrived), part, held, part, whole(rows)],
         outs,
         [whole(out) for out in outs],
         f"residual_back_{half}",
@@ -507,11 +504,11 @@
 
 
 def own_kernel(
-    ids_ref, x_ref, top_ref, attn_a, attn_b, grad_a, grad_b, stay_ref, branch_ref, rows_ref, output_ref, sums_ref
+    ids_ref, x_ref, top_ref, attn_ref, grad_a, grad_b, stay_ref, branch_ref, rows_ref, output_ref, sums_ref
 ):
     first = ids_ref[3] == 0
     choose = lambda a, b: jnp.where(first, a[...].astype(F32), b[...].astype(F32))
-    attn_sum = choose(attn_a, attn_b)
+    attn_sum = attn_ref[...].astype(F32)
     grad = choose(grad_a, grad_b)
     branch = stay_ref[...].astype(F32) + branch_ref[...].astype(F32) + rows_ref[8:9, :]
     output_ref[:, 0, :] = x_ref[0].astype(F32) + rows_ref[5:6, :] * attn_sum + rows_ref[9:10, :] * branch
@@ -524,12 +521,13 @@
     _, count, features = x_full.shape
     part = pl.BlockSpec((1, count, features), lambda i, ids_ref: (ids_ref[1], 0, 0))
     outs = [shape_of((count, 1, features), F32), shape_of((8, features), F32)]
-    rest = (*attn, *grads, stay, branch, rows)
+    held = pl.BlockSpec((None, count, features), lambda i, ids_ref: (ids_ref[3], 0, 0))
+    rest = (*grads, stay, branch, rows)
     return call(
         own_kernel,
         ids,
-        (x_full, top_full, *rest),
-        [part, part] + [whole(a) for a in rest],
+        (x_full, top_full, attn, *rest),
+        [part, part, held] + [whole(a) for a in rest],
         outs,
         [whole(o) for o in outs],
         "own_block",
@@ -538,7 +536,7 @@
     )
 
 
-def matrices_kernel(ids_ref, left_a, left_b, right_a, right_b, out_ref, flat_ref):
+def matrices_kernel(ids_ref, left_a, top_ref, right_a, right_b, rows_ref, out_ref, flat_ref):
     step = pl.program_id(0)
     per = pl.num_programs(0) // 2
 
@@ -548,27 +546,29 @@
 
     @pl.when(step == per)
     def _():
-        flat_ref[...] = left_b[...].T
+        flat_ref[...] = (top_ref[...].astype(F32) * rows_ref[9:10, :]).astype(BF16).T
 
     right = jnp.where(step < per, right_a[...], right_b[...])
     out_ref[...] = dot_nn(flat_ref[...], right).astype(BF16)
 
 
-def matrices(ids, normed, hidden, grad, activated, after=()):
+def matrices(ids, normed, hidden, top_full, activated, rows, after=()):
     seq, features = normed.shape
     width = hidden.shape[1]
     block = 512
     per = width // block
     out = shape_of((features, 2 * width), BF16)
+    top = top_full.reshape(seq, features)
     return call(
         matrices_kernel,
         ids,
-        (normed, grad, hidden, activated),
+        (normed, top, hidden, activated, rows),
         [
             whole(normed),
-            whole(grad),
+            whole(top),
             pl.BlockSpec((seq, block), lambda i, _: (0, jnp.minimum(i, per - 1))),
             pl.BlockSpec((seq, block), lambda i, _: (0, jnp.maximum(i - per, 0))),
+            whole(rows),
         ],
         [out],
         [pl.BlockSpec((features, block), lambda i, _: (0, i))],
@@ -598,21 +598,34 @@
         for pair, att_ref in enumerate((att_a, att_b)):
             part = dot_tn(att_ref[block], ref[...])
             total[pair] = part if index == 0 else total[pair] + part
-    count, _, shard = give_ref.shape
+    count, shard, _ = give_ref.shape
+    values = jnp.concatenate([t.T for t in total], axis=1).astype(BF16)
     for place in range(2 * count):
-        values = jnp.concatenate([t[:, place * shard : (place + 1) * shard] for t in total]).astype(BF16)
-        store_shards(ids_ref, place, values, give_ref, keep_ref)
+        store_shards(ids_ref, place, values[place * shard : (place + 1) * shard], give_ref, keep_ref)
 
 
 def out_grad(ids, attended, grads, places, after=()):
     count, features = grads[0].shape
-    outs = [shape_of((places // 2, 2 * LANES, features // places), BF16)] * 2
+    outs = [shape_of((places // 2, features // places, 2 * LANES), BF16)] * 2
     args = [a.reshape(4, count, LANES) for a in attended] + list(grads)
     return plain(out_grad_kernel, ids, args, outs, "out_grad", after=after)
 
 
 def in_grad_kernel(ids_ref, flat_ref, mixed_ref, *refs):
-    give_ref, keep_ref = refs[-2:]
+    if len(refs) > 2:
+        base_ref, input_ref, own_ref, first_ref, second_ref, give_ref, keep_ref, small_ref = refs
+        small_ref[...] = base_ref[...]
+        small_ref[0:2, :] = input_ref[0:2, :]
+        small_ref[4:5, :] = own_ref[0:1, :]
+        small_ref[5:6, :] = own_ref[1:2, :]
+        small_ref[8:9, :] = own_ref[2:3, :]
+        small_ref[9:10, :] = own_ref[3:4, :]
+        for pair, head_ref in enumerate((first_ref, second_ref)):
+            start = pl.multiple_of(ids_ref[1] * (2 * LANES) + pair * LANES, LANES)
+            small_ref[2:3, pl.ds(start, LANES)] = head_ref[0:1, :]
+            small_ref[3:4, pl.ds(start, LANES)] = head_ref[1:2, :]
+    else:
+        give_ref, keep_ref = refs
     count, held, width = give_ref.shape
     values = dot_nn(flat_ref[...], mixed_ref[...]).astype(BF16)
     shard = values.shape[0] // (2 * count)
@@ -620,30 +633,41 @@
         at = slice(place * shard, (place + 1) * shard)
         part = values[at]
         if held > shard:
-            below = refs[0][:, at].astype(BF16)
+            below = small_ref[:, at].astype(BF16)
             below = jnp.concatenate([below, jnp.zeros((held - shard, width - shard), BF16)], axis=1)
             part = jnp.concatenate([part, below])
         store_shards(ids_ref, place, part, give_ref, keep_ref)
 
 
-def in_grad(pair, ids, flat, mixed, places, after=(), small=None):
+def in_grad(pair, ids, flat, mixed, places, after=(), small=()):
     features = flat.shape[0]
-    held = features // places + (0 if small is None else small.shape[0])
+    held, scratch = features // places, []
+    if small:
+        held += small[0].shape[0]
+        scratch = [pltpu.VMEM(small[0].shape, F32)]
     outs = [shape_of((places // 2, held, mixed.shape[1]), BF16)] * 2
-    args = (flat, mixed) if small is None else (flat, mixed, small)
-    return plain(in_grad_kernel, ids, args, outs, f"in_grad_{pair}", after=after)
-
-
-def low_sum_kernel(ids_ref, keep_ref, arrived_ref, *out_refs):
+    args = (flat, mixed, *small)
+    return plain(in_grad_kernel, ids, args, outs, f"in_grad_{pair}", after=after, scratch=scratch)
+
+
+def low_sum_kernel(parts, ids_ref, *refs):
+    out_refs = refs[2 * parts :]
     high = lax.div(ids_ref[0], 2)
     for step, out_ref in enumerate(out_refs):
         at = lax.bitwise_xor(high, step)
-        out_ref[...] = (keep_ref[at].astype(F32) + arrived_ref[at].astype(F32)).astype(BF16)
-
-
-def low_sum(ids, keep, arrived, name, after=()):
-    outs = [shape_of(keep.shape[1:], BF16)] * keep.shape[0]
-    return plain(low_sum_kernel, ids, (keep, arrived), outs, name, after=after)
+        low = 0
+        for keep_ref, arrived_ref in zip(refs[0 : 2 * parts : 2], refs[1 : 2 * parts : 2]):
+            width = keep_ref.shape[2]
+            total = keep_ref[at].astype(F32) + arrived_ref[at].astype(F32)
+            out_ref[:, low : low + width] = total.astype(BF16)
+            low += width
+
+
+def low_sum(ids, pairs, name, after=()):
+    count, held, _ = pairs[0].shape
+    outs = [shape_of((held, sum(a.shape[2] for a in pairs[::2])), BF16)] * count
+    kernel = functools.partial(low_sum_kernel, len(pairs) // 2)
+    return plain(kernel, ids, pairs, outs, name, after=after)
 
 
 def input_back_kernel(ids_ref, scaled_ref, mixed_a, mixed_b, weight_a, weight_b, give_ref, keep_ref, sums_ref):
@@ -775,7 +799,7 @@
 
 
 def out_gradients(parts):
-    yield (slice(None), slice(None)), sum_refs(parts)
+    yield (slice(None), slice(None)), parts[0][:, 3 * LANES :].T
 
 
 def expand_gradients(parts):
@@ -799,14 +823,15 @@
     return lax.optimization_barrier((array,) + others)[0]
 
 
-def around(array):
+def around(array, *first):
     across = tensor_swap(array, 2)
-    return (array, tensor_swap(array, 1), across, tensor_swap(across, 1))
-
-
-def gather_positions(block, rank):
+    corner = tensor_swap(behind(across, *first) if first else across, 1)
+    return (array, tensor_swap(array, 1), across, corner)
+
+
+def gather_positions(block, rank, *first):
     full = jnp.zeros((4,) + block.shape, block.dtype)
-    for bit, piece in enumerate(around(block)):
+    for bit, piece in enumerate(around(block, *first)):
         full = lax.dynamic_update_slice_in_dim(full, piece[None], rank ^ bit, 0)
     return full
 
@@ -886,52 +911,42 @@
     bias_now = bias_now.reshape(-1, places, shard).transpose(1, 0, 2).reshape(1, -1)
     bias_here = lax.dynamic_slice_in_dim(bias_now, rank * hidden_width, hidden_width, 1)
 
-    kept = ()
-    sums, attn, chips, arrived = [], [], [], []
-    grads, grads_peer = [], []
+    kept = middle(ids, x_full, att_all, out_all, rows_now, weights, bias_here, top_full, held)
+    normed_two, activated, grad_hidden = [array.reshape(seq, array.shape[2]) for array in kept[:3]]
+    branch_give, branch_keep, attn, back_give, back_keep, sums = kept[3:]
+    back_arrived = tensor_swap(back_give, 1)
+    chips, arrived, grads, grads_peer = [], [], [], []
     for half in range(2):
-        kept, (attn_part, back_give, back_keep, sums_part) = middle(
-            half, ids, x_full, att_all, out_all, rows_now, weights, bias_here, top_full, kept, held
+        chips.append(pair_sum(half, ids, back_keep, back_arrived))
+        arrived.append(tensor_swap(chips[half], 2))
+    grad_second = matrices(
+        ids, normed_two, grad_hidden, top_full, activated, rows_now, done("back_sum_1")
+    )
+    for half in range(2):
+        wait = done("residual_back_0" if half == 1 else "matrices")
+        grads.append(
+            residual_back(
+                half, ids, chips[half], arrived[half], x_full, attn, top_full, rows_now, wait
+            )
         )
-        arrived_part = tensor_swap(back_give, 1)
-        held = ()
-        if half == 1:
-            grads.append(
-                residual_back(
-                    0, ids, chips[0], arrived[0], x_full, attn[0], top_full, rows_now, done("middle_1")
-                )
-            )
-            grads_peer.append(tensor_swap(grads[0][0], 1))
-            held = done("residual_back_0")
-        chip = pair_sum(ids, back_keep, arrived_part, f"back_sum_{half}", held)
-        held = done(f"back_sum_{half}")
-        chips.append(chip)
-        arrived.append(tensor_swap(chip, 2))
-        attn.append(attn_part)
-        sums.append(sums_part)
-    normed_two, activated, grad_hidden, grad_branch = [
-        array.reshape(seq, array.shape[2]) for array in kept[:4]
-    ]
-    branch_give, branch_keep = kept[4:]
-    sums = sums[0] + sums[1]
-    grad_second = matrices(ids, normed_two, grad_hidden, grad_branch, activated, held)
-    grads.append(
-        residual_back(
-            1, ids, chips[1], arrived[1], x_full, attn[1], top_full, rows_now, done("matrices")
-        )
-    )
-    grads_peer.append(tensor_swap(grads[1][0], 1))
+        grads_peer.append(tensor_swap(grads[half][0], 1))
     attn_grads = (grads[0][0], grads_peer[0], grads[1][0], grads_peer[1])
     residual_grads = (grads[0][1], grads[1][1])
     second_sum = lax.psum_scatter(
-        behind(grad_second, arrived[1]), "fsdp", scatter_dimension=0, tiled=True
-    )
+        behind(grad_second, arrived[0]), "fsdp", scatter_dimension=0, tiled=True
+    )
+
+    lay = lambda values, start, total: lax.dynamic_update_slice_in_dim(
+        jnp.zeros((total,), F32), values, start, 0
+    )
+    grad_bias = lay(sums[0], rank * hidden_width, expand_bias.shape[0] * places)
+    grad_bias = grad_bias.reshape(places, -1, shard).transpose(1, 0, 2).reshape(-1, features)
+    none = jnp.zeros((6, features), F32)
+    small = jnp.concatenate([none, sums[1:3], none[:2], grad_bias, none[: 16 - small_rows]])
 
     sends = lambda low: [low[0]] + [fsdp_swap(low[step], 2 * step) for step in range(1, places // 2)]
-    out_give, out_keep = out_grad(ids, [each[2] for each in heads], attn_grads, places)
-    out_arrived = fsdp_swap(out_give, 1)
     branch_arrived = tensor_swap(behind(branch_give, chips[1]), 1)
-    give, branch_stay = split_sum(ids, branch_keep, branch_arrived, "branch_sum", done("out_grad"))
+    give, branch_stay = split_sum(ids, branch_keep, branch_arrived, "branch_sum", done("residual_back_1"))
     branch_arrived = tensor_swap(give, 2)
     mixed, head_sums = [], []
     wait = done("branch_sum")
@@ -956,11 +971,14 @@
                 rows_now,
                 done("in_grad_0"),
             )
-            out_low = low_sum(ids, out_keep, out_arrived, "out_low", done("own_block"))
-            wait = done("out_low")
-    in_low = low_sum(ids, in_keep, in_arrived, "in_low_0", done("attend_back_1"))
-    in_sums = sends(in_low)
-    out_sums = sends(out_low)
+            out_give, out_keep = out_grad(
+                ids, [each[2] for each in heads], attn_grads, places, done("own_block")
+            )
+            out_arrived = fsdp_swap(out_give, 1)
+            wait = done("out_grad") + (small,)
+    first_sums = sends(
+        low_sum(ids, (in_keep, in_arrived, out_keep, out_arrived), "in_low_0", done("attend_back_1"))
+    )
     input_give, input_keep, input_sums = input_back(
         ids,
         scaled_one.reshape(4, rows, features),
@@ -969,50 +987,32 @@
         done("in_low_0"),
     )
 
-    lay = lambda values, start, total: lax.dynamic_update_slice_in_dim(
-        jnp.zeros((total,), F32), values, start, 0
-    )
-    head_sums = jnp.concatenate(head_sums, axis=1)
-    grad_rows = jnp.stack(
-        [
-            input_sums[0],
-            input_sums[1],
-            lay(head_sums[0], rank * head_width, features),
-            lay(head_sums[1], rank * head_width, features),
-            own_sums[0],
-            own_sums[1],
-            sums[1],
-            sums[2],
-            own_sums[2],
-            own_sums[3],
-        ]
-    )
-    grad_bias = lay(sums[0], rank * hidden_width, expand_bias.shape[0] * places)
-    grad_bias = grad_bias.reshape(places, -1, shard).transpose(1, 0, 2).reshape(-1, features)
-    small = jnp.concatenate([grad_rows, grad_bias, jnp.zeros((16 - small_rows, features), F32)])
-    in_give, in_keep = in_grad(1, ids, normed_flat, mixed[1], places, (), small)
+    in_give, in_keep = in_grad(
+        1, ids, normed_flat, mixed[1], places, (), (small, input_sums, own_sums, *head_sums)
+    )
     in_arrived = fsdp_swap(in_give, 1)
     give, stay = split_sum(ids, input_keep, tensor_swap(input_give, 1), "input_sum", done("in_grad_1"))
     input_arrived = tensor_swap(give, 2)
-    sum_first = high_sum(ids, in_sums, "in_sum_0", done("input_sum"))
     in_low = low_sum(
-        ids, in_keep, behind(in_arrived, input_arrived), "in_low_1", done("in_sum_0")
-    )
-    in_sums = [sum_first] + sends(in_low)
+        ids, (in_keep, behind(in_arrived, input_arrived)), "in_low_1", done("input_sum")
+    )
+    second_sums = sends(in_low)
     input_grad = input_grad_of(
         ids, stay, input_arrived, x_full, residual_grads, rows_now, done("in_low_1")
     )
+    sum_first = high_sum(ids, first_sums, "in_sum_0", done("input_grad"))
+    in_sums = [sum_first] + second_sums
     new_out = adam(
         out_gradients,
         WEIGHT_DECAY,
         True,
         ids,
-        out_sums,
+        (sum_first,),
         project_out,
         moment_project_out,
         second_project_out,
         "adam_out",
-        done("input_grad"),
+        done("in_sum_0"),
     )
     second = (second_sum,)
     new_expand = adam(

time: 328 us -> 313 us (0.954)
  Pallas kernels: 157 us -> 145 us
  starting transfers between devices: 46.8 us -> 40.2 us
    ppermute x28 -> x27, waiting for transfers between devices: 14.1 us -> 28.5 us  [tensor_swap(): lax.ppermute(array, 'tensor', [(rank, rank ^ bit) for rank in range(4)])]
    pallas_call x30 -> x28, Pallas kernels: 157 us -> 145 us  [call(): pl.pallas_call(run, grid_spec=pltpu.PrefetchScalarGridSpec(num_scalar_pre...]
    ppermute x20 -> x17, waiting for transfers between devices: 41 us -> 29.1 us  [fsdp_swap(): lax.ppermute(array, 'fsdp', [(rank, rank ^ bit) for rank in range(size)])]
    ppermute x20 -> x17, starting transfers between devices: 30.8 us -> 23.6 us  [fsdp_swap(): lax.ppermute(array, 'fsdp', [(rank, rank ^ bit) for rank in range(size)])]
    unnamed x185 -> x148, local copies, waits for them, and re-layouts: 27.2 us -> 23.1 us
    ppermute x28 -> x27, starting transfers between devices: 15.8 us -> 16.3 us  [tensor_swap(): lax.ppermute(array, 'tensor', [(rank, rank ^ bit) for rank in range(4)])]
  transfers between devices with their start and end apart: 50 -> 46, of which waited for: 16 -> 14; matrix products, arithmetic and copies ran while one was open for 6% -> 7% of each run, Pallas kernels for 40% -> 35%
where the time goes in v4:
time: 313 us; the launch traced here: 310 us
  Pallas kernels  145 us (46%)
  waiting for transfers between devices  62.1 us (20%)
  starting transfers between devices  40.2 us (13%)
  local copies, waits for them, and re-layouts  39.9 us (13%)
  between operations  15.4 us (5%)
  other arithmetic  6.72 us (2%)
    pallas_call x28, Pallas kernels, call(): pl.pallas_call(run, grid_spec=pltpu.PrefetchScalarGridSpec(num_scalar_pre...  145 us
    ppermute x17, waiting for transfers between devices, fsdp_swap(): lax.ppermute(array, 'fsdp', [(rank, rank ^ bit) for rank in range(size)])  29.1 us
    ppermute x27, waiting for transfers between devices, tensor_swap(): lax.ppermute(array, 'tensor', [(rank, rank ^ bit) for rank in range(4)])  28.5 us
    ppermute x17, starting transfers between devices, fsdp_swap(): lax.ppermute(array, 'fsdp', [(rank, rank ^ bit) for rank in range(size)])  23.6 us
    unnamed x148, local copies, waits for them, and re-layouts  23.1 us
    ppermute x27, starting transfers between devices, tensor_swap(): lax.ppermute(array, 'tensor', [(rank, rank ^ bit) for rank in range(4)])  16.3 us
    dynamic_update_slice x8, local copies, waits for them, and re-layouts, gather_positions(): full = lax.dynamic_update_slice_in_dim(full, piece[None], rank ^ bit, 0)  9.81 us
  transfers between devices with their start and end apart: 46, of which 14 were waited for; matrix products, arithmetic and copies ran while one was open for 7% of the time, Pallas kernels for 35%

profile of v4, /device:TPU:0, one launch (start us, length us, event | category | flops | bytes accessed | tf_op | source)
XLA Modules:
  0.0 309.6 jit_solution(5136465731391526673)
XLA Ops:
  7.3 2.5 copy.67
  9.8 2.9 collective-permute-start.1
  14.8 3.1 pack.1
  17.9 1.6 collective-permute-start.6
  19.5 2.6 collective-permute-start.7
  24.5 7.8 %collective-permute-done.7 = bf16[128,512]{1,0:T(8,128)(2,1)S(1)} collective-permute-done((bf16[128,512]{1,0:T(8,128)(2,1)}, bf16[128,512]{1,0:T(8,128)(2,1)S(1)}, u32[]{:S(2)}, u32[]{:S(2)}) %collective-permute-start.7) | collective-permute-done | bytes 131104 | tf_op jit(solution)/shard_map/ppermute | solution.py:819
  33.3 2.0 collective-permute-start.10
  38.2 1.7 bitcast_dynamic-update-slice_fusion.7
  41.4 1.6 collective-permute-start.9
  43.0 6.4 %collective-permute-done.11 = bf16[128,640]{1,0:T(8,128)(2,1)} collective-permute-done((bf16[128,640]{1,0:T(8,128)(2,1)S(1)}, bf16[128,640]{1,0:T(8,128)(2,1)}, u32[]{:S(2)}, u32[]{:S(2)}) %collective-permute-start.11) | collective-permute-done | bytes 163872 | tf_op jit(solution)/shard_map/ppermute | solution.py:819
  50.6 1.7 collective-permute-start.13
  56.4 4.5 %collective-permute-done.9.refs_3_ = bf16[4,128,512]{2,1,0:T(8,128)(2,1)S(1)} collective-permute-done((bf16[4,128,512]{2,1,0:T(8,128)(2,1)S(1)}, bf16[4,128,512]{2,1,0:T(8,128)(2,1)S(1)}, u32[]{:S(2)}, u32[]{:S(2)}) %collective-permute-start.9) | collective-permute-done | bytes 524320 | tf_op jit(solution)/shard_map/ppermute | solution.py:819
  60.9 9.6 %attend_0.1 = (f32[16,1024]{1,0:T(8,128)S(1)}, bf16[1376,1024]{1,0:T(8,128)(2,1)S(1)}, bf16[1376,1024]{1,0:T(8,128)(2,1)S(1)}, bf16[1024,384]{1,0:T(8,128)(2,1)S...) custom-call(s32[4]{0:T(128)S(1)} %copy-done.33, ...), custom_call_target="tpu_custom_call" | custom-call | flops 77552680960 | tf_op jit(solution)/shard_map/attend_0/pallas_call | solution.py:81
  70.5 1.6 copy-done.10
  73.0 2.5 collective-permute-done.13.refs_2_.refs_3_
  77.4 8.6 %attend_1.1 = (bf16[1024,384]{1,0:T(8,128)(2,1)S(1)}, bf16[1376,384]{1,0:T(8,128)(2,1)S(1)}, bf16[1376,128]{1,0:T(8,128)(2,1)S(1)}, bf16[1376,256]{1,0:T(8,128)(2,1)S(1)}, f32[8,128]{1,0:T(8,128)S(1)}) custom-call(s32[4]{0:T(128)S(1)} %copy-done.33, s32[1376,1]{1,0:T(8,128)S(1)} %copy-done.23, bf16[4,128,640]{2,1,0:T(8,128)(2,1)S(1)} %pad_maximum_fusion.refs_1_.refs_2_, ...), custom_call_target="tpu_custom_call" | custom-call | flops 77552680960 | tf_op jit(solution)/shard_map/attend_1/pallas_call | solution.py:81
  88.8 1.5 collective-permute-start.17
  90.8 1.8 copy-done.13
  93.9 1.6 copy-done.5
  98.5 1.5 collective-permute-start.16
  102.4 5.6 %collective-permute-done.16 = bf16[1376,128]{1,0:T(8,128)(2,1)S(1)} collective-permute-done((bf16[1376,128]{1,0:T(8,128)(2,1)S(1)}, bf16[1376,128]{1,0:T(8,128)(2,1)S(1)}, u32[]{:S(2)}, u32[]{:S(2)}) %collective-permute-start.16) | collective-permute-done | bytes 352288 | tf_op jit(solution)/shard_map/ppermute | solution.py:814
  112.7 4.5 %all-gather.2.cloned.1.call-done.refs_15_.refs_16_ = bf16[1024,2048]{1,0:T(8,128)(2,1)} async-done(((bf16[128,2048]{1,0:T(8,128)(2,1)}), bf16[1024,2048]{1,0:T(8,128)(2,1)}) %all-gather.2.cloned.1.call-update) | async-done | bytes 4194320 | tf_op jit(solution)/shard_map/all_gather | solution.py:887
  117.2 27.9 %middle.1 = (bf16[4,344,1024]{2,1,0:T(8,128)(2,1)}, bf16[4,344,1024]{2,1,0:T(8,128)(2,1)}, bf16[4,344,1024]{2,1,0:T(8,128)(2,1)}, bf16[2,344,1024]{2,1,0:T(8,128...) custom-call(s32[4]{0:T(128)} %pad_add_fusion.refs_0_, ...), custom_call_target="tpu_custom_call" | custom-call | flops 14428405760 | tf_op jit(solution)/shard_map/middle/pallas_call | solution.py:81
  145.2 3.4 %collective-permute-done.23.refs_2_ = bf16[2,344,1024]{2,1,0:T(8,128)(2,1)S(1)} collective-permute-done((bf16[2,344,1024]{2,1,0:T(8,128)(2,1)}, bf16[2,344,1024]{2,1,0:T(8,128)(2,1)S(1)}, u32[]{:S(2)}, u32[]{:S(2)}) %collective-permute-start.23) | collective-permute-done | bytes 1409056 | tf_op jit(solution)/shard_map/ppermute | solution.py:814
  153.9 14.1 %matrices.1 = (bf16[1024,2048]{1,0:T(8,128)(2,1)}, f32[8,128]{1,0:T(8,128)}) custom-call(s32[4]{0:T(128)} %pad_add_fusion.refs_0_, bf16[1376,1024]{1,0:T(8,128)(2,1)} %bitcast.84, bf16[1376,1024]{1,0:T(8,128)(2,1)} %bitcast.75, bf16[1376,1024]{1,0:T(8,128)(2,1)} %bitcast.86, bf16[1376,1024]{1,0:T(8,128)(2,1)} %bitcast.85, f32[16,1024]{1,0:T(8,128)} %copy-done.14, ...), custom_call_target="tpu_custom_call" | custom-call | tf_op jit(solution)/shard_map/matrices/pallas_call | solution.py:81
  169.0 1.5 collective-permute-start.25
  170.6 5.0 %residual_back_0.1 = (bf16[344,1024]{1,0:T(8,128)(2,1)}, bf16[344,1024]{1,0:T(8,128)(2,1)}, f32[8,128]{1,0:T(8,128)}) custom-call(s32[4]{0:T(128)} %pad_add_fusion.refs_0_, bf16[344,1024]{1,0:T(8,128)(2,1)} %copy-done.27, bf16[344,1024]{1,0:T(8,128)(2,1)} %copy-done.55, bf16[4,344,1024]{2,1,0:T(8,128)(2,1)} %copy-done.2, ...), custom_call_target="tpu_custom_call" | custom-call | tf_op jit(solution)/shard_map/residual_back_0/pallas_call | solution.py:81
  175.5 11.7 %collective-permute-done.25.refs_2_ = bf16[344,1024]{1,0:T(8,128)(2,1)S(1)} collective-permute-done((bf16[344,1024]{1,0:T(8,128)(2,1)S(1)}, bf16[344,1024]{1,0:T(8,128)(2,1)S(1)}, u32[]{:S(2)}, u32[]{:S(2)}) %collective-permute-start.25) | collective-permute-done | bytes 704544 | tf_op jit(solution)/shard_map/ppermute | solution.py:814
  188.1 5.1 %residual_back_1.1 = (bf16[344,1024]{1,0:T(8,128)(2,1)}, bf16[344,1024]{1,0:T(8,128)(2,1)}, f32[8,128]{1,0:T(8,128)}) custom-call(s32[4]{0:T(128)} %pad_add_fusion.refs_0_, bf16[344,1024]{1,0:T(8,128)(2,1)} %copy-done.26, bf16[344,1024]{1,0:T(8,128)(2,1)} %copy-done.56, bf16[4,344,1024]{2,1,0:T(8,128)(2,1)} %copy-done.2, ...), custom_call_target="tpu_custom_call" | custom-call | tf_op jit(solution)/shard_map/residual_back_1/pallas_call | solution.py:81
  196.8 2.0 concatenate.7.refs_11_.refs_3_
  200.6 1.5 collective-permute-start.27
  203.3 13.1 %attend_back_0.1 = (bf16[1376,384]{1,0:T(8,128)(2,1)S(1)}, f32[8,128]{1,0:T(8,128)S(1)}, f32[8,128]{1,0:T(8,128)}) custom-call(s32[4]{0:T(128)S(1)} %copy-done.35, s32[1376,1]{1,0:T(8,128)S(1)} %copy-done.24, bf16[1376,384]{1,0:T(8,128)(2,1)S(1)} %copy-done.48, bf16[1376,256]{1,0:T(8,128)(2,1)S(1)} %copy-done.52, bf16[1376,128]{1,0:T(8,128)(2,1)S(1)} %copy-done.30, ...), custom_call_target="tpu_custom_call" | custom-call | flops 9694085120 | tf_op jit(solution)/shard_map/attend_back_0/pallas_call | solution.py:81
  216.5 2.7 in_grad_0.1
  219.9 3.1 own_block.1
  223.0 3.6 %out_grad.1 = (bf16[4,128,256]{2,1,0:T(8,128)(2,1)S(1)}, bf16[4,128,256]{2,1,0:T(8,128)(2,1)S(1)}, f32[8,128]{1,0:T(8,128)S(1)}) custom-call(s32[4]{0:T(128)S(1)} %copy-done.35, bf16[4,344,128]{2,1,0:T(8,128)(2,1)S(1)} %bitcast.81, bf16[4,344,128]{2,1,0:T(8,128)(2,1)S(1)} %bitcast.83, bf16[344,1024]{1,0:T(8,128)(2,1)} %get-tuple-element.170.refs_5_.refs_3_, ...), custom_call_target="tpu_custom_call" | custom-call | tf_op jit(solution)/shard_map/out_grad/pallas_call | solution.py:81
  226.6 1.5 collective-permute-start.31
  228.2 13.2 %attend_back_1.1 = (bf16[1376,384]{1,0:T(8,128)(2,1)S(1)}, f32[8,128]{1,0:T(8,128)S(1)}, f32[8,128]{1,0:T(8,128)S(1)}) custom-call(s32[4]{0:T(128)S(1)} %copy-done.35, s32[1376,1]{1,0:T(8,128)S(1)} %copy-done.24, bf16[1376,384]{1,0:T(8,128)(2,1)S(1)} %copy-done.46, bf16[1376,256]{1,0:T(8,128)(2,1)S(1)} %copy-done.50, bf16[1376,128]{1,0:T(8,128)(2,1)S(1)} %copy-done.32, ...), custom_call_target="tpu_custom_call" | custom-call | flops 9694085120 | tf_op jit(solution)/shard_map/attend_back_1/pallas_call | solution.py:81
  242.1 5.6 %input_back.1 = (bf16[2,344,1024]{2,1,0:T(8,128)(2,1)S(1)}, bf16[2,344,1024]{2,1,0:T(8,128)(2,1)S(1)}, f32[8,1024]{1,0:T(8,128)S(1)}, f32[8,128]{1,0:T(8,128)}) custom-call(s32[4]{0:T(128)S(1)} %copy-done.35, bf16[4,344,1024]{2,1,0:T(8,128)(2,1)S(1)} %bitcast.79, bf16[4,344,384]{2,1,0:T(8,128)(2,1)S(1)} %bitcast.77, bf16[4,344,384]{2,1,0:T(8,128)(2,1)S(1)} %bitcast.78, ...), custom_call_target="tpu_custom_call" | custom-call | tf_op jit(solution)/shard_map/input_back/pallas_call | solution.py:81
  247.7 2.5 in_grad_1.1
  256.0 2.2 collective-permute-start.37
  258.2 7.0 %collective-permute-done.34.refs_2_ = bf16[4,144,384]{2,1,0:T(8,128)(2,1)S(1)} collective-permute-done((bf16[4,144,384]{2,1,0:T(8,128)(2,1)S(1)}, bf16[4,144,384]{2,1,0:T(8,128)(2,1)S(1)}, u32[]{:S(2)}, u32[]{:S(2)}) %collective-permute-start.34) | collective-permute-done | bytes 442400 | tf_op jit(solution)/shard_map/ppermute | solution.py:819
  265.2 5.4 %collective-permute-done.33.refs_2_ = bf16[344,1024]{1,0:T(8,128)(2,1)S(1)} collective-permute-done((bf16[344,1024]{1,0:T(8,128)(2,1)S(1)}, bf16[344,1024]{1,0:T(8,128)(2,1)S(1)}, u32[]{:S(2)}, u32[]{:S(2)}) %collective-permute-start.33) | collective-permute-done | bytes 704544 | tf_op jit(solution)/shard_map/ppermute | solution.py:814
  274.0 2.3 collective-permute-start.40
  276.3 5.2 %input_grad.1 = (f32[344,1,1024]{2,1,0:T(1,128)}, f32[8,128]{1,0:T(8,128)}) custom-call(s32[4]{0:T(128)} %pad_add_fusion.refs_0_, bf16[344,1024]{1,0:T(8,128)(2,1)} %copy-done.22, bf16[344,1024]{1,0:T(8,128)(2,1)} %copy-done.54, bf16[4,344,1024]{2,1,0:T(8,128)(2,1)} %copy-done.2, bf16[344,1024]{1,0:T(8,128)(2,1)} %get-tuple-element.157.refs_4_, ...), custom_call_target="tpu_custom_call" | custom-call | tf_op jit(solution)/shard_map/input_grad/pallas_call | solution.py:81
  284.1 2.7 adam_out.1
  287.0 4.0 %adam_expand.1 = (f32[128,1024]{1,0:T(8,128)}, f32[128,1024]{1,0:T(8,128)}, f32[128,1024]{1,0:T(8,128)}, f32[128,1024]{1,0:T(8,128)}, f32[8,128]{1,0:T(8,128)}) custom-call(s32[4]{0:T(128)} %pad_add_fusion.refs_0_, bf16[128,2048]{1,0:T(8,128)(2,1)} %reduce-scatter.2.cloned.1.call-done.refs_1_, f32[128,1024]{1,0:T(8,128)} %refs_2_.6, f32[128,1024]{1,0:T(8,128)} %refs_3_.6, ...), custom_call_target="tpu_custom_call" | custom-call | tf_op jit(solution)/shard_map/adam_expand/pallas_call | solution.py:81
  291.0 4.0 %adam_contract.1 = (f32[1024,128]{1,0:T(8,128)}, f32[1024,128]{1,0:T(8,128)}, f32[1024,128]{1,0:T(8,128)}, f32[1024,128]{1,0:T(8,128)}, f32[8,128]{1,0:T(8,128)}) custom-call(s32[4]{0:T(128)} %pad_add_fusion.refs_0_, bf16[128,2048]{1,0:T(8,128)(2,1)} %reduce-scatter.2.cloned.1.call-done.refs_1_, f32[1024,128]{1,0:T(8,128)} %refs_2_.7, f32[1024,128]{1,0:T(8,128)} %refs_3_.7, ...), custom_call_target="tpu_custom_call" | custom-call | tf_op jit(solution)/shard_map/adam_contract/pallas_call | solution.py:81
  296.8 3.6 %adam_in.1 = (f32[3,128,256]{2,1,0:T(8,128)}, f32[3,128,256]{2,1,0:T(8,128)}, f32[3,128,256]{2,1,0:T(8,128)}, f32[3,128,256]{2,1,0:T(8,128)}, f32[8,128]{1,0:T(8,128)}) custom-call(s32[4]{0:T(128)} %pad_add_fusion.refs_0_, f32[128,640]{1,0:T(8,128)} %copy-done.17, bf16[144,384]{1,0:T(8,128)(2,1)} %copy-done.38, bf16[144,384]{1,0:T(8,128)(2,1)} %copy-done.58, ...), custom_call_target="tpu_custom_call" | custom-call | tf_op jit(solution)/shard_map/adam_in/pallas_call | solution.py:81
  (254 shorter events, 63.2 us)
Async XLA Ops:
  7.2 109.9 %all-gather.2.cloned.1.call-start = ((), (), s32[]{:S(2)}) async-start(), calls=%async_computation.1 | async-start | bytes 4718592 | tf_op jit(solution)/shard_map/all_gather | solution.py:887
  9.8 28.0 %collective-permute-start.1 = (bf16[344,1024]{1,0:T(8,128)(2,1)}, bf16[344,1024]{1,0:T(8,128)(2,1)}, u32[]{:S(2)}, u32[]{:S(2)}) collective-permute-start(bf16[344,1024]{1,0:T(8,128)(2,1)} %bitcast.74), channel_id=1, source_target_pairs={{0,2},{1,3},{2,0},{3,1},{4,6},{5,7},{6,4},{7,5},{8,10},{9,11},{10,... | collective-permute-start | bytes 2113544 | tf_op jit(solution)/shard_map/ppermute | solution.py:814
  17.9 6.6 %collective-permute-start.6 = (bf16[128,512]{1,0:T(8,128)(2,1)}, bf16[128,512]{1,0:T(8,128)(2,1)S(1)}, u32[]{:S(2)}, u32[]{:S(2)}) collective-permute-start(bf16[128,512]{1,0:T(8,128)(2,1)} %get-tuple-element.134), channel_id=1, source_target_pairs={{0,8},{4,12},{8,0},{12,4},{16,24},{20,28},{24,16},{28,20},{1,9},{5... | collective-permute-start | bytes 393224 | tf_op jit(solution)/shard_map/ppermute | solution.py:819
  19.5 12.9 %collective-permute-start.7 = (bf16[128,512]{1,0:T(8,128)(2,1)}, bf16[128,512]{1,0:T(8,128)(2,1)S(1)}, u32[]{:S(2)}, u32[]{:S(2)}) collective-permute-start(bf16[128,512]{1,0:T(8,128)(2,1)} %get-tuple-element.134), channel_id=1, source_target_pairs={{0,16},{4,20},{8,24},{12,28},{16,0},{20,4},{24,8},{28,12},{1,17},{... | collective-permute-start | bytes 393224 | tf_op jit(solution)/shard_map/ppermute | solution.py:819
  22.1 10.3 %collective-permute-start.8 = (bf16[128,512]{1,0:T(8,128)(2,1)}, bf16[128,512]{1,0:T(8,128)(2,1)S(1)}, u32[]{:S(2)}, u32[]{:S(2)}) collective-permute-start(bf16[128,512]{1,0:T(8,128)(2,1)} %get-tuple-element.134), channel_id=1, source_target_pairs={{0,24},{4,28},{8,16},{12,20},{16,8},{20,12},{24,0},{28,4},{1,25},{... | collective-permute-start | bytes 393224 | tf_op jit(solution)/shard_map/ppermute | solution.py:819
  22.3 30.0 %collective-permute-start = (bf16[344,1024]{1,0:T(8,128)(2,1)}, bf16[344,1024]{1,0:T(8,128)(2,1)}, u32[]{:S(2)}, u32[]{:S(2)}) collective-permute-start(bf16[344,1024]{1,0:T(8,128)(2,1)} %bitcast.74), channel_id=1, source_target_pairs={{0,1},{1,0},{2,3},{3,2},{4,5},{5,4},{6,7},{7,6},{8,9},{9,8},{10,11... | collective-permute-start | bytes 2113544 | tf_op jit(solution)/shard_map/ppermute | solution.py:814
  33.3 8.1 %collective-permute-start.10 = (bf16[128,640]{1,0:T(8,128)(2,1)S(1)}, bf16[128,640]{1,0:T(8,128)(2,1)}, u32[]{:S(2)}, u32[]{:S(2)}) collective-permute-start(bf16[128,640]{1,0:T(8,128)(2,1)S(1)} %copy-done.57), channel_id=1, source_target_pairs={{0,8},{4,12},{8,0},{12,4},{16,24},{20,28},{24,16},{28,20},{1,9},{5... | collective-permute-start | bytes 491528 | tf_op jit(solution)/shard_map/ppermute | solution.py:819
  35.4 14.0 %collective-permute-start.11 = (bf16[128,640]{1,0:T(8,128)(2,1)S(1)}, bf16[128,640]{1,0:T(8,128)(2,1)}, u32[]{:S(2)}, u32[]{:S(2)}) collective-permute-start(bf16[128,640]{1,0:T(8,128)(2,1)S(1)} %copy-done.57), channel_id=1, source_target_pairs={{0,16},{4,20},{8,24},{12,28},{16,0},{20,4},{24,8},{28,12},{1,17},{... | collective-permute-start | bytes 491528 | tf_op jit(solution)/shard_map/ppermute | solution.py:819
  36.4 12.9 %collective-permute-start.12 = (bf16[128,640]{1,0:T(8,128)(2,1)S(1)}, bf16[128,640]{1,0:T(8,128)(2,1)}, u32[]{:S(2)}, u32[]{:S(2)}) collective-permute-start(bf16[128,640]{1,0:T(8,128)(2,1)S(1)} %copy-done.57), channel_id=1, source_target_pairs={{0,24},{4,28},{8,16},{12,20},{16,8},{20,12},{24,0},{28,4},{1,25},{... | collective-permute-start | bytes 491528 | tf_op jit(solution)/shard_map/ppermute | solution.py:819
  37.8 16.7 %collective-permute-start.2 = (bf16[344,1024]{1,0:T(8,128)(2,1)}, bf16[344,1024]{1,0:T(8,128)(2,1)}, u32[]{:S(2)}, u32[]{:S(2)}) collective-permute-start(bf16[344,1024]{1,0:T(8,128)(2,1)} %collective-permute-done.1), channel_id=1, source_target_pairs={{0,1},{1,0},{2,3},{3,2},{4,5},{5,4},{6,7},{7,6},{8,9},{9,8},{10,11... | collective-permute-start | bytes 2113544 | tf_op jit(solution)/shard_map/ppermute | solution.py:814
  41.1 19.8 %copy-start.33 = (s32[4]{0:T(128)S(1)}, s32[4]{0:T(128)}, u32[]{:S(2)}) copy-start(s32[4]{0:T(128)} %pad_add_fusion.refs_0_) | copy-start | bytes 52
  41.1 245.8 %reduce-scatter.2.cloned.1.call-start = ((), (), s32[]{:S(2)}) async-start(), calls=%async_computation.2 | async-start | bytes 4718592 | tf_op jit(solution)/shard_map/reduce_scatter | solution.py:935
  41.4 19.5 %collective-permute-start.9 = (bf16[4,128,512]{2,1,0:T(8,128)(2,1)S(1)}, bf16[4,128,512]{2,1,0:T(8,128)(2,1)S(1)}, u32[]{:S(2)}, u32[]{:S(2)}) collective-permute-start(bf16[4,128,512]{2,1,0:T(8,128)(2,1)S(1)} %pad_maximum_fusion.1.refs_2_), channel_id=1, source_target_pairs={{0,4},{4,0},{8,12},{12,8},{16,20},{20,16},{24,28},{28,24},{1,5},{5... | collective-permute-start | bytes 1572872 | tf_op jit(solution)/shard_map/ppermute | solution.py:819
  50.6 24.9 %collective-permute-start.13 = (bf16[4,128,640]{2,1,0:T(8,128)(2,1)S(1)}, bf16[4,128,640]{2,1,0:T(8,128)(2,1)S(1)}, u32[]{:S(2)}, u32[]{:S(2)}) collective-permute-start(bf16[4,128,640]{2,1,0:T(8,128)(2,1)S(1)} %pad_maximum_fusion.refs_1_.refs_2_), channel_id=1, source_target_pairs={{0,4},{4,0},{8,12},{12,8},{16,20},{20,16},{24,28},{28,24},{1,5},{5... | collective-permute-start | bytes 1966088 | tf_op jit(solution)/shard_map/ppermute | solution.py:819
  55.7 44.8 %collective-permute-start.3 = (bf16[344,1024]{1,0:T(8,128)(2,1)}, bf16[344,1024]{1,0:T(8,128)(2,1)}, u32[]{:S(2)}, u32[]{:S(2)}) collective-permute-start(bf16[344,1024]{1,0:T(8,128)(2,1)} %fusion), channel_id=1, source_target_pairs={{0,1},{1,0},{2,3},{3,2},{4,5},{5,4},{6,7},{7,6},{8,9},{9,8},{10,11... | collective-permute-start | bytes 2113544 | tf_op jit(solution)/shard_map/ppermute | solution.py:814
  55.8 34.4 %collective-permute-start.4 = (bf16[344,1024]{1,0:T(8,128)(2,1)}, bf16[344,1024]{1,0:T(8,128)(2,1)}, u32[]{:S(2)}, u32[]{:S(2)}) collective-permute-start(bf16[344,1024]{1,0:T(8,128)(2,1)} %fusion), channel_id=1, source_target_pairs={{0,2},{1,3},{2,0},{3,1},{4,6},{5,7},{6,4},{7,5},{8,10},{9,11},{10,... | collective-permute-start | bytes 2113544 | tf_op jit(solution)/shard_map/ppermute | solution.py:814
  76.9 23.7 %collective-permute-start.21 = (bf16[1024,256]{1,0:T(8,128)(2,1)}, bf16[1024,256]{1,0:T(8,128)(2,1)}, u32[]{:S(2)}, u32[]{:S(2)}) collective-permute-start(bf16[1024,256]{1,0:T(8,128)(2,1)} %get-tuple-element.143.refs_10_.refs_9_), channel_id=1, source_target_pairs={{0,2},{1,3},{2,0},{3,1},{4,6},{5,7},{6,4},{7,5},{8,10},{9,11},{10,... | collective-permute-start | bytes 1572872 | tf_op jit(solution)/shard_map/ppermute | solution.py:814
  88.8 9.7 %collective-permute-start.17 = (bf16[1376,128]{1,0:T(8,128)(2,1)S(1)}, bf16[1376,128]{1,0:T(8,128)(2,1)}, u32[]{:S(2)}, u32[]{:S(2)}) collective-permute-start(bf16[1376,128]{1,0:T(8,128)(2,1)S(1)} %get-tuple-element.142.refs_4_), channel_id=1, source_target_pairs={{0,2},{1,3},{2,0},{3,1},{4,6},{5,7},{6,4},{7,5},{8,10},{9,11},{10,... | collective-permute-start | bytes 1056776 | tf_op jit(solution)/shard_map/ppermute | solution.py:814
  90.3 17.7 %collective-permute-start.5 = (bf16[344,1024]{1,0:T(8,128)(2,1)}, bf16[344,1024]{1,0:T(8,128)(2,1)}, u32[]{:S(2)}, u32[]{:S(2)}) collective-permute-start(bf16[344,1024]{1,0:T(8,128)(2,1)} %collective-permute-done.4), channel_id=1, source_target_pairs={{0,1},{1,0},{2,3},{3,2},{4,5},{5,4},{6,7},{7,6},{8,9},{9,8},{10,11... | collective-permute-start | bytes 2113544 | tf_op jit(solution)/shard_map/ppermute | solution.py:814
  90.3 12.0 %collective-permute-start.15 = (bf16[1376,128]{1,0:T(8,128)(2,1)S(1)}, bf16[1376,128]{1,0:T(8,128)(2,1)S(1)}, u32[]{:S(2)}, u32[]{:S(2)}) collective-permute-start(bf16[1376,128]{1,0:T(8,128)(2,1)S(1)} %get-tuple-element.142.refs_4_), channel_id=1, source_target_pairs={{0,1},{1,0},{2,3},{3,2},{4,5},{5,4},{6,7},{7,6},{8,9},{9,8},{10,11... | collective-permute-start | bytes 1056776 | tf_op jit(solution)/shard_map/ppermute | solution.py:814
  98.5 9.5 %collective-permute-start.16 = (bf16[1376,128]{1,0:T(8,128)(2,1)S(1)}, bf16[1376,128]{1,0:T(8,128)(2,1)S(1)}, u32[]{:S(2)}, u32[]{:S(2)}) collective-permute-start(bf16[1376,128]{1,0:T(8,128)(2,1)S(1)} %copy-done.29), channel_id=1, source_target_pairs={{0,2},{1,3},{2,0},{3,1},{4,6},{5,7},{6,4},{7,5},{8,10},{9,11},{10,... | collective-permute-start | bytes 1056776 | tf_op jit(solution)/shard_map/ppermute | solution.py:814
  100.6 10.3 %collective-permute-start.20 = (bf16[1024,256]{1,0:T(8,128)(2,1)}, bf16[1024,256]{1,0:T(8,128)(2,1)}, u32[]{:S(2)}, u32[]{:S(2)}) collective-permute-start(bf16[1024,256]{1,0:T(8,128)(2,1)} %get-tuple-element.143.refs_10_.refs_9_), channel_id=1, source_target_pairs={{0,1},{1,0},{2,3},{3,2},{4,5},{5,4},{6,7},{7,6},{8,9},{9,8},{10,11... | collective-permute-start | bytes 1572872 | tf_op jit(solution)/shard_map/ppermute | solution.py:814
  100.6 12.1 %collective-permute-start.22 = (bf16[1024,256]{1,0:T(8,128)(2,1)}, bf16[1024,256]{1,0:T(8,128)(2,1)}, u32[]{:S(2)}, u32[]{:S(2)}) collective-permute-start(bf16[1024,256]{1,0:T(8,128)(2,1)} %collective-permute-done.21.refs_12_), channel_id=1, source_target_pairs={{0,1},{1,0},{2,3},{3,2},{4,5},{5,4},{6,7},{7,6},{8,9},{9,8},{10,11... | collective-permute-start | bytes 1572872 | tf_op jit(solution)/shard_map/ppermute | solution.py:814
  102.2 8.5 %collective-permute-start.14 = (bf16[1376,128]{1,0:T(8,128)(2,1)S(1)}, bf16[1376,128]{1,0:T(8,128)(2,1)S(1)}, u32[]{:S(2)}, u32[]{:S(2)}) collective-permute-start(bf16[1376,128]{1,0:T(8,128)(2,1)S(1)} %copy-done.29), channel_id=1, source_target_pairs={{0,1},{1,0},{2,3},{3,2},{4,5},{5,4},{6,7},{7,6},{8,9},{9,8},{10,11... | collective-permute-start | bytes 1056776 | tf_op jit(solution)/shard_map/ppermute | solution.py:814
  107.9 2.9 collective-permute-start.19
  108.0 2.9 collective-permute-start.18
  117.2 31.4 %copy-start.34 = (s32[4]{0:T(128)S(1)}, s32[4]{0:T(128)}, u32[]{:S(2)}) copy-start(s32[4]{0:T(128)} %pad_add_fusion.refs_0_) | copy-start | bytes 52
  145.1 3.5 %collective-permute-start.23 = (bf16[2,344,1024]{2,1,0:T(8,128)(2,1)}, bf16[2,344,1024]{2,1,0:T(8,128)(2,1)S(1)}, u32[]{:S(2)}, u32[]{:S(2)}) collective-permute-start(bf16[2,344,1024]{2,1,0:T(8,128)(2,1)} %get-tuple-element.150), channel_id=1, source_target_pairs={{0,1},{1,0},{2,3},{3,2},{4,5},{5,4},{6,7},{7,6},{8,9},{9,8},{10,11... | collective-permute-start | bytes 4227080 | tf_op jit(solution)/shard_map/ppermute | solution.py:814
  151.1 17.8 %collective-permute-start.24 = (bf16[344,1024]{1,0:T(8,128)(2,1)S(1)}, bf16[344,1024]{1,0:T(8,128)(2,1)S(1)}, u32[]{:S(2)}, u32[]{:S(2)}) collective-permute-start(bf16[344,1024]{1,0:T(8,128)(2,1)S(1)} %get-tuple-element.151.refs_1_), channel_id=1, source_target_pairs={{0,2},{1,3},{2,0},{3,1},{4,6},{5,7},{6,4},{7,5},{8,10},{9,11},{10,... | collective-permute-start | bytes 2113544 | tf_op jit(solution)/shard_map/ppermute | solution.py:814
  168.9 29.9 %collective-permute-start.26 = (bf16[2,344,1024]{2,1,0:T(8,128)(2,1)}, bf16[2,344,1024]{2,1,0:T(8,128)(2,1)S(1)}, u32[]{:S(2)}, u32[]{:S(2)}) collective-permute-start(bf16[2,344,1024]{2,1,0:T(8,128)(2,1)} %get-tuple-element.163), channel_id=1, source_target_pairs={{0,1},{1,0},{2,3},{3,2},{4,5},{5,4},{6,7},{7,6},{8,9},{9,8},{10,11... | collective-permute-start | bytes 4227080 | tf_op jit(solution)/shard_map/ppermute | solution.py:814
  169.0 18.2 %collective-permute-start.25 = (bf16[344,1024]{1,0:T(8,128)(2,1)S(1)}, bf16[344,1024]{1,0:T(8,128)(2,1)S(1)}, u32[]{:S(2)}, u32[]{:S(2)}) collective-permute-start(bf16[344,1024]{1,0:T(8,128)(2,1)S(1)} %get-tuple-element.158.refs_1_), channel_id=1, source_target_pairs={{0,2},{1,3},{2,0},{3,1},{4,6},{5,7},{6,4},{7,5},{8,10},{9,11},{10,... | collective-permute-start | bytes 2113544 | tf_op jit(solution)/shard_map/ppermute | solution.py:814
  193.2 9.0 %collective-permute-start.29 = (bf16[344,1024]{1,0:T(8,128)(2,1)}, bf16[344,1024]{1,0:T(8,128)(2,1)}, u32[]{:S(2)}, u32[]{:S(2)}) collective-permute-start(bf16[344,1024]{1,0:T(8,128)(2,1)} %get-tuple-element.171.refs_7_.refs_5_), channel_id=1, source_target_pairs={{0,1},{1,0},{2,3},{3,2},{4,5},{5,4},{6,7},{7,6},{8,9},{9,8},{10,11... | collective-permute-start | bytes 2113544 | tf_op jit(solution)/shard_map/ppermute | solution.py:814
  193.2 9.0 %collective-permute-start.28 = (bf16[344,1024]{1,0:T(8,128)(2,1)}, bf16[344,1024]{1,0:T(8,128)(2,1)}, u32[]{:S(2)}, u32[]{:S(2)}) collective-permute-start(bf16[344,1024]{1,0:T(8,128)(2,1)} %get-tuple-element.170.refs_5_.refs_3_), channel_id=1, source_target_pairs={{0,1},{1,0},{2,3},{3,2},{4,5},{5,4},{6,7},{7,6},{8,9},{9,8},{10,11... | collective-permute-start | bytes 2113544 | tf_op jit(solution)/shard_map/ppermute | solution.py:814
  200.6 19.2 %collective-permute-start.27 = (bf16[344,1024]{1,0:T(8,128)(2,1)S(1)}, bf16[344,1024]{1,0:T(8,128)(2,1)S(1)}, u32[]{:S(2)}, u32[]{:S(2)}) collective-permute-start(bf16[344,1024]{1,0:T(8,128)(2,1)S(1)} %get-tuple-element.166), channel_id=1, source_target_pairs={{0,2},{1,3},{2,0},{3,1},{4,6},{5,7},{6,4},{7,5},{8,10},{9,11},{10,... | collective-permute-start | bytes 2113544 | tf_op jit(solution)/shard_map/ppermute | solution.py:814
  219.2 22.2 %collective-permute-start.30 = (bf16[4,128,384]{2,1,0:T(8,128)(2,1)S(1)}, bf16[4,128,384]{2,1,0:T(8,128)(2,1)S(1)}, u32[]{:S(2)}, u32[]{:S(2)}) collective-permute-start(bf16[4,128,384]{2,1,0:T(8,128)(2,1)S(1)} %get-tuple-element.186), channel_id=1, source_target_pairs={{0,4},{4,0},{8,12},{12,8},{16,20},{20,16},{24,28},{28,24},{1,5},{5... | collective-permute-start | bytes 1179656 | tf_op jit(solution)/shard_map/ppermute | solution.py:819
  226.6 14.8 %collective-permute-start.31 = (bf16[4,128,256]{2,1,0:T(8,128)(2,1)S(1)}, bf16[4,128,256]{2,1,0:T(8,128)(2,1)S(1)}, u32[]{:S(2)}, u32[]{:S(2)}) collective-permute-start(bf16[4,128,256]{2,1,0:T(8,128)(2,1)S(1)} %get-tuple-element.188), channel_id=1, source_target_pairs={{0,4},{4,0},{8,12},{12,8},{16,20},{20,16},{24,28},{28,24},{1,5},{5... | collective-permute-start | bytes 786440 | tf_op jit(solution)/shard_map/ppermute | solution.py:819
  247.7 3.2 %collective-permute-start.32 = (bf16[2,344,1024]{2,1,0:T(8,128)(2,1)S(1)}, bf16[2,344,1024]{2,1,0:T(8,128)(2,1)S(1)}, u32[]{:S(2)}, u32[]{:S(2)}) collective-permute-start(bf16[2,344,1024]{2,1,0:T(8,128)(2,1)S(1)} %get-tuple-element.192), channel_id=1, source_target_pairs={{0,1},{1,0},{2,3},{3,2},{4,5},{5,4},{6,7},{7,6},{8,9},{9,8},{10,11... | collective-permute-start | bytes 4227080 | tf_op jit(solution)/shard_map/ppermute | solution.py:814
  252.8 17.8 %collective-permute-start.33 = (bf16[344,1024]{1,0:T(8,128)(2,1)S(1)}, bf16[344,1024]{1,0:T(8,128)(2,1)S(1)}, u32[]{:S(2)}, u32[]{:S(2)}) collective-permute-start(bf16[344,1024]{1,0:T(8,128)(2,1)S(1)} %get-tuple-element.199), channel_id=1, source_target_pairs={{0,2},{1,3},{2,0},{3,1},{4,6},{5,7},{6,4},{7,5},{8,10},{9,11},{10,... | collective-permute-start | bytes 2113544 | tf_op jit(solution)/shard_map/ppermute | solution.py:814
  253.3 11.9 %collective-permute-start.34 = (bf16[4,144,384]{2,1,0:T(8,128)(2,1)S(1)}, bf16[4,144,384]{2,1,0:T(8,128)(2,1)S(1)}, u32[]{:S(2)}, u32[]{:S(2)}) collective-permute-start(bf16[4,144,384]{2,1,0:T(8,128)(2,1)S(1)} %get-tuple-element.201), channel_id=1, source_target_pairs={{0,4},{4,0},{8,12},{12,8},{16,20},{20,16},{24,28},{28,24},{1,5},{5... | collective-permute-start | bytes 1327112 | tf_op jit(solution)/shard_map/ppermute | solution.py:819
  253.8 20.1 %collective-permute-start.35 = (bf16[128,640]{1,0:T(8,128)(2,1)S(1)}, bf16[128,640]{1,0:T(8,128)(2,1)S(1)}, u32[]{:S(2)}, u32[]{:S(2)}) collective-permute-start(bf16[128,640]{1,0:T(8,128)(2,1)S(1)} %get-tuple-element.207), channel_id=1, source_target_pairs={{0,8},{4,12},{8,0},{12,4},{16,24},{20,28},{24,16},{28,20},{1,9},{5... | collective-permute-start | bytes 491528 | tf_op jit(solution)/shard_map/ppermute | solution.py:819
  254.7 26.7 %collective-permute-start.36 = (bf16[128,640]{1,0:T(8,128)(2,1)S(1)}, bf16[128,640]{1,0:T(8,128)(2,1)S(1)}, u32[]{:S(2)}, u32[]{:S(2)}) collective-permute-start(bf16[128,640]{1,0:T(8,128)(2,1)S(1)} %get-tuple-element.208), channel_id=1, source_target_pairs={{0,16},{4,20},{8,24},{12,28},{16,0},{20,4},{24,8},{28,12},{1,17},{... | collective-permute-start | bytes 491528 | tf_op jit(solution)/shard_map/ppermute | solution.py:819
  256.0 25.4 %collective-permute-start.37 = (bf16[128,640]{1,0:T(8,128)(2,1)S(1)}, bf16[128,640]{1,0:T(8,128)(2,1)S(1)}, u32[]{:S(2)}, u32[]{:S(2)}) collective-permute-start(bf16[128,640]{1,0:T(8,128)(2,1)S(1)} %get-tuple-element.209), channel_id=1, source_target_pairs={{0,24},{4,28},{8,16},{12,20},{16,8},{20,12},{24,0},{28,4},{1,25},{... | collective-permute-start | bytes 491528 | tf_op jit(solution)/shard_map/ppermute | solution.py:819
  271.9 14.9 %collective-permute-start.38 = (bf16[144,384]{1,0:T(8,128)(2,1)S(1)}, bf16[144,384]{1,0:T(8,128)(2,1)S(1)}, u32[]{:S(2)}, u32[]{:S(2)}) collective-permute-start(bf16[144,384]{1,0:T(8,128)(2,1)S(1)} %get-tuple-element.213), channel_id=1, source_target_pairs={{0,8},{4,12},{8,0},{12,4},{16,24},{20,28},{24,16},{28,20},{1,9},{5... | collective-permute-start | bytes 331784 | tf_op jit(solution)/shard_map/ppermute | solution.py:819
  272.7 14.2 %collective-permute-start.39 = (bf16[144,384]{1,0:T(8,128)(2,1)S(1)}, bf16[144,384]{1,0:T(8,128)(2,1)S(1)}, u32[]{:S(2)}, u32[]{:S(2)}) collective-permute-start(bf16[144,384]{1,0:T(8,128)(2,1)S(1)} %get-tuple-element.214), channel_id=1, source_target_pairs={{0,16},{4,20},{8,24},{12,28},{16,0},{20,4},{24,8},{28,12},{1,17},{... | collective-permute-start | bytes 331784 | tf_op jit(solution)/shard_map/ppermute | solution.py:819
  274.0 12.9 %collective-permute-start.40 = (bf16[144,384]{1,0:T(8,128)(2,1)S(1)}, bf16[144,384]{1,0:T(8,128)(2,1)S(1)}, u32[]{:S(2)}, u32[]{:S(2)}) collective-permute-start(bf16[144,384]{1,0:T(8,128)(2,1)S(1)} %get-tuple-element.215), channel_id=1, source_target_pairs={{0,24},{4,28},{8,16},{12,20},{16,8},{20,12},{24,0},{28,4},{1,25},{... | collective-permute-start | bytes 331784 | tf_op jit(solution)/shard_map/ppermute | solution.py:819
  295.0 5.5 %collective-permute-start.41 = (f32[16,128]{1,0:T(8,128)S(1)}, f32[16,128]{1,0:T(8,128)S(1)}, u32[]{:S(2)}, u32[]{:S(2)}) collective-permute-start(f32[16,128]{1,0:T(8,128)S(1)} %convert_add_fusion), channel_id=1, source_target_pairs={{0,1},{1,0},{2,3},{3,2},{4,5},{5,4},{6,7},{7,6},{8,9},{9,8},{10,11... | collective-permute-start | bytes 24584 | tf_op jit(solution)/shard_map/ppermute | solution.py:814
  295.0 5.5 %collective-permute-start.42 = (f32[16,128]{1,0:T(8,128)S(1)}, f32[16,128]{1,0:T(8,128)S(1)}, u32[]{:S(2)}, u32[]{:S(2)}) collective-permute-start(f32[16,128]{1,0:T(8,128)S(1)} %convert_add_fusion), channel_id=1, source_target_pairs={{0,2},{1,3},{2,0},{3,1},{4,6},{5,7},{6,4},{7,5},{8,10},{9,11},{10,... | collective-permute-start | bytes 24584 | tf_op jit(solution)/shard_map/ppermute | solution.py:814
  295.5 5.0 %collective-permute-start.43 = (f32[16,128]{1,0:T(8,128)S(1)}, f32[16,128]{1,0:T(8,128)S(1)}, u32[]{:S(2)}, u32[]{:S(2)}) collective-permute-start(f32[16,128]{1,0:T(8,128)S(1)} %convert_add_fusion), channel_id=1, source_target_pairs={{0,3},{1,2},{2,1},{3,0},{4,7},{5,6},{6,5},{7,4},{8,11},{9,10},{10,... | collective-permute-start | bytes 24584 | tf_op jit(solution)/shard_map/ppermute | solution.py:814
  (71 other events, 558.9 us)
Sparse Core Ops, SparseCore 0:
  41.2 75.8 all-gather.1
  169.0 97.2 reduce-scatter.1

commit v5 on v4

--- a/solution.py
+++ b/solution.py
@@ -20,7 +20,7 @@
 DENSITY_NORM = 0.3989422804014327
 SCORE_SCALE = HEAD_DIM ** (-0.5)
 LANES = 128
-TILE = 512
+TILE = 352
 CHUNK = 256
 LONG = 4
 SMALL = 16
@@ -357,7 +357,7 @@
         outs,
         [whole(o) for o in outs],
         f"attend_back_{pair}",
-        cost=(80 * seq * seq * HEAD_DIM, 0, 0),
+        cost=((1 - pair) * 80 * seq * seq * HEAD_DIM, 0, 0),
         vmem=LARGE,
         scratch=[
             pltpu.VMEM((seq, LANES), F32),
@@ -736,7 +736,6 @@
         [whole(o) for o in outs],
         "input_grad",
         after=after,
-        vmem=ALL,
     )[0]
 
 
@@ -769,7 +768,6 @@
         outs,
         name,
         after=after,
-        vmem=ALL,
     )
 
 
@@ -922,8 +920,23 @@
     grad_second = matrices(
         ids, normed_two, grad_hidden, top_full, activated, rows_now, done("back_sum_1")
     )
+    lay = lambda values, start, total: lax.dynamic_update_slice_in_dim(
+        jnp.zeros((total,), F32), values, start, 0
+    )
+    grad_bias = lay(sums[0], rank * hidden_width, expand_bias.shape[0] * places)
+    grad_bias = grad_bias.reshape(places, -1, shard).transpose(1, 0, 2).reshape(-1, features)
+    none = jnp.zeros((6, features), F32)
+    small = jnp.concatenate([none, sums[1:3], none[:2], grad_bias, none[: 16 - small_rows]])
+
+    branch_arrived = tensor_swap(behind(branch_give, chips[1]), 1)
     for half in range(2):
-        wait = done("residual_back_0" if half == 1 else "matrices")
+        wait = done("matrices")
+        if half == 1:
+            give, branch_stay = split_sum(
+                ids, branch_keep, branch_arrived, "branch_sum", done("residual_back_0")
+            )
+            branch_arrived = tensor_swap(give, 2)
+            wait = done("branch_sum") + (small,)
         grads.append(
             residual_back(
                 half, ids, chips[half], arrived[half], x_full, attn, top_full, rows_now, wait
@@ -936,20 +949,9 @@
         behind(grad_second, arrived[0]), "fsdp", scatter_dimension=0, tiled=True
     )
 
-    lay = lambda values, start, total: lax.dynamic_update_slice_in_dim(
-        jnp.zeros((total,), F32), values, start, 0
-    )
-    grad_bias = lay(sums[0], rank * hidden_width, expand_bias.shape[0] * places)
-    grad_bias = grad_bias.reshape(places, -1, shard).transpose(1, 0, 2).reshape(-1, features)
-    none = jnp.zeros((6, features), F32)
-    small = jnp.concatenate([none, sums[1:3], none[:2], grad_bias, none[: 16 - small_rows]])
-
     sends = lambda low: [low[0]] + [fsdp_swap(low[step], 2 * step) for step in range(1, places // 2)]
-    branch_arrived = tensor_swap(behind(branch_give, chips[1]), 1)
-    give, branch_stay = split_sum(ids, branch_keep, branch_arrived, "branch_sum", done("residual_back_1"))
-    branch_arrived = tensor_swap(give, 2)
     mixed, head_sums = [], []
-    wait = done("branch_sum")
+    wait = done("residual_back_1")
     for pair in range(2):
         weight, qkv, attended, queries = heads[pair]
         mixed_pair, pair_sums = attend_back(
@@ -975,7 +977,7 @@
                 ids, [each[2] for each in heads], attn_grads, places, done("own_block")
             )
             out_arrived = fsdp_swap(out_give, 1)
-            wait = done("out_grad") + (small,)
+            wait = done("out_grad")
     first_sums = sends(
         low_sum(ids, (in_keep, in_arrived, out_keep, out_arrived), "in_low_0", done("attend_back_1"))
     )

time: 313 us -> 311 us (level)
  Pallas kernels: 145 us -> 138 us
    ppermute x17, waiting for transfers between devices: 29.1 us -> 38.9 us  [fsdp_swap(): lax.ppermute(array, 'fsdp', [(rank, rank ^ bit) for rank in range(size)])]
    pallas_call x28, Pallas kernels: 145 us -> 138 us  [call(): pl.pallas_call(run, grid_spec=pltpu.PrefetchScalarGridSpec(num_scalar_pre...]
    ppermute x27, waiting for transfers between devices: 28.5 us -> 23.4 us  [tensor_swap(): lax.ppermute(array, 'tensor', [(rank, rank ^ bit) for rank in range(4)])]
    unnamed x148 -> x168, local copies, waits for them, and re-layouts: 23.1 us -> 25 us
  transfers between devices with their start and end apart: 46 -> 46, of which waited for: 14 -> 19; matrix products, arithmetic and copies ran while one was open for 7% -> 7% of each run, Pallas kernels for 35% -> 34%
where the time goes in v5:
time: 311 us; the launch traced here: 307 us
  Pallas kernels  138 us (44%)
  waiting for transfers between devices  64.7 us (21%)
  local copies, waits for them, and re-layouts  40.7 us (13%)
  starting transfers between devices  40.7 us (13%)
  between operations  15.2 us (5%)
  other arithmetic  7.56 us (2%)
    pallas_call x28, Pallas kernels, call(): pl.pallas_call(run, grid_spec=pltpu.PrefetchScalarGridSpec(num_scalar_pre...  138 us
    ppermute x17, waiting for transfers between devices, fsdp_swap(): lax.ppermute(array, 'fsdp', [(rank, rank ^ bit) for rank in range(size)])  38.9 us
    unnamed x168, local copies, waits for them, and re-layouts  25 us
    ppermute x17, starting transfers between devices, fsdp_swap(): lax.ppermute(array, 'fsdp', [(rank, rank ^ bit) for rank in range(size)])  23.5 us
    ppermute x27, waiting for transfers between devices, tensor_swap(): lax.ppermute(array, 'tensor', [(rank, rank ^ bit) for rank in range(4)])  23.4 us
    ppermute x27, starting transfers between devices, tensor_swap(): lax.ppermute(array, 'tensor', [(rank, rank ^ bit) for rank in range(4)])  17 us
    dynamic_update_slice x8, local copies, waits for them, and re-layouts, gather_positions(): full = lax.dynamic_update_slice_in_dim(full, piece[None], rank ^ bit, 0)  9.81 us
  transfers between devices with their start and end apart: 46, of which 19 were waited for; matrix products, arithmetic and copies ran while one was open for 7% of the time, Pallas kernels for 34%

profile of v5, /device:TPU:0, one launch (start us, length us, event | category | flops | bytes accessed | tf_op | source)
XLA Modules:
  0.0 306.7 jit_solution(14649458888236774177)
XLA Ops:
  7.3 2.5 copy.67
  9.8 2.9 collective-permute-start.1
  14.8 3.1 %pack.1 = (bf16[128,512]{1,0:T(8,128)(2,1)}, bf16[128,640]{1,0:T(8,128)(2,1)}, bf16[128,2048]{1,0:T(8,128)(2,1)}, f32[8,128]{1,0:T(8,128)}) custom-call(s32[4]{0:T(128)} %pad_add_fusion.refs_0_, f32[3,128,256]{2,1,0:T(8,128)} %bitcast.80, f32[256,128]{1,0:T(8,128)} %refs_2_.5, f32[128,1024]{1,0:T(8,128)} %refs_2_.6, f32[1024,128]{1,0:T(8,128)} %refs_2_.7, ...), custom_call_target="tpu_custom_call" | custom-call | tf_op jit(solution)/shard_map/pack/pallas_call | solution.py:81
  17.9 1.6 collective-permute-start.6
  19.5 2.6 collective-permute-start.7
  24.5 7.8 %collective-permute-done.7 = bf16[128,512]{1,0:T(8,128)(2,1)S(1)} collective-permute-done((bf16[128,512]{1,0:T(8,128)(2,1)}, bf16[128,512]{1,0:T(8,128)(2,1)S(1)}, u32[]{:S(2)}, u32[]{:S(2)}) %collective-permute-start.7) | collective-permute-done | bytes 131104 | tf_op jit(solution)/shard_map/ppermute | solution.py:817
  32.3 1.8 pad_maximum_fusion.1.refs_2_
  34.1 2.0 collective-permute-start.10
  38.9 1.7 bitcast_dynamic-update-slice_fusion.7
  41.7 1.5 collective-permute-start.9
  43.2 7.1 %collective-permute-done.11 = bf16[128,640]{1,0:T(8,128)(2,1)} collective-permute-done((bf16[128,640]{1,0:T(8,128)(2,1)}, bf16[128,640]{1,0:T(8,128)(2,1)}, u32[]{:S(2)}, u32[]{:S(2)}) %collective-permute-start.11) | collective-permute-done | bytes 163872 | tf_op jit(solution)/shard_map/ppermute | solution.py:817
  51.6 1.6 collective-permute-start.13
  57.4 4.6 %collective-permute-done.9.refs_3_ = bf16[4,128,512]{2,1,0:T(8,128)(2,1)S(1)} collective-permute-done((bf16[4,128,512]{2,1,0:T(8,128)(2,1)}, bf16[4,128,512]{2,1,0:T(8,128)(2,1)S(1)}, u32[]{:S(2)}, u32[]{:S(2)}) %collective-permute-start.9) | collective-permute-done | bytes 524320 | tf_op jit(solution)/shard_map/ppermute | solution.py:817
  62.0 10.0 %attend_0.1 = (f32[16,1024]{1,0:T(8,128)S(1)}, bf16[1376,1024]{1,0:T(8,128)(2,1)S(1)}, bf16[1376,1024]{1,0:T(8,128)(2,1)S(1)}, bf16[1024,384]{1,0:T(8,128)(2,1)S...) custom-call(s32[4]{0:T(128)S(1)} %copy-done.47, ...), custom_call_target="tpu_custom_call" | custom-call | flops 77552680960 | tf_op jit(solution)/shard_map/attend_0/pallas_call | solution.py:81
  77.4 9.7 %attend_1.1 = (bf16[1024,384]{1,0:T(8,128)(2,1)S(1)}, bf16[1376,384]{1,0:T(8,128)(2,1)S(1)}, bf16[1376,128]{1,0:T(8,128)(2,1)}, bf16[1376,256]{1,0:T(8,128)(2,1)S(1)}, f32[8,128]{1,0:T(8,128)S(1)}) custom-call(s32[4]{0:T(128)S(1)} %copy-done.47, s32[1376,1]{1,0:T(8,128)S(1)} %copy.55.refs_1_, bf16[4,128,640]{2,1,0:T(8,128)(2,1)S(1)} %pad_maximum_fusion.refs_1_.refs_2_, ...), custom_call_target="tpu_custom_call" | custom-call | flops 77552680960 | tf_op jit(solution)/shard_map/attend_1/pallas_call | solution.py:81
  89.9 1.6 collective-permute-start.17
  92.7 1.8 copy-done.13
  95.9 1.6 copy-done.5
  103.4 6.4 %collective-permute-done.16 = bf16[1376,128]{1,0:T(8,128)(2,1)S(1)} collective-permute-done((bf16[1376,128]{1,0:T(8,128)(2,1)S(1)}, bf16[1376,128]{1,0:T(8,128)(2,1)S(1)}, u32[]{:S(2)}, u32[]{:S(2)}) %collective-permute-start.16) | collective-permute-done | bytes 352288 | tf_op jit(solution)/shard_map/ppermute | solution.py:812
  114.6 2.4 all-gather.2.cloned.1.call-done.refs_15_.refs_16_
  116.9 27.9 %middle.1 = (bf16[4,344,1024]{2,1,0:T(8,128)(2,1)}, bf16[4,344,1024]{2,1,0:T(8,128)(2,1)}, bf16[4,344,1024]{2,1,0:T(8,128)(2,1)}, bf16[2,344,1024]{2,1,0:T(8,128...) custom-call(s32[4]{0:T(128)} %pad_add_fusion.refs_0_, ...), custom_call_target="tpu_custom_call" | custom-call | flops 14428405760 | tf_op jit(solution)/shard_map/middle/pallas_call | solution.py:81
  144.9 3.4 %collective-permute-done.23.refs_2_ = bf16[2,344,1024]{2,1,0:T(8,128)(2,1)S(1)} collective-permute-done((bf16[2,344,1024]{2,1,0:T(8,128)(2,1)}, bf16[2,344,1024]{2,1,0:T(8,128)(2,1)S(1)}, u32[]{:S(2)}, u32[]{:S(2)}) %collective-permute-start.23) | collective-permute-done | bytes 1409056 | tf_op jit(solution)/shard_map/ppermute | solution.py:812
  153.6 14.1 %matrices.1 = (bf16[1024,2048]{1,0:T(8,128)(2,1)}, f32[8,128]{1,0:T(8,128)}) custom-call(s32[4]{0:T(128)} %pad_add_fusion.refs_0_, bf16[1376,1024]{1,0:T(8,128)(2,1)} %bitcast.86, bf16[1376,1024]{1,0:T(8,128)(2,1)} %bitcast.76, bf16[1376,1024]{1,0:T(8,128)(2,1)} %bitcast.88, bf16[1376,1024]{1,0:T(8,128)(2,1)} %bitcast.87, f32[16,1024]{1,0:T(8,128)} %copy-done.21, ...), custom_call_target="tpu_custom_call" | custom-call | tf_op jit(solution)/shard_map/matrices/pallas_call | solution.py:81
  169.6 1.5 collective-permute-start.25
  174.4 5.1 %residual_back_0.1 = (bf16[344,1024]{1,0:T(8,128)(2,1)}, bf16[344,1024]{1,0:T(8,128)(2,1)}, f32[8,128]{1,0:T(8,128)}) custom-call(s32[4]{0:T(128)} %pad_add_fusion.refs_0_, bf16[344,1024]{1,0:T(8,128)(2,1)} %copy-done.34, bf16[344,1024]{1,0:T(8,128)(2,1)} %copy-done.70, bf16[4,344,1024]{2,1,0:T(8,128)(2,1)} %copy-done, ...), custom_call_target="tpu_custom_call" | custom-call | tf_op jit(solution)/shard_map/residual_back_0/pallas_call | solution.py:81
  182.0 5.9 %collective-permute-done.25.refs_2_ = bf16[344,1024]{1,0:T(8,128)(2,1)} collective-permute-done((bf16[344,1024]{1,0:T(8,128)(2,1)S(1)}, bf16[344,1024]{1,0:T(8,128)(2,1)}, u32[]{:S(2)}, u32[]{:S(2)}) %collective-permute-start.25) | collective-permute-done | bytes 704544 | tf_op jit(solution)/shard_map/ppermute | solution.py:812
  187.9 5.2 %residual_back_1.1 = (bf16[344,1024]{1,0:T(8,128)(2,1)}, bf16[344,1024]{1,0:T(8,128)(2,1)}, f32[8,128]{1,0:T(8,128)}) custom-call(s32[4]{0:T(128)} %pad_add_fusion.refs_0_, bf16[344,1024]{1,0:T(8,128)(2,1)} %copy-done.33, bf16[344,1024]{1,0:T(8,128)(2,1)} %collective-permute-done.25.refs_2_, bf16[4,344,1024]{2,1,0:T(8,128)(2,1)} %copy-done, ...), custom_call_target="tpu_custom_call" | custom-call | tf_op jit(solution)/shard_map/residual_back_1/pallas_call | solution.py:81
  193.1 1.5 collective-permute-start.27
  197.4 13.3 %attend_back_0.1 = (bf16[1376,384]{1,0:T(8,128)(2,1)S(1)}, f32[8,128]{1,0:T(8,128)S(1)}, f32[8,128]{1,0:T(8,128)}) custom-call(s32[4]{0:T(128)S(1)} %copy-done.50, s32[1376,1]{1,0:T(8,128)S(1)} %copy.55.refs_1_, bf16[1376,384]{1,0:T(8,128)(2,1)S(1)} %copy-done.66, bf16[1376,256]{1,0:T(8,128)(2,1)S(1)} %copy-done.68, bf16[1376,128]{1,0:T(8,128)(2,1)S(1)} %copy-done.46, ...), custom_call_target="tpu_custom_call" | custom-call | flops 9694085120 | tf_op jit(solution)/shard_map/attend_back_0/pallas_call | solution.py:81
  210.8 2.5 in_grad_0.1
  213.9 3.0 own_block.1
  216.9 3.1 %out_grad.1 = (bf16[4,128,256]{2,1,0:T(8,128)(2,1)S(1)}, bf16[4,128,256]{2,1,0:T(8,128)(2,1)S(1)}, f32[8,128]{1,0:T(8,128)S(1)}) custom-call(s32[4]{0:T(128)S(1)} %copy-done.50, bf16[4,344,128]{2,1,0:T(8,128)(2,1)S(1)} %bitcast.85, bf16[4,344,128]{2,1,0:T(8,128)(2,1)} %bitcast.25.refs_3_.refs_2_, bf16[344,1024]{1,0:T(8,128)(2,1)S(1)} %copy-done.14, ...), custom_call_target="tpu_custom_call" | custom-call | tf_op jit(solution)/shard_map/out_grad/pallas_call | solution.py:81
  220.0 1.6 collective-permute-start.31
  221.6 13.2 %attend_back_1.1 = (bf16[1376,384]{1,0:T(8,128)(2,1)S(1)}, f32[8,128]{1,0:T(8,128)S(1)}, f32[8,128]{1,0:T(8,128)S(1)}) custom-call(s32[4]{0:T(128)S(1)} %copy-done.50, s32[1376,1]{1,0:T(8,128)S(1)} %copy.55.refs_1_, bf16[1376,384]{1,0:T(8,128)(2,1)S(1)} %copy-done.26, bf16[1376,256]{1,0:T(8,128)(2,1)S(1)} %copy-done.32, ...), custom_call_target="tpu_custom_call" | custom-call | tf_op jit(solution)/shard_map/attend_back_1/pallas_call | solution.py:81
  236.4 5.5 %input_back.1 = (bf16[2,344,1024]{2,1,0:T(8,128)(2,1)S(1)}, bf16[2,344,1024]{2,1,0:T(8,128)(2,1)S(1)}, f32[8,1024]{1,0:T(8,128)S(1)}, f32[8,128]{1,0:T(8,128)}) custom-call(s32[4]{0:T(128)S(1)} %copy-done.50, bf16[4,344,1024]{2,1,0:T(8,128)(2,1)S(1)} %bitcast.79, bf16[4,344,384]{2,1,0:T(8,128)(2,1)S(1)} %bitcast.77, bf16[4,344,384]{2,1,0:T(8,128)(2,1)S(1)} %bitcast.78, ...), custom_call_target="tpu_custom_call" | custom-call | tf_op jit(solution)/shard_map/input_back/pallas_call | solution.py:81
  241.9 2.5 in_grad_1.1
  246.1 1.5 collective-permute-start.33
  250.7 1.9 collective-permute-start.37
  252.6 7.0 %collective-permute-done.34.refs_2_ = bf16[4,144,384]{2,1,0:T(8,128)(2,1)S(1)} collective-permute-done((bf16[4,144,384]{2,1,0:T(8,128)(2,1)S(1)}, bf16[4,144,384]{2,1,0:T(8,128)(2,1)S(1)}, u32[]{:S(2)}, u32[]{:S(2)}) %collective-permute-start.34) | collective-permute-done | bytes 442400 | tf_op jit(solution)/shard_map/ppermute | solution.py:817
  259.5 4.4 %collective-permute-done.33.refs_2_ = bf16[344,1024]{1,0:T(8,128)(2,1)S(1)} collective-permute-done((bf16[344,1024]{1,0:T(8,128)(2,1)S(1)}, bf16[344,1024]{1,0:T(8,128)(2,1)S(1)}, u32[]{:S(2)}, u32[]{:S(2)}) %collective-permute-start.33) | collective-permute-done | bytes 704544 | tf_op jit(solution)/shard_map/ppermute | solution.py:812
  267.2 1.9 collective-permute-start.40
  269.1 3.0 input_grad.1
  272.1 1.8 collective-permute-done.37.refs_4_
  276.0 7.4 %collective-permute-done.39.refs_4_ = bf16[144,384]{1,0:T(8,128)(2,1)S(1)} collective-permute-done((bf16[144,384]{1,0:T(8,128)(2,1)S(1)}, bf16[144,384]{1,0:T(8,128)(2,1)S(1)}, u32[]{:S(2)}, u32[]{:S(2)}) %collective-permute-start.39) | collective-permute-done | bytes 110624 | tf_op jit(solution)/shard_map/ppermute | solution.py:817
  286.6 2.2 adam_expand.1
  290.9 2.3 adam_contract.1
  293.2 1.6 collective-permute-start.42
  295.1 2.0 adam_in.1
  (274 shorter events, 70.9 us)
Async XLA Ops:
  7.2 109.7 %all-gather.2.cloned.1.call-start = ((), (), s32[]{:S(2)}) async-start(), calls=%async_computation.1 | async-start | bytes 4718592 | tf_op jit(solution)/shard_map/all_gather | solution.py:885
  9.8 28.7 %collective-permute-start.1 = (bf16[344,1024]{1,0:T(8,128)(2,1)}, bf16[344,1024]{1,0:T(8,128)(2,1)}, u32[]{:S(2)}, u32[]{:S(2)}) collective-permute-start(bf16[344,1024]{1,0:T(8,128)(2,1)} %bitcast.74), channel_id=1, source_target_pairs={{0,2},{1,3},{2,0},{3,1},{4,6},{5,7},{6,4},{7,5},{8,10},{9,11},{10,... | collective-permute-start | bytes 2113544 | tf_op jit(solution)/shard_map/ppermute | solution.py:812
  17.9 6.6 %collective-permute-start.6 = (bf16[128,512]{1,0:T(8,128)(2,1)}, bf16[128,512]{1,0:T(8,128)(2,1)S(1)}, u32[]{:S(2)}, u32[]{:S(2)}) collective-permute-start(bf16[128,512]{1,0:T(8,128)(2,1)} %get-tuple-element.134), channel_id=1, source_target_pairs={{0,8},{4,12},{8,0},{12,4},{16,24},{20,28},{24,16},{28,20},{1,9},{5... | collective-permute-start | bytes 393224 | tf_op jit(solution)/shard_map/ppermute | solution.py:817
  19.5 12.9 %collective-permute-start.7 = (bf16[128,512]{1,0:T(8,128)(2,1)}, bf16[128,512]{1,0:T(8,128)(2,1)S(1)}, u32[]{:S(2)}, u32[]{:S(2)}) collective-permute-start(bf16[128,512]{1,0:T(8,128)(2,1)} %get-tuple-element.134), channel_id=1, source_target_pairs={{0,16},{4,20},{8,24},{12,28},{16,0},{20,4},{24,8},{28,12},{1,17},{... | collective-permute-start | bytes 393224 | tf_op jit(solution)/shard_map/ppermute | solution.py:817
  22.1 10.3 %collective-permute-start.8 = (bf16[128,512]{1,0:T(8,128)(2,1)}, bf16[128,512]{1,0:T(8,128)(2,1)S(1)}, u32[]{:S(2)}, u32[]{:S(2)}) collective-permute-start(bf16[128,512]{1,0:T(8,128)(2,1)} %get-tuple-element.134), channel_id=1, source_target_pairs={{0,24},{4,28},{8,16},{12,20},{16,8},{20,12},{24,0},{28,4},{1,25},{... | collective-permute-start | bytes 393224 | tf_op jit(solution)/shard_map/ppermute | solution.py:817
  22.3 30.9 %collective-permute-start = (bf16[344,1024]{1,0:T(8,128)(2,1)}, bf16[344,1024]{1,0:T(8,128)(2,1)}, u32[]{:S(2)}, u32[]{:S(2)}) collective-permute-start(bf16[344,1024]{1,0:T(8,128)(2,1)} %bitcast.74), channel_id=1, source_target_pairs={{0,1},{1,0},{2,3},{3,2},{4,5},{5,4},{6,7},{7,6},{8,9},{9,8},{10,11... | collective-permute-start | bytes 2113544 | tf_op jit(solution)/shard_map/ppermute | solution.py:812
  34.1 7.6 %collective-permute-start.10 = (bf16[128,640]{1,0:T(8,128)(2,1)}, bf16[128,640]{1,0:T(8,128)(2,1)}, u32[]{:S(2)}, u32[]{:S(2)}) collective-permute-start(bf16[128,640]{1,0:T(8,128)(2,1)} %get-tuple-element.137), channel_id=1, source_target_pairs={{0,8},{4,12},{8,0},{12,4},{16,24},{20,28},{24,16},{28,20},{1,9},{5... | collective-permute-start | bytes 491528 | tf_op jit(solution)/shard_map/ppermute | solution.py:817
  36.1 14.2 %collective-permute-start.11 = (bf16[128,640]{1,0:T(8,128)(2,1)}, bf16[128,640]{1,0:T(8,128)(2,1)}, u32[]{:S(2)}, u32[]{:S(2)}) collective-permute-start(bf16[128,640]{1,0:T(8,128)(2,1)} %get-tuple-element.137), channel_id=1, source_target_pairs={{0,16},{4,20},{8,24},{12,28},{16,0},{20,4},{24,8},{28,12},{1,17},{... | collective-permute-start | bytes 491528 | tf_op jit(solution)/shard_map/ppermute | solution.py:817
  37.1 13.2 %collective-permute-start.12 = (bf16[128,640]{1,0:T(8,128)(2,1)}, bf16[128,640]{1,0:T(8,128)(2,1)}, u32[]{:S(2)}, u32[]{:S(2)}) collective-permute-start(bf16[128,640]{1,0:T(8,128)(2,1)} %get-tuple-element.137), channel_id=1, source_target_pairs={{0,24},{4,28},{8,16},{12,20},{16,8},{20,12},{24,0},{28,4},{1,25},{... | collective-permute-start | bytes 491528 | tf_op jit(solution)/shard_map/ppermute | solution.py:817
  38.5 16.9 %collective-permute-start.2 = (bf16[344,1024]{1,0:T(8,128)(2,1)}, bf16[344,1024]{1,0:T(8,128)(2,1)}, u32[]{:S(2)}, u32[]{:S(2)}) collective-permute-start(bf16[344,1024]{1,0:T(8,128)(2,1)} %collective-permute-done.1), channel_id=1, source_target_pairs={{0,1},{1,0},{2,3},{3,2},{4,5},{5,4},{6,7},{7,6},{8,9},{9,8},{10,11... | collective-permute-start | bytes 2113544 | tf_op jit(solution)/shard_map/ppermute | solution.py:812
  41.0 244.4 %reduce-scatter.2.cloned.1.call-start = ((), (), s32[]{:S(2)}) async-start(), calls=%async_computation.2 | async-start | bytes 4718592 | tf_op jit(solution)/shard_map/reduce_scatter | solution.py:948
  41.7 20.3 %collective-permute-start.9 = (bf16[4,128,512]{2,1,0:T(8,128)(2,1)}, bf16[4,128,512]{2,1,0:T(8,128)(2,1)S(1)}, u32[]{:S(2)}, u32[]{:S(2)}) collective-permute-start(bf16[4,128,512]{2,1,0:T(8,128)(2,1)} %pad_maximum_fusion.1.refs_2_), channel_id=1, source_target_pairs={{0,4},{4,0},{8,12},{12,8},{16,20},{20,16},{24,28},{28,24},{1,5},{5... | collective-permute-start | bytes 1572872 | tf_op jit(solution)/shard_map/ppermute | solution.py:817
  51.6 23.9 %collective-permute-start.13 = (bf16[4,128,640]{2,1,0:T(8,128)(2,1)S(1)}, bf16[4,128,640]{2,1,0:T(8,128)(2,1)S(1)}, u32[]{:S(2)}, u32[]{:S(2)}) collective-permute-start(bf16[4,128,640]{2,1,0:T(8,128)(2,1)S(1)} %pad_maximum_fusion.refs_1_.refs_2_), channel_id=1, source_target_pairs={{0,4},{4,0},{8,12},{12,8},{16,20},{20,16},{24,28},{28,24},{1,5},{5... | collective-permute-start | bytes 1966088 | tf_op jit(solution)/shard_map/ppermute | solution.py:817
  56.6 44.9 %collective-permute-start.3 = (bf16[344,1024]{1,0:T(8,128)(2,1)}, bf16[344,1024]{1,0:T(8,128)(2,1)}, u32[]{:S(2)}, u32[]{:S(2)}) collective-permute-start(bf16[344,1024]{1,0:T(8,128)(2,1)} %fusion), channel_id=1, source_target_pairs={{0,1},{1,0},{2,3},{3,2},{4,5},{5,4},{6,7},{7,6},{8,9},{9,8},{10,11... | collective-permute-start | bytes 2113544 | tf_op jit(solution)/shard_map/ppermute | solution.py:812
  56.7 34.7 %collective-permute-start.4 = (bf16[344,1024]{1,0:T(8,128)(2,1)}, bf16[344,1024]{1,0:T(8,128)(2,1)}, u32[]{:S(2)}, u32[]{:S(2)}) collective-permute-start(bf16[344,1024]{1,0:T(8,128)(2,1)} %fusion), channel_id=1, source_target_pairs={{0,2},{1,3},{2,0},{3,1},{4,6},{5,7},{6,4},{7,5},{8,10},{9,11},{10,... | collective-permute-start | bytes 2113544 | tf_op jit(solution)/shard_map/ppermute | solution.py:812
  76.9 24.6 %collective-permute-start.21 = (bf16[1024,256]{1,0:T(8,128)(2,1)}, bf16[1024,256]{1,0:T(8,128)(2,1)}, u32[]{:S(2)}, u32[]{:S(2)}) collective-permute-start(bf16[1024,256]{1,0:T(8,128)(2,1)} %get-tuple-element.143.refs_10_.refs_9_), channel_id=1, source_target_pairs={{0,2},{1,3},{2,0},{3,1},{4,6},{5,7},{6,4},{7,5},{8,10},{9,11},{10,... | collective-permute-start | bytes 1572872 | tf_op jit(solution)/shard_map/ppermute | solution.py:812
  89.9 9.7 %collective-permute-start.17 = (bf16[1376,128]{1,0:T(8,128)(2,1)}, bf16[1376,128]{1,0:T(8,128)(2,1)}, u32[]{:S(2)}, u32[]{:S(2)}) collective-permute-start(bf16[1376,128]{1,0:T(8,128)(2,1)} %get-tuple-element.142.refs_4_), channel_id=1, source_target_pairs={{0,2},{1,3},{2,0},{3,1},{4,6},{5,7},{6,4},{7,5},{8,10},{9,11},{10,... | collective-permute-start | bytes 1056776 | tf_op jit(solution)/shard_map/ppermute | solution.py:812
  91.4 18.4 %collective-permute-start.5 = (bf16[344,1024]{1,0:T(8,128)(2,1)}, bf16[344,1024]{1,0:T(8,128)(2,1)}, u32[]{:S(2)}, u32[]{:S(2)}) collective-permute-start(bf16[344,1024]{1,0:T(8,128)(2,1)} %collective-permute-done.4), channel_id=1, source_target_pairs={{0,1},{1,0},{2,3},{3,2},{4,5},{5,4},{6,7},{7,6},{8,9},{9,8},{10,11... | collective-permute-start | bytes 2113544 | tf_op jit(solution)/shard_map/ppermute | solution.py:812
  91.4 11.8 %collective-permute-start.15 = (bf16[1376,128]{1,0:T(8,128)(2,1)}, bf16[1376,128]{1,0:T(8,128)(2,1)S(1)}, u32[]{:S(2)}, u32[]{:S(2)}) collective-permute-start(bf16[1376,128]{1,0:T(8,128)(2,1)} %get-tuple-element.142.refs_4_), channel_id=1, source_target_pairs={{0,1},{1,0},{2,3},{3,2},{4,5},{5,4},{6,7},{7,6},{8,9},{9,8},{10,11... | collective-permute-start | bytes 1056776 | tf_op jit(solution)/shard_map/ppermute | solution.py:812
  99.6 10.2 %collective-permute-start.16 = (bf16[1376,128]{1,0:T(8,128)(2,1)S(1)}, bf16[1376,128]{1,0:T(8,128)(2,1)S(1)}, u32[]{:S(2)}, u32[]{:S(2)}) collective-permute-start(bf16[1376,128]{1,0:T(8,128)(2,1)S(1)} %copy-done.45), channel_id=1, source_target_pairs={{0,2},{1,3},{2,0},{3,1},{4,6},{5,7},{6,4},{7,5},{8,10},{9,11},{10,... | collective-permute-start | bytes 1056776 | tf_op jit(solution)/shard_map/ppermute | solution.py:812
  101.5 11.2 %collective-permute-start.20 = (bf16[1024,256]{1,0:T(8,128)(2,1)}, bf16[1024,256]{1,0:T(8,128)(2,1)}, u32[]{:S(2)}, u32[]{:S(2)}) collective-permute-start(bf16[1024,256]{1,0:T(8,128)(2,1)} %get-tuple-element.143.refs_10_.refs_9_), channel_id=1, source_target_pairs={{0,1},{1,0},{2,3},{3,2},{4,5},{5,4},{6,7},{7,6},{8,9},{9,8},{10,11... | collective-permute-start | bytes 1572872 | tf_op jit(solution)/shard_map/ppermute | solution.py:812
  101.5 13.0 %collective-permute-start.22 = (bf16[1024,256]{1,0:T(8,128)(2,1)}, bf16[1024,256]{1,0:T(8,128)(2,1)}, u32[]{:S(2)}, u32[]{:S(2)}) collective-permute-start(bf16[1024,256]{1,0:T(8,128)(2,1)} %collective-permute-done.21.refs_12_), channel_id=1, source_target_pairs={{0,1},{1,0},{2,3},{3,2},{4,5},{5,4},{6,7},{7,6},{8,9},{9,8},{10,11... | collective-permute-start | bytes 1572872 | tf_op jit(solution)/shard_map/ppermute | solution.py:812
  103.2 9.4 %collective-permute-start.14 = (bf16[1376,128]{1,0:T(8,128)(2,1)S(1)}, bf16[1376,128]{1,0:T(8,128)(2,1)S(1)}, u32[]{:S(2)}, u32[]{:S(2)}) collective-permute-start(bf16[1376,128]{1,0:T(8,128)(2,1)S(1)} %copy-done.45), channel_id=1, source_target_pairs={{0,1},{1,0},{2,3},{3,2},{4,5},{5,4},{6,7},{7,6},{8,9},{9,8},{10,11... | collective-permute-start | bytes 1056776 | tf_op jit(solution)/shard_map/ppermute | solution.py:812
  109.8 2.9 collective-permute-start.19
  109.8 2.9 collective-permute-start.18
  116.9 31.3 %copy-start.48 = (s32[4]{0:T(128)S(1)}, s32[4]{0:T(128)}, u32[]{:S(2)}) copy-start(s32[4]{0:T(128)} %pad_add_fusion.refs_0_) | copy-start | bytes 52
  144.8 3.5 %collective-permute-start.23 = (bf16[2,344,1024]{2,1,0:T(8,128)(2,1)}, bf16[2,344,1024]{2,1,0:T(8,128)(2,1)S(1)}, u32[]{:S(2)}, u32[]{:S(2)}) collective-permute-start(bf16[2,344,1024]{2,1,0:T(8,128)(2,1)} %get-tuple-element.150), channel_id=1, source_target_pairs={{0,1},{1,0},{2,3},{3,2},{4,5},{5,4},{6,7},{7,6},{8,9},{9,8},{10,11... | collective-permute-start | bytes 4227080 | tf_op jit(solution)/shard_map/ppermute | solution.py:812
  150.8 17.8 %collective-permute-start.24 = (bf16[344,1024]{1,0:T(8,128)(2,1)S(1)}, bf16[344,1024]{1,0:T(8,128)(2,1)S(1)}, u32[]{:S(2)}, u32[]{:S(2)}) collective-permute-start(bf16[344,1024]{1,0:T(8,128)(2,1)S(1)} %get-tuple-element.151.refs_1_), channel_id=1, source_target_pairs={{0,2},{1,3},{2,0},{3,1},{4,6},{5,7},{6,4},{7,5},{8,10},{9,11},{10,... | collective-permute-start | bytes 2113544 | tf_op jit(solution)/shard_map/ppermute | solution.py:812
  169.5 10.2 %collective-permute-start.26 = (bf16[2,344,1024]{2,1,0:T(8,128)(2,1)}, bf16[2,344,1024]{2,1,0:T(8,128)(2,1)S(1)}, u32[]{:S(2)}, u32[]{:S(2)}) collective-permute-start(bf16[2,344,1024]{2,1,0:T(8,128)(2,1)} %get-tuple-element.161), channel_id=1, source_target_pairs={{0,1},{1,0},{2,3},{3,2},{4,5},{5,4},{6,7},{7,6},{8,9},{9,8},{10,11... | collective-permute-start | bytes 4227080 | tf_op jit(solution)/shard_map/ppermute | solution.py:812
  169.6 18.3 %collective-permute-start.25 = (bf16[344,1024]{1,0:T(8,128)(2,1)S(1)}, bf16[344,1024]{1,0:T(8,128)(2,1)}, u32[]{:S(2)}, u32[]{:S(2)}) collective-permute-start(bf16[344,1024]{1,0:T(8,128)(2,1)S(1)} %get-tuple-element.158.refs_1_), channel_id=1, source_target_pairs={{0,2},{1,3},{2,0},{3,1},{4,6},{5,7},{6,4},{7,5},{8,10},{9,11},{10,... | collective-permute-start | bytes 2113544 | tf_op jit(solution)/shard_map/ppermute | solution.py:812
  179.5 15.2 %collective-permute-start.28 = (bf16[344,1024]{1,0:T(8,128)(2,1)}, bf16[344,1024]{1,0:T(8,128)(2,1)S(1)}, u32[]{:S(2)}, u32[]{:S(2)}) collective-permute-start(bf16[344,1024]{1,0:T(8,128)(2,1)} %get-tuple-element.171.refs_5_.refs_3_), channel_id=1, source_target_pairs={{0,1},{1,0},{2,3},{3,2},{4,5},{5,4},{6,7},{7,6},{8,9},{9,8},{10,11... | collective-permute-start | bytes 2113544 | tf_op jit(solution)/shard_map/ppermute | solution.py:812
  193.1 2.4 collective-permute-start.29
  193.1 20.7 %collective-permute-start.27 = (bf16[344,1024]{1,0:T(8,128)(2,1)}, bf16[344,1024]{1,0:T(8,128)(2,1)S(1)}, u32[]{:S(2)}, u32[]{:S(2)}) collective-permute-start(bf16[344,1024]{1,0:T(8,128)(2,1)} %copy-done.62), channel_id=1, source_target_pairs={{0,2},{1,3},{2,0},{3,1},{4,6},{5,7},{6,4},{7,5},{8,10},{9,11},{10,... | collective-permute-start | bytes 2113544 | tf_op jit(solution)/shard_map/ppermute | solution.py:812
  213.2 22.4 %collective-permute-start.30 = (bf16[4,128,384]{2,1,0:T(8,128)(2,1)S(1)}, bf16[4,128,384]{2,1,0:T(8,128)(2,1)S(1)}, u32[]{:S(2)}, u32[]{:S(2)}) collective-permute-start(bf16[4,128,384]{2,1,0:T(8,128)(2,1)S(1)} %get-tuple-element.186), channel_id=1, source_target_pairs={{0,4},{4,0},{8,12},{12,8},{16,20},{20,16},{24,28},{28,24},{1,5},{5... | collective-permute-start | bytes 1179656 | tf_op jit(solution)/shard_map/ppermute | solution.py:817
  220.0 15.6 %collective-permute-start.31 = (bf16[4,128,256]{2,1,0:T(8,128)(2,1)S(1)}, bf16[4,128,256]{2,1,0:T(8,128)(2,1)S(1)}, u32[]{:S(2)}, u32[]{:S(2)}) collective-permute-start(bf16[4,128,256]{2,1,0:T(8,128)(2,1)S(1)} %get-tuple-element.188), channel_id=1, source_target_pairs={{0,4},{4,0},{8,12},{12,8},{16,20},{20,16},{24,28},{28,24},{1,5},{5... | collective-permute-start | bytes 786440 | tf_op jit(solution)/shard_map/ppermute | solution.py:817
  241.9 3.2 %collective-permute-start.32 = (bf16[2,344,1024]{2,1,0:T(8,128)(2,1)S(1)}, bf16[2,344,1024]{2,1,0:T(8,128)(2,1)S(1)}, u32[]{:S(2)}, u32[]{:S(2)}) collective-permute-start(bf16[2,344,1024]{2,1,0:T(8,128)(2,1)S(1)} %get-tuple-element.192), channel_id=1, source_target_pairs={{0,1},{1,0},{2,3},{3,2},{4,5},{5,4},{6,7},{7,6},{8,9},{9,8},{10,11... | collective-permute-start | bytes 4227080 | tf_op jit(solution)/shard_map/ppermute | solution.py:812
  246.1 17.9 %collective-permute-start.33 = (bf16[344,1024]{1,0:T(8,128)(2,1)S(1)}, bf16[344,1024]{1,0:T(8,128)(2,1)S(1)}, u32[]{:S(2)}, u32[]{:S(2)}) collective-permute-start(bf16[344,1024]{1,0:T(8,128)(2,1)S(1)} %get-tuple-element.199), channel_id=1, source_target_pairs={{0,2},{1,3},{2,0},{3,1},{4,6},{5,7},{6,4},{7,5},{8,10},{9,11},{10,... | collective-permute-start | bytes 2113544 | tf_op jit(solution)/shard_map/ppermute | solution.py:812
  247.6 11.9 %collective-permute-start.34 = (bf16[4,144,384]{2,1,0:T(8,128)(2,1)S(1)}, bf16[4,144,384]{2,1,0:T(8,128)(2,1)S(1)}, u32[]{:S(2)}, u32[]{:S(2)}) collective-permute-start(bf16[4,144,384]{2,1,0:T(8,128)(2,1)S(1)} %get-tuple-element.201), channel_id=1, source_target_pairs={{0,4},{4,0},{8,12},{12,8},{16,20},{20,16},{24,28},{28,24},{1,5},{5... | collective-permute-start | bytes 1327112 | tf_op jit(solution)/shard_map/ppermute | solution.py:817
  248.2 19.0 %collective-permute-start.35 = (bf16[128,640]{1,0:T(8,128)(2,1)S(1)}, bf16[128,640]{1,0:T(8,128)(2,1)S(1)}, u32[]{:S(2)}, u32[]{:S(2)}) collective-permute-start(bf16[128,640]{1,0:T(8,128)(2,1)S(1)} %get-tuple-element.207), channel_id=1, source_target_pairs={{0,8},{4,12},{8,0},{12,4},{16,24},{20,28},{24,16},{28,20},{1,9},{5... | collective-permute-start | bytes 491528 | tf_op jit(solution)/shard_map/ppermute | solution.py:817
  249.2 22.9 %collective-permute-start.36 = (bf16[128,640]{1,0:T(8,128)(2,1)S(1)}, bf16[128,640]{1,0:T(8,128)(2,1)S(1)}, u32[]{:S(2)}, u32[]{:S(2)}) collective-permute-start(bf16[128,640]{1,0:T(8,128)(2,1)S(1)} %get-tuple-element.208), channel_id=1, source_target_pairs={{0,16},{4,20},{8,24},{12,28},{16,0},{20,4},{24,8},{28,12},{1,17},{... | collective-permute-start | bytes 491528 | tf_op jit(solution)/shard_map/ppermute | solution.py:817
  250.7 23.2 %collective-permute-start.37 = (bf16[128,640]{1,0:T(8,128)(2,1)S(1)}, bf16[128,640]{1,0:T(8,128)(2,1)S(1)}, u32[]{:S(2)}, u32[]{:S(2)}) collective-permute-start(bf16[128,640]{1,0:T(8,128)(2,1)S(1)} %get-tuple-element.209), channel_id=1, source_target_pairs={{0,24},{4,28},{8,16},{12,20},{16,8},{20,12},{24,0},{28,4},{1,25},{... | collective-permute-start | bytes 491528 | tf_op jit(solution)/shard_map/ppermute | solution.py:817
  264.6 11.4 %collective-permute-start.38 = (bf16[144,384]{1,0:T(8,128)(2,1)S(1)}, bf16[144,384]{1,0:T(8,128)(2,1)S(1)}, u32[]{:S(2)}, u32[]{:S(2)}) collective-permute-start(bf16[144,384]{1,0:T(8,128)(2,1)S(1)} %get-tuple-element.213), channel_id=1, source_target_pairs={{0,8},{4,12},{8,0},{12,4},{16,24},{20,28},{24,16},{28,20},{1,9},{5... | collective-permute-start | bytes 331784 | tf_op jit(solution)/shard_map/ppermute | solution.py:817
  265.7 17.7 %collective-permute-start.39 = (bf16[144,384]{1,0:T(8,128)(2,1)S(1)}, bf16[144,384]{1,0:T(8,128)(2,1)S(1)}, u32[]{:S(2)}, u32[]{:S(2)}) collective-permute-start(bf16[144,384]{1,0:T(8,128)(2,1)S(1)} %get-tuple-element.214), channel_id=1, source_target_pairs={{0,16},{4,20},{8,24},{12,28},{16,0},{20,4},{24,8},{28,12},{1,17},{... | collective-permute-start | bytes 331784 | tf_op jit(solution)/shard_map/ppermute | solution.py:817
  267.2 16.2 %collective-permute-start.40 = (bf16[144,384]{1,0:T(8,128)(2,1)S(1)}, bf16[144,384]{1,0:T(8,128)(2,1)S(1)}, u32[]{:S(2)}, u32[]{:S(2)}) collective-permute-start(bf16[144,384]{1,0:T(8,128)(2,1)S(1)} %get-tuple-element.215), channel_id=1, source_target_pairs={{0,24},{4,28},{8,16},{12,20},{16,8},{20,12},{24,0},{28,4},{1,25},{... | collective-permute-start | bytes 331784 | tf_op jit(solution)/shard_map/ppermute | solution.py:817
  272.1 23.0 %copy-start.23 = (f32[128,3,256]{2,0,1:T(8,128)S(1)}, f32[128,3,256]{2,0,1:T(8,128)}, u32[]{:S(2)}) copy-start(f32[128,3,256]{2,0,1:T(8,128)} %param.24) | copy-start | bytes 1179652
  293.2 3.9 %collective-permute-start.41 = (f32[16,128]{1,0:T(8,128)S(1)}, f32[16,128]{1,0:T(8,128)S(1)}, u32[]{:S(2)}, u32[]{:S(2)}) collective-permute-start(f32[16,128]{1,0:T(8,128)S(1)} %convert_add_fusion), channel_id=1, source_target_pairs={{0,1},{1,0},{2,3},{3,2},{4,5},{5,4},{6,7},{7,6},{8,9},{9,8},{10,11... | collective-permute-start | bytes 24584 | tf_op jit(solution)/shard_map/ppermute | solution.py:812
  293.2 3.9 %collective-permute-start.42 = (f32[16,128]{1,0:T(8,128)S(1)}, f32[16,128]{1,0:T(8,128)S(1)}, u32[]{:S(2)}, u32[]{:S(2)}) collective-permute-start(f32[16,128]{1,0:T(8,128)S(1)} %convert_add_fusion), channel_id=1, source_target_pairs={{0,2},{1,3},{2,0},{3,1},{4,6},{5,7},{6,4},{7,5},{8,10},{9,11},{10,... | collective-permute-start | bytes 24584 | tf_op jit(solution)/shard_map/ppermute | solution.py:812
  294.8 3.1 %collective-permute-start.43 = (f32[16,128]{1,0:T(8,128)S(1)}, f32[16,128]{1,0:T(8,128)S(1)}, u32[]{:S(2)}, u32[]{:S(2)}) collective-permute-start(f32[16,128]{1,0:T(8,128)S(1)} %convert_add_fusion), channel_id=1, source_target_pairs={{0,3},{1,2},{2,1},{3,0},{4,7},{5,6},{6,5},{7,4},{8,11},{9,10},{10,... | collective-permute-start | bytes 24584 | tf_op jit(solution)/shard_map/ppermute | solution.py:812
  (81 other events, 636.3 us)
Sparse Core Ops, SparseCore 0:
  41.1 75.8 all-gather.1
  169.6 105.2 reduce-scatter.1

commit v6 on v5

--- a/solution.py
+++ b/solution.py
@@ -996,7 +996,7 @@
     give, stay = split_sum(ids, input_keep, tensor_swap(input_give, 1), "input_sum", done("in_grad_1"))
     input_arrived = tensor_swap(give, 2)
     in_low = low_sum(
-        ids, (in_keep, behind(in_arrived, input_arrived)), "in_low_1", done("input_sum")
+        ids, (in_keep, in_arrived), "in_low_1", done("input_sum")
     )
     second_sums = sends(in_low)
     input_grad = input_grad_of(

time: 311 us -> 313 us (level)
    ppermute x17, waiting for transfers between devices: 38.9 us -> 47 us  [fsdp_swap(): lax.ppermute(array, 'fsdp', [(rank, rank ^ bit) for rank in range(size)])]
    ppermute x27, waiting for transfers between devices: 23.4 us -> 18.2 us  [tensor_swap(): lax.ppermute(array, 'tensor', [(rank, rank ^ bit) for rank in range(4)])]
where the time goes in v6:
time: 313 us; the launch traced here: 309 us
  Pallas kernels  138 us (44%)
  waiting for transfers between devices  67.6 us (22%)
  local copies, waits for them, and re-layouts  40.7 us (13%)
  starting transfers between devices  40.4 us (13%)
  between operations  15.2 us (5%)
  other arithmetic  7.56 us (2%)
    pallas_call x28, Pallas kernels, call(): pl.pallas_call(run, grid_spec=pltpu.PrefetchScalarGridSpec(num_scalar_pre...  138 us
    ppermute x17, waiting for transfers between devices, fsdp_swap(): lax.ppermute(array, 'fsdp', [(rank, rank ^ bit) for rank in range(size)])  47 us
    unnamed x168, local copies, waits for them, and re-layouts  25 us
    ppermute x17, starting transfers between devices, fsdp_swap(): lax.ppermute(array, 'fsdp', [(rank, rank ^ bit) for rank in range(size)])  23.1 us
    ppermute x27, waiting for transfers between devices, tensor_swap(): lax.ppermute(array, 'tensor', [(rank, rank ^ bit) for rank in range(4)])  18.2 us
    ppermute x27, starting transfers between devices, tensor_swap(): lax.ppermute(array, 'tensor', [(rank, rank ^ bit) for rank in range(4)])  17 us
    dynamic_update_slice x8, local copies, waits for them, and re-layouts, gather_positions(): full = lax.dynamic_update_slice_in_dim(full, piece[None], rank ^ bit, 0)  9.81 us
  transfers between devices with their start and end apart: 46, of which 19 were waited for; matrix products, arithmetic and copies ran while one was open for 7% of the time, Pallas kernels for 34%

profile of v6, /device:TPU:0, one launch (start us, length us, event | category | flops | bytes accessed | tf_op | source)
XLA Modules:
  0.0 309.2 jit_solution(16330050048265511891)
XLA Ops:
  7.3 2.5 copy.67
  9.8 2.9 collective-permute-start.1
  14.8 3.1 pack.1
  17.9 1.6 collective-permute-start.6
  19.5 2.6 collective-permute-start.7
  24.5 7.8 %collective-permute-done.7 = bf16[128,512]{1,0:T(8,128)(2,1)S(1)} collective-permute-done((bf16[128,512]{1,0:T(8,128)(2,1)}, bf16[128,512]{1,0:T(8,128)(2,1)S(1)}, u32[]{:S(2)}, u32[]{:S(2)}) %collective-permute-start.7) | collective-permute-done | bytes 131104 | tf_op jit(solution)/shard_map/ppermute | solution.py:817
  32.3 1.8 pad_maximum_fusion.1.refs_2_
  34.1 2.0 collective-permute-start.10
  38.9 1.7 bitcast_dynamic-update-slice_fusion.7
  41.7 1.5 collective-permute-start.9
  43.2 7.1 %collective-permute-done.11 = bf16[128,640]{1,0:T(8,128)(2,1)} collective-permute-done((bf16[128,640]{1,0:T(8,128)(2,1)}, bf16[128,640]{1,0:T(8,128)(2,1)}, u32[]{:S(2)}, u32[]{:S(2)}) %collective-permute-start.11) | collective-permute-done | bytes 163872 | tf_op jit(solution)/shard_map/ppermute | solution.py:817
  51.6 1.6 collective-permute-start.13
  57.4 4.6 %collective-permute-done.9.refs_3_ = bf16[4,128,512]{2,1,0:T(8,128)(2,1)S(1)} collective-permute-done((bf16[4,128,512]{2,1,0:T(8,128)(2,1)}, bf16[4,128,512]{2,1,0:T(8,128)(2,1)S(1)}, u32[]{:S(2)}, u32[]{:S(2)}) %collective-permute-start.9) | collective-permute-done | bytes 524320 | tf_op jit(solution)/shard_map/ppermute | solution.py:817
  62.0 10.0 %attend_0.1 = (f32[16,1024]{1,0:T(8,128)S(1)}, bf16[1376,1024]{1,0:T(8,128)(2,1)S(1)}, bf16[1376,1024]{1,0:T(8,128)(2,1)S(1)}, bf16[1024,384]{1,0:T(8,128)(2,1)S...) custom-call(s32[4]{0:T(128)S(1)} %copy-done.47, ...), custom_call_target="tpu_custom_call" | custom-call | flops 77552680960 | tf_op jit(solution)/shard_map/attend_0/pallas_call | solution.py:81
  77.4 9.7 %attend_1.1 = (bf16[1024,384]{1,0:T(8,128)(2,1)S(1)}, bf16[1376,384]{1,0:T(8,128)(2,1)S(1)}, bf16[1376,128]{1,0:T(8,128)(2,1)}, bf16[1376,256]{1,0:T(8,128)(2,1)S(1)}, f32[8,128]{1,0:T(8,128)S(1)}) custom-call(s32[4]{0:T(128)S(1)} %copy-done.47, s32[1376,1]{1,0:T(8,128)S(1)} %copy.55.refs_1_, bf16[4,128,640]{2,1,0:T(8,128)(2,1)S(1)} %pad_maximum_fusion.refs_1_.refs_2_, ...), custom_call_target="tpu_custom_call" | custom-call | flops 77552680960 | tf_op jit(solution)/shard_map/attend_1/pallas_call | solution.py:81
  89.9 1.6 collective-permute-start.17
  92.7 1.8 copy-done.13
  95.9 1.6 copy-done.5
  103.4 6.4 %collective-permute-done.16 = bf16[1376,128]{1,0:T(8,128)(2,1)S(1)} collective-permute-done((bf16[1376,128]{1,0:T(8,128)(2,1)S(1)}, bf16[1376,128]{1,0:T(8,128)(2,1)S(1)}, u32[]{:S(2)}, u32[]{:S(2)}) %collective-permute-start.16) | collective-permute-done | bytes 352288 | tf_op jit(solution)/shard_map/ppermute | solution.py:812
  114.6 2.4 all-gather.2.cloned.1.call-done.refs_15_.refs_16_
  116.9 27.9 %middle.1 = (bf16[4,344,1024]{2,1,0:T(8,128)(2,1)}, bf16[4,344,1024]{2,1,0:T(8,128)(2,1)}, bf16[4,344,1024]{2,1,0:T(8,128)(2,1)}, bf16[2,344,1024]{2,1,0:T(8,128...) custom-call(s32[4]{0:T(128)} %pad_add_fusion.refs_0_, ...), custom_call_target="tpu_custom_call" | custom-call | flops 14428405760 | tf_op jit(solution)/shard_map/middle/pallas_call | solution.py:81
  144.9 3.4 %collective-permute-done.23.refs_2_ = bf16[2,344,1024]{2,1,0:T(8,128)(2,1)S(1)} collective-permute-done((bf16[2,344,1024]{2,1,0:T(8,128)(2,1)}, bf16[2,344,1024]{2,1,0:T(8,128)(2,1)S(1)}, u32[]{:S(2)}, u32[]{:S(2)}) %collective-permute-start.23) | collective-permute-done | bytes 1409056 | tf_op jit(solution)/shard_map/ppermute | solution.py:812
  153.6 14.1 %matrices.1 = (bf16[1024,2048]{1,0:T(8,128)(2,1)}, f32[8,128]{1,0:T(8,128)}) custom-call(s32[4]{0:T(128)} %pad_add_fusion.refs_0_, bf16[1376,1024]{1,0:T(8,128)(2,1)} %bitcast.86, bf16[1376,1024]{1,0:T(8,128)(2,1)} %bitcast.76, bf16[1376,1024]{1,0:T(8,128)(2,1)} %bitcast.88, bf16[1376,1024]{1,0:T(8,128)(2,1)} %bitcast.87, f32[16,1024]{1,0:T(8,128)} %copy-done.21, ...), custom_call_target="tpu_custom_call" | custom-call | tf_op jit(solution)/shard_map/matrices/pallas_call | solution.py:81
  169.6 1.5 collective-permute-start.25
  174.4 5.1 %residual_back_0.1 = (bf16[344,1024]{1,0:T(8,128)(2,1)}, bf16[344,1024]{1,0:T(8,128)(2,1)}, f32[8,128]{1,0:T(8,128)}) custom-call(s32[4]{0:T(128)} %pad_add_fusion.refs_0_, bf16[344,1024]{1,0:T(8,128)(2,1)} %copy-done.34, bf16[344,1024]{1,0:T(8,128)(2,1)} %copy-done.70, bf16[4,344,1024]{2,1,0:T(8,128)(2,1)} %copy-done, ...), custom_call_target="tpu_custom_call" | custom-call | tf_op jit(solution)/shard_map/residual_back_0/pallas_call | solution.py:81
  182.0 5.9 %collective-permute-done.25.refs_2_ = bf16[344,1024]{1,0:T(8,128)(2,1)} collective-permute-done((bf16[344,1024]{1,0:T(8,128)(2,1)S(1)}, bf16[344,1024]{1,0:T(8,128)(2,1)}, u32[]{:S(2)}, u32[]{:S(2)}) %collective-permute-start.25) | collective-permute-done | bytes 704544 | tf_op jit(solution)/shard_map/ppermute | solution.py:812
  187.9 5.2 %residual_back_1.1 = (bf16[344,1024]{1,0:T(8,128)(2,1)}, bf16[344,1024]{1,0:T(8,128)(2,1)}, f32[8,128]{1,0:T(8,128)}) custom-call(s32[4]{0:T(128)} %pad_add_fusion.refs_0_, bf16[344,1024]{1,0:T(8,128)(2,1)} %copy-done.33, bf16[344,1024]{1,0:T(8,128)(2,1)} %collective-permute-done.25.refs_2_, bf16[4,344,1024]{2,1,0:T(8,128)(2,1)} %copy-done, ...), custom_call_target="tpu_custom_call" | custom-call | tf_op jit(solution)/shard_map/residual_back_1/pallas_call | solution.py:81
  193.1 1.5 collective-permute-start.27
  197.4 13.3 %attend_back_0.1 = (bf16[1376,384]{1,0:T(8,128)(2,1)S(1)}, f32[8,128]{1,0:T(8,128)S(1)}, f32[8,128]{1,0:T(8,128)}) custom-call(s32[4]{0:T(128)S(1)} %copy-done.50, s32[1376,1]{1,0:T(8,128)S(1)} %copy.55.refs_1_, bf16[1376,384]{1,0:T(8,128)(2,1)S(1)} %copy-done.66, bf16[1376,256]{1,0:T(8,128)(2,1)S(1)} %copy-done.68, bf16[1376,128]{1,0:T(8,128)(2,1)S(1)} %copy-done.46, ...), custom_call_target="tpu_custom_call" | custom-call | flops 9694085120 | tf_op jit(solution)/shard_map/attend_back_0/pallas_call | solution.py:81
  210.8 2.5 in_grad_0.1
  213.9 3.0 own_block.1
  216.9 3.1 %out_grad.1 = (bf16[4,128,256]{2,1,0:T(8,128)(2,1)S(1)}, bf16[4,128,256]{2,1,0:T(8,128)(2,1)S(1)}, f32[8,128]{1,0:T(8,128)S(1)}) custom-call(s32[4]{0:T(128)S(1)} %copy-done.50, bf16[4,344,128]{2,1,0:T(8,128)(2,1)S(1)} %bitcast.85, bf16[4,344,128]{2,1,0:T(8,128)(2,1)} %bitcast.25.refs_3_.refs_2_, bf16[344,1024]{1,0:T(8,128)(2,1)S(1)} %copy-done.14, ...), custom_call_target="tpu_custom_call" | custom-call | tf_op jit(solution)/shard_map/out_grad/pallas_call | solution.py:81
  220.0 1.6 collective-permute-start.31
  221.6 13.2 %attend_back_1.1 = (bf16[1376,384]{1,0:T(8,128)(2,1)S(1)}, f32[8,128]{1,0:T(8,128)S(1)}, f32[8,128]{1,0:T(8,128)S(1)}) custom-call(s32[4]{0:T(128)S(1)} %copy-done.50, s32[1376,1]{1,0:T(8,128)S(1)} %copy.55.refs_1_, bf16[1376,384]{1,0:T(8,128)(2,1)S(1)} %copy-done.26, bf16[1376,256]{1,0:T(8,128)(2,1)S(1)} %copy-done.32, ...), custom_call_target="tpu_custom_call" | custom-call | tf_op jit(solution)/shard_map/attend_back_1/pallas_call | solution.py:81
  236.4 5.5 %input_back.1 = (bf16[2,344,1024]{2,1,0:T(8,128)(2,1)S(1)}, bf16[2,344,1024]{2,1,0:T(8,128)(2,1)S(1)}, f32[8,1024]{1,0:T(8,128)S(1)}, f32[8,128]{1,0:T(8,128)}) custom-call(s32[4]{0:T(128)S(1)} %copy-done.50, bf16[4,344,1024]{2,1,0:T(8,128)(2,1)S(1)} %bitcast.79, bf16[4,344,384]{2,1,0:T(8,128)(2,1)S(1)} %bitcast.77, bf16[4,344,384]{2,1,0:T(8,128)(2,1)S(1)} %bitcast.78, ...), custom_call_target="tpu_custom_call" | custom-call | tf_op jit(solution)/shard_map/input_back/pallas_call | solution.py:81
  241.9 2.5 in_grad_1.1
  246.1 1.5 collective-permute-start.33
  247.6 11.7 %collective-permute-done.34.refs_2_ = bf16[4,144,384]{2,1,0:T(8,128)(2,1)S(1)} collective-permute-done((bf16[4,144,384]{2,1,0:T(8,128)(2,1)S(1)}, bf16[4,144,384]{2,1,0:T(8,128)(2,1)S(1)}, u32[]{:S(2)}, u32[]{:S(2)}) %collective-permute-start.34) | collective-permute-done | bytes 442400 | tf_op jit(solution)/shard_map/ppermute | solution.py:817
  260.0 1.6 collective-permute-start.38
  261.5 2.4 collective-permute-start.39
  265.0 2.3 collective-permute-done.38.refs_3_
  268.3 4.7 %collective-permute-done.39.refs_4_ = bf16[144,384]{1,0:T(8,128)(2,1)S(1)} collective-permute-done((bf16[144,384]{1,0:T(8,128)(2,1)S(1)}, bf16[144,384]{1,0:T(8,128)(2,1)S(1)}, u32[]{:S(2)}, u32[]{:S(2)}) %collective-permute-start.39) | collective-permute-done | bytes 110624 | tf_op jit(solution)/shard_map/ppermute | solution.py:817
  273.1 2.3 collective-permute-start.37
  277.4 3.0 input_grad.1
  280.4 5.6 %collective-permute-done.36.refs_3_ = bf16[128,640]{1,0:T(8,128)(2,1)S(1)} collective-permute-done((bf16[128,640]{1,0:T(8,128)(2,1)S(1)}, bf16[128,640]{1,0:T(8,128)(2,1)S(1)}, u32[]{:S(2)}, u32[]{:S(2)}) %collective-permute-start.36) | collective-permute-done | bytes 163872 | tf_op jit(solution)/shard_map/ppermute | solution.py:817
  289.2 2.2 adam_expand.1
  293.6 2.3 adam_contract.1
  297.8 2.0 adam_in.1
  (274 shorter events, 68.8 us)
Async XLA Ops:
  7.2 109.7 %all-gather.2.cloned.1.call-start = ((), (), s32[]{:S(2)}) async-start(), calls=%async_computation.1 | async-start | bytes 4718592 | tf_op jit(solution)/shard_map/all_gather | solution.py:885
  9.8 28.7 %collective-permute-start.1 = (bf16[344,1024]{1,0:T(8,128)(2,1)}, bf16[344,1024]{1,0:T(8,128)(2,1)}, u32[]{:S(2)}, u32[]{:S(2)}) collective-permute-start(bf16[344,1024]{1,0:T(8,128)(2,1)} %bitcast.74), channel_id=1, source_target_pairs={{0,2},{1,3},{2,0},{3,1},{4,6},{5,7},{6,4},{7,5},{8,10},{9,11},{10,... | collective-permute-start | bytes 2113544 | tf_op jit(solution)/shard_map/ppermute | solution.py:812
  17.9 6.6 %collective-permute-start.6 = (bf16[128,512]{1,0:T(8,128)(2,1)}, bf16[128,512]{1,0:T(8,128)(2,1)S(1)}, u32[]{:S(2)}, u32[]{:S(2)}) collective-permute-start(bf16[128,512]{1,0:T(8,128)(2,1)} %get-tuple-element.133), channel_id=1, source_target_pairs={{0,8},{4,12},{8,0},{12,4},{16,24},{20,28},{24,16},{28,20},{1,9},{5... | collective-permute-start | bytes 393224 | tf_op jit(solution)/shard_map/ppermute | solution.py:817
  19.5 12.9 %collective-permute-start.7 = (bf16[128,512]{1,0:T(8,128)(2,1)}, bf16[128,512]{1,0:T(8,128)(2,1)S(1)}, u32[]{:S(2)}, u32[]{:S(2)}) collective-permute-start(bf16[128,512]{1,0:T(8,128)(2,1)} %get-tuple-element.133), channel_id=1, source_target_pairs={{0,16},{4,20},{8,24},{12,28},{16,0},{20,4},{24,8},{28,12},{1,17},{... | collective-permute-start | bytes 393224 | tf_op jit(solution)/shard_map/ppermute | solution.py:817
  22.1 10.3 %collective-permute-start.8 = (bf16[128,512]{1,0:T(8,128)(2,1)}, bf16[128,512]{1,0:T(8,128)(2,1)S(1)}, u32[]{:S(2)}, u32[]{:S(2)}) collective-permute-start(bf16[128,512]{1,0:T(8,128)(2,1)} %get-tuple-element.133), channel_id=1, source_target_pairs={{0,24},{4,28},{8,16},{12,20},{16,8},{20,12},{24,0},{28,4},{1,25},{... | collective-permute-start | bytes 393224 | tf_op jit(solution)/shard_map/ppermute | solution.py:817
  22.3 30.9 %collective-permute-start = (bf16[344,1024]{1,0:T(8,128)(2,1)}, bf16[344,1024]{1,0:T(8,128)(2,1)}, u32[]{:S(2)}, u32[]{:S(2)}) collective-permute-start(bf16[344,1024]{1,0:T(8,128)(2,1)} %bitcast.74), channel_id=1, source_target_pairs={{0,1},{1,0},{2,3},{3,2},{4,5},{5,4},{6,7},{7,6},{8,9},{9,8},{10,11... | collective-permute-start | bytes 2113544 | tf_op jit(solution)/shard_map/ppermute | solution.py:812
  34.1 7.6 %collective-permute-start.10 = (bf16[128,640]{1,0:T(8,128)(2,1)}, bf16[128,640]{1,0:T(8,128)(2,1)}, u32[]{:S(2)}, u32[]{:S(2)}) collective-permute-start(bf16[128,640]{1,0:T(8,128)(2,1)} %get-tuple-element.136), channel_id=1, source_target_pairs={{0,8},{4,12},{8,0},{12,4},{16,24},{20,28},{24,16},{28,20},{1,9},{5... | collective-permute-start | bytes 491528 | tf_op jit(solution)/shard_map/ppermute | solution.py:817
  36.1 14.2 %collective-permute-start.11 = (bf16[128,640]{1,0:T(8,128)(2,1)}, bf16[128,640]{1,0:T(8,128)(2,1)}, u32[]{:S(2)}, u32[]{:S(2)}) collective-permute-start(bf16[128,640]{1,0:T(8,128)(2,1)} %get-tuple-element.136), channel_id=1, source_target_pairs={{0,16},{4,20},{8,24},{12,28},{16,0},{20,4},{24,8},{28,12},{1,17},{... | collective-permute-start | bytes 491528 | tf_op jit(solution)/shard_map/ppermute | solution.py:817
  37.1 13.2 %collective-permute-start.12 = (bf16[128,640]{1,0:T(8,128)(2,1)}, bf16[128,640]{1,0:T(8,128)(2,1)}, u32[]{:S(2)}, u32[]{:S(2)}) collective-permute-start(bf16[128,640]{1,0:T(8,128)(2,1)} %get-tuple-element.136), channel_id=1, source_target_pairs={{0,24},{4,28},{8,16},{12,20},{16,8},{20,12},{24,0},{28,4},{1,25},{... | collective-permute-start | bytes 491528 | tf_op jit(solution)/shard_map/ppermute | solution.py:817
  38.5 16.9 %collective-permute-start.2 = (bf16[344,1024]{1,0:T(8,128)(2,1)}, bf16[344,1024]{1,0:T(8,128)(2,1)}, u32[]{:S(2)}, u32[]{:S(2)}) collective-permute-start(bf16[344,1024]{1,0:T(8,128)(2,1)} %collective-permute-done.1), channel_id=1, source_target_pairs={{0,1},{1,0},{2,3},{3,2},{4,5},{5,4},{6,7},{7,6},{8,9},{9,8},{10,11... | collective-permute-start | bytes 2113544 | tf_op jit(solution)/shard_map/ppermute | solution.py:812
  40.9 21.1 %copy-start.47 = (s32[4]{0:T(128)S(1)}, s32[4]{0:T(128)}, u32[]{:S(2)}) copy-start(s32[4]{0:T(128)} %pad_add_fusion.refs_0_) | copy-start | bytes 52
  41.0 247.1 %reduce-scatter.2.cloned.1.call-start = ((), (), s32[]{:S(2)}) async-start(), calls=%async_computation.2 | async-start | bytes 4718592 | tf_op jit(solution)/shard_map/reduce_scatter | solution.py:948
  41.7 20.3 %collective-permute-start.9 = (bf16[4,128,512]{2,1,0:T(8,128)(2,1)}, bf16[4,128,512]{2,1,0:T(8,128)(2,1)S(1)}, u32[]{:S(2)}, u32[]{:S(2)}) collective-permute-start(bf16[4,128,512]{2,1,0:T(8,128)(2,1)} %pad_maximum_fusion.1.refs_2_), channel_id=1, source_target_pairs={{0,4},{4,0},{8,12},{12,8},{16,20},{20,16},{24,28},{28,24},{1,5},{5... | collective-permute-start | bytes 1572872 | tf_op jit(solution)/shard_map/ppermute | solution.py:817
  51.6 23.9 %collective-permute-start.13 = (bf16[4,128,640]{2,1,0:T(8,128)(2,1)S(1)}, bf16[4,128,640]{2,1,0:T(8,128)(2,1)S(1)}, u32[]{:S(2)}, u32[]{:S(2)}) collective-permute-start(bf16[4,128,640]{2,1,0:T(8,128)(2,1)S(1)} %pad_maximum_fusion.refs_1_.refs_2_), channel_id=1, source_target_pairs={{0,4},{4,0},{8,12},{12,8},{16,20},{20,16},{24,28},{28,24},{1,5},{5... | collective-permute-start | bytes 1966088 | tf_op jit(solution)/shard_map/ppermute | solution.py:817
  56.6 44.9 %collective-permute-start.3 = (bf16[344,1024]{1,0:T(8,128)(2,1)}, bf16[344,1024]{1,0:T(8,128)(2,1)}, u32[]{:S(2)}, u32[]{:S(2)}) collective-permute-start(bf16[344,1024]{1,0:T(8,128)(2,1)} %fusion), channel_id=1, source_target_pairs={{0,1},{1,0},{2,3},{3,2},{4,5},{5,4},{6,7},{7,6},{8,9},{9,8},{10,11... | collective-permute-start | bytes 2113544 | tf_op jit(solution)/shard_map/ppermute | solution.py:812
  56.7 34.7 %collective-permute-start.4 = (bf16[344,1024]{1,0:T(8,128)(2,1)}, bf16[344,1024]{1,0:T(8,128)(2,1)}, u32[]{:S(2)}, u32[]{:S(2)}) collective-permute-start(bf16[344,1024]{1,0:T(8,128)(2,1)} %fusion), channel_id=1, source_target_pairs={{0,2},{1,3},{2,0},{3,1},{4,6},{5,7},{6,4},{7,5},{8,10},{9,11},{10,... | collective-permute-start | bytes 2113544 | tf_op jit(solution)/shard_map/ppermute | solution.py:812
  76.9 24.6 %collective-permute-start.21 = (bf16[1024,256]{1,0:T(8,128)(2,1)}, bf16[1024,256]{1,0:T(8,128)(2,1)}, u32[]{:S(2)}, u32[]{:S(2)}) collective-permute-start(bf16[1024,256]{1,0:T(8,128)(2,1)} %get-tuple-element.142.refs_10_.refs_9_), channel_id=1, source_target_pairs={{0,2},{1,3},{2,0},{3,1},{4,6},{5,7},{6,4},{7,5},{8,10},{9,11},{10,... | collective-permute-start | bytes 1572872 | tf_op jit(solution)/shard_map/ppermute | solution.py:812
  89.9 9.7 %collective-permute-start.17 = (bf16[1376,128]{1,0:T(8,128)(2,1)}, bf16[1376,128]{1,0:T(8,128)(2,1)}, u32[]{:S(2)}, u32[]{:S(2)}) collective-permute-start(bf16[1376,128]{1,0:T(8,128)(2,1)} %get-tuple-element.141.refs_4_), channel_id=1, source_target_pairs={{0,2},{1,3},{2,0},{3,1},{4,6},{5,7},{6,4},{7,5},{8,10},{9,11},{10,... | collective-permute-start | bytes 1056776 | tf_op jit(solution)/shard_map/ppermute | solution.py:812
  91.4 18.4 %collective-permute-start.5 = (bf16[344,1024]{1,0:T(8,128)(2,1)}, bf16[344,1024]{1,0:T(8,128)(2,1)}, u32[]{:S(2)}, u32[]{:S(2)}) collective-permute-start(bf16[344,1024]{1,0:T(8,128)(2,1)} %collective-permute-done.4), channel_id=1, source_target_pairs={{0,1},{1,0},{2,3},{3,2},{4,5},{5,4},{6,7},{7,6},{8,9},{9,8},{10,11... | collective-permute-start | bytes 2113544 | tf_op jit(solution)/shard_map/ppermute | solution.py:812
  91.4 11.8 %collective-permute-start.15 = (bf16[1376,128]{1,0:T(8,128)(2,1)}, bf16[1376,128]{1,0:T(8,128)(2,1)S(1)}, u32[]{:S(2)}, u32[]{:S(2)}) collective-permute-start(bf16[1376,128]{1,0:T(8,128)(2,1)} %get-tuple-element.141.refs_4_), channel_id=1, source_target_pairs={{0,1},{1,0},{2,3},{3,2},{4,5},{5,4},{6,7},{7,6},{8,9},{9,8},{10,11... | collective-permute-start | bytes 1056776 | tf_op jit(solution)/shard_map/ppermute | solution.py:812
  99.6 10.2 %collective-permute-start.16 = (bf16[1376,128]{1,0:T(8,128)(2,1)S(1)}, bf16[1376,128]{1,0:T(8,128)(2,1)S(1)}, u32[]{:S(2)}, u32[]{:S(2)}) collective-permute-start(bf16[1376,128]{1,0:T(8,128)(2,1)S(1)} %copy-done.45), channel_id=1, source_target_pairs={{0,2},{1,3},{2,0},{3,1},{4,6},{5,7},{6,4},{7,5},{8,10},{9,11},{10,... | collective-permute-start | bytes 1056776 | tf_op jit(solution)/shard_map/ppermute | solution.py:812
  101.5 11.2 %collective-permute-start.20 = (bf16[1024,256]{1,0:T(8,128)(2,1)}, bf16[1024,256]{1,0:T(8,128)(2,1)}, u32[]{:S(2)}, u32[]{:S(2)}) collective-permute-start(bf16[1024,256]{1,0:T(8,128)(2,1)} %get-tuple-element.142.refs_10_.refs_9_), channel_id=1, source_target_pairs={{0,1},{1,0},{2,3},{3,2},{4,5},{5,4},{6,7},{7,6},{8,9},{9,8},{10,11... | collective-permute-start | bytes 1572872 | tf_op jit(solution)/shard_map/ppermute | solution.py:812
  101.5 13.0 %collective-permute-start.22 = (bf16[1024,256]{1,0:T(8,128)(2,1)}, bf16[1024,256]{1,0:T(8,128)(2,1)}, u32[]{:S(2)}, u32[]{:S(2)}) collective-permute-start(bf16[1024,256]{1,0:T(8,128)(2,1)} %collective-permute-done.21.refs_12_), channel_id=1, source_target_pairs={{0,1},{1,0},{2,3},{3,2},{4,5},{5,4},{6,7},{7,6},{8,9},{9,8},{10,11... | collective-permute-start | bytes 1572872 | tf_op jit(solution)/shard_map/ppermute | solution.py:812
  103.2 9.4 %collective-permute-start.14 = (bf16[1376,128]{1,0:T(8,128)(2,1)S(1)}, bf16[1376,128]{1,0:T(8,128)(2,1)S(1)}, u32[]{:S(2)}, u32[]{:S(2)}) collective-permute-start(bf16[1376,128]{1,0:T(8,128)(2,1)S(1)} %copy-done.45), channel_id=1, source_target_pairs={{0,1},{1,0},{2,3},{3,2},{4,5},{5,4},{6,7},{7,6},{8,9},{9,8},{10,11... | collective-permute-start | bytes 1056776 | tf_op jit(solution)/shard_map/ppermute | solution.py:812
  109.8 2.9 collective-permute-start.19
  109.8 2.9 collective-permute-start.18
  116.9 31.3 %copy-start.48 = (s32[4]{0:T(128)S(1)}, s32[4]{0:T(128)}, u32[]{:S(2)}) copy-start(s32[4]{0:T(128)} %pad_add_fusion.refs_0_) | copy-start | bytes 52
  144.8 3.5 %collective-permute-start.23 = (bf16[2,344,1024]{2,1,0:T(8,128)(2,1)}, bf16[2,344,1024]{2,1,0:T(8,128)(2,1)S(1)}, u32[]{:S(2)}, u32[]{:S(2)}) collective-permute-start(bf16[2,344,1024]{2,1,0:T(8,128)(2,1)} %get-tuple-element.149), channel_id=1, source_target_pairs={{0,1},{1,0},{2,3},{3,2},{4,5},{5,4},{6,7},{7,6},{8,9},{9,8},{10,11... | collective-permute-start | bytes 4227080 | tf_op jit(solution)/shard_map/ppermute | solution.py:812
  150.8 17.8 %collective-permute-start.24 = (bf16[344,1024]{1,0:T(8,128)(2,1)S(1)}, bf16[344,1024]{1,0:T(8,128)(2,1)S(1)}, u32[]{:S(2)}, u32[]{:S(2)}) collective-permute-start(bf16[344,1024]{1,0:T(8,128)(2,1)S(1)} %get-tuple-element.150.refs_1_), channel_id=1, source_target_pairs={{0,2},{1,3},{2,0},{3,1},{4,6},{5,7},{6,4},{7,5},{8,10},{9,11},{10,... | collective-permute-start | bytes 2113544 | tf_op jit(solution)/shard_map/ppermute | solution.py:812
  169.5 10.2 %collective-permute-start.26 = (bf16[2,344,1024]{2,1,0:T(8,128)(2,1)}, bf16[2,344,1024]{2,1,0:T(8,128)(2,1)S(1)}, u32[]{:S(2)}, u32[]{:S(2)}) collective-permute-start(bf16[2,344,1024]{2,1,0:T(8,128)(2,1)} %get-tuple-element.160), channel_id=1, source_target_pairs={{0,1},{1,0},{2,3},{3,2},{4,5},{5,4},{6,7},{7,6},{8,9},{9,8},{10,11... | collective-permute-start | bytes 4227080 | tf_op jit(solution)/shard_map/ppermute | solution.py:812
  169.6 18.3 %collective-permute-start.25 = (bf16[344,1024]{1,0:T(8,128)(2,1)S(1)}, bf16[344,1024]{1,0:T(8,128)(2,1)}, u32[]{:S(2)}, u32[]{:S(2)}) collective-permute-start(bf16[344,1024]{1,0:T(8,128)(2,1)S(1)} %get-tuple-element.157.refs_1_), channel_id=1, source_target_pairs={{0,2},{1,3},{2,0},{3,1},{4,6},{5,7},{6,4},{7,5},{8,10},{9,11},{10,... | collective-permute-start | bytes 2113544 | tf_op jit(solution)/shard_map/ppermute | solution.py:812
  179.5 15.2 %collective-permute-start.28 = (bf16[344,1024]{1,0:T(8,128)(2,1)}, bf16[344,1024]{1,0:T(8,128)(2,1)S(1)}, u32[]{:S(2)}, u32[]{:S(2)}) collective-permute-start(bf16[344,1024]{1,0:T(8,128)(2,1)} %get-tuple-element.170.refs_5_.refs_3_), channel_id=1, source_target_pairs={{0,1},{1,0},{2,3},{3,2},{4,5},{5,4},{6,7},{7,6},{8,9},{9,8},{10,11... | collective-permute-start | bytes 2113544 | tf_op jit(solution)/shard_map/ppermute | solution.py:812
  193.1 2.4 collective-permute-start.29
  193.1 20.7 %collective-permute-start.27 = (bf16[344,1024]{1,0:T(8,128)(2,1)}, bf16[344,1024]{1,0:T(8,128)(2,1)S(1)}, u32[]{:S(2)}, u32[]{:S(2)}) collective-permute-start(bf16[344,1024]{1,0:T(8,128)(2,1)} %copy-done.62), channel_id=1, source_target_pairs={{0,2},{1,3},{2,0},{3,1},{4,6},{5,7},{6,4},{7,5},{8,10},{9,11},{10,... | collective-permute-start | bytes 2113544 | tf_op jit(solution)/shard_map/ppermute | solution.py:812
  213.2 22.4 %collective-permute-start.30 = (bf16[4,128,384]{2,1,0:T(8,128)(2,1)S(1)}, bf16[4,128,384]{2,1,0:T(8,128)(2,1)S(1)}, u32[]{:S(2)}, u32[]{:S(2)}) collective-permute-start(bf16[4,128,384]{2,1,0:T(8,128)(2,1)S(1)} %get-tuple-element.185), channel_id=1, source_target_pairs={{0,4},{4,0},{8,12},{12,8},{16,20},{20,16},{24,28},{28,24},{1,5},{5... | collective-permute-start | bytes 1179656 | tf_op jit(solution)/shard_map/ppermute | solution.py:817
  220.0 15.6 %collective-permute-start.31 = (bf16[4,128,256]{2,1,0:T(8,128)(2,1)S(1)}, bf16[4,128,256]{2,1,0:T(8,128)(2,1)S(1)}, u32[]{:S(2)}, u32[]{:S(2)}) collective-permute-start(bf16[4,128,256]{2,1,0:T(8,128)(2,1)S(1)} %get-tuple-element.187), channel_id=1, source_target_pairs={{0,4},{4,0},{8,12},{12,8},{16,20},{20,16},{24,28},{28,24},{1,5},{5... | collective-permute-start | bytes 786440 | tf_op jit(solution)/shard_map/ppermute | solution.py:817
  241.9 3.2 %collective-permute-start.32 = (bf16[2,344,1024]{2,1,0:T(8,128)(2,1)S(1)}, bf16[2,344,1024]{2,1,0:T(8,128)(2,1)S(1)}, u32[]{:S(2)}, u32[]{:S(2)}) collective-permute-start(bf16[2,344,1024]{2,1,0:T(8,128)(2,1)S(1)} %get-tuple-element.191), channel_id=1, source_target_pairs={{0,1},{1,0},{2,3},{3,2},{4,5},{5,4},{6,7},{7,6},{8,9},{9,8},{10,11... | collective-permute-start | bytes 4227080 | tf_op jit(solution)/shard_map/ppermute | solution.py:812
  244.4 14.9 %collective-permute-start.34 = (bf16[4,144,384]{2,1,0:T(8,128)(2,1)S(1)}, bf16[4,144,384]{2,1,0:T(8,128)(2,1)S(1)}, u32[]{:S(2)}, u32[]{:S(2)}) collective-permute-start(bf16[4,144,384]{2,1,0:T(8,128)(2,1)S(1)} %get-tuple-element.200), channel_id=1, source_target_pairs={{0,4},{4,0},{8,12},{12,8},{16,20},{20,16},{24,28},{28,24},{1,5},{5... | collective-permute-start | bytes 1327112 | tf_op jit(solution)/shard_map/ppermute | solution.py:817
  246.1 31.2 %collective-permute-start.33 = (bf16[344,1024]{1,0:T(8,128)(2,1)S(1)}, bf16[344,1024]{1,0:T(8,128)(2,1)S(1)}, u32[]{:S(2)}, u32[]{:S(2)}) collective-permute-start(bf16[344,1024]{1,0:T(8,128)(2,1)S(1)} %get-tuple-element.198), channel_id=1, source_target_pairs={{0,2},{1,3},{2,0},{3,1},{4,6},{5,7},{6,4},{7,5},{8,10},{9,11},{10,... | collective-permute-start | bytes 2113544 | tf_op jit(solution)/shard_map/ppermute | solution.py:812
  260.0 7.3 %collective-permute-start.38 = (bf16[144,384]{1,0:T(8,128)(2,1)S(1)}, bf16[144,384]{1,0:T(8,128)(2,1)S(1)}, u32[]{:S(2)}, u32[]{:S(2)}) collective-permute-start(bf16[144,384]{1,0:T(8,128)(2,1)S(1)} %get-tuple-element.211), channel_id=1, source_target_pairs={{0,8},{4,12},{8,0},{12,4},{16,24},{20,28},{24,16},{28,20},{1,9},{5... | collective-permute-start | bytes 331784 | tf_op jit(solution)/shard_map/ppermute | solution.py:817
  261.5 11.6 %collective-permute-start.39 = (bf16[144,384]{1,0:T(8,128)(2,1)S(1)}, bf16[144,384]{1,0:T(8,128)(2,1)S(1)}, u32[]{:S(2)}, u32[]{:S(2)}) collective-permute-start(bf16[144,384]{1,0:T(8,128)(2,1)S(1)} %get-tuple-element.212), channel_id=1, source_target_pairs={{0,16},{4,20},{8,24},{12,28},{16,0},{20,4},{24,8},{28,12},{1,17},{... | collective-permute-start | bytes 331784 | tf_op jit(solution)/shard_map/ppermute | solution.py:817
  263.9 11.5 %collective-permute-start.40 = (bf16[144,384]{1,0:T(8,128)(2,1)S(1)}, bf16[144,384]{1,0:T(8,128)(2,1)S(1)}, u32[]{:S(2)}, u32[]{:S(2)}) collective-permute-start(bf16[144,384]{1,0:T(8,128)(2,1)S(1)} %get-tuple-element.213), channel_id=1, source_target_pairs={{0,24},{4,28},{8,16},{12,20},{16,8},{20,12},{24,0},{28,4},{1,25},{... | collective-permute-start | bytes 331784 | tf_op jit(solution)/shard_map/ppermute | solution.py:817
  264.4 16.0 %collective-permute-start.35 = (bf16[128,640]{1,0:T(8,128)(2,1)S(1)}, bf16[128,640]{1,0:T(8,128)(2,1)S(1)}, u32[]{:S(2)}, u32[]{:S(2)}) collective-permute-start(bf16[128,640]{1,0:T(8,128)(2,1)S(1)} %get-tuple-element.205), channel_id=1, source_target_pairs={{0,8},{4,12},{8,0},{12,4},{16,24},{20,28},{24,16},{28,20},{1,9},{5... | collective-permute-start | bytes 491528 | tf_op jit(solution)/shard_map/ppermute | solution.py:817
  267.3 18.7 %collective-permute-start.36 = (bf16[128,640]{1,0:T(8,128)(2,1)S(1)}, bf16[128,640]{1,0:T(8,128)(2,1)S(1)}, u32[]{:S(2)}, u32[]{:S(2)}) collective-permute-start(bf16[128,640]{1,0:T(8,128)(2,1)S(1)} %get-tuple-element.206), channel_id=1, source_target_pairs={{0,16},{4,20},{8,24},{12,28},{16,0},{20,4},{24,8},{28,12},{1,17},{... | collective-permute-start | bytes 491528 | tf_op jit(solution)/shard_map/ppermute | solution.py:817
  273.1 12.9 %collective-permute-start.37 = (bf16[128,640]{1,0:T(8,128)(2,1)S(1)}, bf16[128,640]{1,0:T(8,128)(2,1)S(1)}, u32[]{:S(2)}, u32[]{:S(2)}) collective-permute-start(bf16[128,640]{1,0:T(8,128)(2,1)S(1)} %get-tuple-element.207), channel_id=1, source_target_pairs={{0,24},{4,28},{8,16},{12,20},{16,8},{20,12},{24,0},{28,4},{1,25},{... | collective-permute-start | bytes 491528 | tf_op jit(solution)/shard_map/ppermute | solution.py:817
  295.9 3.9 %collective-permute-start.41 = (f32[16,128]{1,0:T(8,128)S(1)}, f32[16,128]{1,0:T(8,128)S(1)}, u32[]{:S(2)}, u32[]{:S(2)}) collective-permute-start(f32[16,128]{1,0:T(8,128)S(1)} %convert_add_fusion), channel_id=1, source_target_pairs={{0,1},{1,0},{2,3},{3,2},{4,5},{5,4},{6,7},{7,6},{8,9},{9,8},{10,11... | collective-permute-start | bytes 24584 | tf_op jit(solution)/shard_map/ppermute | solution.py:812
  295.9 3.9 %collective-permute-start.42 = (f32[16,128]{1,0:T(8,128)S(1)}, f32[16,128]{1,0:T(8,128)S(1)}, u32[]{:S(2)}, u32[]{:S(2)}) collective-permute-start(f32[16,128]{1,0:T(8,128)S(1)} %convert_add_fusion), channel_id=1, source_target_pairs={{0,2},{1,3},{2,0},{3,1},{4,6},{5,7},{6,4},{7,5},{8,10},{9,11},{10,... | collective-permute-start | bytes 24584 | tf_op jit(solution)/shard_map/ppermute | solution.py:812
  297.4 3.1 collective-permute-start.43
  (81 other events, 615.5 us)
Sparse Core Ops, SparseCore 0:
  41.1 75.8 all-gather.1
  169.6 94.4 reduce-scatter.1
